TPU v7x, 32 devices: a whole 2x2x4 slice. The times are simulated.
32 devices in a mesh: groups: 2 (over x), leaf: 4 (over y, core), inner: 4 (over z).
Axes of the slice: x: 2, y: 2, z: 4, core: 2. Of those that a mesh axis runs over, the one named last changes fastest.
Arguments:
- anomalies: bfloat16 [65536, 256], P(('leaf', 'inner'), 'groups'), parts along dimension 1, may hold values from -6 to 6
- leaf_basis: bfloat16 [128, 64, 512], P(('leaf', 'inner')), may hold values from -0.25 to 0.25
- near_blocks: bfloat16 [128, 5, 512, 512], P(('leaf', 'inner')), may hold values from -0.125 to 0.125
- near_ids: int32 [128, 5], P(('leaf', 'inner')), may hold values from 0 to 127, as said below
- transfer_leaf: bfloat16 [128, 64, 64], P(('leaf', 'inner')), may hold values from -0.25 to 0.25
- transfer_mid: bfloat16 [16, 64, 64], P(('leaf', 'inner')), may hold values from -0.375 to 0.375
- far_ids: int32 [16, 4], P(('leaf', 'inner')), may hold values from 0 to 15, as said below
- far_count: int32 [16], P(('leaf', 'inner')), may hold values from 1 to 4
- mid_couple: bfloat16 [16, 4, 64, 64], P(('leaf', 'inner')), may hold values from -0.375 to 0.375
- top_couple: bfloat16 [4, 4, 64, 64], P('leaf'), may hold values from -0.375 to 0.375
Outputs:
- localized: bfloat16 [65536, 256], P(('leaf', 'inner'), 'groups'), parts along dimension 1
There are 2 independent parts, one for each index of `groups`. A program takes and returns all parts, laid end to end along the dimension named above; an argument that names none is the same for every part. Nothing has to cross between parts.
Inputs may be any that keep to these rules, and one draw needn't show every extreme that they name: `near_ids`: slot 0 of leaf l is l itself; the other slots name leaves at most 8 leaves away from l, repeats allowed. `far_ids`: the partners of cluster c are distinct, differ from c - 1, c and c + 1, and lie in row groups c // 4 - 1 to c // 4 + 1 (row group of d: d // 4); slots from far_count[c] on are ignored.
All inputs are finite; a program needn't handle non-finite values.
Results may differ from a plain program's by a relative error of at most 0.0065.
Values may be sent and summed in bfloat16 or wider, within the bound.
No kernel may reach another device: no remote copies, remote signals or barrier semaphores. Data moves between devices by JAX's collectives and lax.ppermute only.
A program may use at most 128 MiB of HBM per device.

v0:
```python
import jax
import jax.numpy as jnp
from jax import lax
from jax.sharding import PartitionSpec as P


def padded(x, sides, width):
    for axis, dim in sides:
        count, length = (lax.axis_size(axis), x.shape[dim])
        up = [(i, (i + 1) % count) for i in range(count - 1)]
        down = [(j, i) for i, j in up]
        last = lax.slice_in_dim(x, length - width, length, axis=dim)
        first = lax.slice_in_dim(x, 0, width, axis=dim)
        before = lax.ppermute(last, axis, up)
        after = lax.ppermute(first, axis, down)
        x = jnp.concatenate([before, x, after], axis=dim)
    return x


def local(
    anomalies,
    leaf_basis,
    near_blocks,
    near_ids,
    transfer_leaf,
    transfer_mid,
    far_ids,
    far_count,
    mid_couple,
    top_couple,
):
    leaf_dev = leaf_basis.shape[0]
    leaf_rows = leaf_basis.shape[2]
    columns = anomalies.shape[1]
    far_slots = far_ids.shape[1]
    inner_size = lax.axis_size("inner")
    leaf_size = lax.axis_size("leaf")
    row_group = lax.axis_index("leaf")
    cluster = row_group * inner_size + lax.axis_index("inner")
    blocks = anomalies.reshape(leaf_dev, leaf_rows, columns)
    skeleton = jnp.einsum(
        "lri,lin->lrn", leaf_basis, blocks, preferred_element_type=jnp.float32
    ).astype(jnp.bfloat16)
    mid_skel = jnp.einsum(
        "lrs,lrn->sn", transfer_leaf, skeleton, preferred_element_type=jnp.float32
    ).astype(jnp.bfloat16)
    mid_map = transfer_mid[0]
    top_term = jnp.einsum("rs,rn->sn", mid_map, mid_skel, preferred_element_type=jnp.float32)
    summed = lax.psum(top_term.astype(jnp.bfloat16), "inner")
    top_skel = lax.all_gather(summed[None], "leaf", axis=0, tiled=True)
    group_ids = jnp.arange(leaf_size, dtype=jnp.int32)
    admissible = (jnp.abs(group_ids - row_group) >= 2).astype(jnp.bfloat16)
    coupling = top_couple[0] * admissible[:, None, None]
    top_down = jnp.einsum(
        "hrs,hsn->rn", coupling, top_skel, preferred_element_type=jnp.float32
    ).astype(jnp.bfloat16)
    group_mids = lax.all_gather(mid_skel[None], "inner", axis=0, tiled=True)
    window = padded(group_mids, (("leaf", 0),), inner_size)
    far_local = far_ids[0] - (row_group - 1) * inner_size
    chosen = window[far_local]
    partial_terms = jnp.einsum(
        "krs,ksn->krn", mid_couple[0], chosen, preferred_element_type=jnp.float32
    )
    live_slots = jnp.arange(far_slots, dtype=jnp.int32) < far_count[0]
    far_sum = jnp.sum(jnp.where(live_slots[:, None, None], partial_terms, 0.0), axis=0)
    parent_term = jnp.dot(mid_map, top_down, preferred_element_type=jnp.float32)
    mid_down = (far_sum + parent_term).astype(jnp.bfloat16)
    leaf_down = jnp.einsum(
        "lrs,sn->lrn", transfer_leaf, mid_down, preferred_element_type=jnp.float32
    ).astype(jnp.bfloat16)
    far_out = jnp.einsum("lri,lrn->lin", leaf_basis, leaf_down, preferred_element_type=jnp.float32)
    extended = padded(blocks, ((("leaf", "inner"), 0),), leaf_dev)
    first_leaf = cluster * leaf_dev - leaf_dev
    near_local = near_ids - first_leaf
    picked = extended[near_local]
    near_out = jnp.einsum("lkij,lkjn->lin", near_blocks, picked, preferred_element_type=jnp.float32)
    return (far_out + near_out).astype(jnp.bfloat16).reshape(leaf_dev * leaf_rows, columns)


def solution(mesh):
    return jax.shard_map(
        local,
        mesh=mesh,
        in_specs=(
            P(("leaf", "inner"), "groups"),
            P(("leaf", "inner"), None, None),
            P(("leaf", "inner"), None, None, None),
            P(("leaf", "inner"), None),
            P(("leaf", "inner"), None, None),
            P(("leaf", "inner"), None, None),
            P(("leaf", "inner"), None),
            P(("leaf", "inner")),
            P(("leaf", "inner"), None, None, None),
            P("leaf", None, None, None),
        ),
        out_specs=P(("leaf", "inner"), "groups"),
        check_vma=False,
    )
```

profile of v0, /device:TPU:1, one launch (start us, length us, event | category | flops | bytes accessed | tf_op | source)
XLA Modules:
  0.0 120.5 jit_solution(3168874302598981733)
XLA Ops:
  0.0 0.0 copy-start
  0.0 1.0 copy-done
  1.0 1.7 %fusion.9 = bf16[128,64]{0,1:T(8,128)(2,1)S(1)} fusion(bf16[8,64,64]{2,1,0:T(8,128)(2,1)} %param.14, bf16[8,64,512]{2,1,0:T(8,128)(2,1)S(1)} %copy-done, bf16[8,512,128]{2,1,0:T(8,128)(2,1)} %bitcast.65), kind=kOutput, calls=%fused_computation.18 | convolution fusion | flops 75571200 | bytes 1654784 | tf_op jit(solution)/shard_map/lrs,lrn->sn/dot_general | solution.py:44
  2.7 11.8 %all-gather = bf16[256,128]{1,0:T(8,128)(2,1)S(1)} all-gather(bf16[64,128]{1,0:T(8,128)(2,1)S(1)} %bitcast.72), channel_id=2, replica_groups=mesh['groups'=2,'leaf'=4,'inner'=4] {'inner'}, dimensions={0}, use_global_device_ids=true | all-gather | bytes 81920 | tf_op jit(solution)/shard_map/all_gather | solution.py:57
  14.5 5.1 %collective-permute-start.1 = (bf16[4,64,128]{2,1,0:T(8,128)(2,1)S(1)}, bf16[4,64,128]{2,1,0:T(8,128)(2,1)S(1)}, u32[]{:S(2)}, u32[]{:S(2)}) collective-permute-start(bf16[4,64,128]{2,1,0:T(8,128)(2,1)S(1)} %bitcast.69), channel_id=1, source_target_pairs={{4,0},{8,4},{12,8},{5,1},{9,5},{13,9},{6,2},{10,6},{14,10},{7,3},{... | collective-permute-start | bytes 196616 | tf_op jit(solution)/shard_map/ppermute | solution.py:15
  19.6 3.0 %collective-permute-start = (bf16[4,64,128]{2,1,0:T(8,128)(2,1)S(1)}, bf16[4,64,128]{2,1,0:T(8,128)(2,1)S(1)}, u32[]{:S(2)}, u32[]{:S(2)}) collective-permute-start(bf16[4,64,128]{2,1,0:T(8,128)(2,1)S(1)} %bitcast.70), channel_id=1, source_target_pairs={{0,4},{4,8},{8,12},{1,5},{5,9},{9,13},{2,6},{6,10},{10,14},{3,7},{... | collective-permute-start | bytes 196616 | tf_op jit(solution)/shard_map/ppermute | solution.py:14
  22.6 4.4 %collective-permute-start.3 = (bf16[8,512,128]{2,1,0:T(8,128)(2,1)}, bf16[8,512,128]{2,1,0:T(8,128)(2,1)}, u32[]{:S(2)}, u32[]{:S(2)}) collective-permute-start(bf16[8,512,128]{2,1,0:T(8,128)(2,1)} %bitcast.66), channel_id=1, source_target_pairs={{1,0},{2,1},{3,2},{4,3},{5,4},{6,5},{7,6},{8,7},{9,8},{10,9},{11,1... | collective-permute-start | bytes 3145736 | tf_op jit(solution)/shard_map/ppermute | solution.py:15
  27.0 1.9 %collective-permute-start.2 = (bf16[8,512,128]{2,1,0:T(8,128)(2,1)}, bf16[8,512,128]{2,1,0:T(8,128)(2,1)}, u32[]{:S(2)}, u32[]{:S(2)}) collective-permute-start(bf16[8,512,128]{2,1,0:T(8,128)(2,1)} %bitcast.67), channel_id=1, source_target_pairs={{0,1},{1,2},{2,3},{3,4},{4,5},{5,6},{6,7},{7,8},{8,9},{9,10},{10,1... | collective-permute-start | bytes 3145736 | tf_op jit(solution)/shard_map/ppermute | solution.py:14
  28.9 0.7 compare_select_fusion
  29.6 0.1 reshape.50
  29.7 0.7 fusion.17
  31.1 0.9 fusion.10
  32.0 47.6 %psum.7 = bf16[1,64,128]{2,1,0:T(8,128)(2,1)S(1)} all-reduce(bf16[1,64,128]{2,1,0:T(8,128)(2,1)S(1)} %fusion.10), channel_id=1, replica_groups=mesh['groups'=2,'leaf'=4,'inner'=4] {'inner'}, use_global_device_ids=true, to_apply=%region_1.2 | all-reduce | flops 8192 | bytes 32768 | tf_op jit(solution)/shard_map/psum | solution.py:49
  79.6 11.2 %all_gather.7 = bf16[4,64,128]{2,1,0:T(8,128)(2,1)S(1)} all-gather(bf16[1,64,128]{2,1,0:T(8,128)(2,1)S(1)} %psum.7), channel_id=1, replica_groups=mesh['groups'=2,'leaf'=4,'inner'=4] {'leaf'}, dimensions={0}, use_global_device_ids=true | all-gather | bytes 81920 | tf_op jit(solution)/shard_map/all_gather | solution.py:50
  90.8 0.0 collective-permute-done.1
  90.8 0.0 collective-permute-done
  90.8 0.6 gather_fusion
  91.4 1.0 fusion.5
  92.4 1.3 %fusion.11 = bf16[128,64,1]{0,1,2:T(8,128)(2,1)S(1)} fusion(f32[128,64]{0,1:T(8,128)S(1)} %fusion.5, bf16[4,64,128]{2,1,0:T(8,128)(2,1)S(1)} %all_gather.7, bf16[1,4,64,64]{3,2,1,0:T(8,128)(2,1)} %param.19, bf16[4]{0:T(256)(128)(2,1)S(1)} %compare_convert_fusion, bf16[1,64,64]{2,1,0:T(8,128)(2,1)} %param.15), kind=kOutput, calls=%fused_computation.21 | convolution fusion | flops 5283840 | bytes 155656 | tf_op jit(solution)/shard_map/dot_general | solution.py:66
  93.6 1.5 %fusion.3 = f32[8,128,512]{2,1,0:T(8,128)S(1)} fusion(bf16[8,64,512]{2,1,0:T(8,128)(2,1)S(1)} %copy-done, bf16[128,64,1]{0,1,2:T(8,128)(2,1)S(1)} %fusion.11, bf16[8,64,64]{2,1,0:T(8,128)(2,1)} %param.14), kind=kOutput, calls=%fused_computation.9 | convolution fusion | flops 75563008 | bytes 2703360 | tf_op jit(solution)/shard_map/lri,lrn->lin/dot_general | solution.py:71
  95.2 0.0 collective-permute-done.3
  95.2 0.0 collective-permute-done.2
  95.2 3.3 %pad_maximum_fusion = bf16[24,512,128]{2,1,0:T(8,128)(2,1)} fusion(bf16[8,512,128]{2,1,0:T(8,128)(2,1)} %collective-permute-done.3, bf16[8,512,128]{2,1,0:T(8,128)(2,1)} %bitcast.68, bf16[8,512,128]{2,1,0:T(8,128)(2,1)} %collective-permute-done.2), kind=kLoop, calls=%fused_computation.2 | loop fusion | flops 3145728 | bytes 6291456 | tf_op jit(solution)/shard_map/concatenate | solution.py:16
  98.5 6.5 %gather_fusion.1 = bf16[40,512,128]{2,1,0:T(8,128)(2,1)} fusion(bf16[24,512,128]{2,1,0:T(8,128)(2,1)} %pad_maximum_fusion, s32[1024]{0:T(1024)S(1)} %pad_clamp_fusion), kind=kCustom, calls=%fused_computation.1 | custom fusion | bytes 10485920 | tf_op jit(solution)/shard_map/gather | solution.py:75
  105.0 13.3 %fusion.1 = bf16[8,512,128]{1,2,0:T(8,128)(2,1)} fusion(f32[8,128,512]{2,1,0:T(8,128)S(1)} %fusion.3, bf16[8,5,512,128]{3,2,1,0:T(8,128)(2,1)} %bitcast.64, bf16[8,5,512,512]{3,2,1,0:T(8,128)(2,1)} %param.12), kind=kOutput, calls=%fused_computation.5 | convolution fusion | flops 2685403136 | bytes 29360128 | tf_op jit(solution)/shard_map/lkij,lkjn->lin/dot_general | solution.py:76
  118.3 2.3 %copy.18 = bf16[8,512,128]{2,1,0:T(8,128)(2,1)} copy(bf16[8,512,128]{1,2,0:T(8,128)(2,1)} %fusion.1) | data formatting | bytes 2097152 | tf_op jit(solution)/shard_map/convert_element_type | solution.py:77
  (5 shorter events, 0.1 us)
Async XLA Ops:
  0.0 1.0 copy-start
  14.5 76.3 %collective-permute-start.1 = (bf16[4,64,128]{2,1,0:T(8,128)(2,1)S(1)}, bf16[4,64,128]{2,1,0:T(8,128)(2,1)S(1)}, u32[]{:S(2)}, u32[]{:S(2)}) collective-permute-start(bf16[4,64,128]{2,1,0:T(8,128)(2,1)S(1)} %bitcast.69), channel_id=1, source_target_pairs={{4,0},{8,4},{12,8},{5,1},{9,5},{13,9},{6,2},{10,6},{14,10},{7,3},{... | collective-permute-start | bytes 196616 | tf_op jit(solution)/shard_map/ppermute | solution.py:15
  19.6 71.2 %collective-permute-start = (bf16[4,64,128]{2,1,0:T(8,128)(2,1)S(1)}, bf16[4,64,128]{2,1,0:T(8,128)(2,1)S(1)}, u32[]{:S(2)}, u32[]{:S(2)}) collective-permute-start(bf16[4,64,128]{2,1,0:T(8,128)(2,1)S(1)} %bitcast.70), channel_id=1, source_target_pairs={{0,4},{4,8},{8,12},{1,5},{5,9},{9,13},{2,6},{6,10},{10,14},{3,7},{... | collective-permute-start | bytes 196616 | tf_op jit(solution)/shard_map/ppermute | solution.py:14
  22.6 72.5 %collective-permute-start.3 = (bf16[8,512,128]{2,1,0:T(8,128)(2,1)}, bf16[8,512,128]{2,1,0:T(8,128)(2,1)}, u32[]{:S(2)}, u32[]{:S(2)}) collective-permute-start(bf16[8,512,128]{2,1,0:T(8,128)(2,1)} %bitcast.66), channel_id=1, source_target_pairs={{1,0},{2,1},{3,2},{4,3},{5,4},{6,5},{7,6},{8,7},{9,8},{10,9},{11,1... | collective-permute-start | bytes 3145736 | tf_op jit(solution)/shard_map/ppermute | solution.py:15
  27.0 68.2 %collective-permute-start.2 = (bf16[8,512,128]{2,1,0:T(8,128)(2,1)}, bf16[8,512,128]{2,1,0:T(8,128)(2,1)}, u32[]{:S(2)}, u32[]{:S(2)}) collective-permute-start(bf16[8,512,128]{2,1,0:T(8,128)(2,1)} %bitcast.67), channel_id=1, source_target_pairs={{0,1},{1,2},{2,3},{3,4},{4,5},{5,6},{6,7},{7,8},{8,9},{9,10},{10,1... | collective-permute-start | bytes 3145736 | tf_op jit(solution)/shard_map/ppermute | solution.py:14
where the time goes:
time: 121 us
  blocking collectives  70.5 us (58%)
  matrix products  19.7 us (16%)
  starting transfers between devices  14.4 us (12%)
  local copies, waits for them, and re-layouts  10.5 us (9%)
  other arithmetic  4.69 us (4%)
    psum x1, blocking collectives, local(): summed = lax.psum(top_term.astype(jnp.bfloat16), 'inner')  47.6 us
    dot_general x1, matrix products, local(): jnp.einsum('lkij,lkjn->lin', near_blocks, picked, preferred_element_type=...  13.3 us
    all_gather x1, blocking collectives, local(): group_mids = lax.all_gather(mid_skel[None], 'inner', axis=0, tiled=True)  11.8 us
    all_gather x1, blocking collectives, local(): top_skel = lax.all_gather(summed[None], 'leaf', axis=0, tiled=True)  11.2 us
    ppermute x2, starting transfers between devices, padded(): after = lax.ppermute(first, axis, down)  9.46 us
    gather x1, local copies, waits for them, and re-layouts, local(): picked = extended[near_local]  6.51 us
    ppermute x2, starting transfers between devices, padded(): before = lax.ppermute(last, axis, up)  4.97 us
    concatenate x2, other arithmetic, padded(): x = jnp.concatenate([before, x, after], axis=dim)  3.31 us
  transfers between devices with their start and end apart: 4, of which 0 were waited for; matrix products, arithmetic and copies ran while one was open for 6% of the time, Pallas kernels for 0%

commit v1 on v0

v1 whole, which is shorter than its diff:
```python
import functools

import jax
import jax.numpy as jnp
from jax import lax
from jax.experimental import pallas as pl
from jax.experimental.pallas import tpu as pltpu
from jax.sharding import PartitionSpec as P

MIB = 1 << 20
VMEM = pl.BlockSpec(memory_space=pltpu.VMEM)
SMEM = pl.BlockSpec(memory_space=pltpu.SMEM)
ANY = pl.BlockSpec(memory_space=pl.ANY)
HBM = pl.BlockSpec(memory_space=pltpu.HBM)


def dot(a, b):
    return lax.dot_general(a, b, (((1,), (0,)), ((), ())), preferred_element_type=jnp.float32)


def dot_t(a, b):
    return lax.dot_general(a, b, (((0,), (0,)), ((), ())), preferred_element_type=jnp.float32)


def call(kernel, out_shape, in_specs, out_specs, scratch, flops, moved, vmem):
    return pl.pallas_call(
        kernel,
        out_shape=out_shape,
        in_specs=in_specs,
        out_specs=out_specs,
        scratch_shapes=scratch,
        cost_estimate=pl.CostEstimate(flops=flops, bytes_accessed=moved, transcendentals=0),
        compiler_params=pltpu.CompilerParams(vmem_limit_bytes=vmem),
    )


def up_kernel(x_ref, basis_ref, leaf_map_ref, mid_map_ref, out_ref):
    leaves, rank, rows = basis_ref.shape
    mid = jnp.zeros((rank, x_ref.shape[1]), jnp.float32)
    for leaf in range(leaves):
        skeleton = dot(basis_ref[leaf], x_ref[leaf * rows : (leaf + 1) * rows, :])
        mid += dot_t(leaf_map_ref[leaf], skeleton.astype(jnp.bfloat16))
    mid = mid.astype(jnp.bfloat16)
    out_ref[:rank, :] = mid
    out_ref[rank:, :] = dot_t(mid_map_ref[0], mid).astype(jnp.bfloat16)


def group_kernel(count, *refs):
    parts, out_ref, top_ref = refs[:count], refs[count], refs[count + 1]
    rank = top_ref.shape[0]
    top = jnp.zeros(top_ref.shape, jnp.float32)
    for i, part in enumerate(parts):
        out_ref[i * rank : (i + 1) * rank, :] = part[:rank, :]
        top += part[rank:, :].astype(jnp.float32)
    top = top.astype(jnp.bfloat16)
    out_ref[count * rank :, :] = top
    top_ref[...] = top


def down_kernel(leaf_size, inner_size, *refs):
    far_ids, far_count, own, before, after = refs[:5]
    tops = dict(zip(range(2, leaf_size - 1), refs[5:]))
    couple, mid_couple, mid_map, leaf_map, out_ref, window = refs[5 + len(tops) :]
    rank = mid_map.shape[1]
    group = lax.axis_index("leaf")
    inner = lax.axis_index("inner")
    last = inner_size * rank
    top_down = jnp.zeros((rank, own.shape[1]), jnp.float32)
    for shift in range(1, leaf_size):
        source = lax.rem(group - shift + leaf_size, leaf_size)
        if shift == 1:
            top = before[last:, :]
        elif shift == leaf_size - 1:
            top = after[last:, :]
        else:
            top = tops[shift][...]
        term = dot(couple[0, source], top)
        top_down += jnp.where(jnp.abs(source - group) >= 2, term, 0.0)
    for i, part in enumerate((before, own, after)):
        window[i * last : (i + 1) * last, :] = part[:last, :]
    total = dot(mid_map[0], top_down.astype(jnp.bfloat16))
    for slot in range(mid_couple.shape[1]):
        live = slot < far_count[0]
        partner = jnp.where(live, far_ids[0, slot], group * inner_size)
        side = partner // inner_size - group + 1
        place = lax.rem(inner - lax.rem(partner, inner_size) + inner_size, inner_size)
        at = pl.multiple_of((side * inner_size + place) * rank, rank)
        term = dot(mid_couple[0, slot], window[pl.ds(at, rank), :])
        total += jnp.where(live, term, 0.0)
    total = total.astype(jnp.bfloat16)
    for leaf in range(leaf_map.shape[0]):
        out_ref[leaf * rank : (leaf + 1) * rank, :] = dot(leaf_map[leaf], total).astype(jnp.bfloat16)


def listed(ids_ref, slot_list, place_list, ends, place_of):
    leaves, near = ids_ref.shape
    first = (lax.axis_index("leaf") * lax.axis_size("inner") + lax.axis_index("inner")) * leaves

    def one(leaf, count):
        for k in range(near):
            at_hand, place = place_of(ids_ref[leaf, k] - first)
            slot_list[count] = leaf * near + k
            place_list[count] = place
            count += at_hand.astype(jnp.int32)
        ends[leaf] = count
        return count

    return lax.fori_loop(0, leaves, one, 0)


def near_products(blocks_ref, near, lists, count, buffer, sems, start_ready, leaf_done, x_ref, total):
    slot_list, place_list, ends = lists
    depth, rows, _ = buffer.shape
    leaves = blocks_ref.shape[0]

    def copy(i):
        slot = slot_list[i]
        at = lax.rem(i, depth)
        return pltpu.make_async_copy(blocks_ref.at[slot // near, lax.rem(slot, near)], buffer.at[at], sems.at[at])

    def begin(i, carry):
        copy(i).start()
        return carry

    lax.fori_loop(0, jnp.minimum(count, depth), begin, 0)
    start_ready()

    def one(leaf, begin_at):
        end_at = ends[leaf]

        def product(i, carry):
            copy(i).wait()
            at = pl.multiple_of(place_list[i] * rows, rows)
            here = pl.ds(pl.multiple_of(leaf * rows, rows), rows)
            total[here, :] += dot(buffer[lax.rem(i, depth)], x_ref[pl.ds(at, rows), :])

            @pl.when(i + depth < count)
            def _():
                copy(i + depth).start()

            return carry

        lax.fori_loop(begin_at, end_at, product, 0)
        leaf_done(leaf)
        return end_at

    lax.fori_loop(0, leaves, one, 0)


def own_kernel(ids_ref, x_ref, blocks_ref, total, slot_list, place_list, ends, buffer, sems):
    leaves, near = ids_ref.shape

    def place_of(offset):
        return (offset >= 0) & (offset < leaves), offset

    lists = (slot_list, place_list, ends)
    count = listed(ids_ref, *lists, place_of)

    def clear():
        total[...] = jnp.zeros_like(total)

    near_products(blocks_ref, near, lists, count, buffer, sems, clear, lambda leaf: None, x_ref, total)


def close_kernel(ids_ref, before, after, blocks_ref, sum_ref, down_ref, basis_ref, total, slot_list, place_list, ends, buffer, sems, x_ref, x_sems):
    leaves, near = ids_ref.shape
    half = leaves // 2
    rank, rows = basis_ref.shape[1:]

    def place_of(offset):
        ahead = offset >= leaves
        ok = ((offset < 0) & (offset >= -half)) | (ahead & (offset < leaves + half))
        return ok, jnp.where(ahead, offset - leaves + half, offset + half)

    lists = (slot_list, place_list, ends)
    count = listed(ids_ref, *lists, place_of)

    def ready():
        cut = half * rows
        one = pltpu.make_async_copy(before, x_ref.at[:cut], x_sems.at[0])
        two = pltpu.make_async_copy(after, x_ref.at[cut:], x_sems.at[1])
        one.start()
        two.start()
        for leaf in range(leaves):
            here = slice(leaf * rows, (leaf + 1) * rows)
            total[here, :] = sum_ref[here, :] + dot_t(basis_ref[leaf], down_ref[leaf * rank : (leaf + 1) * rank, :])
        one.wait()
        two.wait()

    near_products(blocks_ref, near, lists, count, buffer, sems, ready, lambda leaf: None, x_ref, total)


def last_kernel(ids_ref, before, after, blocks_ref, sum_ref, out_ref, slot_list, place_list, ends, buffer, sems, x_ref, x_sems, total, result, out_sems):
    leaves, near = ids_ref.shape
    half = leaves // 2
    rows = buffer.shape[1]

    def place_of(offset):
        ahead = offset >= leaves
        ok = (offset < -half) | (offset >= leaves + half)
        return ok, jnp.where(ahead, offset - leaves, offset + leaves)

    lists = (slot_list, place_list, ends)
    cut = half * rows
    loads = (
        pltpu.make_async_copy(sum_ref, total, x_sems.at[2]),
        pltpu.make_async_copy(before, x_ref.at[:cut], x_sems.at[0]),
        pltpu.make_async_copy(after, x_ref.at[cut:], x_sems.at[1]),
    )
    for load in loads:
        load.start()
    count = listed(ids_ref, *lists, place_of)

    def ready():
        for load in loads:
            load.wait()

    def store(leaf):
        here = pl.ds(pl.multiple_of(leaf * rows, rows), rows)
        return pltpu.make_async_copy(result.at[here], out_ref.at[here], out_sems.at[leaf])

    def leaf_done(leaf):
        here = pl.ds(pl.multiple_of(leaf * rows, rows), rows)
        result[here, :] = total[here, :].astype(result.dtype)
        store(leaf).start()

    near_products(blocks_ref, near, lists, count, buffer, sems, ready, leaf_done, x_ref, total)
    for leaf in range(leaves):
        store(leaf).wait()


def local(anomalies, leaf_basis, near_blocks, near_ids, transfer_leaf, transfer_mid, far_ids, far_count, mid_couple, top_couple):
    leaves, rank, rows = leaf_basis.shape
    near = near_blocks.shape[1]
    columns = anomalies.shape[1]
    inner_size = lax.axis_size("inner")
    leaf_size = lax.axis_size("leaf")
    devices = leaf_size * inner_size
    half = leaves // 2
    cut = half * rows
    bf16 = jnp.bfloat16

    def shaped(*shape, dtype=bf16):
        return jax.ShapeDtypeStruct(shape, dtype)

    def shifted(x, axis, size, shift):
        return lax.ppermute(x, axis, [(i, (i + shift) % size) for i in range(size)])

    up = [(i, i + 1) for i in range(devices - 1)]
    down = [(j, i) for i, j in up]
    both = ("leaf", "inner")
    first, second = anomalies[:cut], anomalies[cut:]
    before_close = lax.ppermute(second, both, up)
    after_close = lax.ppermute(first, both, down)

    part = call(up_kernel, shaped(2 * rank, columns), [VMEM] * 4, VMEM, [], 2 * rows * rank * leaves * columns, anomalies.size * 3, 16 * MIB)(
        anomalies, leaf_basis, transfer_leaf, transfer_mid
    )
    parts = [part] + [shifted(part, "inner", inner_size, s) for s in range(1, inner_size)]

    first, second, _ = lax.optimization_barrier((first, second, part))
    before_far = lax.ppermute(first, both, up)
    after_far = lax.ppermute(second, both, down)

    def scratch(depth):
        slots = leaves * near + 1
        return [
            pltpu.SMEM((slots,), jnp.int32),
            pltpu.SMEM((slots,), jnp.int32),
            pltpu.SMEM((leaves,), jnp.int32),
            pltpu.VMEM((depth, rows, rows), bf16),
            pltpu.SemaphoreType.DMA((depth,)),
        ]

    wide = shaped(leaves * rows, columns, dtype=jnp.float32)
    flops = 2 * rows * rows * columns
    own_sum = call(own_kernel, wide, [SMEM, VMEM, HBM], VMEM, scratch(8), 20 * flops, 20 * rows * rows * 2, 16 * MIB)(
        near_ids, anomalies, near_blocks
    )

    group, top = call(functools.partial(group_kernel, inner_size), (shaped((inner_size + 1) * rank, columns), shaped(rank, columns)), [VMEM] * inner_size, (VMEM, VMEM), [], 1000, 1000, 16 * MIB)(*parts)
    before_group = shifted(group, "leaf", leaf_size, 1)
    after_group = shifted(group, "leaf", leaf_size, leaf_size - 1)
    tops = [shifted(top, "leaf", leaf_size, s) for s in range(2, leaf_size - 1)]
    leaf_down = call(
        functools.partial(down_kernel, leaf_size, inner_size),
        shaped(leaves * rank, columns),
        [SMEM, SMEM] + [VMEM] * (7 + len(tops)),
        VMEM,
        [pltpu.VMEM((3 * inner_size * rank, columns), bf16)],
        1000,
        1000,
        16 * MIB,
    )(far_ids, far_count, group, before_group, after_group, *tops, top_couple, mid_couple, transfer_mid, transfer_leaf)

    close_scratch = scratch(8) + [pltpu.VMEM((2 * cut, columns), bf16), pltpu.SemaphoreType.DMA((3,))]
    close_sum = call(close_kernel, wide, [SMEM, ANY, ANY, HBM, VMEM, VMEM, VMEM], VMEM, close_scratch, 12 * flops, 12 * rows * rows * 2, 24 * MIB)(
        near_ids, before_close, after_close, near_blocks, own_sum, leaf_down, leaf_basis
    )
    last_scratch = scratch(16) + [
        pltpu.VMEM((2 * cut, columns), bf16),
        pltpu.SemaphoreType.DMA((3,)),
        pltpu.VMEM((leaves * rows, columns), jnp.float32),
        pltpu.VMEM((leaves * rows, columns), bf16),
        pltpu.SemaphoreType.DMA((leaves,)),
    ]
    return call(last_kernel, shaped(leaves * rows, columns), [SMEM, ANY, ANY, HBM, ANY], ANY, last_scratch, 6 * flops, 6 * rows * rows * 2, 24 * MIB)(
        near_ids, before_far, after_far, near_blocks, close_sum
    )


def solution(mesh):
    return jax.shard_map(
        local,
        mesh=mesh,
        in_specs=(
            P(("leaf", "inner"), "groups"),
            P(("leaf", "inner"), None, None),
            P(("leaf", "inner"), None, None, None),
            P(("leaf", "inner"), None),
            P(("leaf", "inner"), None, None),
            P(("leaf", "inner"), None, None),
            P(("leaf", "inner"), None),
            P(("leaf", "inner")),
            P(("leaf", "inner"), None, None, None),
            P("leaf", None, None, None),
        ),
        out_specs=P(("leaf", "inner"), "groups"),
        check_vma=False,
    )
```

time: 121 us -> 107 us (0.88)
  blocking collectives: 70.5 us -> 0 us
  waiting for transfers between devices: 0.01 us -> 47 us
  Pallas kernels: 0 us -> 20.9 us
  matrix products: 19.7 us -> 0 us
  starting transfers between devices: 14.4 us -> 21.9 us
  local copies, waits for them, and re-layouts: 10.5 us -> 15.3 us
  other arithmetic: 4.69 us -> 0 us
    psum x1 -> x0, blocking collectives: 47.6 us -> none  [local(): summed = lax.psum(top_term.astype(jnp.bfloat16), 'inner')]
    ppermute x4 -> x10, waiting for transfers between devices: 0.01 us -> 47 us  [the longest x6 47 us: shifted(): return lax.ppermute(x, axis, [(i, (i + shift) % size) for i in range(size)])]
    all_gather x2 -> x0, blocking collectives: 22.9 us -> none  [the longest x1 11.8 us: local(): group_mids = lax.all_gather(mid_skel[None], 'inner', axis=0, tiled=True)]
    pallas_call x0 -> x6, Pallas kernels: none -> 20.9 us  [the longest x1 10.2 us: local(): call(own_kernel, wide, [SMEM, VMEM, HBM], VMEM, scratch(8), 20 * flops, 2...]
    dot_general x6 -> x0, matrix products: 19.7 us -> none  [the longest x1 13.3 us: local(): jnp.einsum('lkij,lkjn->lin', near_blocks, picked, preferred_element_type=...]
    unnamed x2 -> x20, local copies, waits for them, and re-layouts: 1.04 us -> 14 us
    ppermute x4 -> x10, starting transfers between devices: 14.4 us -> 21.9 us  [the longest x6 6.04 us: shifted(): return lax.ppermute(x, axis, [(i, (i + shift) % size) for i in range(size)])]
    gather x2 -> x0, local copies, waits for them, and re-layouts: 7.08 us -> none  [the longest x1 6.51 us: local(): picked = extended[near_local]]
  transfers between devices with their start and end apart: 4 -> 10, of which waited for: 0 -> 5; matrix products, arithmetic and copies ran while one was open for 6% -> 0% of each run, Pallas kernels for 0% -> 16%
where the time goes in v1:
time: 107 us; the launch traced here: 106 us
  waiting for transfers between devices  47 us (44%)
  starting transfers between devices  21.9 us (20%)
  Pallas kernels  20.9 us (20%)
  local copies, waits for them, and re-layouts  15.3 us (14%)
    ppermute x6, waiting for transfers between devices, shifted(): return lax.ppermute(x, axis, [(i, (i + shift) % size) for i in range(size)])  47 us
    unnamed x20, local copies, waits for them, and re-layouts  14 us
    pallas_call x1, Pallas kernels, local(): call(own_kernel, wide, [SMEM, VMEM, HBM], VMEM, scratch(8), 20 * flops, 2...  10.2 us
    ppermute x6, starting transfers between devices, shifted(): return lax.ppermute(x, axis, [(i, (i + shift) % size) for i in range(size)])  6.04 us
    ppermute x1, starting transfers between devices, local(): after_far = lax.ppermute(second, both, down)  5.44 us
    pallas_call x1, Pallas kernels, local(): call(close_kernel, wide, [SMEM, ANY, ANY, HBM, VMEM, VMEM, VMEM], VMEM, c...  4.85 us
    ppermute x1, starting transfers between devices, local(): after_close = lax.ppermute(first, both, down)  4.51 us
    ppermute x1, starting transfers between devices, local(): before_close = lax.ppermute(second, both, up)  4.03 us
  transfers between devices with their start and end apart: 10, of which 5 were waited for; matrix products, arithmetic and copies ran while one was open for 0% of the time, Pallas kernels for 16%

profile of v1, /device:TPU:1, one launch (start us, length us, event | category | flops | bytes accessed | tf_op | source)
XLA Modules:
  0.0 106.1 jit_solution(14568870412501536438)
XLA Ops:
  0.0 0.0 copy-start.2
  0.0 0.0 copy-start.5
  0.0 0.0 copy-start.4
  0.0 0.0 copy-start.3
  0.0 0.0 copy-start.8
  0.0 1.4 %fusion = (bf16[2048,128]{1,0:T(8,128)(2,1)S(1)}, bf16[2048,128]{1,0:T(8,128)(2,1)S(1)}) fusion(bf16[4096,128]{1,0:T(8,128)(2,1)} %x_ref.3), kind=kLoop, calls=%fused_computation | loop fusion | bytes 2097152 | tf_op jit(solution)/shard_map/slice | solution.py:252
  1.4 4.0 %collective-permute-start.2 = (bf16[2048,128]{1,0:T(8,128)(2,1)S(1)}, bf16[2048,128]{1,0:T(8,128)(2,1)S(1)}, u32[]{:S(2)}, u32[]{:S(2)}) collective-permute-start(bf16[2048,128]{1,0:T(8,128)(2,1)S(1)} %get-tuple-element.10), channel_id=1, source_target_pairs={{0,1},{1,2},{2,3},{3,4},{4,5},{5,6},{6,7},{7,8},{8,9},{9,10},{10,1... | collective-permute-start | bytes 1572872 | tf_op jit(solution)/shard_map/ppermute | solution.py:253
  5.5 4.5 %collective-permute-start.3 = (bf16[2048,128]{1,0:T(8,128)(2,1)S(1)}, bf16[2048,128]{1,0:T(8,128)(2,1)S(1)}, u32[]{:S(2)}, u32[]{:S(2)}) collective-permute-start(bf16[2048,128]{1,0:T(8,128)(2,1)S(1)} %get-tuple-element.9), channel_id=1, source_target_pairs={{1,0},{2,1},{3,2},{4,3},{5,4},{6,5},{7,6},{8,7},{9,8},{10,9},{11,1... | collective-permute-start | bytes 1572872 | tf_op jit(solution)/shard_map/ppermute | solution.py:254
  10.0 0.0 copy-done.2
  10.0 0.0 copy-done.5
  10.0 0.0 copy-done.4
  10.0 0.0 copy-done.3
  10.0 0.9 shard_map.100.refs_0_
  11.0 1.9 %collective-permute-start = (bf16[2048,128]{1,0:T(8,128)(2,1)S(1)}, bf16[2048,128]{1,0:T(8,128)(2,1)S(1)}, u32[]{:S(2)}, u32[]{:S(2)}) collective-permute-start(bf16[2048,128]{1,0:T(8,128)(2,1)S(1)} %get-tuple-element.9), channel_id=1, source_target_pairs={{0,1},{1,2},{2,3},{3,4},{4,5},{5,6},{6,7},{7,8},{8,9},{9,10},{10,1... | collective-permute-start | bytes 1572872 | tf_op jit(solution)/shard_map/ppermute | solution.py:262
  12.9 5.4 %collective-permute-start.1 = (bf16[2048,128]{1,0:T(8,128)(2,1)S(1)}, bf16[2048,128]{1,0:T(8,128)(2,1)S(1)}, u32[]{:S(2)}, u32[]{:S(2)}) collective-permute-start(bf16[2048,128]{1,0:T(8,128)(2,1)S(1)} %get-tuple-element.10), channel_id=1, source_target_pairs={{1,0},{2,1},{3,2},{4,3},{5,4},{6,5},{7,6},{8,7},{9,8},{10,9},{11,1... | collective-permute-start | bytes 1572872 | tf_op jit(solution)/shard_map/ppermute | solution.py:263
  18.3 1.9 %collective-permute-start.6 = (bf16[128,128]{1,0:T(8,128)(2,1)S(1)}, bf16[128,128]{1,0:T(8,128)(2,1)S(1)}, u32[]{:S(2)}, u32[]{:S(2)}) collective-permute-start(bf16[128,128]{1,0:T(8,128)(2,1)S(1)} %shard_map.100.refs_0_), channel_id=1, source_target_pairs={{0,3},{1,0},{2,1},{3,2},{4,7},{5,4},{6,5},{7,6},{8,11},{9,8},{10,9... | collective-permute-start | bytes 98312 | tf_op jit(solution)/shard_map/ppermute | solution.py:247
  20.2 34.9 %collective-permute-done.6.refs_3_ = bf16[128,128]{1,0:T(8,128)(2,1)S(1)} collective-permute-done((bf16[128,128]{1,0:T(8,128)(2,1)S(1)}, bf16[128,128]{1,0:T(8,128)(2,1)S(1)}, u32[]{:S(2)}, u32[]{:S(2)}) %collective-permute-start.6) | collective-permute-done | bytes 32800 | tf_op jit(solution)/shard_map/ppermute | solution.py:247
  55.1 0.2 collective-permute-start.5
  55.3 3.8 %collective-permute-done.5.refs_2_ = bf16[128,128]{1,0:T(8,128)(2,1)S(1)} collective-permute-done((bf16[128,128]{1,0:T(8,128)(2,1)S(1)}, bf16[128,128]{1,0:T(8,128)(2,1)S(1)}, u32[]{:S(2)}, u32[]{:S(2)}) %collective-permute-start.5) | collective-permute-done | bytes 32800 | tf_op jit(solution)/shard_map/ppermute | solution.py:247
  59.1 0.0 collective-permute-start.4
  59.1 4.6 %collective-permute-done.4.refs_1_ = bf16[128,128]{1,0:T(8,128)(2,1)S(1)} collective-permute-done((bf16[128,128]{1,0:T(8,128)(2,1)S(1)}, bf16[128,128]{1,0:T(8,128)(2,1)S(1)}, u32[]{:S(2)}, u32[]{:S(2)}) %collective-permute-start.4) | collective-permute-done | bytes 32800 | tf_op jit(solution)/shard_map/ppermute | solution.py:247
  63.7 0.1 collective-permute-start.9
  63.8 2.6 %collective-permute-done.9.refs_5_ = bf16[64,128]{1,0:T(8,128)(2,1)S(1)} collective-permute-done((bf16[64,128]{1,0:T(8,128)(2,1)S(1)}, bf16[64,128]{1,0:T(8,128)(2,1)S(1)}, u32[]{:S(2)}, u32[]{:S(2)}) %collective-permute-start.9) | collective-permute-done | bytes 16416 | tf_op jit(solution)/shard_map/ppermute | solution.py:247
  66.4 3.9 %collective-permute-start.8 = (bf16[320,128]{1,0:T(8,128)(2,1)S(1)}, bf16[320,128]{1,0:T(8,128)(2,1)S(1)}, u32[]{:S(2)}, u32[]{:S(2)}) collective-permute-start(bf16[320,128]{1,0:T(8,128)(2,1)S(1)} %get-tuple-element.11.refs_2_), channel_id=1, source_target_pairs={{0,12},{4,0},{8,4},{12,8},{1,13},{5,1},{9,5},{13,9},{2,14},{6,2},{... | collective-permute-start | bytes 245768 | tf_op jit(solution)/shard_map/ppermute | solution.py:247
  70.3 0.0 copy-start.9
  71.0 1.1 %collective-permute-done.8.refs_4_ = bf16[320,128]{1,0:T(8,128)(2,1)S(1)} collective-permute-done((bf16[320,128]{1,0:T(8,128)(2,1)S(1)}, bf16[320,128]{1,0:T(8,128)(2,1)S(1)}, u32[]{:S(2)}, u32[]{:S(2)}) %collective-permute-start.8) | collective-permute-done | bytes 81952 | tf_op jit(solution)/shard_map/ppermute | solution.py:247
  72.1 0.0 collective-permute-start.7
  72.1 0.0 copy-done.8
  72.1 0.0 copy-start
  72.1 7.0 %copy-done = bf16[8,5,512,512]{3,2,1,0:T(8,128)(2,1)S(1)} copy-done((bf16[8,5,512,512]{3,2,1,0:T(8,128)(2,1)S(1)}, bf16[8,5,512,512]{3,2,1,0:T(8,128)(2,1)}, u32[]{:S(2)}) %copy-start) | copy-done | bytes 20971544
  79.0 0.0 copy-start.6
  79.0 0.0 copy-start.7
  79.0 10.2 %shard_map.101.sum_ref = f32[4096,128]{1,0:T(8,128)S(1)} custom-call(s32[8,5]{1,0:T(8,128)S(1)} %copy-done.8, bf16[4096,128]{1,0:T(8,128)(2,1)S(1)} %copy-done.2, bf16[8,5,512,512]{3,2,1,0:T(8,128)(2,1)S(1)} %copy-done), custom_call_target="tpu_custom_call" | custom-call | flops 1342177280 | bytes 10485760 | tf_op jit(solution)/shard_map/pallas_call | solution.py:277
  89.2 0.0 collective-permute-done.7.refs_3_
  89.2 0.0 copy-done.9
  89.2 0.0 copy-done.6
  89.3 0.0 copy-done.7
  89.3 1.0 shard_map.103.down_ref
  90.3 0.0 collective-permute-done.2.before
  90.3 0.0 collective-permute-done.3.after
  90.3 0.0 copy-start.1
  90.3 7.0 %copy-done.1 = bf16[8,5,512,512]{3,2,1,0:T(8,128)(2,1)S(1)} copy-done((bf16[8,5,512,512]{3,2,1,0:T(8,128)(2,1)S(1)}, bf16[8,5,512,512]{3,2,1,0:T(8,128)(2,1)}, u32[]{:S(2)}) %copy-start.1) | copy-done | bytes 20971544
  97.2 4.8 %shard_map.104.sum_ref = f32[4096,128]{1,0:T(8,128)S(1)} custom-call(s32[8,5]{1,0:T(8,128)S(1)} %copy-done.8, bf16[2048,128]{1,0:T(8,128)(2,1)S(1)} %collective-permute-done.2.before, bf16[2048,128]{1,0:T(8,128)(2,1)S(1)} %collective-permute-done.3.after, bf16[8,5,512,512]{3,2,1,0:T(8,128)(2,1)S(1)} %copy-done.1, f32[4096,128]{1,0:T(8,128)S(1)} %shard_map.101.sum_ref, ...), custom_call_target="tpu_custom_call" | custom-call | flops 805306368 | bytes 6291456 | tf_op jit(solution)/shard_map/pallas_call | solution.py:297
  102.1 0.0 collective-permute-done.before
  102.1 0.0 collective-permute-done.1.after
  102.1 3.9 %shard_map.105 = bf16[4096,128]{1,0:T(8,128)(2,1)} custom-call(s32[8,5]{1,0:T(8,128)S(1)} %copy-done.8, bf16[2048,128]{1,0:T(8,128)(2,1)S(1)} %collective-permute-done.before, bf16[2048,128]{1,0:T(8,128)(2,1)S(1)} %collective-permute-done.1.after, bf16[8,5,512,512]{3,2,1,0:T(8,128)(2,1)S(1)} %copy-done.1, f32[4096,128]{1,0:T(8,128)S(1)} %shard_map.104.sum_ref), custom_call_target="tpu_custom_call" | custom-call | flops 402653184 | bytes 3145728 | tf_op jit(solution)/shard_map/pallas_call | solution.py:307
  (1 shorter events, 0.0 us)
Async XLA Ops:
  0.0 10.0 %copy-start.2 = (bf16[4096,128]{1,0:T(8,128)(2,1)S(1)}, bf16[4096,128]{1,0:T(8,128)(2,1)}, u32[]{:S(2)}) copy-start(bf16[4096,128]{1,0:T(8,128)(2,1)} %x_ref.3) | copy-start | bytes 3145732
  0.0 10.0 %copy-start.5 = (bf16[1,64,64]{2,1,0:T(8,128)(2,1)S(1)}, bf16[1,64,64]{2,1,0:T(8,128)(2,1)}, u32[]{:S(2)}) copy-start(bf16[1,64,64]{2,1,0:T(8,128)(2,1)} %refs_8_.1) | copy-start | bytes 24580
  0.0 10.0 %copy-start.4 = (bf16[8,64,64]{2,1,0:T(8,128)(2,1)S(1)}, bf16[8,64,64]{2,1,0:T(8,128)(2,1)}, u32[]{:S(2)}) copy-start(bf16[8,64,64]{2,1,0:T(8,128)(2,1)} %refs_9_.1) | copy-start | bytes 196612
  0.0 10.0 %copy-start.3 = (bf16[8,64,512]{2,1,0:T(8,128)(2,1)S(1)}, bf16[8,64,512]{2,1,0:T(8,128)(2,1)}, u32[]{:S(2)}) copy-start(bf16[8,64,512]{2,1,0:T(8,128)(2,1)} %basis_ref.3) | copy-start | bytes 1572868
  0.0 72.0 %copy-start.8 = (s32[8,5]{1,0:T(8,128)S(1)}, s32[8,5]{1,0:T(8,128)}, u32[]{:S(2)}) copy-start(s32[8,5]{1,0:T(8,128)} %ids_ref.5) | copy-start | bytes 484
  1.4 88.8 %collective-permute-start.2 = (bf16[2048,128]{1,0:T(8,128)(2,1)S(1)}, bf16[2048,128]{1,0:T(8,128)(2,1)S(1)}, u32[]{:S(2)}, u32[]{:S(2)}) collective-permute-start(bf16[2048,128]{1,0:T(8,128)(2,1)S(1)} %get-tuple-element.10), channel_id=1, source_target_pairs={{0,1},{1,2},{2,3},{3,4},{4,5},{5,6},{6,7},{7,8},{8,9},{9,10},{10,1... | collective-permute-start | bytes 1572872 | tf_op jit(solution)/shard_map/ppermute | solution.py:253
  5.5 84.8 %collective-permute-start.3 = (bf16[2048,128]{1,0:T(8,128)(2,1)S(1)}, bf16[2048,128]{1,0:T(8,128)(2,1)S(1)}, u32[]{:S(2)}, u32[]{:S(2)}) collective-permute-start(bf16[2048,128]{1,0:T(8,128)(2,1)S(1)} %get-tuple-element.9), channel_id=1, source_target_pairs={{1,0},{2,1},{3,2},{4,3},{5,4},{6,5},{7,6},{8,7},{9,8},{10,9},{11,1... | collective-permute-start | bytes 1572872 | tf_op jit(solution)/shard_map/ppermute | solution.py:254
  11.0 91.1 %collective-permute-start = (bf16[2048,128]{1,0:T(8,128)(2,1)S(1)}, bf16[2048,128]{1,0:T(8,128)(2,1)S(1)}, u32[]{:S(2)}, u32[]{:S(2)}) collective-permute-start(bf16[2048,128]{1,0:T(8,128)(2,1)S(1)} %get-tuple-element.9), channel_id=1, source_target_pairs={{0,1},{1,2},{2,3},{3,4},{4,5},{5,6},{6,7},{7,8},{8,9},{9,10},{10,1... | collective-permute-start | bytes 1572872 | tf_op jit(solution)/shard_map/ppermute | solution.py:262
  12.9 89.2 %collective-permute-start.1 = (bf16[2048,128]{1,0:T(8,128)(2,1)S(1)}, bf16[2048,128]{1,0:T(8,128)(2,1)S(1)}, u32[]{:S(2)}, u32[]{:S(2)}) collective-permute-start(bf16[2048,128]{1,0:T(8,128)(2,1)S(1)} %get-tuple-element.10), channel_id=1, source_target_pairs={{1,0},{2,1},{3,2},{4,3},{5,4},{6,5},{7,6},{8,7},{9,8},{10,9},{11,1... | collective-permute-start | bytes 1572872 | tf_op jit(solution)/shard_map/ppermute | solution.py:263
  18.3 36.8 %collective-permute-start.6 = (bf16[128,128]{1,0:T(8,128)(2,1)S(1)}, bf16[128,128]{1,0:T(8,128)(2,1)S(1)}, u32[]{:S(2)}, u32[]{:S(2)}) collective-permute-start(bf16[128,128]{1,0:T(8,128)(2,1)S(1)} %shard_map.100.refs_0_), channel_id=1, source_target_pairs={{0,3},{1,0},{2,1},{3,2},{4,7},{5,4},{6,5},{7,6},{8,11},{9,8},{10,9... | collective-permute-start | bytes 98312 | tf_op jit(solution)/shard_map/ppermute | solution.py:247
  55.1 4.0 %collective-permute-start.5 = (bf16[128,128]{1,0:T(8,128)(2,1)S(1)}, bf16[128,128]{1,0:T(8,128)(2,1)S(1)}, u32[]{:S(2)}, u32[]{:S(2)}) collective-permute-start(bf16[128,128]{1,0:T(8,128)(2,1)S(1)} %shard_map.100.refs_0_), channel_id=1, source_target_pairs={{0,2},{1,3},{2,0},{3,1},{4,6},{5,7},{6,4},{7,5},{8,10},{9,11},{10,... | collective-permute-start | bytes 98312 | tf_op jit(solution)/shard_map/ppermute | solution.py:247
  59.1 4.6 %collective-permute-start.4 = (bf16[128,128]{1,0:T(8,128)(2,1)S(1)}, bf16[128,128]{1,0:T(8,128)(2,1)S(1)}, u32[]{:S(2)}, u32[]{:S(2)}) collective-permute-start(bf16[128,128]{1,0:T(8,128)(2,1)S(1)} %shard_map.100.refs_0_), channel_id=1, source_target_pairs={{0,1},{1,2},{2,3},{3,0},{4,5},{5,6},{6,7},{7,4},{8,9},{9,10},{10,1... | collective-permute-start | bytes 98312 | tf_op jit(solution)/shard_map/ppermute | solution.py:247
  63.7 2.7 %collective-permute-start.9 = (bf16[64,128]{1,0:T(8,128)(2,1)S(1)}, bf16[64,128]{1,0:T(8,128)(2,1)S(1)}, u32[]{:S(2)}, u32[]{:S(2)}) collective-permute-start(bf16[64,128]{1,0:T(8,128)(2,1)S(1)} %get-tuple-element.12), channel_id=1, source_target_pairs={{0,8},{4,12},{8,0},{12,4},{1,9},{5,13},{9,1},{13,5},{2,10},{6,14},... | collective-permute-start | bytes 49160 | tf_op jit(solution)/shard_map/ppermute | solution.py:247
  66.4 5.7 %collective-permute-start.8 = (bf16[320,128]{1,0:T(8,128)(2,1)S(1)}, bf16[320,128]{1,0:T(8,128)(2,1)S(1)}, u32[]{:S(2)}, u32[]{:S(2)}) collective-permute-start(bf16[320,128]{1,0:T(8,128)(2,1)S(1)} %get-tuple-element.11.refs_2_), channel_id=1, source_target_pairs={{0,12},{4,0},{8,4},{12,8},{1,13},{5,1},{9,5},{13,9},{2,14},{6,2},{... | collective-permute-start | bytes 245768 | tf_op jit(solution)/shard_map/ppermute | solution.py:247
  70.3 18.9 %copy-start.9 = (s32[1,4]{1,0:T(1,128)S(1)}, s32[1,4]{1,0:T(1,128)}, u32[]{:S(2)}) copy-start(s32[1,4]{1,0:T(1,128)} %refs_0_.1) | copy-start | bytes 52
  72.1 17.2 %collective-permute-start.7 = (bf16[320,128]{1,0:T(8,128)(2,1)S(1)}, bf16[320,128]{1,0:T(8,128)(2,1)S(1)}, u32[]{:S(2)}, u32[]{:S(2)}) collective-permute-start(bf16[320,128]{1,0:T(8,128)(2,1)S(1)} %get-tuple-element.11.refs_2_), channel_id=1, source_target_pairs={{0,4},{4,8},{8,12},{12,0},{1,5},{5,9},{9,13},{13,1},{2,6},{6,10},{... | collective-permute-start | bytes 245768 | tf_op jit(solution)/shard_map/ppermute | solution.py:247
  72.1 7.0 %copy-start = (bf16[8,5,512,512]{3,2,1,0:T(8,128)(2,1)S(1)}, bf16[8,5,512,512]{3,2,1,0:T(8,128)(2,1)}, u32[]{:S(2)}) copy-start(bf16[8,5,512,512]{3,2,1,0:T(8,128)(2,1)} %blocks_ref.5) | copy-start | bytes 62914564
  79.0 10.2 %copy-start.6 = (bf16[1,4,64,64]{3,2,1,0:T(8,128)(2,1)S(1)}, bf16[1,4,64,64]{3,2,1,0:T(8,128)(2,1)}, u32[]{:S(2)}) copy-start(bf16[1,4,64,64]{3,2,1,0:T(8,128)(2,1)} %refs_6_.1) | copy-start | bytes 98308
  79.0 10.2 %copy-start.7 = (bf16[1,4,64,64]{3,2,1,0:T(8,128)(2,1)S(1)}, bf16[1,4,64,64]{3,2,1,0:T(8,128)(2,1)}, u32[]{:S(2)}) copy-start(bf16[1,4,64,64]{3,2,1,0:T(8,128)(2,1)} %refs_7_.1) | copy-start | bytes 98308
  90.3 7.0 %copy-start.1 = (bf16[8,5,512,512]{3,2,1,0:T(8,128)(2,1)S(1)}, bf16[8,5,512,512]{3,2,1,0:T(8,128)(2,1)}, u32[]{:S(2)}) copy-start(bf16[8,5,512,512]{3,2,1,0:T(8,128)(2,1)} %blocks_ref.5) | copy-start | bytes 62914564

commit v2 on v1

--- a/solution.py
+++ b/solution.py
@@ -7,11 +7,10 @@
 from jax.experimental.pallas import tpu as pltpu
 from jax.sharding import PartitionSpec as P
 
-MIB = 1 << 20
+VMEM_GRANT = 46 << 20
 VMEM = pl.BlockSpec(memory_space=pltpu.VMEM)
 SMEM = pl.BlockSpec(memory_space=pltpu.SMEM)
 ANY = pl.BlockSpec(memory_space=pl.ANY)
-HBM = pl.BlockSpec(memory_space=pltpu.HBM)
 
 
 def dot(a, b):
@@ -45,13 +44,12 @@
     out_ref[rank:, :] = dot_t(mid_map_ref[0], mid).astype(jnp.bfloat16)
 
 
-def group_kernel(count, *refs):
-    parts, out_ref, top_ref = refs[:count], refs[count], refs[count + 1]
+def group_kernel(count, parts_ref, out_ref, top_ref):
     rank = top_ref.shape[0]
     top = jnp.zeros(top_ref.shape, jnp.float32)
-    for i, part in enumerate(parts):
-        out_ref[i * rank : (i + 1) * rank, :] = part[:rank, :]
-        top += part[rank:, :].astype(jnp.float32)
+    for i in range(count):
+        out_ref[i * rank : (i + 1) * rank, :] = parts_ref[2 * i * rank : (2 * i + 1) * rank, :]
+        top += parts_ref[(2 * i + 1) * rank : (2 * i + 2) * rank, :].astype(jnp.float32)
     top = top.astype(jnp.bfloat16)
     out_ref[count * rank :, :] = top
     top_ref[...] = top
@@ -83,7 +81,7 @@
         live = slot < far_count[0]
         partner = jnp.where(live, far_ids[0, slot], group * inner_size)
         side = partner // inner_size - group + 1
-        place = lax.rem(inner - lax.rem(partner, inner_size) + inner_size, inner_size)
+        place = inner ^ lax.rem(partner, inner_size)
         at = pl.multiple_of((side * inner_size + place) * rank, rank)
         term = dot(mid_couple[0, slot], window[pl.ds(at, rank), :])
         total += jnp.where(live, term, 0.0)
@@ -162,50 +160,53 @@
     near_products(blocks_ref, near, lists, count, buffer, sems, clear, lambda leaf: None, x_ref, total)
 
 
-def close_kernel(ids_ref, before, after, blocks_ref, sum_ref, down_ref, basis_ref, total, slot_list, place_list, ends, buffer, sems, x_ref, x_sems):
+def close_kernel(early, step, ids_ref, *refs):
+    parts = refs[: 2 * early]
+    blocks_ref, sum_ref, down_ref, basis_ref, total, slot_list, place_list, ends, buffer, sems, x_ref, x_sems = refs[2 * early :]
     leaves, near = ids_ref.shape
-    half = leaves // 2
     rank, rows = basis_ref.shape[1:]
+    size = step * rows
+    reach = early * step
 
     def place_of(offset):
         ahead = offset >= leaves
-        ok = ((offset < 0) & (offset >= -half)) | (ahead & (offset < leaves + half))
-        return ok, jnp.where(ahead, offset - leaves + half, offset + half)
-
+        ok = ((offset < 0) & (offset >= -reach)) | (ahead & (offset < leaves + reach))
+        return ok, jnp.where(ahead, offset - leaves + reach, offset + reach)
+
+    loads = []
+    for wave in range(early):
+        for side, place in enumerate((early - 1 - wave, early + wave)):
+            index = 2 * wave + side
+            loads.append(pltpu.make_async_copy(parts[index], x_ref.at[place * size : (place + 1) * size], x_sems.at[index]))
+    for load in loads:
+        load.start()
     lists = (slot_list, place_list, ends)
     count = listed(ids_ref, *lists, place_of)
 
     def ready():
-        cut = half * rows
-        one = pltpu.make_async_copy(before, x_ref.at[:cut], x_sems.at[0])
-        two = pltpu.make_async_copy(after, x_ref.at[cut:], x_sems.at[1])
-        one.start()
-        two.start()
         for leaf in range(leaves):
             here = slice(leaf * rows, (leaf + 1) * rows)
             total[here, :] = sum_ref[here, :] + dot_t(basis_ref[leaf], down_ref[leaf * rank : (leaf + 1) * rank, :])
-        one.wait()
-        two.wait()
+        for load in loads:
+            load.wait()
 
     near_products(blocks_ref, near, lists, count, buffer, sems, ready, lambda leaf: None, x_ref, total)
 
 
-def last_kernel(ids_ref, before, after, blocks_ref, sum_ref, out_ref, slot_list, place_list, ends, buffer, sems, x_ref, x_sems, total, result, out_sems):
+def last_kernel(step, ids_ref, before, after, blocks_ref, sum_ref, out_ref, slot_list, place_list, ends, buffer, sems, x_ref, x_sems, total, result, out_sems):
     leaves, near = ids_ref.shape
-    half = leaves // 2
     rows = buffer.shape[1]
+    size = step * rows
 
     def place_of(offset):
-        ahead = offset >= leaves
-        ok = (offset < -half) | (offset >= leaves + half)
-        return ok, jnp.where(ahead, offset - leaves, offset + leaves)
+        ok = (offset < step - leaves) | (offset >= 2 * leaves - step)
+        return ok, jnp.where(offset >= leaves, offset - 2 * leaves + 2 * step, offset + leaves)
 
     lists = (slot_list, place_list, ends)
-    cut = half * rows
     loads = (
         pltpu.make_async_copy(sum_ref, total, x_sems.at[2]),
-        pltpu.make_async_copy(before, x_ref.at[:cut], x_sems.at[0]),
-        pltpu.make_async_copy(after, x_ref.at[cut:], x_sems.at[1]),
+        pltpu.make_async_copy(before, x_ref.at[:size], x_sems.at[0]),
+        pltpu.make_async_copy(after, x_ref.at[size:], x_sems.at[1]),
     )
     for load in loads:
         load.start()
@@ -236,9 +237,9 @@
     inner_size = lax.axis_size("inner")
     leaf_size = lax.axis_size("leaf")
     devices = leaf_size * inner_size
-    half = leaves // 2
-    cut = half * rows
     bf16 = jnp.bfloat16
+    waves = 4
+    step = leaves // waves
 
     def shaped(*shape, dtype=bf16):
         return jax.ShapeDtypeStruct(shape, dtype)
@@ -248,19 +249,17 @@
 
     up = [(i, i + 1) for i in range(devices - 1)]
     down = [(j, i) for i, j in up]
-    both = ("leaf", "inner")
-    first, second = anomalies[:cut], anomalies[cut:]
-    before_close = lax.ppermute(second, both, up)
-    after_close = lax.ppermute(first, both, down)
-
-    part = call(up_kernel, shaped(2 * rank, columns), [VMEM] * 4, VMEM, [], 2 * rows * rank * leaves * columns, anomalies.size * 3, 16 * MIB)(
-        anomalies, leaf_basis, transfer_leaf, transfer_mid
-    )
-    parts = [part] + [shifted(part, "inner", inner_size, s) for s in range(1, inner_size)]
-
-    first, second, _ = lax.optimization_barrier((first, second, part))
-    before_far = lax.ppermute(first, both, up)
-    after_far = lax.ppermute(second, both, down)
+
+    size = step * rows
+    quarters = [lax.slice_in_dim(anomalies, i * size, (i + 1) * size) for i in range(waves)]
+
+    def halo_parts(number):
+        return quarters[waves - 1 - number], quarters[number]
+
+    def wave(x, number):
+        ahead = lax.ppermute(lax.slice_in_dim(x, (waves - 1 - number) * size, (waves - number) * size), ("leaf", "inner"), up)
+        back = lax.ppermute(lax.slice_in_dim(x, number * size, (number + 1) * size), ("leaf", "inner"), down)
+        return ahead, back
 
     def scratch(depth):
         slots = leaves * near + 1
@@ -272,16 +271,36 @@
             pltpu.SemaphoreType.DMA((depth,)),
         ]
 
-    wide = shaped(leaves * rows, columns, dtype=jnp.float32)
-    flops = 2 * rows * rows * columns
-    own_sum = call(own_kernel, wide, [SMEM, VMEM, HBM], VMEM, scratch(8), 20 * flops, 20 * rows * rows * 2, 16 * MIB)(
-        near_ids, anomalies, near_blocks
-    )
-
-    group, top = call(functools.partial(group_kernel, inner_size), (shaped((inner_size + 1) * rank, columns), shaped(rank, columns)), [VMEM] * inner_size, (VMEM, VMEM), [], 1000, 1000, 16 * MIB)(*parts)
+    halo = [wave(anomalies, 0)]
+    x_up, _ = lax.optimization_barrier((anomalies, halo_parts(0)))
+    part = call(up_kernel, shaped(2 * rank, columns), [VMEM] * 4, VMEM, [], 2 * rows * rank * leaves * columns, anomalies.size * 3, VMEM_GRANT)(
+        x_up, leaf_basis, transfer_leaf, transfer_mid
+    )
+    later, gathered = lax.optimization_barrier((anomalies, part))
+    halo.append(wave(later, 1))
+    reach = 1
+    while reach < inner_size:
+        partner = lax.ppermute(gathered, "inner", [(i, i ^ reach) for i in range(inner_size)])
+        partner, gathered, halo[0] = lax.optimization_barrier((partner, gathered, halo[0]))
+        gathered = jnp.concatenate([gathered, partner])
+        if reach == 1:
+            later, gathered = lax.optimization_barrier((anomalies, gathered))
+            halo.append(wave(later, 2))
+        reach *= 2
+    gathered, halo[1] = lax.optimization_barrier((gathered, halo[1]))
+    group, top = call(functools.partial(group_kernel, inner_size), (shaped((inner_size + 1) * rank, columns), shaped(rank, columns)), [VMEM], (VMEM, VMEM), [], 1000, 1000, VMEM_GRANT)(gathered)
+    later, group, top = lax.optimization_barrier((anomalies, group, top))
     before_group = shifted(group, "leaf", leaf_size, 1)
     after_group = shifted(group, "leaf", leaf_size, leaf_size - 1)
     tops = [shifted(top, "leaf", leaf_size, s) for s in range(2, leaf_size - 1)]
+    halo.append(wave(later, 3))
+
+    wide = shaped(leaves * rows, columns, dtype=jnp.float32)
+    flops = 2 * rows * rows * columns
+    x_own, _ = lax.optimization_barrier((anomalies, group))
+    own_sum = call(own_kernel, wide, [SMEM, VMEM, ANY], VMEM, scratch(8), 20 * flops, 20 * rows * rows * 2, VMEM_GRANT)(
+        near_ids, x_own, near_blocks
+    )
     leaf_down = call(
         functools.partial(down_kernel, leaf_size, inner_size),
         shaped(leaves * rank, columns),
@@ -290,22 +309,23 @@
         [pltpu.VMEM((3 * inner_size * rank, columns), bf16)],
         1000,
         1000,
-        16 * MIB,
+        VMEM_GRANT,
     )(far_ids, far_count, group, before_group, after_group, *tops, top_couple, mid_couple, transfer_mid, transfer_leaf)
 
-    close_scratch = scratch(8) + [pltpu.VMEM((2 * cut, columns), bf16), pltpu.SemaphoreType.DMA((3,))]
-    close_sum = call(close_kernel, wide, [SMEM, ANY, ANY, HBM, VMEM, VMEM, VMEM], VMEM, close_scratch, 12 * flops, 12 * rows * rows * 2, 24 * MIB)(
-        near_ids, before_close, after_close, near_blocks, own_sum, leaf_down, leaf_basis
+    early = waves - 1
+    close_scratch = scratch(16) + [pltpu.VMEM((2 * early * step * rows, columns), bf16), pltpu.SemaphoreType.DMA((2 * early,))]
+    close_sum = call(functools.partial(close_kernel, early, step), wide, [SMEM] + [ANY] * (2 * early + 1) + [VMEM] * 3, VMEM, close_scratch, 16 * flops, 16 * rows * rows * 2, VMEM_GRANT)(
+        near_ids, *[x for pair in halo[:early] for x in pair], near_blocks, own_sum, leaf_down, leaf_basis
     )
     last_scratch = scratch(16) + [
-        pltpu.VMEM((2 * cut, columns), bf16),
+        pltpu.VMEM((2 * step * rows, columns), bf16),
         pltpu.SemaphoreType.DMA((3,)),
         pltpu.VMEM((leaves * rows, columns), jnp.float32),
         pltpu.VMEM((leaves * rows, columns), bf16),
         pltpu.SemaphoreType.DMA((leaves,)),
     ]
-    return call(last_kernel, shaped(leaves * rows, columns), [SMEM, ANY, ANY, HBM, ANY], ANY, last_scratch, 6 * flops, 6 * rows * rows * 2, 24 * MIB)(
-        near_ids, before_far, after_far, near_blocks, close_sum
+    return call(functools.partial(last_kernel, step), shaped(leaves * rows, columns), [SMEM, ANY, ANY, ANY, ANY], ANY, last_scratch, 6 * flops, 6 * rows * rows * 2, VMEM_GRANT)(
+        near_ids, *halo[early], near_blocks, close_sum
     )
 
 

time: 107 us -> 72.7 us (0.68)
  waiting for transfers between devices: 47 us -> 11.8 us
  starting transfers between devices: 21.9 us -> 32.5 us
  local copies, waits for them, and re-layouts: 15.3 us -> 5.09 us
    ppermute x6 -> x3, waiting for transfers between devices: 47 us -> 0.47 us  [shifted(): return lax.ppermute(x, axis, [(i, (i + shift) % size) for i in range(size)])]
    ppermute x4 -> x10, starting transfers between devices: 15.9 us -> 30.3 us  [the longest x4 16.9 us: wave(): lax.ppermute(lax.slice_in_dim(x, number * size, (number + 1) * size), ('l...]
    ppermute x4 -> x10, waiting for transfers between devices: 0.01 us -> 11.3 us  [the longest x2 11.3 us: local(): lax.ppermute(gathered, 'inner', [(i, i ^ reach) for i in range(inner_size)])]
    unnamed x20 -> x22, local copies, waits for them, and re-layouts: 14 us -> 3.92 us
    ppermute x6 -> x3, starting transfers between devices: 6.04 us -> 2.23 us  [shifted(): return lax.ppermute(x, axis, [(i, (i + shift) % size) for i in range(size)])]
  transfers between devices with their start and end apart: 10 -> 13, of which waited for: 5 -> 2; matrix products, arithmetic and copies ran while one was open for 0% -> 0% of each run, Pallas kernels for 16% -> 24%
where the time goes in v2:
time: 72.7 us; the launch traced here: 71.9 us
  starting transfers between devices  32.5 us (45%)
  Pallas kernels  21.5 us (30%)
  waiting for transfers between devices  11.8 us (16%)
  local copies, waits for them, and re-layouts  5.09 us (7%)
  between operations  1 us (1%)
    ppermute x4, starting transfers between devices, wave(): lax.ppermute(lax.slice_in_dim(x, number * size, (number + 1) * size), ('l...  16.9 us
    ppermute x4, starting transfers between devices, wave(): lax.ppermute(lax.slice_in_dim(x, (waves - 1 - number) * size, (waves - nu...  13.3 us
    ppermute x2, waiting for transfers between devices, local(): lax.ppermute(gathered, 'inner', [(i, i ^ reach) for i in range(inner_size)])  11.3 us
    pallas_call x1, Pallas kernels, local(): call(functools.partial(close_kernel, early, step), wide, [SMEM] + [ANY] *...  8.08 us
    pallas_call x1, Pallas kernels, local(): call(own_kernel, wide, [SMEM, VMEM, ANY], VMEM, scratch(8), 20 * flops, 2...  7.13 us
    pallas_call x1, Pallas kernels, local(): call(functools.partial(last_kernel, step), shaped(leaves * rows, columns)...  4.35 us
    unnamed x22, local copies, waits for them, and re-layouts  3.92 us
    ppermute x3, starting transfers between devices, shifted(): return lax.ppermute(x, axis, [(i, (i + shift) % size) for i in range(size)])  2.23 us
  transfers between devices with their start and end apart: 13, of which 2 were waited for; matrix products, arithmetic and copies ran while one was open for 0% of the time, Pallas kernels for 24%

profile of v2, /device:TPU:1, one launch (start us, length us, event | category | flops | bytes accessed | tf_op | source)
XLA Modules:
  0.0 71.9 jit_solution(6870074025737686323)
XLA Ops:
  0.0 1.1 %fusion.3 = (bf16[1024,128]{1,0:T(8,128)(2,1)S(1)}, bf16[1024,128]{1,0:T(8,128)(2,1)S(1)}) fusion(bf16[4096,128]{1,0:T(8,128)(2,1)} %x_ref.1), kind=kLoop, calls=%fused_computation.5 | loop fusion | bytes 1048576 | tf_op jit(solution)/shard_map/slice | solution.py:254
  1.1 4.0 %collective-permute-start.1 = (bf16[1024,128]{1,0:T(8,128)(2,1)S(1)}, bf16[1024,128]{1,0:T(8,128)(2,1)S(1)}, u32[]{:S(2)}, u32[]{:S(2)}) collective-permute-start(bf16[1024,128]{1,0:T(8,128)(2,1)S(1)} %get-tuple-element.56), channel_id=1, source_target_pairs={{0,1},{1,2},{2,3},{3,4},{4,5},{5,6},{6,7},{7,8},{8,9},{9,10},{10,1... | collective-permute-start | bytes 786440 | tf_op jit(solution)/shard_map/ppermute | solution.py:260
  5.1 4.5 %collective-permute-start.2 = (bf16[1024,128]{1,0:T(8,128)(2,1)S(1)}, bf16[1024,128]{1,0:T(8,128)(2,1)S(1)}, u32[]{:S(2)}, u32[]{:S(2)}) collective-permute-start(bf16[1024,128]{1,0:T(8,128)(2,1)S(1)} %get-tuple-element.55), channel_id=1, source_target_pairs={{1,0},{2,1},{3,2},{4,3},{5,4},{6,5},{7,6},{8,7},{9,8},{10,9},{11,1... | collective-permute-start | bytes 786440 | tf_op jit(solution)/shard_map/ppermute | solution.py:261
  9.6 0.0 copy-start
  9.6 1.2 %copy-done = bf16[4096,128]{1,0:T(8,128)(2,1)S(1)} copy-done((bf16[4096,128]{1,0:T(8,128)(2,1)S(1)}, bf16[4096,128]{1,0:T(8,128)(2,1)}, u32[]{:S(2)}) %copy-start) | copy-done | bytes 1048600
  10.9 1.0 %copy-done.2 = bf16[8,64,512]{2,1,0:T(8,128)(2,1)S(1)} copy-done((bf16[8,64,512]{2,1,0:T(8,128)(2,1)S(1)}, bf16[8,64,512]{2,1,0:T(8,128)(2,1)}, u32[]{:S(2)}) %copy-start.2) | copy-done | bytes 524312
  11.9 0.9 %copy-done.4 = bf16[8,64,64]{2,1,0:T(8,128)(2,1)S(1)} copy-done((bf16[8,64,64]{2,1,0:T(8,128)(2,1)S(1)}, bf16[8,64,64]{2,1,0:T(8,128)(2,1)}, u32[]{:S(2)}) %copy-start.4) | copy-done | bytes 65560
  12.8 0.7 copy-done.5
  13.5 0.9 %shard_map.100 = bf16[128,128]{1,0:T(8,128)(2,1)S(1)} custom-call(bf16[4096,128]{1,0:T(8,128)(2,1)S(1)} %copy-done, bf16[8,64,512]{2,1,0:T(8,128)(2,1)S(1)} %copy-done.2, bf16[8,64,64]{2,1,0:T(8,128)(2,1)S(1)} %copy-done.4, bf16[1,64,64]{2,1,0:T(8,128)(2,1)S(1)} %copy-done.5), custom_call_target="tpu_custom_call" | custom-call | flops 67108864 | bytes 1572864 | tf_op jit(solution)/shard_map/pallas_call | solution.py:276
  14.5 0.1 collective-permute-start
  14.6 3.4 %collective-permute-start.4 = (bf16[1024,128]{1,0:T(8,128)(2,1)S(1)}, bf16[1024,128]{1,0:T(8,128)(2,1)S(1)}, u32[]{:S(2)}, u32[]{:S(2)}) collective-permute-start(bf16[1024,128]{1,0:T(8,128)(2,1)S(1)} %get-tuple-element.54), channel_id=1, source_target_pairs={{0,1},{1,2},{2,3},{3,4},{4,5},{5,6},{6,7},{7,8},{8,9},{9,10},{10,1... | collective-permute-start | bytes 786440 | tf_op jit(solution)/shard_map/ppermute | solution.py:260
  17.9 4.0 %collective-permute-start.5 = (bf16[1024,128]{1,0:T(8,128)(2,1)S(1)}, bf16[1024,128]{1,0:T(8,128)(2,1)S(1)}, u32[]{:S(2)}, u32[]{:S(2)}) collective-permute-start(bf16[1024,128]{1,0:T(8,128)(2,1)S(1)} %get-tuple-element.53), channel_id=1, source_target_pairs={{1,0},{2,1},{3,2},{4,3},{5,4},{6,5},{7,6},{8,7},{9,8},{10,9},{11,1... | collective-permute-start | bytes 786440 | tf_op jit(solution)/shard_map/ppermute | solution.py:261
  22.0 0.0 collective-permute-done
  22.0 0.0 collective-permute-done.1.refs_0_
  22.0 0.0 collective-permute-done.2.refs_1_
  22.0 0.1 collective-permute-start.3
  22.1 4.0 %collective-permute-start.8 = (bf16[1024,128]{1,0:T(8,128)(2,1)S(1)}, bf16[1024,128]{1,0:T(8,128)(2,1)S(1)}, u32[]{:S(2)}, u32[]{:S(2)}) collective-permute-start(bf16[1024,128]{1,0:T(8,128)(2,1)S(1)} %get-tuple-element.50), channel_id=1, source_target_pairs={{0,1},{1,2},{2,3},{3,4},{4,5},{5,6},{6,7},{7,8},{8,9},{9,10},{10,1... | collective-permute-start | bytes 786440 | tf_op jit(solution)/shard_map/ppermute | solution.py:260
  26.1 3.4 %collective-permute-start.9 = (bf16[1024,128]{1,0:T(8,128)(2,1)S(1)}, bf16[1024,128]{1,0:T(8,128)(2,1)S(1)}, u32[]{:S(2)}, u32[]{:S(2)}) collective-permute-start(bf16[1024,128]{1,0:T(8,128)(2,1)S(1)} %get-tuple-element.49), channel_id=1, source_target_pairs={{1,0},{2,1},{3,2},{4,3},{5,4},{6,5},{7,6},{8,7},{9,8},{10,9},{11,1... | collective-permute-start | bytes 786440 | tf_op jit(solution)/shard_map/ppermute | solution.py:261
  29.5 11.3 %collective-permute-done.3 = bf16[256,128]{1,0:T(8,128)(2,1)S(1)} collective-permute-done((bf16[256,128]{1,0:T(8,128)(2,1)S(1)}, bf16[256,128]{1,0:T(8,128)(2,1)S(1)}, u32[]{:S(2)}, u32[]{:S(2)}) %collective-permute-start.3) | collective-permute-done | bytes 65568 | tf_op jit(solution)/shard_map/ppermute | solution.py:283
  40.8 0.0 collective-permute-done.4.refs_2_
  40.8 0.0 collective-permute-done.5.refs_3_
  40.8 0.1 collective-permute-start.10
  40.9 2.1 %collective-permute-start.12 = (bf16[64,128]{1,0:T(8,128)(2,1)S(1)}, bf16[64,128]{1,0:T(8,128)(2,1)S(1)}, u32[]{:S(2)}, u32[]{:S(2)}) collective-permute-start(bf16[64,128]{1,0:T(8,128)(2,1)S(1)} %get-tuple-element.48), channel_id=1, source_target_pairs={{0,8},{4,12},{8,0},{12,4},{1,9},{5,13},{9,1},{13,5},{2,10},{6,14},... | collective-permute-start | bytes 49160 | tf_op jit(solution)/shard_map/ppermute | solution.py:248
  43.0 0.0 copy-done.1
  43.1 1.9 %collective-permute-start.6 = (bf16[1024,128]{1,0:T(8,128)(2,1)S(1)}, bf16[1024,128]{1,0:T(8,128)(2,1)S(1)}, u32[]{:S(2)}, u32[]{:S(2)}) collective-permute-start(bf16[1024,128]{1,0:T(8,128)(2,1)S(1)} %get-tuple-element.52), channel_id=1, source_target_pairs={{0,1},{1,2},{2,3},{3,4},{4,5},{5,6},{6,7},{7,8},{8,9},{9,10},{10,1... | collective-permute-start | bytes 786440 | tf_op jit(solution)/shard_map/ppermute | solution.py:260
  45.0 0.5 collective-permute-done.12.refs_5_
  45.5 5.0 %collective-permute-start.7 = (bf16[1024,128]{1,0:T(8,128)(2,1)S(1)}, bf16[1024,128]{1,0:T(8,128)(2,1)S(1)}, u32[]{:S(2)}, u32[]{:S(2)}) collective-permute-start(bf16[1024,128]{1,0:T(8,128)(2,1)S(1)} %get-tuple-element.51), channel_id=1, source_target_pairs={{1,0},{2,1},{3,2},{4,3},{5,4},{6,5},{7,6},{8,7},{9,8},{10,9},{11,1... | collective-permute-start | bytes 786440 | tf_op jit(solution)/shard_map/ppermute | solution.py:261
  51.1 0.0 copy-start.6
  51.1 0.0 copy-start.7
  51.1 0.0 copy-start.8
  51.1 0.0 copy-start.10
  51.2 0.0 copy-start.3
  51.2 0.0 collective-permute-done.10.refs_3_
  51.2 0.1 collective-permute-start.11
  51.2 0.0 copy-done.9
  51.2 7.1 %shard_map.102.refs_7_ = f32[4096,128]{1,0:T(8,128)S(1)} custom-call(s32[8,5]{1,0:T(8,128)S(1)} %copy-done.9, bf16[4096,128]{1,0:T(8,128)(2,1)S(1)} %copy-done.1, bf16[8,5,512,512]{3,2,1,0:T(8,128)(2,1)} %blocks_ref.3), custom_call_target="tpu_custom_call" | custom-call | flops 1342177280 | bytes 10485760 | tf_op jit(solution)/shard_map/pallas_call | solution.py:301
  58.4 0.0 collective-permute-done.11.refs_4_
  58.4 0.0 copy-done.6
  58.4 0.0 copy-done.7
  58.4 0.0 copy-done.8
  58.4 0.0 copy-done.10
  58.4 1.0 %shard_map.103.refs_8_ = bf16[512,128]{1,0:T(8,128)(2,1)S(1)} custom-call(s32[1,4]{1,0:T(1,128)S(1)} %copy-done.10, s32[1]{0:T(128)S(6)} %copy.11.refs_1_, bf16[320,128]{1,0:T(8,128)(2,1)S(1)} %get-tuple-element.46.refs_2_, bf16[320,128]{1,0:T(8,128)(2,1)S(1)} %collective-permute-done.10.refs_3_, bf16[320,128]{1,0:T(8,128)(2,1)S(1)} %collective-permute-done.11.refs_4_, ...), custom_call_target="tpu_custom_call" | custom-call | flops 1000 | bytes 1000 | tf_op jit(solution)/shard_map/pallas_call | solution.py:304
  59.4 0.0 collective-permute-done.8.refs_4_
  59.4 0.0 collective-permute-done.9.refs_5_
  59.5 8.1 %shard_map.104.sum_ref = f32[4096,128]{1,0:T(8,128)S(1)} custom-call(s32[8,5]{1,0:T(8,128)S(1)} %copy-done.9, bf16[1024,128]{1,0:T(8,128)(2,1)S(1)} %collective-permute-done.1.refs_0_, bf16[1024,128]{1,0:T(8,128)(2,1)S(1)} %collective-permute-done.2.refs_1_, bf16[1024,128]{1,0:T(8,128)(2,1)S(1)} %collective-permute-done.4.refs_2_, ...), custom_call_target="tpu_custom_call" | custom-call | flops 1073741824 | bytes 8388608 | tf_op jit(solution)/shard_map/pallas_call | solution.py:317
  67.6 0.0 collective-permute-done.6.before
  67.6 0.0 collective-permute-done.7.after
  67.6 4.4 %shard_map.105 = bf16[4096,128]{1,0:T(8,128)(2,1)} custom-call(s32[8,5]{1,0:T(8,128)S(1)} %copy-done.9, bf16[1024,128]{1,0:T(8,128)(2,1)S(1)} %collective-permute-done.6.before, bf16[1024,128]{1,0:T(8,128)(2,1)S(1)} %collective-permute-done.7.after, bf16[8,5,512,512]{3,2,1,0:T(8,128)(2,1)} %blocks_ref.3, f32[4096,128]{1,0:T(8,128)S(1)} %shard_map.104.sum_ref), custom_call_target="tpu_custom_call" | custom-call | flops 402653184 | bytes 3145728 | tf_op jit(solution)/shard_map/pallas_call | solution.py:327
  (12 shorter events, 0.2 us)
Async XLA Ops:
  1.1 20.9 %collective-permute-start.1 = (bf16[1024,128]{1,0:T(8,128)(2,1)S(1)}, bf16[1024,128]{1,0:T(8,128)(2,1)S(1)}, u32[]{:S(2)}, u32[]{:S(2)}) collective-permute-start(bf16[1024,128]{1,0:T(8,128)(2,1)S(1)} %get-tuple-element.56), channel_id=1, source_target_pairs={{0,1},{1,2},{2,3},{3,4},{4,5},{5,6},{6,7},{7,8},{8,9},{9,10},{10,1... | collective-permute-start | bytes 786440 | tf_op jit(solution)/shard_map/ppermute | solution.py:260
  5.1 16.9 %collective-permute-start.2 = (bf16[1024,128]{1,0:T(8,128)(2,1)S(1)}, bf16[1024,128]{1,0:T(8,128)(2,1)S(1)}, u32[]{:S(2)}, u32[]{:S(2)}) collective-permute-start(bf16[1024,128]{1,0:T(8,128)(2,1)S(1)} %get-tuple-element.55), channel_id=1, source_target_pairs={{1,0},{2,1},{3,2},{4,3},{5,4},{6,5},{7,6},{8,7},{9,8},{10,9},{11,1... | collective-permute-start | bytes 786440 | tf_op jit(solution)/shard_map/ppermute | solution.py:261
  9.6 1.2 %copy-start = (bf16[4096,128]{1,0:T(8,128)(2,1)S(1)}, bf16[4096,128]{1,0:T(8,128)(2,1)}, u32[]{:S(2)}) copy-start(bf16[4096,128]{1,0:T(8,128)(2,1)} %x_ref.1) | copy-start | bytes 3145732
  10.9 1.0 %copy-start.2 = (bf16[8,64,512]{2,1,0:T(8,128)(2,1)S(1)}, bf16[8,64,512]{2,1,0:T(8,128)(2,1)}, u32[]{:S(2)}) copy-start(bf16[8,64,512]{2,1,0:T(8,128)(2,1)} %refs_9_.3) | copy-start | bytes 1572868
  11.9 0.9 %copy-start.4 = (bf16[8,64,64]{2,1,0:T(8,128)(2,1)S(1)}, bf16[8,64,64]{2,1,0:T(8,128)(2,1)}, u32[]{:S(2)}) copy-start(bf16[8,64,64]{2,1,0:T(8,128)(2,1)} %refs_9_.2) | copy-start | bytes 196612
  12.8 0.7 copy-start.5
  13.5 29.5 %copy-start.1 = (bf16[4096,128]{1,0:T(8,128)(2,1)S(1)}, bf16[4096,128]{1,0:T(8,128)(2,1)}, u32[]{:S(2)}) copy-start(bf16[4096,128]{1,0:T(8,128)(2,1)} %x_ref.1) | copy-start | bytes 3145732
  14.5 36.8 %copy-start.9 = (s32[8,5]{1,0:T(8,128)S(1)}, s32[8,5]{1,0:T(8,128)}, u32[]{:S(2)}) copy-start(s32[8,5]{1,0:T(8,128)} %ids_ref.5) | copy-start | bytes 484
  14.5 7.5 %collective-permute-start = (bf16[128,128]{1,0:T(8,128)(2,1)S(1)}, bf16[128,128]{1,0:T(8,128)(2,1)S(1)}, u32[]{:S(2)}, u32[]{:S(2)}) collective-permute-start(bf16[128,128]{1,0:T(8,128)(2,1)S(1)} %shard_map.100), channel_id=1, source_target_pairs={{0,1},{1,0},{2,3},{3,2},{4,5},{5,4},{6,7},{7,6},{8,9},{9,8},{10,11... | collective-permute-start | bytes 98312 | tf_op jit(solution)/shard_map/ppermute | solution.py:283
  14.6 26.2 %collective-permute-start.4 = (bf16[1024,128]{1,0:T(8,128)(2,1)S(1)}, bf16[1024,128]{1,0:T(8,128)(2,1)S(1)}, u32[]{:S(2)}, u32[]{:S(2)}) collective-permute-start(bf16[1024,128]{1,0:T(8,128)(2,1)S(1)} %get-tuple-element.54), channel_id=1, source_target_pairs={{0,1},{1,2},{2,3},{3,4},{4,5},{5,6},{6,7},{7,8},{8,9},{9,10},{10,1... | collective-permute-start | bytes 786440 | tf_op jit(solution)/shard_map/ppermute | solution.py:260
  17.9 22.9 %collective-permute-start.5 = (bf16[1024,128]{1,0:T(8,128)(2,1)S(1)}, bf16[1024,128]{1,0:T(8,128)(2,1)S(1)}, u32[]{:S(2)}, u32[]{:S(2)}) collective-permute-start(bf16[1024,128]{1,0:T(8,128)(2,1)S(1)} %get-tuple-element.53), channel_id=1, source_target_pairs={{1,0},{2,1},{3,2},{4,3},{5,4},{6,5},{7,6},{8,7},{9,8},{10,9},{11,1... | collective-permute-start | bytes 786440 | tf_op jit(solution)/shard_map/ppermute | solution.py:261
  22.0 18.8 %collective-permute-start.3 = (bf16[256,128]{1,0:T(8,128)(2,1)S(1)}, bf16[256,128]{1,0:T(8,128)(2,1)S(1)}, u32[]{:S(2)}, u32[]{:S(2)}) collective-permute-start(bf16[256,128]{1,0:T(8,128)(2,1)S(1)} %pad_maximum_fusion.1), channel_id=1, source_target_pairs={{0,2},{1,3},{2,0},{3,1},{4,6},{5,7},{6,4},{7,5},{8,10},{9,11},{10,... | collective-permute-start | bytes 196616 | tf_op jit(solution)/shard_map/ppermute | solution.py:283
  22.1 37.3 %collective-permute-start.8 = (bf16[1024,128]{1,0:T(8,128)(2,1)S(1)}, bf16[1024,128]{1,0:T(8,128)(2,1)S(1)}, u32[]{:S(2)}, u32[]{:S(2)}) collective-permute-start(bf16[1024,128]{1,0:T(8,128)(2,1)S(1)} %get-tuple-element.50), channel_id=1, source_target_pairs={{0,1},{1,2},{2,3},{3,4},{4,5},{5,6},{6,7},{7,8},{8,9},{9,10},{10,1... | collective-permute-start | bytes 786440 | tf_op jit(solution)/shard_map/ppermute | solution.py:260
  26.1 33.3 %collective-permute-start.9 = (bf16[1024,128]{1,0:T(8,128)(2,1)S(1)}, bf16[1024,128]{1,0:T(8,128)(2,1)S(1)}, u32[]{:S(2)}, u32[]{:S(2)}) collective-permute-start(bf16[1024,128]{1,0:T(8,128)(2,1)S(1)} %get-tuple-element.49), channel_id=1, source_target_pairs={{1,0},{2,1},{3,2},{4,3},{5,4},{6,5},{7,6},{8,7},{9,8},{10,9},{11,1... | collective-permute-start | bytes 786440 | tf_op jit(solution)/shard_map/ppermute | solution.py:261
  40.8 10.3 %collective-permute-start.10 = (bf16[320,128]{1,0:T(8,128)(2,1)S(1)}, bf16[320,128]{1,0:T(8,128)(2,1)S(1)}, u32[]{:S(2)}, u32[]{:S(2)}) collective-permute-start(bf16[320,128]{1,0:T(8,128)(2,1)S(1)} %get-tuple-element.46.refs_2_), channel_id=1, source_target_pairs={{0,4},{4,8},{8,12},{12,0},{1,5},{5,9},{9,13},{13,1},{2,6},{6,10},{... | collective-permute-start | bytes 245768 | tf_op jit(solution)/shard_map/ppermute | solution.py:248
  40.9 4.5 %collective-permute-start.12 = (bf16[64,128]{1,0:T(8,128)(2,1)S(1)}, bf16[64,128]{1,0:T(8,128)(2,1)S(1)}, u32[]{:S(2)}, u32[]{:S(2)}) collective-permute-start(bf16[64,128]{1,0:T(8,128)(2,1)S(1)} %get-tuple-element.48), channel_id=1, source_target_pairs={{0,8},{4,12},{8,0},{12,4},{1,9},{5,13},{9,1},{13,5},{2,10},{6,14},... | collective-permute-start | bytes 49160 | tf_op jit(solution)/shard_map/ppermute | solution.py:248
  43.1 24.5 %collective-permute-start.6 = (bf16[1024,128]{1,0:T(8,128)(2,1)S(1)}, bf16[1024,128]{1,0:T(8,128)(2,1)S(1)}, u32[]{:S(2)}, u32[]{:S(2)}) collective-permute-start(bf16[1024,128]{1,0:T(8,128)(2,1)S(1)} %get-tuple-element.52), channel_id=1, source_target_pairs={{0,1},{1,2},{2,3},{3,4},{4,5},{5,6},{6,7},{7,8},{8,9},{9,10},{10,1... | collective-permute-start | bytes 786440 | tf_op jit(solution)/shard_map/ppermute | solution.py:260
  45.5 22.1 %collective-permute-start.7 = (bf16[1024,128]{1,0:T(8,128)(2,1)S(1)}, bf16[1024,128]{1,0:T(8,128)(2,1)S(1)}, u32[]{:S(2)}, u32[]{:S(2)}) collective-permute-start(bf16[1024,128]{1,0:T(8,128)(2,1)S(1)} %get-tuple-element.51), channel_id=1, source_target_pairs={{1,0},{2,1},{3,2},{4,3},{5,4},{6,5},{7,6},{8,7},{9,8},{10,9},{11,1... | collective-permute-start | bytes 786440 | tf_op jit(solution)/shard_map/ppermute | solution.py:261
  51.1 7.3 %copy-start.6 = (bf16[1,64,64]{2,1,0:T(8,128)(2,1)S(1)}, bf16[1,64,64]{2,1,0:T(8,128)(2,1)}, u32[]{:S(2)}) copy-start(bf16[1,64,64]{2,1,0:T(8,128)(2,1)} %refs_8_.1) | copy-start | bytes 24580
  51.1 7.3 %copy-start.7 = (bf16[1,4,64,64]{3,2,1,0:T(8,128)(2,1)S(1)}, bf16[1,4,64,64]{3,2,1,0:T(8,128)(2,1)}, u32[]{:S(2)}) copy-start(bf16[1,4,64,64]{3,2,1,0:T(8,128)(2,1)} %refs_6_.2) | copy-start | bytes 98308
  51.1 7.3 %copy-start.8 = (bf16[1,4,64,64]{3,2,1,0:T(8,128)(2,1)S(1)}, bf16[1,4,64,64]{3,2,1,0:T(8,128)(2,1)}, u32[]{:S(2)}) copy-start(bf16[1,4,64,64]{3,2,1,0:T(8,128)(2,1)} %refs_7_.1) | copy-start | bytes 98308
  51.1 7.3 %copy-start.10 = (s32[1,4]{1,0:T(1,128)S(1)}, s32[1,4]{1,0:T(1,128)}, u32[]{:S(2)}) copy-start(s32[1,4]{1,0:T(1,128)} %refs_0_.1) | copy-start | bytes 52
  51.2 8.3 %copy-start.3 = (bf16[8,64,512]{2,1,0:T(8,128)(2,1)S(1)}, bf16[8,64,512]{2,1,0:T(8,128)(2,1)}, u32[]{:S(2)}) copy-start(bf16[8,64,512]{2,1,0:T(8,128)(2,1)} %refs_9_.3) | copy-start | bytes 1572868
  51.2 7.2 %collective-permute-start.11 = (bf16[320,128]{1,0:T(8,128)(2,1)S(1)}, bf16[320,128]{1,0:T(8,128)(2,1)S(1)}, u32[]{:S(2)}, u32[]{:S(2)}) collective-permute-start(bf16[320,128]{1,0:T(8,128)(2,1)S(1)} %get-tuple-element.46.refs_2_), channel_id=1, source_target_pairs={{0,12},{4,0},{8,4},{12,8},{1,13},{5,1},{9,5},{13,9},{2,14},{6,2},{... | collective-permute-start | bytes 245768 | tf_op jit(solution)/shard_map/ppermute | solution.py:248

commit v3 on v1

v3 whole, which is shorter than its diff:
```python
import functools

import jax
import jax.numpy as jnp
from jax import lax
from jax.experimental import pallas as pl
from jax.experimental.pallas import tpu as pltpu
from jax.sharding import PartitionSpec as P

MIB = 1 << 20
VMEM = pl.BlockSpec(memory_space=pltpu.VMEM)
SMEM = pl.BlockSpec(memory_space=pltpu.SMEM)
ANY = pl.BlockSpec(memory_space=pl.ANY)


def held(x, space):
    return pltpu.with_memory_space_constraint(x, space)


def resident(*shape):
    return pltpu.VMEM(shape, jnp.bfloat16)


def dot(a, b):
    return lax.dot_general(a, b, (((1,), (0,)), ((), ())), preferred_element_type=jnp.float32)


def dot_t(a, b):
    return lax.dot_general(a, b, (((0,), (0,)), ((), ())), preferred_element_type=jnp.float32)


def call(kernel, out_shape, in_specs, out_specs, scratch, flops, moved, vmem, aliases=None):
    return pl.pallas_call(
        kernel,
        out_shape=out_shape,
        in_specs=in_specs,
        out_specs=out_specs,
        scratch_shapes=scratch,
        cost_estimate=pl.CostEstimate(flops=flops, bytes_accessed=moved, transcendentals=0),
        compiler_params=pltpu.CompilerParams(vmem_limit_bytes=vmem),
        input_output_aliases=aliases or {},
    )


def up_kernel(early, x_ref, basis_ref, leaf_map_ref, mid_map_ref, out_ref, *refs):
    pieces, (x, basis, leaf_map, mid_map, sems, piece_sems) = refs[:4], refs[4:]
    leaves, rank, rows = basis.shape
    loads = [pltpu.make_async_copy(leaf_map_ref, leaf_map, sems.at[leaves]), pltpu.make_async_copy(mid_map_ref, mid_map, sems.at[leaves + 1])]
    parts = []
    for leaf in range(leaves):
        here = slice(leaf * rows, (leaf + 1) * rows)
        parts.append(pltpu.make_async_copy(x_ref.at[here], x.at[here], sems.at[leaf]))
        parts.append(pltpu.make_async_copy(basis_ref.at[leaf], basis.at[leaf], sems.at[leaves + 2 + leaf]))
    for load in parts[:2] + loads + parts[2:]:
        load.start()
    cuts = ((leaves - early, leaves), (0, early), (0, leaves - early), (early, leaves))
    copies = [pltpu.make_async_copy(x_ref.at[a * rows : b * rows], piece, piece_sems.at[i]) for i, (piece, (a, b)) in enumerate(zip(pieces, cuts))]
    for copy in copies:
        copy.start()
    mid = jnp.zeros((rank, x.shape[1]), jnp.float32)
    for leaf in range(leaves):
        parts[2 * leaf].wait()
        parts[2 * leaf + 1].wait()
        if leaf == 0:
            loads[0].wait()
        skeleton = dot(basis[leaf], x[leaf * rows : (leaf + 1) * rows, :])
        mid += dot_t(leaf_map[leaf], skeleton.astype(jnp.bfloat16))
    loads[1].wait()
    mid = mid.astype(jnp.bfloat16)
    out_ref[:rank, :] = mid
    out_ref[rank:, :] = dot_t(mid_map[0], mid).astype(jnp.bfloat16)
    for copy in copies:
        copy.wait()


def gate_kernel(*refs):
    pass


def group_kernel(count, parts_ref, out_ref, top_ref):
    rank = top_ref.shape[0]
    top = jnp.zeros(top_ref.shape, jnp.float32)
    for i in range(count):
        out_ref[i * rank : (i + 1) * rank, :] = parts_ref[2 * i * rank : (2 * i + 1) * rank, :]
        top += parts_ref[(2 * i + 1) * rank : (2 * i + 2) * rank, :].astype(jnp.float32)
    top = top.astype(jnp.bfloat16)
    out_ref[count * rank :, :] = top
    top_ref[...] = top


def down_kernel(leaf_size, inner_size, *refs):
    far_ids, far_count, own, before, after = refs[:5]
    tops = dict(zip(range(2, leaf_size - 1), refs[5:]))
    couple, mid_couple, mid_map, leaf_map, out_ref, window = refs[5 + len(tops) :]
    rank = mid_map.shape[1]
    group = lax.axis_index("leaf")
    inner = lax.axis_index("inner")
    last = inner_size * rank
    top_down = jnp.zeros((rank, own.shape[1]), jnp.float32)
    for shift in range(1, leaf_size):
        source = lax.rem(group - shift + leaf_size, leaf_size)
        if shift == 1:
            top = before[last:, :]
        elif shift == leaf_size - 1:
            top = after[last:, :]
        else:
            top = tops[shift][...]
        term = dot(couple[0, source], top)
        top_down += jnp.where(jnp.abs(source - group) >= 2, term, 0.0)
    for i, part in enumerate((before, own, after)):
        window[i * last : (i + 1) * last, :] = part[:last, :]
    total = dot(mid_map[0], top_down.astype(jnp.bfloat16))
    for slot in range(mid_couple.shape[1]):
        live = slot < far_count[0]
        partner = jnp.where(live, far_ids[0, slot], group * inner_size)
        side = partner // inner_size - group + 1
        place = inner ^ lax.rem(partner, inner_size)
        at = pl.multiple_of((side * inner_size + place) * rank, rank)
        term = dot(mid_couple[0, slot], window[pl.ds(at, rank), :])
        total += jnp.where(live, term, 0.0)
    total = total.astype(jnp.bfloat16)
    for leaf in range(leaf_map.shape[0]):
        out_ref[leaf * rank : (leaf + 1) * rank, :] = dot(leaf_map[leaf], total).astype(jnp.bfloat16)


def listed(ids_ref, lists, kind_of):
    leaves, near = ids_ref.shape
    first = (lax.axis_index("leaf") * lax.axis_size("inner") + lax.axis_index("inner")) * leaves

    def one(leaf, counts):
        for k in range(near):
            offset = ids_ref[leaf, k] - first
            grown = []
            for (slots, places), count, (member, place) in zip(lists, counts, kind_of(offset)):
                slots[count] = leaf * near + k
                places[count] = place
                grown.append(count + member.astype(jnp.int32))
            counts = tuple(grown)
        return counts

    return lax.fori_loop(0, leaves, one, (jnp.int32(0),) * len(lists))


def add_products(near, kind, count, blocks, x_ref, total, arrived=lambda slot: None):
    slots, places = kind
    rows = blocks.shape[1]

    def product(i):
        slot = slots[i]
        arrived(slot)
        at = pl.multiple_of(places[i] * rows, rows)
        here = pl.ds(pl.multiple_of(slot // near * rows, rows), rows)
        return here, dot(blocks[slot], x_ref[pl.ds(at, rows), :])

    def pair(j, carry):
        one, first = product(2 * j)
        two, second = product(2 * j + 1)
        total[one, :] += first
        total[two, :] += second
        return carry

    lax.fori_loop(0, count // 2, pair, 0)

    @pl.when(lax.rem(count, 2) == 1)
    def _():
        here, term = product(count - 1)
        total[here, :] += term


def own_kernel(ids_ref, x_any, blocks_ref, total, blocks, own_slots, own_places, other_slots, other_places, x_ref, x_sem, sems):
    leaves, near = ids_ref.shape
    load = pltpu.make_async_copy(x_any, x_ref, x_sem)
    load.start()

    def kind_of(offset):
        own = (offset >= 0) & (offset < leaves)
        return (own, offset), (jnp.logical_not(own), 0)

    kinds = ((own_slots, own_places), (other_slots, other_places))
    own_count, other_count = listed(ids_ref, kinds, kind_of)

    def copy(slot):
        return pltpu.make_async_copy(blocks_ref.at[slot], blocks.at[slot], sems.at[slot])

    def begin(slots):
        def one(i, carry):
            copy(slots[i]).start()
            return carry

        return one

    lax.fori_loop(0, own_count, begin(own_slots), 0)
    lax.fori_loop(0, other_count, begin(other_slots), 0)
    total[...] = jnp.zeros_like(total)
    load.wait()
    add_products(near, kinds[0], own_count, blocks, x_ref, total, lambda slot: copy(slot).wait())

    def finish(i, carry):
        copy(other_slots[i]).wait()
        return carry

    lax.fori_loop(0, other_count, finish, 0)


def close_kernel(early, ids_ref, before, after, blocks, sum_ref, down_ref, basis_ref, total, *lists):
    leaves, near = ids_ref.shape
    rank, rows = basis_ref.shape[1:]

    def kind_of(offset):
        return ((offset < 0) & (offset >= -early), offset + early), ((offset >= leaves) & (offset < leaves + early), offset - leaves)

    kinds = (lists[:2], lists[2:])
    counts = listed(ids_ref, kinds, kind_of)
    for leaf in range(leaves):
        here = slice(leaf * rows, (leaf + 1) * rows)
        total[here, :] = sum_ref[here, :] + dot_t(basis_ref[leaf], down_ref[leaf * rank : (leaf + 1) * rank, :])
    for kind, count, x_ref in zip(kinds, counts, (before, after)):
        add_products(near, kind, count, blocks, x_ref, total)


def last_kernel(early, ids_ref, before, after, blocks, sum_ref, out_ref, *refs):
    lists, (total, result, sems) = refs[:4], refs[4:]
    leaves, near = ids_ref.shape
    rows = blocks.shape[1]

    def kind_of(offset):
        return (offset < -early, offset + leaves), (offset >= leaves + early, offset - leaves - early)

    kinds = (lists[:2], lists[2:])
    counts = listed(ids_ref, kinds, kind_of)
    total[...] = sum_ref[...]
    for kind, count, x_ref in zip(kinds, counts, (before, after)):
        add_products(near, kind, count, blocks, x_ref, total)
    stores = []
    for leaf in range(leaves):
        here = slice(leaf * rows, (leaf + 1) * rows)
        result[here, :] = total[here, :].astype(result.dtype)
        stores.append(pltpu.make_async_copy(result.at[here], out_ref.at[here], sems.at[leaf]))
        stores[-1].start()
    for store in stores:
        store.wait()


def local(anomalies, leaf_basis, near_blocks, near_ids, transfer_leaf, transfer_mid, far_ids, far_count, mid_couple, top_couple):
    leaves, rank, rows = leaf_basis.shape
    near = near_blocks.shape[1]
    columns = anomalies.shape[1]
    inner_size = lax.axis_size("inner")
    leaf_size = lax.axis_size("leaf")
    devices = leaf_size * inner_size
    bf16 = jnp.bfloat16
    early = leaves - leaves * 3 // 8
    late = leaves - early

    def shaped(*shape, dtype=bf16):
        return jax.ShapeDtypeStruct(shape, dtype)

    def shifted(x, axis, size, shift):
        return lax.ppermute(x, axis, [(i, (i + shift) % size) for i in range(size)])

    up = [(i, i + 1) for i in range(devices - 1)]
    down = [(j, i) for i, j in up]

    def wave(ahead, back):
        return lax.ppermute(ahead, ("leaf", "inner"), up), lax.ppermute(back, ("leaf", "inner"), down)

    x_hbm = held(anomalies, pltpu.HBM)
    ids = near_ids
    part, *pieces = call(
        functools.partial(up_kernel, early),
        [resident(2 * rank, columns)] + [shaped(n * rows, columns) for n in (early, early, late, late)],
        [ANY] * 4,
        [VMEM] + [ANY] * 4,
        [
            pltpu.VMEM(anomalies.shape, bf16),
            pltpu.VMEM(leaf_basis.shape, bf16),
            pltpu.VMEM(transfer_leaf.shape, bf16),
            pltpu.VMEM(transfer_mid.shape, bf16),
            pltpu.SemaphoreType.DMA((2 * leaves + 2,)),
            pltpu.SemaphoreType.DMA((4,)),
        ],
        2 * rows * rank * leaves * columns,
        anomalies.size * 3,
        8 * MIB,
    )(x_hbm, *[held(x, pltpu.HBM) for x in (leaf_basis, transfer_leaf, transfer_mid)])

    first_pieces = call(gate_kernel, [shaped(early * rows, columns)] * 2, [ANY] * 3, [ANY] * 2, [], 1000, 1000, 8 * MIB, {1: 0, 2: 1})(part, *pieces[:2])
    gathered = part
    reach = 1
    while reach < inner_size:
        partner = lax.ppermute(gathered, "inner", [(i, i ^ reach) for i in range(inner_size)])
        if reach == 1:
            partner, first_pieces = lax.optimization_barrier((partner, first_pieces))
        gathered = jnp.concatenate([gathered, partner])
        if reach == 1:
            gathered, x_own, last_pieces = lax.optimization_barrier((gathered, anomalies, pieces[2:]))
            near_halo = wave(*first_pieces)
            far_halo = wave(*last_pieces)
        reach *= 2

    slots = leaves * near
    lists = [pltpu.SMEM((slots + 1,), jnp.int32)] * 4
    wide = shaped(leaves * rows, columns, dtype=jnp.float32)
    flops = 2 * rows * rows * columns
    own_sum, blocks = call(
        own_kernel,
        (wide, resident(slots, rows, rows)),
        [SMEM, ANY, ANY],
        (VMEM, VMEM),
        lists + [pltpu.VMEM(anomalies.shape, bf16), pltpu.SemaphoreType.DMA, pltpu.SemaphoreType.DMA((slots,))],
        20 * flops,
        slots * rows * rows * 4,
        12 * MIB,
    )(ids, held(x_own, pltpu.HBM), held(near_blocks.reshape(slots, rows, rows), pltpu.HBM))

    blocks = held(blocks, pltpu.VMEM)
    gathered, near_halo, own_sum = lax.optimization_barrier((gathered, near_halo, own_sum))
    group, top = call(functools.partial(group_kernel, inner_size), (shaped((inner_size + 1) * rank, columns), shaped(rank, columns)), [VMEM], (VMEM, VMEM), [], 1000, 1000, 8 * MIB)(gathered)
    before_group = shifted(group, "leaf", leaf_size, 1)
    after_group = shifted(group, "leaf", leaf_size, leaf_size - 1)
    tops = [shifted(top, "leaf", leaf_size, s) for s in range(2, leaf_size - 1)]
    leaf_down = call(
        functools.partial(down_kernel, leaf_size, inner_size),
        shaped(leaves * rank, columns),
        [SMEM, SMEM] + [VMEM] * (7 + len(tops)),
        VMEM,
        [pltpu.VMEM((3 * inner_size * rank, columns), bf16)],
        1000,
        1000,
        8 * MIB,
    )(far_ids, far_count, group, before_group, after_group, *tops, top_couple, mid_couple, transfer_mid, transfer_leaf)

    close_sum = call(functools.partial(close_kernel, early), wide, [SMEM] + [VMEM] * 6, VMEM, lists, 15 * flops, 15 * rows * rows * 2, 8 * MIB)(
        ids, *near_halo, blocks, own_sum, leaf_down, leaf_basis
    )
    last_scratch = lists + [
        pltpu.VMEM((leaves * rows, columns), jnp.float32),
        pltpu.VMEM((leaves * rows, columns), bf16),
        pltpu.SemaphoreType.DMA((leaves,)),
    ]
    return call(functools.partial(last_kernel, early), shaped(leaves * rows, columns), [SMEM] + [VMEM] * 4, ANY, last_scratch, 4 * flops, 4 * rows * rows * 2, 8 * MIB)(
        ids, *far_halo, blocks, close_sum
    )


def solution(mesh):
    return jax.shard_map(
        local,
        mesh=mesh,
        in_specs=(
            P(("leaf", "inner"), "groups"),
            P(("leaf", "inner"), None, None),
            P(("leaf", "inner"), None, None, None),
            P(("leaf", "inner"), None),
            P(("leaf", "inner"), None, None),
            P(("leaf", "inner"), None, None),
            P(("leaf", "inner"), None),
            P(("leaf", "inner")),
            P(("leaf", "inner"), None, None, None),
            P("leaf", None, None, None),
        ),
        out_specs=P(("leaf", "inner"), "groups"),
        check_vma=False,
    )
```

time: 107 us -> 68.5 us (0.64)
  waiting for transfers between devices: 47 us -> 25.2 us
  local copies, waits for them, and re-layouts: 15.3 us -> 0.71 us
  starting transfers between devices: 21.9 us -> 20.7 us
    ppermute x6 -> x3, waiting for transfers between devices: 47 us -> 2.66 us  [shifted(): return lax.ppermute(x, axis, [(i, (i + shift) % size) for i in range(size)])]
    ppermute x4 -> x6, waiting for transfers between devices: 0.01 us -> 22.6 us  [the longest x2 22.6 us: local(): lax.ppermute(gathered, 'inner', [(i, i ^ reach) for i in range(inner_size)])]
    unnamed x20 -> x14, local copies, waits for them, and re-layouts: 14 us -> 0.71 us
    ppermute x6 -> x3, starting transfers between devices: 6.04 us -> 2.06 us  [shifted(): return lax.ppermute(x, axis, [(i, (i + shift) % size) for i in range(size)])]
    ppermute x4 -> x6, starting transfers between devices: 15.9 us -> 18.6 us  [the longest x2 9.94 us: wave(): lax.ppermute(back, ('leaf', 'inner'), down)]
    slice x1 -> x0, local copies, waits for them, and re-layouts: 1.39 us -> none  [local(): first, second = (anomalies[:cut], anomalies[cut:])]
    pallas_call x4 -> x5, Pallas kernels: 19.9 us -> 20.1 us  [the longest x1 9.4 us: local(): call(own_kernel, (wide, resident(slots, rows, rows)), [SMEM, ANY, ANY], (...]
  transfers between devices with their start and end apart: 10 -> 9, of which waited for: 5 -> 3; matrix products, arithmetic and copies ran while one was open for 0% -> 0% of each run, Pallas kernels for 16% -> 22%
where the time goes in v3:
time: 68.5 us; the launch traced here: 68.6 us
  waiting for transfers between devices  25.2 us (37%)
  Pallas kernels  21.1 us (31%)
  starting transfers between devices  20.7 us (30%)
  between operations  0.86 us (1%)
  local copies, waits for them, and re-layouts  0.71 us (1%)
    ppermute x2, waiting for transfers between devices, local(): lax.ppermute(gathered, 'inner', [(i, i ^ reach) for i in range(inner_size)])  22.6 us
    ppermute x2, starting transfers between devices, wave(): lax.ppermute(back, ('leaf', 'inner'), down)  9.94 us
    pallas_call x1, Pallas kernels, local(): call(own_kernel, (wide, resident(slots, rows, rows)), [SMEM, ANY, ANY], (...  9.4 us
    ppermute x2, starting transfers between devices, wave(): lax.ppermute(ahead, ('leaf', 'inner'), up)  6.43 us
    pallas_call x1, Pallas kernels, local(): call(functools.partial(close_kernel, early), wide, [SMEM] + [VMEM] * 6, V...  4.65 us
    pallas_call x1, Pallas kernels, local(): call(functools.partial(last_kernel, early), shaped(leaves * rows, columns...  3.09 us
    pallas_call x1, Pallas kernels, local(): call(functools.partial(up_kernel, early), [resident(2 * rank, columns)] +...  2.91 us
    ppermute x3, waiting for transfers between devices, shifted(): return lax.ppermute(x, axis, [(i, (i + shift) % size) for i in range(size)])  2.66 us
  transfers between devices with their start and end apart: 9, of which 3 were waited for; matrix products, arithmetic and copies ran while one was open for 0% of the time, Pallas kernels for 22%

profile of v3, /device:TPU:1, one launch (start us, length us, event | category | flops | bytes accessed | tf_op | source)
XLA Modules:
  0.0 68.6 jit_solution(1711785050080779631)
XLA Ops:
  0.0 0.0 copy-start.2
  0.0 0.0 copy-start.1
  0.0 0.0 copy-start
  0.0 0.0 copy-start.3
  0.0 0.0 copy-start.4
  0.0 0.0 copy-start.6
  0.0 2.9 %shard_map.100 = (bf16[128,128]{1,0:T(8,128)(2,1)S(1)}, bf16[2560,128]{1,0:T(8,128)(2,1)S(1)}, bf16[2560,128]{1,0:T(8,128)(2,1)S(1)}, bf16[1536,128]{1,0:T(8,128)(2,1)S(1)}, bf16[1536,128]{1,0:T(8,128)(2,1)S(1)}) custom-call(bf16[4096,128]{1,0:T(8,128)(2,1)} %x_any, bf16[8,64,512]{2,1,0:T(8,128)(2,1)} %basis_ref.3, bf16[8,64,64]{2,1,0:T(8,128)(2,1)} %refs_9_.1, ...), custom_call_target="tpu_custom_call" | custom-call | flops 67108864 | bytes 1572864 | tf_op jit(solution)/shard_map/pallas_call | solution.py:269
  3.0 2.2 %collective-permute-start = (bf16[128,128]{1,0:T(8,128)(2,1)S(1)}, bf16[128,128]{1,0:T(8,128)(2,1)S(1)}, u32[]{:S(2)}, u32[]{:S(2)}) collective-permute-start(bf16[128,128]{1,0:T(8,128)(2,1)S(1)} %get-tuple-element.27.refs_0_), channel_id=1, source_target_pairs={{0,1},{1,0},{2,3},{3,2},{4,5},{5,4},{6,7},{7,6},{8,9},{9,8},{10,11... | collective-permute-start | bytes 98312 | tf_op jit(solution)/shard_map/ppermute | solution.py:291
  5.2 1.3 %collective-permute-done = bf16[128,128]{1,0:T(8,128)(2,1)S(1)} collective-permute-done((bf16[128,128]{1,0:T(8,128)(2,1)S(1)}, bf16[128,128]{1,0:T(8,128)(2,1)S(1)}, u32[]{:S(2)}, u32[]{:S(2)}) %collective-permute-start) | collective-permute-done | bytes 32800 | tf_op jit(solution)/shard_map/ppermute | solution.py:291
  6.5 3.4 %collective-permute-start.4 = (bf16[2560,128]{1,0:T(8,128)(2,1)S(1)}, bf16[2560,128]{1,0:T(8,128)(2,1)S(1)}, u32[]{:S(2)}, u32[]{:S(2)}) collective-permute-start(bf16[2560,128]{1,0:T(8,128)(2,1)S(1)} %get-tuple-element.40), channel_id=1, source_target_pairs={{0,1},{1,2},{2,3},{3,4},{4,5},{5,6},{6,7},{7,8},{8,9},{9,10},{10,1... | collective-permute-start | bytes 1966088 | tf_op jit(solution)/shard_map/ppermute | solution.py:265
  9.8 5.7 %collective-permute-start.5 = (bf16[2560,128]{1,0:T(8,128)(2,1)S(1)}, bf16[2560,128]{1,0:T(8,128)(2,1)S(1)}, u32[]{:S(2)}, u32[]{:S(2)}) collective-permute-start(bf16[2560,128]{1,0:T(8,128)(2,1)S(1)} %get-tuple-element.41), channel_id=1, source_target_pairs={{1,0},{2,1},{3,2},{4,3},{5,4},{6,5},{7,6},{8,7},{9,8},{10,9},{11,1... | collective-permute-start | bytes 1966088 | tf_op jit(solution)/shard_map/ppermute | solution.py:265
  15.5 0.1 collective-permute-start.3
  15.6 3.1 %collective-permute-start.1 = (bf16[1536,128]{1,0:T(8,128)(2,1)S(1)}, bf16[1536,128]{1,0:T(8,128)(2,1)S(1)}, u32[]{:S(2)}, u32[]{:S(2)}) collective-permute-start(bf16[1536,128]{1,0:T(8,128)(2,1)S(1)} %get-tuple-element.35), channel_id=1, source_target_pairs={{0,1},{1,2},{2,3},{3,4},{4,5},{5,6},{6,7},{7,8},{8,9},{9,10},{10,1... | collective-permute-start | bytes 1179656 | tf_op jit(solution)/shard_map/ppermute | solution.py:265
  18.6 4.3 %collective-permute-start.2 = (bf16[1536,128]{1,0:T(8,128)(2,1)S(1)}, bf16[1536,128]{1,0:T(8,128)(2,1)S(1)}, u32[]{:S(2)}, u32[]{:S(2)}) collective-permute-start(bf16[1536,128]{1,0:T(8,128)(2,1)S(1)} %get-tuple-element.36), channel_id=1, source_target_pairs={{1,0},{2,1},{3,2},{4,3},{5,4},{6,5},{7,6},{8,7},{9,8},{10,9},{11,1... | collective-permute-start | bytes 1179656 | tf_op jit(solution)/shard_map/ppermute | solution.py:265
  22.9 0.0 copy-start.5
  23.0 0.7 copy-done.5
  23.6 9.4 %shard_map.102 = (f32[4096,128]{1,0:T(8,128)S(1)}, bf16[40,512,512]{2,1,0:T(8,128)(2,1)S(1)}) custom-call(s32[8,5]{1,0:T(8,128)S(1)} %copy-done.5, bf16[4096,128]{1,0:T(8,128)(2,1)} %x_any, bf16[40,512,512]{2,1,0:T(8,128)(2,1)} %bitcast.1), custom_call_target="tpu_custom_call" | custom-call | flops 1342177280 | bytes 41943040 | tf_op jit(solution)/shard_map/pallas_call | solution.py:305
  33.0 21.3 %collective-permute-done.3 = bf16[256,128]{1,0:T(8,128)(2,1)S(1)} collective-permute-done((bf16[256,128]{1,0:T(8,128)(2,1)S(1)}, bf16[256,128]{1,0:T(8,128)(2,1)S(1)}, u32[]{:S(2)}, u32[]{:S(2)}) %collective-permute-start.3) | collective-permute-done | bytes 65568 | tf_op jit(solution)/shard_map/ppermute | solution.py:291
  54.3 0.0 collective-permute-done.4.before
  54.3 0.0 collective-permute-done.5.after
  54.4 0.6 collective-permute-start.7
  55.0 1.2 %collective-permute-start.6 = (bf16[320,128]{1,0:T(8,128)(2,1)S(1)}, bf16[320,128]{1,0:T(8,128)(2,1)S(1)}, u32[]{:S(2)}, u32[]{:S(2)}) collective-permute-start(bf16[320,128]{1,0:T(8,128)(2,1)S(1)} %get-tuple-element.47.refs_2_), channel_id=1, source_target_pairs={{0,4},{4,8},{8,12},{12,0},{1,5},{5,9},{9,13},{13,1},{2,6},{6,10},{... | collective-permute-start | bytes 245768 | tf_op jit(solution)/shard_map/ppermute | solution.py:259
  56.2 0.3 collective-permute-start.8
  57.1 2.7 %collective-permute-done.8.refs_5_ = bf16[64,128]{1,0:T(8,128)(2,1)S(1)} collective-permute-done((bf16[64,128]{1,0:T(8,128)(2,1)S(1)}, bf16[64,128]{1,0:T(8,128)(2,1)S(1)}, u32[]{:S(2)}, u32[]{:S(2)}) %collective-permute-start.8) | collective-permute-done | bytes 16416 | tf_op jit(solution)/shard_map/ppermute | solution.py:259
  59.7 0.0 collective-permute-done.7.refs_4_
  59.7 0.0 collective-permute-done.6.refs_3_
  59.7 0.0 copy-done.2
  59.7 0.0 copy-done.1
  59.8 0.0 copy-done.3
  59.8 0.0 copy-done.4
  59.8 0.0 copy-done.6
  59.8 1.0 %shard_map.104.down_ref = bf16[512,128]{1,0:T(8,128)(2,1)S(1)} custom-call(s32[1,4]{1,0:T(1,128)S(1)} %copy-done.6, s32[1]{0:T(128)S(6)} %copy.15.refs_1_, bf16[320,128]{1,0:T(8,128)(2,1)S(1)} %get-tuple-element.47.refs_2_, bf16[320,128]{1,0:T(8,128)(2,1)S(1)} %collective-permute-done.6.refs_3_, bf16[320,128]{1,0:T(8,128)(2,1)S(1)} %collective-permute-done.7.refs_4_, ...), custom_call_target="tpu_custom_call" | custom-call | flops 1000 | bytes 1000 | tf_op jit(solution)/shard_map/pallas_call | solution.py:322
  60.8 0.0 copy-done
  60.8 4.7 %shard_map.105.sum_ref = f32[4096,128]{1,0:T(8,128)S(1)} custom-call(s32[8,5]{1,0:T(8,128)S(1)} %copy-done.5, bf16[2560,128]{1,0:T(8,128)(2,1)S(1)} %collective-permute-done.4.before, bf16[2560,128]{1,0:T(8,128)(2,1)S(1)} %collective-permute-done.5.after, bf16[40,512,512]{2,1,0:T(8,128)(2,1)S(1)} %get-tuple-element.38.blocks, ...), custom_call_target="tpu_custom_call" | custom-call | flops 1006632960 | bytes 7864320 | tf_op jit(solution)/shard_map/pallas_call | solution.py:333
  65.4 0.0 collective-permute-done.1.before
  65.5 0.0 collective-permute-done.2.after
  65.5 3.1 %shard_map.106 = bf16[4096,128]{1,0:T(8,128)(2,1)} custom-call(s32[8,5]{1,0:T(8,128)S(1)} %copy-done.5, bf16[1536,128]{1,0:T(8,128)(2,1)S(1)} %collective-permute-done.1.before, bf16[1536,128]{1,0:T(8,128)(2,1)S(1)} %collective-permute-done.2.after, bf16[40,512,512]{2,1,0:T(8,128)(2,1)S(1)} %get-tuple-element.38.blocks, f32[4096,128]{1,0:T(8,128)S(1)} %shard_map.105.sum_ref), custom_call_target="tpu_custom_call" | custom-call | flops 268435456 | bytes 2097152 | tf_op jit(solution)/shard_map/pallas_call | solution.py:341
  (4 shorter events, 0.0 us)
Async XLA Ops:
  0.0 59.7 %copy-start.2 = (bf16[1,64,64]{2,1,0:T(8,128)(2,1)S(1)}, bf16[1,64,64]{2,1,0:T(8,128)(2,1)}, u32[]{:S(2)}) copy-start(bf16[1,64,64]{2,1,0:T(8,128)(2,1)} %refs_8_.1) | copy-start | bytes 24580
  0.0 59.7 %copy-start.1 = (bf16[8,64,64]{2,1,0:T(8,128)(2,1)S(1)}, bf16[8,64,64]{2,1,0:T(8,128)(2,1)}, u32[]{:S(2)}) copy-start(bf16[8,64,64]{2,1,0:T(8,128)(2,1)} %refs_9_.1) | copy-start | bytes 196612
  0.0 60.8 %copy-start = (bf16[8,64,512]{2,1,0:T(8,128)(2,1)S(1)}, bf16[8,64,512]{2,1,0:T(8,128)(2,1)}, u32[]{:S(2)}) copy-start(bf16[8,64,512]{2,1,0:T(8,128)(2,1)} %basis_ref.3) | copy-start | bytes 1572868
  0.0 59.7 %copy-start.3 = (bf16[1,4,64,64]{3,2,1,0:T(8,128)(2,1)S(1)}, bf16[1,4,64,64]{3,2,1,0:T(8,128)(2,1)}, u32[]{:S(2)}) copy-start(bf16[1,4,64,64]{3,2,1,0:T(8,128)(2,1)} %refs_6_.1) | copy-start | bytes 98308
  0.0 59.7 %copy-start.4 = (bf16[1,4,64,64]{3,2,1,0:T(8,128)(2,1)S(1)}, bf16[1,4,64,64]{3,2,1,0:T(8,128)(2,1)}, u32[]{:S(2)}) copy-start(bf16[1,4,64,64]{3,2,1,0:T(8,128)(2,1)} %refs_7_.1) | copy-start | bytes 98308
  0.0 59.7 %copy-start.6 = (s32[1,4]{1,0:T(1,128)S(1)}, s32[1,4]{1,0:T(1,128)}, u32[]{:S(2)}) copy-start(s32[1,4]{1,0:T(1,128)} %refs_0_.1) | copy-start | bytes 52
  3.0 3.5 %collective-permute-start = (bf16[128,128]{1,0:T(8,128)(2,1)S(1)}, bf16[128,128]{1,0:T(8,128)(2,1)S(1)}, u32[]{:S(2)}, u32[]{:S(2)}) collective-permute-start(bf16[128,128]{1,0:T(8,128)(2,1)S(1)} %get-tuple-element.27.refs_0_), channel_id=1, source_target_pairs={{0,1},{1,0},{2,3},{3,2},{4,5},{5,4},{6,7},{7,6},{8,9},{9,8},{10,11... | collective-permute-start | bytes 98312 | tf_op jit(solution)/shard_map/ppermute | solution.py:291
  6.5 47.9 %collective-permute-start.4 = (bf16[2560,128]{1,0:T(8,128)(2,1)S(1)}, bf16[2560,128]{1,0:T(8,128)(2,1)S(1)}, u32[]{:S(2)}, u32[]{:S(2)}) collective-permute-start(bf16[2560,128]{1,0:T(8,128)(2,1)S(1)} %get-tuple-element.40), channel_id=1, source_target_pairs={{0,1},{1,2},{2,3},{3,4},{4,5},{5,6},{6,7},{7,8},{8,9},{9,10},{10,1... | collective-permute-start | bytes 1966088 | tf_op jit(solution)/shard_map/ppermute | solution.py:265
  9.8 44.5 %collective-permute-start.5 = (bf16[2560,128]{1,0:T(8,128)(2,1)S(1)}, bf16[2560,128]{1,0:T(8,128)(2,1)S(1)}, u32[]{:S(2)}, u32[]{:S(2)}) collective-permute-start(bf16[2560,128]{1,0:T(8,128)(2,1)S(1)} %get-tuple-element.41), channel_id=1, source_target_pairs={{1,0},{2,1},{3,2},{4,3},{5,4},{6,5},{7,6},{8,7},{9,8},{10,9},{11,1... | collective-permute-start | bytes 1966088 | tf_op jit(solution)/shard_map/ppermute | solution.py:265
  15.5 38.8 %collective-permute-start.3 = (bf16[256,128]{1,0:T(8,128)(2,1)S(1)}, bf16[256,128]{1,0:T(8,128)(2,1)S(1)}, u32[]{:S(2)}, u32[]{:S(2)}) collective-permute-start(bf16[256,128]{1,0:T(8,128)(2,1)S(1)} %pad_maximum_fusion.1), channel_id=1, source_target_pairs={{0,2},{1,3},{2,0},{3,1},{4,6},{5,7},{6,4},{7,5},{8,10},{9,11},{10,... | collective-permute-start | bytes 196616 | tf_op jit(solution)/shard_map/ppermute | solution.py:291
  15.6 49.9 %collective-permute-start.1 = (bf16[1536,128]{1,0:T(8,128)(2,1)S(1)}, bf16[1536,128]{1,0:T(8,128)(2,1)S(1)}, u32[]{:S(2)}, u32[]{:S(2)}) collective-permute-start(bf16[1536,128]{1,0:T(8,128)(2,1)S(1)} %get-tuple-element.35), channel_id=1, source_target_pairs={{0,1},{1,2},{2,3},{3,4},{4,5},{5,6},{6,7},{7,8},{8,9},{9,10},{10,1... | collective-permute-start | bytes 1179656 | tf_op jit(solution)/shard_map/ppermute | solution.py:265
  18.6 46.8 %collective-permute-start.2 = (bf16[1536,128]{1,0:T(8,128)(2,1)S(1)}, bf16[1536,128]{1,0:T(8,128)(2,1)S(1)}, u32[]{:S(2)}, u32[]{:S(2)}) collective-permute-start(bf16[1536,128]{1,0:T(8,128)(2,1)S(1)} %get-tuple-element.36), channel_id=1, source_target_pairs={{1,0},{2,1},{3,2},{4,3},{5,4},{6,5},{7,6},{8,7},{9,8},{10,9},{11,1... | collective-permute-start | bytes 1179656 | tf_op jit(solution)/shard_map/ppermute | solution.py:265
  22.9 0.7 %copy-start.5 = (s32[8,5]{1,0:T(8,128)S(1)}, s32[8,5]{1,0:T(8,128)}, u32[]{:S(2)}) copy-start(s32[8,5]{1,0:T(8,128)} %ids_ref.5) | copy-start | bytes 484
  54.4 5.4 %collective-permute-start.7 = (bf16[320,128]{1,0:T(8,128)(2,1)S(1)}, bf16[320,128]{1,0:T(8,128)(2,1)S(1)}, u32[]{:S(2)}, u32[]{:S(2)}) collective-permute-start(bf16[320,128]{1,0:T(8,128)(2,1)S(1)} %get-tuple-element.47.refs_2_), channel_id=1, source_target_pairs={{0,12},{4,0},{8,4},{12,8},{1,13},{5,1},{9,5},{13,9},{2,14},{6,2},{... | collective-permute-start | bytes 245768 | tf_op jit(solution)/shard_map/ppermute | solution.py:259
  55.0 4.7 %collective-permute-start.6 = (bf16[320,128]{1,0:T(8,128)(2,1)S(1)}, bf16[320,128]{1,0:T(8,128)(2,1)S(1)}, u32[]{:S(2)}, u32[]{:S(2)}) collective-permute-start(bf16[320,128]{1,0:T(8,128)(2,1)S(1)} %get-tuple-element.47.refs_2_), channel_id=1, source_target_pairs={{0,4},{4,8},{8,12},{12,0},{1,5},{5,9},{9,13},{13,1},{2,6},{6,10},{... | collective-permute-start | bytes 245768 | tf_op jit(solution)/shard_map/ppermute | solution.py:259
  56.2 3.6 %collective-permute-start.8 = (bf16[64,128]{1,0:T(8,128)(2,1)S(1)}, bf16[64,128]{1,0:T(8,128)(2,1)S(1)}, u32[]{:S(2)}, u32[]{:S(2)}) collective-permute-start(bf16[64,128]{1,0:T(8,128)(2,1)S(1)} %get-tuple-element.48), channel_id=1, source_target_pairs={{0,8},{4,12},{8,0},{12,4},{1,9},{5,13},{9,1},{13,5},{2,10},{6,14},... | collective-permute-start | bytes 49160 | tf_op jit(solution)/shard_map/ppermute | solution.py:259

commit v4 on v3

v4 whole, which is shorter than its diff:
```python
import functools

import jax
import jax.numpy as jnp
from jax import lax
from jax.experimental import pallas as pl
from jax.experimental.pallas import tpu as pltpu
from jax.sharding import PartitionSpec as P

MIB = 1 << 20
VMEM = pl.BlockSpec(memory_space=pltpu.VMEM)
SMEM = pl.BlockSpec(memory_space=pltpu.SMEM)
ANY = pl.BlockSpec(memory_space=pl.ANY)


def held(x, space):
    return pltpu.with_memory_space_constraint(x, space)


def resident(*shape):
    return pltpu.VMEM(shape, jnp.bfloat16)


def dot(a, b):
    return lax.dot_general(a, b, (((1,), (0,)), ((), ())), preferred_element_type=jnp.float32)


def dot_t(a, b):
    return lax.dot_general(a, b, (((0,), (0,)), ((), ())), preferred_element_type=jnp.float32)


def call(kernel, out_shape, in_specs, out_specs, scratch, flops, moved, vmem, aliases=None):
    return pl.pallas_call(
        kernel,
        out_shape=out_shape,
        in_specs=in_specs,
        out_specs=out_specs,
        scratch_shapes=scratch,
        cost_estimate=pl.CostEstimate(flops=flops, bytes_accessed=moved, transcendentals=0),
        compiler_params=pltpu.CompilerParams(vmem_limit_bytes=vmem),
        input_output_aliases=aliases or {},
    )


def up_kernel(x_ref, basis_ref, leaf_map_ref, mid_map_ref, out_ref, low, high, relay, x, basis, leaf_map, mid_map, skeleton, sems, piece_sems):
    leaves, rank, rows = basis.shape
    cut = low.shape[0]
    parts = []
    for leaf in range(leaves):
        here = slice(leaf * rows, (leaf + 1) * rows)
        parts.append(pltpu.make_async_copy(x_ref.at[here], x.at[here], sems.at[leaf]))
        parts.append(pltpu.make_async_copy(basis_ref.at[leaf], basis.at[leaf], sems.at[leaves + leaf]))
    maps = [pltpu.make_async_copy(leaf_map_ref, leaf_map, sems.at[2 * leaves]), pltpu.make_async_copy(mid_map_ref, mid_map, sems.at[2 * leaves + 1])]
    edge = pl.multiple_of(jnp.where(lax.axis_index("inner") == 0, cut, 0), rows)
    sources = (x_ref.at[:cut], x_ref.at[cut:], x_ref.at[pl.ds(edge, cut)])
    copies = [pltpu.make_async_copy(source, piece, piece_sems.at[i]) for i, (source, piece) in enumerate(zip(sources, (low, high, relay)))]
    for copy in parts + maps + copies:
        copy.start()
    for leaf in range(leaves):
        parts[2 * leaf].wait()
        parts[2 * leaf + 1].wait()
        skeleton[leaf * rank : (leaf + 1) * rank, :] = dot(basis[leaf], x[leaf * rows : (leaf + 1) * rows, :]).astype(jnp.bfloat16)
    for copy in maps:
        copy.wait()
    mid = dot_t(leaf_map[...], skeleton[...]).astype(jnp.bfloat16)
    out_ref[:rank, :] = mid
    out_ref[rank:, :] = dot_t(mid_map[...], mid).astype(jnp.bfloat16)
    for copy in copies:
        copy.wait()


def group_kernel(count, *refs):
    parts, out_ref, top_ref = refs[:count], refs[count], refs[count + 1]
    rank = top_ref.shape[0]
    top = jnp.zeros(top_ref.shape, jnp.float32)
    for i, part in enumerate(parts):
        out_ref[i * rank : (i + 1) * rank, :] = part[:rank, :]
        top += part[rank:, :].astype(jnp.float32)
    top = top.astype(jnp.bfloat16)
    out_ref[count * rank :, :] = top
    top_ref[...] = top


def down_kernel(leaf_size, inner_size, *refs):
    far_ids, far_count, own, before, after = refs[:5]
    tops = dict(zip(range(2, leaf_size - 1), refs[5:]))
    couple, mid_couple, mid_map, leaf_map, out_ref, window = refs[5 + len(tops) :]
    rank = mid_map.shape[1]
    group = lax.axis_index("leaf")
    inner = lax.axis_index("inner")
    last = inner_size * rank
    top_down = jnp.zeros((rank, own.shape[1]), jnp.float32)
    for shift in range(1, leaf_size):
        source = lax.rem(group - shift + leaf_size, leaf_size)
        if shift == 1:
            top = before[last:, :]
        elif shift == leaf_size - 1:
            top = after[last:, :]
        else:
            top = tops[shift][...]
        term = dot(couple[0, source], top)
        top_down += jnp.where(jnp.abs(source - group) >= 2, term, 0.0)
    for i, part in enumerate((before, own, after)):
        window[i * last : (i + 1) * last, :] = part[:last, :]
    total = dot(mid_map[0], top_down.astype(jnp.bfloat16))
    for slot in range(mid_couple.shape[1]):
        live = slot < far_count[0]
        partner = jnp.where(live, far_ids[0, slot], group * inner_size)
        side = partner // inner_size - group + 1
        place = inner ^ lax.rem(partner, inner_size)
        at = pl.multiple_of((side * inner_size + place) * rank, rank)
        term = dot(mid_couple[0, slot], window[pl.ds(at, rank), :])
        total += jnp.where(live, term, 0.0)
    total = total.astype(jnp.bfloat16)
    for leaf in range(leaf_map.shape[0]):
        out_ref[leaf * rank : (leaf + 1) * rank, :] = dot(leaf_map[leaf], total).astype(jnp.bfloat16)


def listed(ids_ref, lists, kind_of):
    leaves, near = ids_ref.shape
    first = (lax.axis_index("leaf") * lax.axis_size("inner") + lax.axis_index("inner")) * leaves

    def one(leaf, counts):
        for k in range(near):
            offset = ids_ref[leaf, k] - first
            grown = []
            for (slots, places), count, (member, place) in zip(lists, counts, kind_of(offset)):
                slots[count] = leaf * near + k
                places[count] = place
                grown.append(count + member.astype(jnp.int32))
            counts = tuple(grown)
        return counts

    return lax.fori_loop(0, leaves, one, (jnp.int32(0),) * len(lists))


def add_products(near, kind, count, blocks, partner, total, arrived=lambda slot: None):
    slots, places = kind
    rows = blocks.shape[1]

    def product(i):
        slot = slots[i]
        arrived(slot)
        at = pl.ds(pl.multiple_of(places[i] * rows, rows), rows)
        here = pl.ds(pl.multiple_of(slot // near * rows, rows), rows)
        return here, dot(blocks[slot], partner(at))

    def pair(j, carry):
        one, first = product(2 * j)
        two, second = product(2 * j + 1)
        total[one, :] += first
        total[two, :] += second
        return carry

    lax.fori_loop(0, count // 2, pair, 0)

    @pl.when(lax.rem(count, 2) == 1)
    def _():
        here, term = product(count - 1)
        total[here, :] += term


def own_kernel(ids_ref, x_any, blocks_ref, total, blocks, own_slots, own_places, other_slots, other_places, x_ref, x_sem, sems):
    leaves, near = ids_ref.shape
    load = pltpu.make_async_copy(x_any, x_ref, x_sem)
    load.start()

    def kind_of(offset):
        own = (offset >= 0) & (offset < leaves)
        return (own, offset), (jnp.logical_not(own), 0)

    kinds = ((own_slots, own_places), (other_slots, other_places))
    own_count, other_count = listed(ids_ref, kinds, kind_of)

    def copy(slot):
        return pltpu.make_async_copy(blocks_ref.at[slot], blocks.at[slot], sems.at[slot])

    def begin(slots):
        def one(i, carry):
            copy(slots[i]).start()
            return carry

        return one

    lax.fori_loop(0, own_count, begin(own_slots), 0)
    lax.fori_loop(0, other_count, begin(other_slots), 0)
    total[...] = jnp.zeros_like(total)
    load.wait()
    add_products(near, kinds[0], own_count, blocks, lambda at: x_ref[at, :], total, lambda slot: copy(slot).wait())

    def finish(i, carry):
        copy(other_slots[i]).wait()
        return carry

    lax.fori_loop(0, other_count, finish, 0)


def close_kernel(half, ids_ref, before, after, blocks, sum_ref, down_ref, basis_ref, total, *lists):
    leaves, near = ids_ref.shape
    rank, rows = basis_ref.shape[1:]

    def kind_of(offset):
        return ((offset < 0) & (offset >= -half), offset + half), ((offset >= leaves) & (offset < leaves + half), offset - leaves)

    kinds = (lists[:2], lists[2:])
    counts = listed(ids_ref, kinds, kind_of)
    for leaf in range(leaves):
        here = slice(leaf * rows, (leaf + 1) * rows)
        total[here, :] = sum_ref[here, :] + dot_t(basis_ref[leaf], down_ref[leaf * rank : (leaf + 1) * rank, :])
    for kind, count, x_ref in zip(kinds, counts, (before, after)):
        add_products(near, kind, count, blocks, lambda at, x_ref=x_ref: x_ref[at, :], total)


def last_kernel(half, ids_ref, before, after, blocks, sum_ref, out_ref, *refs):
    lists, (total, result, sems) = refs[:4], refs[4:]
    leaves, near = ids_ref.shape
    rows = blocks.shape[1]

    def kind_of(offset):
        return (offset < -half, offset + leaves), (offset >= leaves + half, offset - leaves - half)

    kinds = (lists[:2], lists[2:])
    counts = listed(ids_ref, kinds, kind_of)
    total[...] = sum_ref[...]
    for kind, count, x_ref in zip(kinds, counts, (before, after)):
        add_products(near, kind, count, blocks, lambda at, x_ref=x_ref: x_ref[at, :], total)
    stores = []
    for leaf in range(leaves):
        here = slice(leaf * rows, (leaf + 1) * rows)
        result[here, :] = total[here, :].astype(result.dtype)
        stores.append(pltpu.make_async_copy(result.at[here], out_ref.at[here], sems.at[leaf]))
        stores[-1].start()
    for store in stores:
        store.wait()


def local(anomalies, leaf_basis, near_blocks, near_ids, transfer_leaf, transfer_mid, far_ids, far_count, mid_couple, top_couple):
    leaves, rank, rows = leaf_basis.shape
    near = near_blocks.shape[1]
    columns = anomalies.shape[1]
    inner_size = lax.axis_size("inner")
    leaf_size = lax.axis_size("leaf")
    bf16 = jnp.bfloat16
    half = leaves // 2
    cut = half * rows
    inner = lax.axis_index("inner")

    def shaped(*shape, dtype=bf16):
        return jax.ShapeDtypeStruct(shape, dtype)

    def shifted(x, axis, size, shift):
        return lax.ppermute(x, axis, [(i, (i + shift) % size) for i in range(size)])

    first, last = 0, inner_size - 1
    line = [(leaf * inner_size + i, leaf * inner_size + i + 1) for leaf in range(leaf_size) for i in range(last)]
    groups = range(leaf_size)

    def place(leaf, i):
        return leaf * inner_size + i

    def passed(x, pairs):
        return lax.ppermute(x, ("leaf", "inner"), pairs)

    hop_first = [(place(g, last), place(g + 1, last)) for g in groups[:-1]] + [(place(g, first), place(g - 1, first)) for g in groups[1:]]

    x_hbm = held(anomalies, pltpu.HBM)
    part, low, high, relay = call(
        up_kernel,
        [resident(2 * rank, columns)] + [resident(cut, columns)] * 3,
        [ANY] * 4,
        [VMEM] + [ANY] * 3,
        [
            pltpu.VMEM(anomalies.shape, bf16),
            pltpu.VMEM(leaf_basis.shape, bf16),
            pltpu.VMEM((leaves * rank, rank), bf16),
            pltpu.VMEM((rank, rank), bf16),
            pltpu.VMEM((leaves * rank, columns), bf16),
            pltpu.SemaphoreType.DMA((2 * leaves + 2,)),
            pltpu.SemaphoreType.DMA((3,)),
        ],
        1000,
        1000,
        8 * MIB,
    )(x_hbm, *[held(x, pltpu.HBM) for x in (leaf_basis, transfer_leaf.reshape(leaves * rank, rank), transfer_mid.reshape(rank, rank))])

    parts = [part] + [lax.ppermute(part, "inner", [(i, i ^ s) for i in range(inner_size)]) for s in range(1, inner_size)]
    parts, low, high, relay = lax.optimization_barrier((parts, low, high, relay))
    chain = [(i, i + 1) for i in range(leaf_size * inner_size - 1)]
    ahead = passed(high, chain)
    back = passed(low, [(j, i) for i, j in chain])

    group, top = call(functools.partial(group_kernel, inner_size), (resident((inner_size + 1) * rank, columns), resident(rank, columns)), [VMEM] * inner_size, (VMEM, VMEM), [], 1000, 1000, 8 * MIB)(*parts)
    relayed = passed(relay, hop_first)
    before_group = shifted(group, "leaf", leaf_size, 1)
    after_group = shifted(group, "leaf", leaf_size, leaf_size - 1)
    tops = [shifted(top, "leaf", leaf_size, s) for s in range(2, leaf_size - 1)]
    far_low, far_high = jnp.where(inner == last, relayed, low), jnp.where(inner == first, relayed, high)
    far_low, far_high, x_own = lax.optimization_barrier((far_low, far_high, anomalies))
    far_ahead = passed(far_low, line + [(place(g, last), place(g, first)) for g in groups[1:]])
    far_back = passed(far_high, [(j, i) for i, j in line] + [(place(g, first), place(g, last)) for g in groups[:-1]])

    leaf_down = call(
        functools.partial(down_kernel, leaf_size, inner_size),
        shaped(leaves * rank, columns),
        [SMEM, SMEM] + [VMEM] * (7 + len(tops)),
        VMEM,
        [pltpu.VMEM((3 * inner_size * rank, columns), bf16)],
        1000,
        1000,
        8 * MIB,
    )(far_ids, far_count, group, before_group, after_group, *tops, top_couple, mid_couple, transfer_mid, transfer_leaf)

    x_own, leaf_down = lax.optimization_barrier((x_own, leaf_down))
    ids = near_ids
    slots = leaves * near
    lists = [pltpu.SMEM((slots + 1,), jnp.int32)] * 4
    wide = shaped(leaves * rows, columns, dtype=jnp.float32)
    own_sum, blocks = call(
        own_kernel,
        (wide, resident(slots, rows, rows)),
        [SMEM, ANY, ANY],
        (VMEM, VMEM),
        lists + [pltpu.VMEM(anomalies.shape, bf16), pltpu.SemaphoreType.DMA, pltpu.SemaphoreType.DMA((slots,))],
        1000,
        1000,
        12 * MIB,
    )(ids, held(x_own, pltpu.HBM), held(near_blocks.reshape(slots, rows, rows), pltpu.HBM))

    blocks = held(blocks, pltpu.VMEM)
    ahead, back, own_sum = lax.optimization_barrier((ahead, back, own_sum))
    close_sum = call(functools.partial(close_kernel, half), wide, [SMEM] + [VMEM] * 6, VMEM, lists, 1000, 1000, 8 * MIB)(
        ids, ahead, back, blocks, own_sum, leaf_down, leaf_basis
    )
    last_scratch = lists + [
        pltpu.VMEM((leaves * rows, columns), jnp.float32),
        pltpu.VMEM((leaves * rows, columns), bf16),
        pltpu.SemaphoreType.DMA((leaves,)),
    ]
    return call(functools.partial(last_kernel, half), shaped(leaves * rows, columns), [SMEM] + [VMEM] * 4, ANY, last_scratch, 1000, 1000, 8 * MIB)(
        ids, far_ahead, far_back, blocks, close_sum
    )


def solution(mesh):
    return jax.shard_map(
        local,
        mesh=mesh,
        in_specs=(
            P(("leaf", "inner"), "groups"),
            P(("leaf", "inner"), None, None),
            P(("leaf", "inner"), None, None, None),
            P(("leaf", "inner"), None),
            P(("leaf", "inner"), None, None),
            P(("leaf", "inner"), None, None),
            P(("leaf", "inner"), None),
            P(("leaf", "inner")),
            P(("leaf", "inner"), None, None, None),
            P("leaf", None, None, None),
        ),
        out_specs=P(("leaf", "inner"), "groups"),
        check_vma=False,
    )
```

time: 68.5 us -> 63.9 us (0.933)
  the two profiles are of different devices: /device:TPU:1 before, /device:TPU:0 now
where the time goes in v4:
time: 63.9 us; the launch traced here: 63.3 us
  starting transfers between devices  26.2 us (41%)
  Pallas kernels  20.6 us (32%)
  waiting for transfers between devices  11 us (17%)
  local copies, waits for them, and re-layouts  4.64 us (7%)
  between operations  0.82 us (1%)
    ppermute x5, starting transfers between devices, passed(): return lax.ppermute(x, ('leaf', 'inner'), pairs)  13.3 us
    pallas_call x1, Pallas kernels, local(): call(own_kernel, (wide, resident(slots, rows, rows)), [SMEM, ANY, ANY], (...  8.31 us
    ppermute x3, starting transfers between devices, shifted(): return lax.ppermute(x, axis, [(i, (i + shift) % size) for i in range(size)])  7.09 us
    ppermute x3, waiting for transfers between devices, shifted(): return lax.ppermute(x, axis, [(i, (i + shift) % size) for i in range(size)])  6.79 us
    ppermute x3, starting transfers between devices, local(): lax.ppermute(part, 'inner', [(i, i ^ s) for i in range(inner_size)])  5.75 us
    pallas_call x1, Pallas kernels, local(): call(functools.partial(close_kernel, half), wide, [SMEM] + [VMEM] * 6, VM...  4.81 us
    unnamed x16, local copies, waits for them, and re-layouts  4.64 us
    ppermute x3, waiting for transfers between devices, local(): lax.ppermute(part, 'inner', [(i, i ^ s) for i in range(inner_size)])  4.17 us
  transfers between devices with their start and end apart: 11, of which 5 were waited for; matrix products, arithmetic and copies ran while one was open for 0% of the time, Pallas kernels for 22%

profile of v4, /device:TPU:0, one launch (start us, length us, event | category | flops | bytes accessed | tf_op | source)
XLA Modules:
  0.0 63.3 jit_solution(4888711612129062100)
XLA Ops:
  0.0 0.0 copy-start
  0.0 0.0 copy-start.6
  0.0 2.8 %shard_map.100 = (bf16[128,128]{1,0:T(8,128)(2,1)S(1)}, bf16[2048,128]{1,0:T(8,128)(2,1)S(1)}, bf16[2048,128]{1,0:T(8,128)(2,1)S(1)}, bf16[2048,128]{1,0:T(8,128)(2,1)S(1)}) custom-call(bf16[4096,128]{1,0:T(8,128)(2,1)} %x_any, bf16[8,64,512]{2,1,0:T(8,128)(2,1)} %basis_ref.3, bf16[512,64]{1,0:T(8,128)(2,1)} %bitcast.3, bf16[64,64]{1,0:T(8,128)(2,1)} %bitcast.4), custom_call_target="tpu_custom_call" | custom-call | flops 1000 | bytes 1000 | tf_op jit(solution)/shard_map/pallas_call | solution.py:267
  2.8 5.1 %collective-permute-start.2 = (bf16[128,128]{1,0:T(8,128)(2,1)S(1)}, bf16[128,128]{1,0:T(8,128)(2,1)S(1)}, u32[]{:S(2)}, u32[]{:S(2)}) collective-permute-start(bf16[128,128]{1,0:T(8,128)(2,1)S(1)} %get-tuple-element.38.refs_0_), channel_id=1, source_target_pairs={{0,3},{1,2},{2,1},{3,0},{4,7},{5,6},{6,5},{7,4},{8,11},{9,10},{10,... | collective-permute-start | bytes 98312 | tf_op jit(solution)/shard_map/ppermute | solution.py:286
  7.9 0.0 collective-permute-start.1
  7.9 0.6 %collective-permute-start = (bf16[128,128]{1,0:T(8,128)(2,1)S(1)}, bf16[128,128]{1,0:T(8,128)(2,1)S(1)}, u32[]{:S(2)}, u32[]{:S(2)}) collective-permute-start(bf16[128,128]{1,0:T(8,128)(2,1)S(1)} %get-tuple-element.38.refs_0_), channel_id=1, source_target_pairs={{0,1},{1,0},{2,3},{3,2},{4,5},{5,4},{6,7},{7,6},{8,9},{9,8},{10,11... | collective-permute-start | bytes 98312 | tf_op jit(solution)/shard_map/ppermute | solution.py:286
  8.5 1.3 %collective-permute-done.2.refs_3_ = bf16[128,128]{1,0:T(8,128)(2,1)S(1)} collective-permute-done((bf16[128,128]{1,0:T(8,128)(2,1)S(1)}, bf16[128,128]{1,0:T(8,128)(2,1)S(1)}, u32[]{:S(2)}, u32[]{:S(2)}) %collective-permute-start.2) | collective-permute-done | bytes 32800 | tf_op jit(solution)/shard_map/ppermute | solution.py:286
  9.8 2.9 %collective-permute-done.1.refs_2_ = bf16[128,128]{1,0:T(8,128)(2,1)S(1)} collective-permute-done((bf16[128,128]{1,0:T(8,128)(2,1)S(1)}, bf16[128,128]{1,0:T(8,128)(2,1)S(1)}, u32[]{:S(2)}, u32[]{:S(2)}) %collective-permute-start.1) | collective-permute-done | bytes 32800 | tf_op jit(solution)/shard_map/ppermute | solution.py:286
  12.7 0.0 collective-permute-done.refs_1_
  12.7 1.3 %collective-permute-start.3 = (bf16[2048,128]{1,0:T(8,128)(2,1)S(1)}, bf16[2048,128]{1,0:T(8,128)(2,1)S(1)}, u32[]{:S(2)}, u32[]{:S(2)}) collective-permute-start(bf16[2048,128]{1,0:T(8,128)(2,1)S(1)} %get-tuple-element.32), channel_id=1, source_target_pairs={{3,7},{7,11},{11,15},{4,0},{8,4},{12,8},{19,23},{23,27},{27,31},{2... | collective-permute-start | bytes 1572872 | tf_op jit(solution)/shard_map/ppermute | solution.py:262
  14.0 1.3 %collective-permute-start.10 = (bf16[2048,128]{1,0:T(8,128)(2,1)S(1)}, bf16[2048,128]{1,0:T(8,128)(2,1)S(1)}, u32[]{:S(2)}, u32[]{:S(2)}) collective-permute-start(bf16[2048,128]{1,0:T(8,128)(2,1)S(1)} %get-tuple-element.33), channel_id=1, source_target_pairs={{1,0},{2,1},{3,2},{4,3},{5,4},{6,5},{7,6},{8,7},{9,8},{10,9},{11,1... | collective-permute-start | bytes 1572872 | tf_op jit(solution)/shard_map/ppermute | solution.py:262
  15.3 4.6 %collective-permute-start.9 = (bf16[2048,128]{1,0:T(8,128)(2,1)S(1)}, bf16[2048,128]{1,0:T(8,128)(2,1)S(1)}, u32[]{:S(2)}, u32[]{:S(2)}) collective-permute-start(bf16[2048,128]{1,0:T(8,128)(2,1)S(1)} %get-tuple-element.34), channel_id=1, source_target_pairs={{0,1},{1,2},{2,3},{3,4},{4,5},{5,6},{6,7},{7,8},{8,9},{9,10},{10,1... | collective-permute-start | bytes 1572872 | tf_op jit(solution)/shard_map/ppermute | solution.py:262
  19.9 0.0 collective-permute-done.3
  19.9 0.1 broadcast_select_fusion
  20.0 1.9 %collective-permute-start.4 = (bf16[2048,128]{1,0:T(8,128)(2,1)S(1)}, bf16[2048,128]{1,0:T(8,128)(2,1)S(1)}, u32[]{:S(2)}, u32[]{:S(2)}) collective-permute-start(bf16[2048,128]{1,0:T(8,128)(2,1)S(1)} %get-tuple-element.35), channel_id=1, source_target_pairs={{0,1},{1,2},{2,3},{4,5},{5,6},{6,7},{8,9},{9,10},{10,11},{12,13},{... | collective-permute-start | bytes 1572872 | tf_op jit(solution)/shard_map/ppermute | solution.py:262
  21.9 4.3 %collective-permute-start.5 = (bf16[2048,128]{1,0:T(8,128)(2,1)S(1)}, bf16[2048,128]{1,0:T(8,128)(2,1)S(1)}, u32[]{:S(2)}, u32[]{:S(2)}) collective-permute-start(bf16[2048,128]{1,0:T(8,128)(2,1)S(1)} %get-tuple-element.36), channel_id=1, source_target_pairs={{1,0},{2,1},{3,2},{5,4},{6,5},{7,6},{9,8},{10,9},{11,10},{13,12},{... | collective-permute-start | bytes 1572872 | tf_op jit(solution)/shard_map/ppermute | solution.py:262
  26.2 4.4 %collective-permute-start.8 = (bf16[64,128]{1,0:T(8,128)(2,1)S(1)}, bf16[64,128]{1,0:T(8,128)(2,1)S(1)}, u32[]{:S(2)}, u32[]{:S(2)}) collective-permute-start(bf16[64,128]{1,0:T(8,128)(2,1)S(1)} %get-tuple-element.43), channel_id=1, source_target_pairs={{0,8},{4,12},{8,0},{12,4},{1,9},{5,13},{9,1},{13,5},{2,10},{6,14},... | collective-permute-start | bytes 49160 | tf_op jit(solution)/shard_map/ppermute | solution.py:252
  30.7 1.7 %collective-permute-done.8.refs_5_ = bf16[64,128]{1,0:T(8,128)(2,1)S(1)} collective-permute-done((bf16[64,128]{1,0:T(8,128)(2,1)S(1)}, bf16[64,128]{1,0:T(8,128)(2,1)S(1)}, u32[]{:S(2)}, u32[]{:S(2)}) %collective-permute-start.8) | collective-permute-done | bytes 16416 | tf_op jit(solution)/shard_map/ppermute | solution.py:252
  32.4 1.2 %collective-permute-start.7 = (bf16[320,128]{1,0:T(8,128)(2,1)S(1)}, bf16[320,128]{1,0:T(8,128)(2,1)S(1)}, u32[]{:S(2)}, u32[]{:S(2)}) collective-permute-start(bf16[320,128]{1,0:T(8,128)(2,1)S(1)} %get-tuple-element.42.refs_2_), channel_id=1, source_target_pairs={{0,12},{4,0},{8,4},{12,8},{1,13},{5,1},{9,5},{13,9},{2,14},{6,2},{... | collective-permute-start | bytes 245768 | tf_op jit(solution)/shard_map/ppermute | solution.py:252
  33.6 2.7 %collective-permute-done.7.refs_4_ = bf16[320,128]{1,0:T(8,128)(2,1)S(1)} collective-permute-done((bf16[320,128]{1,0:T(8,128)(2,1)S(1)}, bf16[320,128]{1,0:T(8,128)(2,1)S(1)}, u32[]{:S(2)}, u32[]{:S(2)}) %collective-permute-start.7) | collective-permute-done | bytes 81952 | tf_op jit(solution)/shard_map/ppermute | solution.py:252
  36.3 1.4 %collective-permute-start.6 = (bf16[320,128]{1,0:T(8,128)(2,1)S(1)}, bf16[320,128]{1,0:T(8,128)(2,1)S(1)}, u32[]{:S(2)}, u32[]{:S(2)}) collective-permute-start(bf16[320,128]{1,0:T(8,128)(2,1)S(1)} %get-tuple-element.42.refs_2_), channel_id=1, source_target_pairs={{0,4},{4,8},{8,12},{12,0},{1,5},{5,9},{9,13},{13,1},{2,6},{6,10},{... | collective-permute-start | bytes 245768 | tf_op jit(solution)/shard_map/ppermute | solution.py:252
  38.4 2.4 %collective-permute-done.6.refs_3_ = bf16[320,128]{1,0:T(8,128)(2,1)S(1)} collective-permute-done((bf16[320,128]{1,0:T(8,128)(2,1)S(1)}, bf16[320,128]{1,0:T(8,128)(2,1)S(1)}, u32[]{:S(2)}, u32[]{:S(2)}) %collective-permute-start.6) | collective-permute-done | bytes 81952 | tf_op jit(solution)/shard_map/ppermute | solution.py:252
  40.8 0.0 copy-start.1
  40.8 0.9 %copy-done.1 = bf16[8,64,64]{2,1,0:T(8,128)(2,1)S(1)} copy-done((bf16[8,64,64]{2,1,0:T(8,128)(2,1)S(1)}, bf16[8,64,64]{2,1,0:T(8,128)(2,1)}, u32[]{:S(2)}) %copy-start.1) | copy-done | bytes 65560
  41.7 0.0 copy-start.2
  41.7 0.7 %copy-done.2 = bf16[1,64,64]{2,1,0:T(8,128)(2,1)S(1)} copy-done((bf16[1,64,64]{2,1,0:T(8,128)(2,1)S(1)}, bf16[1,64,64]{2,1,0:T(8,128)(2,1)}, u32[]{:S(2)}) %copy-start.2) | copy-done | bytes 8216
  42.4 0.0 copy-start.3
  42.4 0.8 %copy-done.3 = bf16[1,4,64,64]{3,2,1,0:T(8,128)(2,1)S(1)} copy-done((bf16[1,4,64,64]{3,2,1,0:T(8,128)(2,1)S(1)}, bf16[1,4,64,64]{3,2,1,0:T(8,128)(2,1)}, u32[]{:S(2)}) %copy-start.3) | copy-done | bytes 32792
  43.2 0.0 copy-start.4
  43.2 0.8 %copy-done.4 = bf16[1,4,64,64]{3,2,1,0:T(8,128)(2,1)S(1)} copy-done((bf16[1,4,64,64]{3,2,1,0:T(8,128)(2,1)S(1)}, bf16[1,4,64,64]{3,2,1,0:T(8,128)(2,1)}, u32[]{:S(2)}) %copy-start.4) | copy-done | bytes 32792
  44.1 0.0 copy-start.7
  44.1 0.7 %copy-done.7 = s32[1,4]{1,0:T(1,128)S(1)} copy-done((s32[1,4]{1,0:T(1,128)S(1)}, s32[1,4]{1,0:T(1,128)}, u32[]{:S(2)}) %copy-start.7) | copy-done | bytes 40
  44.7 1.0 %shard_map.102.down_ref = bf16[512,128]{1,0:T(8,128)(2,1)S(1)} custom-call(s32[1,4]{1,0:T(1,128)S(1)} %copy-done.7, s32[1]{0:T(128)S(6)} %copy.11.refs_1_, bf16[320,128]{1,0:T(8,128)(2,1)S(1)} %get-tuple-element.42.refs_2_, bf16[320,128]{1,0:T(8,128)(2,1)S(1)} %collective-permute-done.6.refs_3_, bf16[320,128]{1,0:T(8,128)(2,1)S(1)} %collective-permute-done.7.refs_4_, ...), custom_call_target="tpu_custom_call" | custom-call | flops 1000 | bytes 1000 | tf_op jit(solution)/shard_map/pallas_call | solution.py:302
  45.7 0.0 copy-start.5
  45.7 0.7 %copy-done.5 = s32[8,5]{1,0:T(8,128)S(1)} copy-done((s32[8,5]{1,0:T(8,128)S(1)}, s32[8,5]{1,0:T(8,128)}, u32[]{:S(2)}) %copy-start.5) | copy-done | bytes 184
  46.4 8.3 %shard_map.103 = (f32[4096,128]{1,0:T(8,128)S(1)}, bf16[40,512,512]{2,1,0:T(8,128)(2,1)S(1)}) custom-call(s32[8,5]{1,0:T(8,128)S(1)} %copy-done.5, bf16[4096,128]{1,0:T(8,128)(2,1)} %x_any, bf16[40,512,512]{2,1,0:T(8,128)(2,1)} %bitcast.5), custom_call_target="tpu_custom_call" | custom-call | flops 1000 | bytes 1000 | tf_op jit(solution)/shard_map/pallas_call | solution.py:318
  54.7 0.0 collective-permute-done.10.after
  54.7 0.0 collective-permute-done.9.before
  54.7 0.0 copy-done
  54.7 0.0 copy-done.6
  54.8 4.8 %shard_map.104.sum_ref = f32[4096,128]{1,0:T(8,128)S(1)} custom-call(s32[8,5]{1,0:T(8,128)S(1)} %copy-done.6, bf16[2048,128]{1,0:T(8,128)(2,1)S(1)} %collective-permute-done.9.before, bf16[2048,128]{1,0:T(8,128)(2,1)S(1)} %collective-permute-done.10.after, bf16[40,512,512]{2,1,0:T(8,128)(2,1)S(1)} %get-tuple-element.45.blocks, ...), custom_call_target="tpu_custom_call" | custom-call | flops 1000 | bytes 1000 | tf_op jit(solution)/shard_map/pallas_call | solution.py:331
  59.6 0.0 collective-permute-done.4.before
  59.6 0.0 collective-permute-done.5.after
  59.6 3.7 %shard_map.105 = bf16[4096,128]{1,0:T(8,128)(2,1)} custom-call(s32[8,5]{1,0:T(8,128)S(1)} %copy-done.6, bf16[2048,128]{1,0:T(8,128)(2,1)S(1)} %collective-permute-done.4.before, bf16[2048,128]{1,0:T(8,128)(2,1)S(1)} %collective-permute-done.5.after, bf16[40,512,512]{2,1,0:T(8,128)(2,1)S(1)} %get-tuple-element.45.blocks, f32[4096,128]{1,0:T(8,128)S(1)} %shard_map.104.sum_ref), custom_call_target="tpu_custom_call" | custom-call | flops 1000 | bytes 1000 | tf_op jit(solution)/shard_map/pallas_call | solution.py:339
  (1 shorter events, 0.0 us)
Async XLA Ops:
  0.0 54.7 %copy-start = (bf16[8,64,512]{2,1,0:T(8,128)(2,1)S(1)}, bf16[8,64,512]{2,1,0:T(8,128)(2,1)}, u32[]{:S(2)}) copy-start(bf16[8,64,512]{2,1,0:T(8,128)(2,1)} %basis_ref.3) | copy-start | bytes 1572868
  0.0 54.7 %copy-start.6 = (s32[8,5]{1,0:T(8,128)S(1)}, s32[8,5]{1,0:T(8,128)}, u32[]{:S(2)}) copy-start(s32[8,5]{1,0:T(8,128)} %ids_ref.5) | copy-start | bytes 484
  2.8 7.0 %collective-permute-start.2 = (bf16[128,128]{1,0:T(8,128)(2,1)S(1)}, bf16[128,128]{1,0:T(8,128)(2,1)S(1)}, u32[]{:S(2)}, u32[]{:S(2)}) collective-permute-start(bf16[128,128]{1,0:T(8,128)(2,1)S(1)} %get-tuple-element.38.refs_0_), channel_id=1, source_target_pairs={{0,3},{1,2},{2,1},{3,0},{4,7},{5,6},{6,5},{7,4},{8,11},{9,10},{10,... | collective-permute-start | bytes 98312 | tf_op jit(solution)/shard_map/ppermute | solution.py:286
  7.9 4.8 %collective-permute-start.1 = (bf16[128,128]{1,0:T(8,128)(2,1)S(1)}, bf16[128,128]{1,0:T(8,128)(2,1)S(1)}, u32[]{:S(2)}, u32[]{:S(2)}) collective-permute-start(bf16[128,128]{1,0:T(8,128)(2,1)S(1)} %get-tuple-element.38.refs_0_), channel_id=1, source_target_pairs={{0,2},{1,3},{2,0},{3,1},{4,6},{5,7},{6,4},{7,5},{8,10},{9,11},{10,... | collective-permute-start | bytes 98312 | tf_op jit(solution)/shard_map/ppermute | solution.py:286
  7.9 4.8 %collective-permute-start = (bf16[128,128]{1,0:T(8,128)(2,1)S(1)}, bf16[128,128]{1,0:T(8,128)(2,1)S(1)}, u32[]{:S(2)}, u32[]{:S(2)}) collective-permute-start(bf16[128,128]{1,0:T(8,128)(2,1)S(1)} %get-tuple-element.38.refs_0_), channel_id=1, source_target_pairs={{0,1},{1,0},{2,3},{3,2},{4,5},{5,4},{6,7},{7,6},{8,9},{9,8},{10,11... | collective-permute-start | bytes 98312 | tf_op jit(solution)/shard_map/ppermute | solution.py:286
  12.7 7.2 %collective-permute-start.3 = (bf16[2048,128]{1,0:T(8,128)(2,1)S(1)}, bf16[2048,128]{1,0:T(8,128)(2,1)S(1)}, u32[]{:S(2)}, u32[]{:S(2)}) collective-permute-start(bf16[2048,128]{1,0:T(8,128)(2,1)S(1)} %get-tuple-element.32), channel_id=1, source_target_pairs={{3,7},{7,11},{11,15},{4,0},{8,4},{12,8},{19,23},{23,27},{27,31},{2... | collective-permute-start | bytes 1572872 | tf_op jit(solution)/shard_map/ppermute | solution.py:262
  14.0 40.7 %collective-permute-start.10 = (bf16[2048,128]{1,0:T(8,128)(2,1)S(1)}, bf16[2048,128]{1,0:T(8,128)(2,1)S(1)}, u32[]{:S(2)}, u32[]{:S(2)}) collective-permute-start(bf16[2048,128]{1,0:T(8,128)(2,1)S(1)} %get-tuple-element.33), channel_id=1, source_target_pairs={{1,0},{2,1},{3,2},{4,3},{5,4},{6,5},{7,6},{8,7},{9,8},{10,9},{11,1... | collective-permute-start | bytes 1572872 | tf_op jit(solution)/shard_map/ppermute | solution.py:262
  15.3 39.4 %collective-permute-start.9 = (bf16[2048,128]{1,0:T(8,128)(2,1)S(1)}, bf16[2048,128]{1,0:T(8,128)(2,1)S(1)}, u32[]{:S(2)}, u32[]{:S(2)}) collective-permute-start(bf16[2048,128]{1,0:T(8,128)(2,1)S(1)} %get-tuple-element.34), channel_id=1, source_target_pairs={{0,1},{1,2},{2,3},{3,4},{4,5},{5,6},{6,7},{7,8},{8,9},{9,10},{10,1... | collective-permute-start | bytes 1572872 | tf_op jit(solution)/shard_map/ppermute | solution.py:262
  20.0 39.6 %collective-permute-start.4 = (bf16[2048,128]{1,0:T(8,128)(2,1)S(1)}, bf16[2048,128]{1,0:T(8,128)(2,1)S(1)}, u32[]{:S(2)}, u32[]{:S(2)}) collective-permute-start(bf16[2048,128]{1,0:T(8,128)(2,1)S(1)} %get-tuple-element.35), channel_id=1, source_target_pairs={{0,1},{1,2},{2,3},{4,5},{5,6},{6,7},{8,9},{9,10},{10,11},{12,13},{... | collective-permute-start | bytes 1572872 | tf_op jit(solution)/shard_map/ppermute | solution.py:262
  21.9 37.6 %collective-permute-start.5 = (bf16[2048,128]{1,0:T(8,128)(2,1)S(1)}, bf16[2048,128]{1,0:T(8,128)(2,1)S(1)}, u32[]{:S(2)}, u32[]{:S(2)}) collective-permute-start(bf16[2048,128]{1,0:T(8,128)(2,1)S(1)} %get-tuple-element.36), channel_id=1, source_target_pairs={{1,0},{2,1},{3,2},{5,4},{6,5},{7,6},{9,8},{10,9},{11,10},{13,12},{... | collective-permute-start | bytes 1572872 | tf_op jit(solution)/shard_map/ppermute | solution.py:262
  26.2 6.2 %collective-permute-start.8 = (bf16[64,128]{1,0:T(8,128)(2,1)S(1)}, bf16[64,128]{1,0:T(8,128)(2,1)S(1)}, u32[]{:S(2)}, u32[]{:S(2)}) collective-permute-start(bf16[64,128]{1,0:T(8,128)(2,1)S(1)} %get-tuple-element.43), channel_id=1, source_target_pairs={{0,8},{4,12},{8,0},{12,4},{1,9},{5,13},{9,1},{13,5},{2,10},{6,14},... | collective-permute-start | bytes 49160 | tf_op jit(solution)/shard_map/ppermute | solution.py:252
  32.4 3.9 %collective-permute-start.7 = (bf16[320,128]{1,0:T(8,128)(2,1)S(1)}, bf16[320,128]{1,0:T(8,128)(2,1)S(1)}, u32[]{:S(2)}, u32[]{:S(2)}) collective-permute-start(bf16[320,128]{1,0:T(8,128)(2,1)S(1)} %get-tuple-element.42.refs_2_), channel_id=1, source_target_pairs={{0,12},{4,0},{8,4},{12,8},{1,13},{5,1},{9,5},{13,9},{2,14},{6,2},{... | collective-permute-start | bytes 245768 | tf_op jit(solution)/shard_map/ppermute | solution.py:252
  36.3 4.5 %collective-permute-start.6 = (bf16[320,128]{1,0:T(8,128)(2,1)S(1)}, bf16[320,128]{1,0:T(8,128)(2,1)S(1)}, u32[]{:S(2)}, u32[]{:S(2)}) collective-permute-start(bf16[320,128]{1,0:T(8,128)(2,1)S(1)} %get-tuple-element.42.refs_2_), channel_id=1, source_target_pairs={{0,4},{4,8},{8,12},{12,0},{1,5},{5,9},{9,13},{13,1},{2,6},{6,10},{... | collective-permute-start | bytes 245768 | tf_op jit(solution)/shard_map/ppermute | solution.py:252
  40.8 0.9 %copy-start.1 = (bf16[8,64,64]{2,1,0:T(8,128)(2,1)S(1)}, bf16[8,64,64]{2,1,0:T(8,128)(2,1)}, u32[]{:S(2)}) copy-start(bf16[8,64,64]{2,1,0:T(8,128)(2,1)} %refs_9_.1) | copy-start | bytes 196612
  41.7 0.7 %copy-start.2 = (bf16[1,64,64]{2,1,0:T(8,128)(2,1)S(1)}, bf16[1,64,64]{2,1,0:T(8,128)(2,1)}, u32[]{:S(2)}) copy-start(bf16[1,64,64]{2,1,0:T(8,128)(2,1)} %refs_8_.1) | copy-start | bytes 24580
  42.4 0.8 %copy-start.3 = (bf16[1,4,64,64]{3,2,1,0:T(8,128)(2,1)S(1)}, bf16[1,4,64,64]{3,2,1,0:T(8,128)(2,1)}, u32[]{:S(2)}) copy-start(bf16[1,4,64,64]{3,2,1,0:T(8,128)(2,1)} %refs_6_.1) | copy-start | bytes 98308
  43.2 0.8 %copy-start.4 = (bf16[1,4,64,64]{3,2,1,0:T(8,128)(2,1)S(1)}, bf16[1,4,64,64]{3,2,1,0:T(8,128)(2,1)}, u32[]{:S(2)}) copy-start(bf16[1,4,64,64]{3,2,1,0:T(8,128)(2,1)} %refs_7_.1) | copy-start | bytes 98308
  44.1 0.7 %copy-start.7 = (s32[1,4]{1,0:T(1,128)S(1)}, s32[1,4]{1,0:T(1,128)}, u32[]{:S(2)}) copy-start(s32[1,4]{1,0:T(1,128)} %refs_0_.1) | copy-start | bytes 52
  45.7 0.7 %copy-start.5 = (s32[8,5]{1,0:T(8,128)S(1)}, s32[8,5]{1,0:T(8,128)}, u32[]{:S(2)}) copy-start(s32[8,5]{1,0:T(8,128)} %ids_ref.5) | copy-start | bytes 484

commit v5 on v4

--- a/solution.py
+++ b/solution.py
@@ -42,7 +42,9 @@
     )
 
 
-def up_kernel(x_ref, basis_ref, leaf_map_ref, mid_map_ref, out_ref, low, high, relay, x, basis, leaf_map, mid_map, skeleton, sems, piece_sems):
+def up_kernel(
+    x_ref, basis_ref, leaf_map_ref, mid_map_ref, mid_couple_ref, couple_ref, out_ref, low, high, relay, basis, leaf_map, mid_map, mid_couple, couple, x, skeleton, sems, piece_sems
+):
     leaves, rank, rows = basis.shape
     cut = low.shape[0]
     parts = []
@@ -52,8 +54,8 @@
         parts.append(pltpu.make_async_copy(basis_ref.at[leaf], basis.at[leaf], sems.at[leaves + leaf]))
     maps = [pltpu.make_async_copy(leaf_map_ref, leaf_map, sems.at[2 * leaves]), pltpu.make_async_copy(mid_map_ref, mid_map, sems.at[2 * leaves + 1])]
     edge = pl.multiple_of(jnp.where(lax.axis_index("inner") == 0, cut, 0), rows)
-    sources = (x_ref.at[:cut], x_ref.at[cut:], x_ref.at[pl.ds(edge, cut)])
-    copies = [pltpu.make_async_copy(source, piece, piece_sems.at[i]) for i, (source, piece) in enumerate(zip(sources, (low, high, relay)))]
+    moves = ((x_ref.at[:cut], low), (x_ref.at[cut:], high), (x_ref.at[pl.ds(edge, cut)], relay), (mid_couple_ref, mid_couple), (couple_ref, couple))
+    copies = [pltpu.make_async_copy(source, piece, piece_sems.at[i]) for i, (source, piece) in enumerate(moves)]
     for copy in parts + maps + copies:
         copy.start()
     for leaf in range(leaves):
@@ -69,51 +71,36 @@
         copy.wait()
 
 
-def group_kernel(count, *refs):
-    parts, out_ref, top_ref = refs[:count], refs[count], refs[count + 1]
-    rank = top_ref.shape[0]
-    top = jnp.zeros(top_ref.shape, jnp.float32)
-    for i, part in enumerate(parts):
-        out_ref[i * rank : (i + 1) * rank, :] = part[:rank, :]
-        top += part[rank:, :].astype(jnp.float32)
-    top = top.astype(jnp.bfloat16)
-    out_ref[count * rank :, :] = top
-    top_ref[...] = top
-
-
-def down_kernel(leaf_size, inner_size, *refs):
-    far_ids, far_count, own, before, after = refs[:5]
-    tops = dict(zip(range(2, leaf_size - 1), refs[5:]))
-    couple, mid_couple, mid_map, leaf_map, out_ref, window = refs[5 + len(tops) :]
-    rank = mid_map.shape[1]
+def group_kernel(count, parts_ref, out_ref):
+    rank = parts_ref.shape[0] // (2 * count)
+    top = jnp.zeros((rank, parts_ref.shape[1]), jnp.float32)
+    for i in range(count):
+        at = 2 * i * rank
+        out_ref[i * rank : (i + 1) * rank, :] = parts_ref[at : at + rank, :]
+        top += parts_ref[at + rank : at + 2 * rank, :].astype(jnp.float32)
+    out_ref[count * rank :, :] = top.astype(jnp.bfloat16)
+
+
+def down_kernel(inner_size, far_ids, far_count, groups, couple, mid_couple, mid_map, leaf_map, out_ref):
+    rank = mid_map.shape[0]
     group = lax.axis_index("leaf")
     inner = lax.axis_index("inner")
-    last = inner_size * rank
-    top_down = jnp.zeros((rank, own.shape[1]), jnp.float32)
-    for shift in range(1, leaf_size):
-        source = lax.rem(group - shift + leaf_size, leaf_size)
-        if shift == 1:
-            top = before[last:, :]
-        elif shift == leaf_size - 1:
-            top = after[last:, :]
-        else:
-            top = tops[shift][...]
-        term = dot(couple[0, source], top)
-        top_down += jnp.where(jnp.abs(source - group) >= 2, term, 0.0)
-    for i, part in enumerate((before, own, after)):
-        window[i * last : (i + 1) * last, :] = part[:last, :]
-    total = dot(mid_map[0], top_down.astype(jnp.bfloat16))
-    for slot in range(mid_couple.shape[1]):
+    size = (inner_size + 1) * rank
+    top_down = jnp.zeros((rank, groups.shape[1]), jnp.float32)
+    for i in range(1, couple.shape[0]):
+        other = group ^ i
+        term = dot(couple[other], groups[(i + 1) * size - rank : (i + 1) * size, :])
+        top_down += jnp.where(jnp.abs(other - group) >= 2, term, 0.0)
+    total = dot(mid_map[...], top_down.astype(jnp.bfloat16))
+    for slot in range(mid_couple.shape[0]):
         live = slot < far_count[0]
         partner = jnp.where(live, far_ids[0, slot], group * inner_size)
-        side = partner // inner_size - group + 1
-        place = inner ^ lax.rem(partner, inner_size)
-        at = pl.multiple_of((side * inner_size + place) * rank, rank)
-        term = dot(mid_couple[0, slot], window[pl.ds(at, rank), :])
+        place = (partner // inner_size) ^ group
+        at = pl.multiple_of(place * size + (inner ^ lax.rem(partner, inner_size)) * rank, rank)
+        term = dot(mid_couple[slot], groups[pl.ds(at, rank), :])
         total += jnp.where(live, term, 0.0)
     total = total.astype(jnp.bfloat16)
-    for leaf in range(leaf_map.shape[0]):
-        out_ref[leaf * rank : (leaf + 1) * rank, :] = dot(leaf_map[leaf], total).astype(jnp.bfloat16)
+    out_ref[...] = dot(leaf_map[...], total).astype(jnp.bfloat16)
 
 
 def listed(ids_ref, lists, kind_of):
@@ -137,13 +124,14 @@
 def add_products(near, kind, count, blocks, partner, total, arrived=lambda slot: None):
     slots, places = kind
     rows = blocks.shape[1]
+    cut = rows // 2
 
     def product(i):
         slot = slots[i]
         arrived(slot)
         at = pl.ds(pl.multiple_of(places[i] * rows, rows), rows)
         here = pl.ds(pl.multiple_of(slot // near * rows, rows), rows)
-        return here, dot(blocks[slot], partner(at))
+        return here, dot(blocks[slot, :, :cut], partner(at)[:cut]) + dot(blocks[slot, :, cut:], partner(at)[cut:])
 
     def pair(j, carry):
         one, first = product(2 * j)
@@ -248,9 +236,6 @@
     def shaped(*shape, dtype=bf16):
         return jax.ShapeDtypeStruct(shape, dtype)
 
-    def shifted(x, axis, size, shift):
-        return lax.ppermute(x, axis, [(i, (i + shift) % size) for i in range(size)])
-
     first, last = 0, inner_size - 1
     line = [(leaf * inner_size + i, leaf * inner_size + i + 1) for leaf in range(leaf_size) for i in range(last)]
     groups = range(leaf_size)
@@ -264,51 +249,66 @@
     hop_first = [(place(g, last), place(g + 1, last)) for g in groups[:-1]] + [(place(g, first), place(g - 1, first)) for g in groups[1:]]
 
     x_hbm = held(anomalies, pltpu.HBM)
-    part, low, high, relay = call(
+    part, low, high, relay, basis, leaf_map, mid_map, mid_links, group_links = call(
         up_kernel,
-        [resident(2 * rank, columns)] + [resident(cut, columns)] * 3,
-        [ANY] * 4,
-        [VMEM] + [ANY] * 3,
+        [
+            resident(2 * rank, columns),
+            resident(cut, columns),
+            resident(cut, columns),
+            resident(cut, columns),
+            resident(leaves, rank, rows),
+            resident(leaves * rank, rank),
+            resident(rank, rank),
+            resident(*mid_couple.shape[1:]),
+            resident(*top_couple.shape[1:]),
+        ],
+        [ANY] * 6,
+        [VMEM] + [ANY] * 3 + [VMEM] * 5,
         [
             pltpu.VMEM(anomalies.shape, bf16),
-            pltpu.VMEM(leaf_basis.shape, bf16),
-            pltpu.VMEM((leaves * rank, rank), bf16),
-            pltpu.VMEM((rank, rank), bf16),
             pltpu.VMEM((leaves * rank, columns), bf16),
             pltpu.SemaphoreType.DMA((2 * leaves + 2,)),
-            pltpu.SemaphoreType.DMA((3,)),
+            pltpu.SemaphoreType.DMA((5,)),
         ],
         1000,
         1000,
         8 * MIB,
-    )(x_hbm, *[held(x, pltpu.HBM) for x in (leaf_basis, transfer_leaf.reshape(leaves * rank, rank), transfer_mid.reshape(rank, rank))])
-
-    parts = [part] + [lax.ppermute(part, "inner", [(i, i ^ s) for i in range(inner_size)]) for s in range(1, inner_size)]
-    parts, low, high, relay = lax.optimization_barrier((parts, low, high, relay))
+    )(
+        x_hbm,
+        *[
+            held(x, pltpu.HBM)
+            for x in (leaf_basis, transfer_leaf.reshape(leaves * rank, rank), transfer_mid.reshape(rank, rank), mid_couple[0], top_couple[0])
+        ],
+    )
+
+    def doubled(x, axis, reach):
+        partner = lax.ppermute(x, axis, [(i, i ^ reach) for i in range(lax.axis_size(axis))])
+        return jnp.concatenate([x, partner])
+
+    parts = doubled(part, "inner", 1)
+    parts, low, high = lax.optimization_barrier((parts, low, high))
     chain = [(i, i + 1) for i in range(leaf_size * inner_size - 1)]
     ahead = passed(high, chain)
     back = passed(low, [(j, i) for i, j in chain])
-
-    group, top = call(functools.partial(group_kernel, inner_size), (resident((inner_size + 1) * rank, columns), resident(rank, columns)), [VMEM] * inner_size, (VMEM, VMEM), [], 1000, 1000, 8 * MIB)(*parts)
+    reach = 2
+    while reach < inner_size:
+        parts = doubled(parts, "inner", reach)
+        reach *= 2
+
+    group = call(functools.partial(group_kernel, inner_size), resident((inner_size + 1) * rank, columns), [VMEM], VMEM, [], 1000, 1000, 8 * MIB)(parts)
     relayed = passed(relay, hop_first)
-    before_group = shifted(group, "leaf", leaf_size, 1)
-    after_group = shifted(group, "leaf", leaf_size, leaf_size - 1)
-    tops = [shifted(top, "leaf", leaf_size, s) for s in range(2, leaf_size - 1)]
+    reach = 1
+    while reach < leaf_size:
+        group = doubled(group, "leaf", reach)
+        reach *= 2
     far_low, far_high = jnp.where(inner == last, relayed, low), jnp.where(inner == first, relayed, high)
     far_low, far_high, x_own = lax.optimization_barrier((far_low, far_high, anomalies))
     far_ahead = passed(far_low, line + [(place(g, last), place(g, first)) for g in groups[1:]])
     far_back = passed(far_high, [(j, i) for i, j in line] + [(place(g, first), place(g, last)) for g in groups[:-1]])
 
-    leaf_down = call(
-        functools.partial(down_kernel, leaf_size, inner_size),
-        shaped(leaves * rank, columns),
-        [SMEM, SMEM] + [VMEM] * (7 + len(tops)),
-        VMEM,
-        [pltpu.VMEM((3 * inner_size * rank, columns), bf16)],
-        1000,
-        1000,
-        8 * MIB,
-    )(far_ids, far_count, group, before_group, after_group, *tops, top_couple, mid_couple, transfer_mid, transfer_leaf)
+    leaf_down = call(functools.partial(down_kernel, inner_size), shaped(leaves * rank, columns), [SMEM, SMEM] + [VMEM] * 5, VMEM, [], 1000, 1000, 8 * MIB)(
+        far_ids, far_count, group, group_links, mid_links, mid_map, leaf_map
+    )
 
     x_own, leaf_down = lax.optimization_barrier((x_own, leaf_down))
     ids = near_ids
@@ -329,7 +329,7 @@
     blocks = held(blocks, pltpu.VMEM)
     ahead, back, own_sum = lax.optimization_barrier((ahead, back, own_sum))
     close_sum = call(functools.partial(close_kernel, half), wide, [SMEM] + [VMEM] * 6, VMEM, lists, 1000, 1000, 8 * MIB)(
-        ids, ahead, back, blocks, own_sum, leaf_down, leaf_basis
+        ids, ahead, back, blocks, own_sum, leaf_down, basis
     )
     last_scratch = lists + [
         pltpu.VMEM((leaves * rows, columns), jnp.float32),

time: 63.9 us -> 59.8 us (0.936)
  the two profiles are of different devices: /device:TPU:0 before, /device:TPU:1 now
where the time goes in v5:
time: 59.8 us; the launch traced here: 58.9 us
  starting transfers between devices  21.5 us (36%)
  Pallas kernels  20.9 us (35%)
  waiting for transfers between devices  14.2 us (24%)
  local copies, waits for them, and re-layouts  1.33 us (2%)
  between operations  0.81 us (1%)
    ppermute x5, starting transfers between devices, passed(): return lax.ppermute(x, ('leaf', 'inner'), pairs)  15.4 us
    pallas_call x1, Pallas kernels, local(): call(own_kernel, (wide, resident(slots, rows, rows)), [SMEM, ANY, ANY], (...  9.68 us
    ppermute x4, waiting for transfers between devices, doubled(): lax.ppermute(x, axis, [(i, i ^ reach) for i in range(lax.axis_size(axis))])  7.57 us
    ppermute x5, waiting for transfers between devices, passed(): return lax.ppermute(x, ('leaf', 'inner'), pairs)  6.63 us
    ppermute x4, starting transfers between devices, doubled(): lax.ppermute(x, axis, [(i, i ^ reach) for i in range(lax.axis_size(axis))])  6.15 us
    pallas_call x1, Pallas kernels, local(): call(functools.partial(close_kernel, half), wide, [SMEM] + [VMEM] * 6, VM...  4.64 us
    pallas_call x1, Pallas kernels, local(): call(functools.partial(last_kernel, half), shaped(leaves * rows, columns)...  2.81 us
    pallas_call x1, Pallas kernels, local(): call(up_kernel, [resident(2 * rank, columns), resident(cut, columns), res...  2.73 us
  transfers between devices with their start and end apart: 9, of which 4 were waited for; matrix products, arithmetic and copies ran while one was open for 0% of the time, Pallas kernels for 26%

profile of v5, /device:TPU:1, one launch (start us, length us, event | category | flops | bytes accessed | tf_op | source)
XLA Modules:
  0.0 58.9 jit_solution(17053804065432715902)
XLA Ops:
  0.0 2.7 %shard_map.100 = (bf16[128,128]{1,0:T(8,128)(2,1)S(1)}, bf16[2048,128]{1,0:T(8,128)(2,1)S(1)}, bf16[2048,128]{1,0:T(8,128)(2,1)S(1)}, bf16[2048,128]{1,0:T(8,128...) custom-call(bf16[4096,128]{1,0:T(8,128)(2,1)} %x_any, ...), custom_call_target="tpu_custom_call" | custom-call | flops 1000 | bytes 1000 | tf_op jit(solution)/shard_map/pallas_call | solution.py:252
  2.7 2.0 %collective-permute-start = (bf16[2048,128]{1,0:T(8,128)(2,1)S(1)}, bf16[2048,128]{1,0:T(8,128)(2,1)S(1)}, u32[]{:S(2)}, u32[]{:S(2)}) collective-permute-start(bf16[2048,128]{1,0:T(8,128)(2,1)S(1)} %get-tuple-element.27), channel_id=1, source_target_pairs={{3,7},{7,11},{11,15},{4,0},{8,4},{12,8},{19,23},{23,27},{27,31},{2... | collective-permute-start | bytes 1572872 | tf_op jit(solution)/shard_map/ppermute | solution.py:247
  4.7 0.9 %collective-permute-start.1 = (bf16[128,128]{1,0:T(8,128)(2,1)S(1)}, bf16[128,128]{1,0:T(8,128)(2,1)S(1)}, u32[]{:S(2)}, u32[]{:S(2)}) collective-permute-start(bf16[128,128]{1,0:T(8,128)(2,1)S(1)} %get-tuple-element.28), channel_id=1, source_target_pairs={{0,1},{1,0},{2,3},{3,2},{4,5},{5,4},{6,7},{7,6},{8,9},{9,8},{10,11... | collective-permute-start | bytes 98312 | tf_op jit(solution)/shard_map/ppermute | solution.py:285
  5.6 2.3 %collective-permute-done.1 = bf16[128,128]{1,0:T(8,128)(2,1)S(1)} collective-permute-done((bf16[128,128]{1,0:T(8,128)(2,1)S(1)}, bf16[128,128]{1,0:T(8,128)(2,1)S(1)}, u32[]{:S(2)}, u32[]{:S(2)}) %collective-permute-start.1) | collective-permute-done | bytes 32800 | tf_op jit(solution)/shard_map/ppermute | solution.py:285
  7.9 4.3 %collective-permute-start.4 = (bf16[256,128]{1,0:T(8,128)(2,1)S(1)}, bf16[256,128]{1,0:T(8,128)(2,1)S(1)}, u32[]{:S(2)}, u32[]{:S(2)}) collective-permute-start(bf16[256,128]{1,0:T(8,128)(2,1)S(1)} %pad_maximum_fusion.3), channel_id=1, source_target_pairs={{0,2},{1,3},{2,0},{3,1},{4,6},{5,7},{6,4},{7,5},{8,10},{9,11},{10,... | collective-permute-start | bytes 196616 | tf_op jit(solution)/shard_map/ppermute | solution.py:285
  12.3 2.9 %collective-permute-start.8 = (bf16[2048,128]{1,0:T(8,128)(2,1)S(1)}, bf16[2048,128]{1,0:T(8,128)(2,1)S(1)}, u32[]{:S(2)}, u32[]{:S(2)}) collective-permute-start(bf16[2048,128]{1,0:T(8,128)(2,1)S(1)} %get-tuple-element.31), channel_id=1, source_target_pairs={{1,0},{2,1},{3,2},{4,3},{5,4},{6,5},{7,6},{8,7},{9,8},{10,9},{11,1... | collective-permute-start | bytes 1572872 | tf_op jit(solution)/shard_map/ppermute | solution.py:247
  15.2 0.0 collective-permute-done.4
  15.2 3.5 %collective-permute-start.7 = (bf16[2048,128]{1,0:T(8,128)(2,1)S(1)}, bf16[2048,128]{1,0:T(8,128)(2,1)S(1)}, u32[]{:S(2)}, u32[]{:S(2)}) collective-permute-start(bf16[2048,128]{1,0:T(8,128)(2,1)S(1)} %get-tuple-element.32), channel_id=1, source_target_pairs={{0,1},{1,2},{2,3},{3,4},{4,5},{5,6},{6,7},{7,8},{8,9},{9,10},{10,1... | collective-permute-start | bytes 1572872 | tf_op jit(solution)/shard_map/ppermute | solution.py:247
  18.7 0.8 %collective-permute-start.5 = (bf16[320,128]{1,0:T(8,128)(2,1)S(1)}, bf16[320,128]{1,0:T(8,128)(2,1)S(1)}, u32[]{:S(2)}, u32[]{:S(2)}) collective-permute-start(bf16[320,128]{1,0:T(8,128)(2,1)S(1)} %shard_map.101), channel_id=1, source_target_pairs={{0,4},{4,0},{8,12},{12,8},{1,5},{5,1},{9,13},{13,9},{2,6},{6,2},{1... | collective-permute-start | bytes 245768 | tf_op jit(solution)/shard_map/ppermute | solution.py:285
  19.5 0.0 collective-permute-done
  19.5 0.1 broadcast_select_fusion
  19.6 2.7 %collective-permute-start.2 = (bf16[2048,128]{1,0:T(8,128)(2,1)S(1)}, bf16[2048,128]{1,0:T(8,128)(2,1)S(1)}, u32[]{:S(2)}, u32[]{:S(2)}) collective-permute-start(bf16[2048,128]{1,0:T(8,128)(2,1)S(1)} %get-tuple-element.33), channel_id=1, source_target_pairs={{0,1},{1,2},{2,3},{4,5},{5,6},{6,7},{8,9},{9,10},{10,11},{12,13},{... | collective-permute-start | bytes 1572872 | tf_op jit(solution)/shard_map/ppermute | solution.py:247
  22.4 4.3 %collective-permute-start.3 = (bf16[2048,128]{1,0:T(8,128)(2,1)S(1)}, bf16[2048,128]{1,0:T(8,128)(2,1)S(1)}, u32[]{:S(2)}, u32[]{:S(2)}) collective-permute-start(bf16[2048,128]{1,0:T(8,128)(2,1)S(1)} %get-tuple-element.34), channel_id=1, source_target_pairs={{1,0},{2,1},{3,2},{5,4},{6,5},{7,6},{9,8},{10,9},{11,10},{13,12},{... | collective-permute-start | bytes 1572872 | tf_op jit(solution)/shard_map/ppermute | solution.py:247
  26.7 0.0 collective-permute-done.5
  26.7 0.1 collective-permute-start.6
  27.5 5.3 %collective-permute-done.6 = bf16[640,128]{1,0:T(8,128)(2,1)S(1)} collective-permute-done((bf16[640,128]{1,0:T(8,128)(2,1)S(1)}, bf16[640,128]{1,0:T(8,128)(2,1)S(1)}, u32[]{:S(2)}, u32[]{:S(2)}) %collective-permute-start.6) | collective-permute-done | bytes 163872 | tf_op jit(solution)/shard_map/ppermute | solution.py:285
  32.8 0.0 copy-start.1
  32.8 0.6 %copy-done.1 = s32[1,4]{1,0:T(1,128)S(1)} copy-done((s32[1,4]{1,0:T(1,128)S(1)}, s32[1,4]{1,0:T(1,128)}, u32[]{:S(2)}) %copy-start.1) | copy-done | bytes 40
  33.4 1.0 %shard_map.102.down_ref = bf16[512,128]{1,0:T(8,128)(2,1)S(1)} custom-call(s32[1,4]{1,0:T(1,128)S(1)} %copy-done.1, s32[1]{0:T(128)S(6)} %copy.11.far_count, bf16[1280,128]{1,0:T(8,128)(2,1)S(1)} %pad_maximum_fusion.groups, bf16[4,64,64]{2,1,0:T(8,128)(2,1)S(1)} %get-tuple-element.37.couple, bf16[4,64,64]{2,1,0:T(8,128)(2,1)S(1)} %get-tuple-element.38.mid_couple, ...), custom_call_target="tpu_custom_call" | custom-call | flops 1000 | bytes 1000 | tf_op jit(solution)/shard_map/pallas_call | solution.py:309
  34.4 0.0 copy-start
  34.4 0.7 %copy-done = s32[8,5]{1,0:T(8,128)S(1)} copy-done((s32[8,5]{1,0:T(8,128)S(1)}, s32[8,5]{1,0:T(8,128)}, u32[]{:S(2)}) %copy-start) | copy-done | bytes 184
  35.1 9.7 %shard_map.103 = (f32[4096,128]{1,0:T(8,128)S(1)}, bf16[40,512,512]{2,1,0:T(8,128)(2,1)S(1)}) custom-call(s32[8,5]{1,0:T(8,128)S(1)} %copy-done, bf16[4096,128]{1,0:T(8,128)(2,1)} %x_any, bf16[40,512,512]{2,1,0:T(8,128)(2,1)} %bitcast.5), custom_call_target="tpu_custom_call" | custom-call | flops 1000 | bytes 1000 | tf_op jit(solution)/shard_map/pallas_call | solution.py:318
  44.8 0.0 collective-permute-done.8.after
  44.8 0.0 collective-permute-done.7.before
  44.8 4.6 %shard_map.104.sum_ref = f32[4096,128]{1,0:T(8,128)S(1)} custom-call(s32[8,5]{1,0:T(8,128)S(1)} %copy-done, bf16[2048,128]{1,0:T(8,128)(2,1)S(1)} %collective-permute-done.7.before, bf16[2048,128]{1,0:T(8,128)(2,1)S(1)} %collective-permute-done.8.after, bf16[40,512,512]{2,1,0:T(8,128)(2,1)S(1)} %get-tuple-element.42.blocks, ...), custom_call_target="tpu_custom_call" | custom-call | flops 1000 | bytes 1000 | tf_op jit(solution)/shard_map/pallas_call | solution.py:331
  49.5 0.5 collective-permute-done.2.before
  50.0 6.1 %collective-permute-done.3.after = bf16[2048,128]{1,0:T(8,128)(2,1)S(1)} collective-permute-done((bf16[2048,128]{1,0:T(8,128)(2,1)S(1)}, bf16[2048,128]{1,0:T(8,128)(2,1)S(1)}, u32[]{:S(2)}, u32[]{:S(2)}) %collective-permute-start.3) | collective-permute-done | bytes 524320 | tf_op jit(solution)/shard_map/ppermute | solution.py:247
  56.1 2.8 %shard_map.105 = bf16[4096,128]{1,0:T(8,128)(2,1)} custom-call(s32[8,5]{1,0:T(8,128)S(1)} %copy-done, bf16[2048,128]{1,0:T(8,128)(2,1)S(1)} %collective-permute-done.2.before, bf16[2048,128]{1,0:T(8,128)(2,1)S(1)} %collective-permute-done.3.after, bf16[40,512,512]{2,1,0:T(8,128)(2,1)S(1)} %get-tuple-element.42.blocks, f32[4096,128]{1,0:T(8,128)S(1)} %shard_map.104.sum_ref), custom_call_target="tpu_custom_call" | custom-call | flops 1000 | bytes 1000 | tf_op jit(solution)/shard_map/pallas_call | solution.py:339
  (5 shorter events, 0.1 us)
Async XLA Ops:
  2.7 16.8 %collective-permute-start = (bf16[2048,128]{1,0:T(8,128)(2,1)S(1)}, bf16[2048,128]{1,0:T(8,128)(2,1)S(1)}, u32[]{:S(2)}, u32[]{:S(2)}) collective-permute-start(bf16[2048,128]{1,0:T(8,128)(2,1)S(1)} %get-tuple-element.27), channel_id=1, source_target_pairs={{3,7},{7,11},{11,15},{4,0},{8,4},{12,8},{19,23},{23,27},{27,31},{2... | collective-permute-start | bytes 1572872 | tf_op jit(solution)/shard_map/ppermute | solution.py:247
  4.7 3.2 %collective-permute-start.1 = (bf16[128,128]{1,0:T(8,128)(2,1)S(1)}, bf16[128,128]{1,0:T(8,128)(2,1)S(1)}, u32[]{:S(2)}, u32[]{:S(2)}) collective-permute-start(bf16[128,128]{1,0:T(8,128)(2,1)S(1)} %get-tuple-element.28), channel_id=1, source_target_pairs={{0,1},{1,0},{2,3},{3,2},{4,5},{5,4},{6,7},{7,6},{8,9},{9,8},{10,11... | collective-permute-start | bytes 98312 | tf_op jit(solution)/shard_map/ppermute | solution.py:285
  7.9 7.2 %collective-permute-start.4 = (bf16[256,128]{1,0:T(8,128)(2,1)S(1)}, bf16[256,128]{1,0:T(8,128)(2,1)S(1)}, u32[]{:S(2)}, u32[]{:S(2)}) collective-permute-start(bf16[256,128]{1,0:T(8,128)(2,1)S(1)} %pad_maximum_fusion.3), channel_id=1, source_target_pairs={{0,2},{1,3},{2,0},{3,1},{4,6},{5,7},{6,4},{7,5},{8,10},{9,11},{10,... | collective-permute-start | bytes 196616 | tf_op jit(solution)/shard_map/ppermute | solution.py:285
  12.3 32.5 %collective-permute-start.8 = (bf16[2048,128]{1,0:T(8,128)(2,1)S(1)}, bf16[2048,128]{1,0:T(8,128)(2,1)S(1)}, u32[]{:S(2)}, u32[]{:S(2)}) collective-permute-start(bf16[2048,128]{1,0:T(8,128)(2,1)S(1)} %get-tuple-element.31), channel_id=1, source_target_pairs={{1,0},{2,1},{3,2},{4,3},{5,4},{6,5},{7,6},{8,7},{9,8},{10,9},{11,1... | collective-permute-start | bytes 1572872 | tf_op jit(solution)/shard_map/ppermute | solution.py:247
  15.2 29.6 %collective-permute-start.7 = (bf16[2048,128]{1,0:T(8,128)(2,1)S(1)}, bf16[2048,128]{1,0:T(8,128)(2,1)S(1)}, u32[]{:S(2)}, u32[]{:S(2)}) collective-permute-start(bf16[2048,128]{1,0:T(8,128)(2,1)S(1)} %get-tuple-element.32), channel_id=1, source_target_pairs={{0,1},{1,2},{2,3},{3,4},{4,5},{5,6},{6,7},{7,8},{8,9},{9,10},{10,1... | collective-permute-start | bytes 1572872 | tf_op jit(solution)/shard_map/ppermute | solution.py:247
  18.7 8.0 %collective-permute-start.5 = (bf16[320,128]{1,0:T(8,128)(2,1)S(1)}, bf16[320,128]{1,0:T(8,128)(2,1)S(1)}, u32[]{:S(2)}, u32[]{:S(2)}) collective-permute-start(bf16[320,128]{1,0:T(8,128)(2,1)S(1)} %shard_map.101), channel_id=1, source_target_pairs={{0,4},{4,0},{8,12},{12,8},{1,5},{5,1},{9,13},{13,9},{2,6},{6,2},{1... | collective-permute-start | bytes 245768 | tf_op jit(solution)/shard_map/ppermute | solution.py:285
  19.6 30.4 %collective-permute-start.2 = (bf16[2048,128]{1,0:T(8,128)(2,1)S(1)}, bf16[2048,128]{1,0:T(8,128)(2,1)S(1)}, u32[]{:S(2)}, u32[]{:S(2)}) collective-permute-start(bf16[2048,128]{1,0:T(8,128)(2,1)S(1)} %get-tuple-element.33), channel_id=1, source_target_pairs={{0,1},{1,2},{2,3},{4,5},{5,6},{6,7},{8,9},{9,10},{10,11},{12,13},{... | collective-permute-start | bytes 1572872 | tf_op jit(solution)/shard_map/ppermute | solution.py:247
  22.4 33.7 %collective-permute-start.3 = (bf16[2048,128]{1,0:T(8,128)(2,1)S(1)}, bf16[2048,128]{1,0:T(8,128)(2,1)S(1)}, u32[]{:S(2)}, u32[]{:S(2)}) collective-permute-start(bf16[2048,128]{1,0:T(8,128)(2,1)S(1)} %get-tuple-element.34), channel_id=1, source_target_pairs={{1,0},{2,1},{3,2},{5,4},{6,5},{7,6},{9,8},{10,9},{11,10},{13,12},{... | collective-permute-start | bytes 1572872 | tf_op jit(solution)/shard_map/ppermute | solution.py:247
  26.7 6.0 %collective-permute-start.6 = (bf16[640,128]{1,0:T(8,128)(2,1)S(1)}, bf16[640,128]{1,0:T(8,128)(2,1)S(1)}, u32[]{:S(2)}, u32[]{:S(2)}) collective-permute-start(bf16[640,128]{1,0:T(8,128)(2,1)S(1)} %pad_maximum_fusion.1), channel_id=1, source_target_pairs={{0,8},{4,12},{8,0},{12,4},{1,9},{5,13},{9,1},{13,5},{2,10},{6,14},... | collective-permute-start | bytes 491528 | tf_op jit(solution)/shard_map/ppermute | solution.py:285
  32.8 0.7 %copy-start.1 = (s32[1,4]{1,0:T(1,128)S(1)}, s32[1,4]{1,0:T(1,128)}, u32[]{:S(2)}) copy-start(s32[1,4]{1,0:T(1,128)} %far_ids.1) | copy-start | bytes 52
  34.4 0.7 %copy-start = (s32[8,5]{1,0:T(8,128)S(1)}, s32[8,5]{1,0:T(8,128)}, u32[]{:S(2)}) copy-start(s32[8,5]{1,0:T(8,128)} %ids_ref.5) | copy-start | bytes 484

commit v6 on v4

v6 whole, which is shorter than its diff:
```python
import functools

import jax
import jax.numpy as jnp
from jax import lax
from jax.experimental import pallas as pl
from jax.experimental.pallas import tpu as pltpu
from jax.sharding import PartitionSpec as P

MIB = 1 << 20
VMEM = pl.BlockSpec(memory_space=pltpu.VMEM)
SMEM = pl.BlockSpec(memory_space=pltpu.SMEM)
ANY = pl.BlockSpec(memory_space=pl.ANY)


def held(x, space):
    return pltpu.with_memory_space_constraint(x, space)


def resident(*shape, dtype=jnp.bfloat16):
    return pltpu.VMEM(shape, dtype)


def dot(a, b):
    return lax.dot_general(a, b, (((1,), (0,)), ((), ())), preferred_element_type=jnp.float32)


def dot_t(a, b):
    return lax.dot_general(a, b, (((0,), (0,)), ((), ())), preferred_element_type=jnp.float32)


def call(kernel, out_shape, in_specs, out_specs, scratch, flops, moved, vmem, aliases=None):
    return pl.pallas_call(
        kernel,
        out_shape=out_shape,
        in_specs=in_specs,
        out_specs=out_specs,
        scratch_shapes=scratch,
        cost_estimate=pl.CostEstimate(flops=flops, bytes_accessed=moved, transcendentals=0),
        compiler_params=pltpu.CompilerParams(vmem_limit_bytes=vmem),
        input_output_aliases=aliases or {},
    )


def cut_kernel(cuts, x_ref, *refs):
    pieces, relay, sems = refs[:-2], refs[-2], refs[-1]
    rows = x_ref.shape[0] // cuts[-1]
    edge = jnp.where(lax.axis_index("inner") == 0, (cuts[-1] - relay.shape[0] // rows) * rows, 0)
    sources = [x_ref.at[a * rows : b * rows] for a, b in cuts[:-1]] + [x_ref.at[pl.ds(pl.multiple_of(edge, rows), relay.shape[0])]]
    copies = [pltpu.make_async_copy(source, piece, sems.at[i]) for i, (source, piece) in enumerate(zip(sources, (*pieces, relay)))]
    for copy in copies:
        copy.start()
    for copy in copies:
        copy.wait()


def up_kernel(
    cuts, x_ref, basis_ref, leaf_map_ref, mid_map_ref, mid_couple_ref, couple_ref, out_ref, x, basis, leaf_map, mid_map, mid_couple, couple, *refs
):
    pieces, (skeleton, sems, piece_sems) = refs[:-3], refs[-3:]
    leaves, rank, rows = basis.shape
    parts = []
    for leaf in range(leaves):
        here = slice(leaf * rows, (leaf + 1) * rows)
        parts.append(pltpu.make_async_copy(x_ref.at[here], x.at[here], sems.at[leaf]))
        parts.append(pltpu.make_async_copy(basis_ref.at[leaf], basis.at[leaf], sems.at[leaves + leaf]))
    maps = [pltpu.make_async_copy(leaf_map_ref, leaf_map, sems.at[2 * leaves]), pltpu.make_async_copy(mid_map_ref, mid_map, sems.at[2 * leaves + 1])]
    moves = [(x_ref.at[a * rows : b * rows], piece) for (a, b), piece in zip(cuts, pieces)] + [(mid_couple_ref, mid_couple), (couple_ref, couple)]
    copies = [pltpu.make_async_copy(source, target, piece_sems.at[i]) for i, (source, target) in enumerate(moves)]
    for copy in parts + maps + copies:
        copy.start()
    for leaf in range(leaves):
        parts[2 * leaf].wait()
        parts[2 * leaf + 1].wait()
        skeleton[leaf * rank : (leaf + 1) * rank, :] = dot(basis[leaf], x[leaf * rows : (leaf + 1) * rows, :]).astype(jnp.bfloat16)
    for copy in maps:
        copy.wait()
    mid = dot_t(leaf_map[...], skeleton[...]).astype(jnp.bfloat16)
    out_ref[:rank, :] = mid
    out_ref[rank:, :] = dot_t(mid_map[...], mid).astype(jnp.bfloat16)
    for copy in copies:
        copy.wait()


def group_kernel(count, parts_ref, out_ref, top_ref):
    rank = top_ref.shape[0]
    top = jnp.zeros(top_ref.shape, jnp.float32)
    for i in range(count):
        at = 2 * i * rank
        out_ref[i * rank : (i + 1) * rank, :] = parts_ref[at : at + rank, :]
        top += parts_ref[at + rank : at + 2 * rank, :].astype(jnp.float32)
    top = top.astype(jnp.bfloat16)
    out_ref[count * rank :, :] = top
    top_ref[...] = top


def down_kernel(leaf_size, inner_size, far_ids, far_count, own, before, after, *refs):
    tops = dict(zip(range(2, leaf_size - 1), refs))
    couple, mid_couple, mid_map, leaf_map, basis, _, out_ref, window = refs[len(tops) :]
    rank = mid_map.shape[0]
    group = lax.axis_index("leaf")
    inner = lax.axis_index("inner")
    last = inner_size * rank
    top_down = jnp.zeros((rank, own.shape[1]), jnp.float32)
    for shift in range(1, leaf_size):
        source = lax.rem(group - shift + leaf_size, leaf_size)
        if shift == 1:
            top = before[last:, :]
        elif shift == leaf_size - 1:
            top = after[last:, :]
        else:
            top = tops[shift][...]
        term = dot(couple[source], top)
        top_down += jnp.where(jnp.abs(source - group) >= 2, term, 0.0)
    for i, part in enumerate((before, own, after)):
        window[i * last : (i + 1) * last, :] = part[:last, :]
    total = dot(mid_map[...], top_down.astype(jnp.bfloat16))
    for slot in range(mid_couple.shape[0]):
        live = slot < far_count[0]
        partner = jnp.where(live, far_ids[0, slot], group * inner_size)
        side = partner // inner_size - group + 1
        at = pl.multiple_of((side * inner_size + (inner ^ lax.rem(partner, inner_size))) * rank, rank)
        term = dot(mid_couple[slot], window[pl.ds(at, rank), :])
        total += jnp.where(live, term, 0.0)
    leaf_down = dot(leaf_map[...], total.astype(jnp.bfloat16)).astype(jnp.bfloat16)
    leaves, _, rows = basis.shape
    for leaf in range(leaves):
        out_ref[leaf * rows : (leaf + 1) * rows, :] += dot_t(basis[leaf], leaf_down[leaf * rank : (leaf + 1) * rank, :])


def listed(ids_ref, lists, kind_of):
    leaves, near = ids_ref.shape
    first = (lax.axis_index("leaf") * lax.axis_size("inner") + lax.axis_index("inner")) * leaves

    def one(leaf, counts):
        for k in range(near):
            offset = ids_ref[leaf, k] - first
            grown = []
            for (slots, places), count, (member, place) in zip(lists, counts, kind_of(leaf, offset)):
                slots[count] = leaf * near + k
                places[count] = place
                grown.append(count + member.astype(jnp.int32))
            counts = tuple(grown)
        return counts

    return lax.fori_loop(0, leaves, one, (jnp.int32(0),) * len(lists))


def add_products(near, kind, count, blocks, x_ref, total, arrived=lambda slot: None):
    slots, places = kind
    rows = blocks.shape[1]

    def product(i):
        slot = slots[i]
        arrived(slot)
        at = pl.ds(pl.multiple_of(places[i] * rows, rows), rows)
        here = pl.ds(pl.multiple_of(slot // near * rows, rows), rows)
        return here, dot(blocks[slot], x_ref[at, :])

    def pair(j, carry):
        one, first = product(2 * j)
        two, second = product(2 * j + 1)
        total[one, :] += first
        total[two, :] += second
        return carry

    lax.fori_loop(0, count // 2, pair, 0)

    @pl.when(lax.rem(count, 2) == 1)
    def _():
        here, term = product(count - 1)
        total[here, :] += term


def own_kernel(stop, ids_ref, x_ref, blocks_ref, total, blocks, own_slots, own_places, other_slots, other_places, sems):
    leaves, near = ids_ref.shape

    def kind_of(leaf, offset):
        own = (offset >= 0) & (offset < leaves) & (leaf < stop)
        return (own, offset), (jnp.logical_not(own), 0)

    kinds = ((own_slots, own_places), (other_slots, other_places))
    own_count, other_count = listed(ids_ref, kinds, kind_of)

    def copy(slot):
        return pltpu.make_async_copy(blocks_ref.at[slot], blocks.at[slot], sems.at[slot])

    def begin(slots):
        def one(i, carry):
            copy(slots[i]).start()
            return carry

        return one

    lax.fori_loop(0, own_count, begin(own_slots), 0)
    lax.fori_loop(0, other_count, begin(other_slots), 0)
    total[...] = jnp.zeros_like(total)
    add_products(near, kinds[0], own_count, blocks, x_ref, total, lambda slot: copy(slot).wait())

    def finish(i, carry):
        copy(other_slots[i]).wait()
        return carry

    lax.fori_loop(0, other_count, finish, 0)


def wave_kernel(near_by, far_off, stop, ids_ref, first_before, first_after, before, after, x_ref, blocks, _, total, *lists):
    leaves, near = ids_ref.shape

    def kind_of(leaf, offset):
        return (
            ((offset < 0) & (offset >= -near_by), offset + near_by),
            ((offset >= leaves) & (offset < leaves + near_by), offset - leaves),
            ((offset < -near_by) & (offset >= -far_off), offset + far_off),
            ((offset >= leaves + near_by) & (offset < leaves + far_off), offset - leaves - near_by),
            ((offset >= 0) & (offset < leaves) & (leaf >= stop), offset),
        )

    kinds = [lists[i : i + 2] for i in range(0, len(lists), 2)]
    counts = listed(ids_ref, kinds, kind_of)
    for kind, count, partner in zip(kinds, counts, (first_before, first_after, before, after, x_ref)):
        add_products(near, kind, count, blocks, partner, total)


def last_kernel(near_by, ids_ref, before, after, blocks, _, out_ref, total, *refs):
    lists, (result, sems) = refs[:4], refs[4:]
    leaves, near = ids_ref.shape
    rows = blocks.shape[1]

    def kind_of(leaf, offset):
        return (offset < -near_by, offset + leaves), (offset >= leaves + near_by, offset - leaves - near_by)

    kinds = (lists[:2], lists[2:])
    counts = listed(ids_ref, kinds, kind_of)
    for kind, count, x_ref in zip(kinds, counts, (before, after)):
        add_products(near, kind, count, blocks, x_ref, total)
    stores = []
    for leaf in range(leaves):
        here = slice(leaf * rows, (leaf + 1) * rows)
        result[here, :] = total[here, :].astype(result.dtype)
        stores.append(pltpu.make_async_copy(result.at[here], out_ref.at[here], sems.at[leaf]))
        stores[-1].start()
    for store in stores:
        store.wait()


def local(anomalies, leaf_basis, near_blocks, near_ids, transfer_leaf, transfer_mid, far_ids, far_count, mid_couple, top_couple):
    leaves, rank, rows = leaf_basis.shape
    near = near_blocks.shape[1]
    columns = anomalies.shape[1]
    inner_size = lax.axis_size("inner")
    leaf_size = lax.axis_size("leaf")
    bf16 = jnp.bfloat16
    inner = lax.axis_index("inner")
    first, last = 0, inner_size - 1
    groups = range(leaf_size)

    def place(leaf, i):
        return leaf * inner_size + i

    def passed(x, pairs):
        return lax.ppermute(x, ("leaf", "inner"), pairs)

    def doubled(x, axis, reach):
        partner = lax.ppermute(x, axis, [(i, i ^ reach) for i in range(lax.axis_size(axis))])
        return jnp.concatenate([x, partner])

    chain = [(i, i + 1) for i in range(leaf_size * inner_size - 1)]
    line = [(place(g, i), place(g, i + 1)) for g in groups for i in range(last)]
    hop = [(place(g, last), place(g + 1, last)) for g in groups[:-1]] + [(place(g, first), place(g - 1, first)) for g in groups[1:]]

    one = leaves // 4
    two = one + leaves * 3 // 8
    sizes = [one, one, two - one, two - one, leaves - two, leaves - two]
    cuts = [(leaves - one, leaves), (0, one), (leaves - two, leaves - one), (one, two), (0, leaves - two), (two, leaves)]

    def kernel(body, out_shape, in_specs, out_specs, scratch, aliases=None, flops=1000):
        return call(body, out_shape, in_specs, out_specs, scratch, flops, 1000, 8 * MIB, aliases)

    pieces = [resident(size * rows, columns) for size in sizes]
    ahead, back, relay = kernel(
        functools.partial(cut_kernel, (*cuts[:2], leaves)), [*pieces[:2], pieces[4]], [ANY], [ANY] * 3, [pltpu.SemaphoreType.DMA((3,))]
    )(held(anomalies, pltpu.HBM))
    relayed = passed(relay, hop)
    x_up, ahead, back = lax.optimization_barrier((anomalies, ahead, back))
    halo = [(passed(ahead, chain), passed(back, [(j, i) for i, j in chain]))]

    operands = (x_up, leaf_basis, transfer_leaf.reshape(leaves * rank, rank), transfer_mid.reshape(rank, rank), mid_couple[0], top_couple[0])
    part, x_own, basis, leaf_map, mid_map, mid_links, group_links, *later = kernel(
        functools.partial(up_kernel, cuts[2:]),
        [resident(2 * rank, columns)] + [resident(*x.shape) for x in operands] + pieces[2:],
        [ANY] * 6,
        [VMEM] * 7 + [ANY] * 4,
        [pltpu.VMEM((leaves * rank, columns), bf16), pltpu.SemaphoreType.DMA((2 * leaves + 2,)), pltpu.SemaphoreType.DMA((6,))],
    )(*[held(x, pltpu.HBM) for x in operands])
    low, high = jnp.where(inner == last, relayed, later[2]), jnp.where(inner == first, relayed, later[3])
    part, x_own, ahead, back, low, high = lax.optimization_barrier((part, x_own, *later[:2], low, high))
    parts = doubled(part, "inner", 1)
    halo.append((passed(ahead, chain), passed(back, [(j, i) for i, j in chain])))

    slots = leaves * near
    lists = [pltpu.SMEM((slots + 1,), jnp.int32)] * 2
    wide = resident(leaves * rows, columns, dtype=jnp.float32)
    total, blocks = kernel(
        functools.partial(own_kernel, leaves // 2),
        (wide, resident(slots, rows, rows)),
        [SMEM, VMEM, ANY],
        (VMEM, VMEM),
        lists * 2 + [pltpu.SemaphoreType.DMA((slots,))],
        flops=4 * 10**9,
    )(near_ids, held(x_own, pltpu.VMEM), held(near_blocks.reshape(slots, rows, rows), pltpu.HBM))
    blocks = held(blocks, pltpu.VMEM)

    parts, total, halo[0] = lax.optimization_barrier((parts, total, halo[0]))
    reach = 2
    while reach < inner_size:
        parts = doubled(parts, "inner", reach)
        reach *= 2
    low, high, total = lax.optimization_barrier((low, high, total))
    halo.append(
        (
            passed(low, line + [(place(g, last), place(g, first)) for g in groups[1:]]),
            passed(high, [(j, i) for i, j in line] + [(place(g, first), place(g, last)) for g in groups[:-1]]),
        )
    )

    parts, halo[1] = lax.optimization_barrier((parts, halo[1]))
    group, top = kernel(
        functools.partial(group_kernel, inner_size), (resident((inner_size + 1) * rank, columns), resident(rank, columns)), [VMEM], (VMEM, VMEM), []
    )(parts)

    def shifted(x, shift):
        return lax.ppermute(x, "leaf", [(i, (i + shift) % leaf_size) for i in groups])

    found = [shifted(group, 1), shifted(group, leaf_size - 1)] + [shifted(top, s) for s in range(2, leaf_size - 1)]
    group, total = lax.optimization_barrier((group, total))
    total = kernel(functools.partial(wave_kernel, one, two, leaves // 2), wide, [SMEM] + [VMEM] * 7, VMEM, lists * 5, aliases={7: 0}, flops=10**10)(
        near_ids, *halo[0], *halo[1], x_own, blocks, held(total, pltpu.VMEM)
    )
    found, total = lax.optimization_barrier((found, total))
    total = kernel(
        functools.partial(down_kernel, leaf_size, inner_size),
        wide,
        [SMEM, SMEM] + [VMEM] * (7 + len(found)),
        VMEM,
        [pltpu.VMEM((3 * inner_size * rank, columns), bf16)],
        aliases={8 + len(found): 0},
    )(far_ids, far_count, group, *found, group_links, mid_links, mid_map, leaf_map, basis, held(total, pltpu.VMEM))
    out, _ = kernel(
        functools.partial(last_kernel, two),
        (jax.ShapeDtypeStruct(anomalies.shape, bf16), wide),
        [SMEM] + [VMEM] * 4,
        (ANY, VMEM),
        lists * 2 + [pltpu.VMEM(anomalies.shape, bf16), pltpu.SemaphoreType.DMA((leaves,))],
        aliases={4: 1},
    )(near_ids, *halo[2], blocks, held(total, pltpu.VMEM))
    return out


def solution(mesh):
    return jax.shard_map(
        local,
        mesh=mesh,
        in_specs=(
            P(("leaf", "inner"), "groups"),
            P(("leaf", "inner"), None, None),
            P(("leaf", "inner"), None, None, None),
            P(("leaf", "inner"), None),
            P(("leaf", "inner"), None, None),
            P(("leaf", "inner"), None, None),
            P(("leaf", "inner"), None),
            P(("leaf", "inner")),
            P(("leaf", "inner"), None, None, None),
            P("leaf", None, None, None),
        ),
        out_specs=P(("leaf", "inner"), "groups"),
        check_vma=False,
    )
```

time: 63.9 us -> 87.2 us (1.36)
  the two profiles are of different devices: /device:TPU:0 before, /device:TPU:1 now
where the time goes in v6:
time: 87.2 us; the launch traced here: 87.7 us
  Pallas kernels  52.9 us (61%)
  starting transfers between devices  28.2 us (32%)
  waiting for transfers between devices  4.63 us (5%)
  other arithmetic  1.08 us (1%)
  between operations  0.89 us (1%)
    pallas_call x1, Pallas kernels, local(): kernel(functools.partial(cut_kernel, (*cuts[:2], leaves)), [*pieces[:2],...  28.9 us
    ppermute x7, starting transfers between devices, passed(): return lax.ppermute(x, ('leaf', 'inner'), pairs)  25.5 us
    pallas_call x1, Pallas kernels, local(): kernel(functools.partial(wave_kernel, one, two, leaves // 2), wide, [SMEM...  8.77 us
    pallas_call x1, Pallas kernels, local(): kernel(functools.partial(own_kernel, leaves // 2), (wide, resident(slots,...  8.24 us
    ppermute x2, waiting for transfers between devices, doubled(): lax.ppermute(x, axis, [(i, i ^ reach) for i in range(lax.axis_size(axis))])  4.6 us
    pallas_call x1, Pallas kernels, local(): kernel(functools.partial(last_kernel, two), (jax.ShapeDtypeStruct(anomali...  2.82 us
    pallas_call x1, Pallas kernels, local(): kernel(functools.partial(up_kernel, cuts[2:]), [resident(2 * rank, column...  2.75 us
    ppermute x3, starting transfers between devices, shifted(): lax.ppermute(x, 'leaf', [(i, (i + shift) % leaf_size) for i in groups])  2.25 us
  transfers between devices with their start and end apart: 12, of which 1 were waited for; matrix products, arithmetic and copies ran while one was open for 1% of the time, Pallas kernels for 24%

profile of v6, /device:TPU:1, one launch (start us, length us, event | category | flops | bytes accessed | tf_op | source)
XLA Modules:
  0.0 87.7 jit_solution(13757245462597783827)
XLA Ops:
  0.0 28.9 %shard_map.100 = (bf16[1024,128]{1,0:T(8,128)(2,1)}, bf16[1024,128]{1,0:T(8,128)(2,1)}, bf16[1536,128]{1,0:T(8,128)(2,1)}) custom-call(bf16[4096,128]{1,0:T(8,128)(2,1)} %x_ref.2), custom_call_target="tpu_custom_call" | custom-call | flops 1000 | bytes 1000 | tf_op jit(solution)/shard_map/pallas_call | solution.py:281
  28.9 0.0 copy-start
  28.9 2.0 %collective-permute-start = (bf16[1536,128]{1,0:T(8,128)(2,1)}, bf16[1536,128]{1,0:T(8,128)(2,1)}, u32[]{:S(2)}, u32[]{:S(2)}) collective-permute-start(bf16[1536,128]{1,0:T(8,128)(2,1)} %get-tuple-element.56), channel_id=1, source_target_pairs={{3,7},{7,11},{11,15},{4,0},{8,4},{12,8},{19,23},{23,27},{27,31},{2... | collective-permute-start | bytes 1179656 | tf_op jit(solution)/shard_map/ppermute | solution.py:262
  30.9 3.5 %collective-permute-start.2 = (bf16[1024,128]{1,0:T(8,128)(2,1)}, bf16[1024,128]{1,0:T(8,128)(2,1)}, u32[]{:S(2)}, u32[]{:S(2)}) collective-permute-start(bf16[1024,128]{1,0:T(8,128)(2,1)} %get-tuple-element.64), channel_id=1, source_target_pairs={{0,1},{1,2},{2,3},{3,4},{4,5},{5,6},{6,7},{7,8},{8,9},{9,10},{10,1... | collective-permute-start | bytes 786440 | tf_op jit(solution)/shard_map/ppermute | solution.py:262
  34.4 5.6 %collective-permute-start.3 = (bf16[1024,128]{1,0:T(8,128)(2,1)}, bf16[1024,128]{1,0:T(8,128)(2,1)}, u32[]{:S(2)}, u32[]{:S(2)}) collective-permute-start(bf16[1024,128]{1,0:T(8,128)(2,1)} %get-tuple-element.65), channel_id=1, source_target_pairs={{1,0},{2,1},{3,2},{4,3},{5,4},{6,5},{7,6},{8,7},{9,8},{10,9},{11,1... | collective-permute-start | bytes 786440 | tf_op jit(solution)/shard_map/ppermute | solution.py:262
  40.0 2.8 %shard_map.101 = (bf16[128,128]{1,0:T(8,128)(2,1)S(1)}, bf16[4096,128]{1,0:T(8,128)(2,1)S(1)}, bf16[8,64,512]{2,1,0:T(8,128)(2,1)S(1)}, bf16[512,64]{1,0:T(8,128...) custom-call(bf16[4096,128]{1,0:T(8,128)(2,1)} %x_ref.2, ...), custom_call_target="tpu_custom_call" | custom-call | flops 1000 | bytes 1000 | tf_op jit(solution)/shard_map/pallas_call | solution.py:289
  42.7 0.0 collective-permute-done
  42.8 1.1 %broadcast_select_fusion = (bf16[1536,128]{1,0:T(8,128)(2,1)S(1)}, bf16[1536,128]{1,0:T(8,128)(2,1)S(1)}) fusion(bf16[1536,128]{1,0:T(8,128)(2,1)} %collective-permute-done, bf16[1536,128]{1,0:T(8,128)(2,1)S(1)} %get-tuple-element.58, pred[]{:T(512)S(6)} %eq.7, bf16[1536,128]{1,0:T(8,128)(2,1)S(1)} %get-tuple-element.57, pred[]{:T(512)S(6)} %eq.6), kind=kLoop, calls=%fused_computation | loop fusion | flops 393216 | bytes 1966082 | tf_op jit(solution)/shard_map/jit(_where)/select_n | solution.py:296
  43.8 0.1 collective-permute-start.1
  43.9 3.3 %collective-permute-start.7 = (bf16[1536,128]{1,0:T(8,128)(2,1)S(1)}, bf16[1536,128]{1,0:T(8,128)(2,1)S(1)}, u32[]{:S(2)}, u32[]{:S(2)}) collective-permute-start(bf16[1536,128]{1,0:T(8,128)(2,1)S(1)} %get-tuple-element.71), channel_id=1, source_target_pairs={{0,1},{1,2},{2,3},{3,4},{4,5},{5,6},{6,7},{7,8},{8,9},{9,10},{10,1... | collective-permute-start | bytes 1179656 | tf_op jit(solution)/shard_map/ppermute | solution.py:262
  47.3 4.0 %collective-permute-start.8 = (bf16[1536,128]{1,0:T(8,128)(2,1)S(1)}, bf16[1536,128]{1,0:T(8,128)(2,1)S(1)}, u32[]{:S(2)}, u32[]{:S(2)}) collective-permute-start(bf16[1536,128]{1,0:T(8,128)(2,1)S(1)} %get-tuple-element.72), channel_id=1, source_target_pairs={{1,0},{2,1},{3,2},{4,3},{5,4},{6,5},{7,6},{8,7},{9,8},{10,9},{11,1... | collective-permute-start | bytes 1179656 | tf_op jit(solution)/shard_map/ppermute | solution.py:262
  51.3 0.0 copy-done
  51.3 8.2 %shard_map.102 = (f32[4096,128]{1,0:T(8,128)S(1)}, bf16[40,512,512]{2,1,0:T(8,128)(2,1)S(1)}) custom-call(s32[8,5]{1,0:T(8,128)S(1)} %copy-done, bf16[4096,128]{1,0:T(8,128)(2,1)S(1)} %get-tuple-element.62.x_ref, bf16[40,512,512]{2,1,0:T(8,128)(2,1)} %bitcast.5), custom_call_target="tpu_custom_call" | custom-call | flops 4000000000 | bytes 1000 | tf_op jit(solution)/shard_map/pallas_call | solution.py:304
  59.5 0.0 collective-permute-done.1
  59.6 0.0 collective-permute-done.2.first_before
  59.6 0.0 collective-permute-done.3.first_after
  59.6 0.4 collective-permute-start.6
  60.6 3.5 %collective-permute-start.4 = (bf16[1536,128]{1,0:T(8,128)(2,1)S(1)}, bf16[1536,128]{1,0:T(8,128)(2,1)S(1)}, u32[]{:S(2)}, u32[]{:S(2)}) collective-permute-start(bf16[1536,128]{1,0:T(8,128)(2,1)S(1)} %get-tuple-element.67), channel_id=1, source_target_pairs={{0,1},{1,2},{2,3},{4,5},{5,6},{6,7},{8,9},{9,10},{10,11},{12,13},{... | collective-permute-start | bytes 1179656 | tf_op jit(solution)/shard_map/ppermute | solution.py:262
  64.1 3.6 %collective-permute-start.5 = (bf16[1536,128]{1,0:T(8,128)(2,1)S(1)}, bf16[1536,128]{1,0:T(8,128)(2,1)S(1)}, u32[]{:S(2)}, u32[]{:S(2)}) collective-permute-start(bf16[1536,128]{1,0:T(8,128)(2,1)S(1)} %get-tuple-element.68), channel_id=1, source_target_pairs={{1,0},{2,1},{3,2},{5,4},{6,5},{7,6},{9,8},{10,9},{11,10},{13,12},{... | collective-permute-start | bytes 1179656 | tf_op jit(solution)/shard_map/ppermute | solution.py:262
  67.7 4.6 %collective-permute-done.6 = bf16[256,128]{1,0:T(8,128)(2,1)S(1)} collective-permute-done((bf16[256,128]{1,0:T(8,128)(2,1)S(1)}, bf16[256,128]{1,0:T(8,128)(2,1)S(1)}, u32[]{:S(2)}, u32[]{:S(2)}) %collective-permute-start.6) | collective-permute-done | bytes 65568 | tf_op jit(solution)/shard_map/ppermute | solution.py:265
  72.3 0.0 collective-permute-done.7.before
  72.3 0.0 collective-permute-done.8.after
  72.4 0.8 collective-permute-start.10
  73.2 1.0 %collective-permute-start.9 = (bf16[320,128]{1,0:T(8,128)(2,1)S(1)}, bf16[320,128]{1,0:T(8,128)(2,1)S(1)}, u32[]{:S(2)}, u32[]{:S(2)}) collective-permute-start(bf16[320,128]{1,0:T(8,128)(2,1)S(1)} %get-tuple-element.76.own), channel_id=1, source_target_pairs={{0,4},{4,8},{8,12},{12,0},{1,5},{5,9},{9,13},{13,1},{2,6},{6,10},{... | collective-permute-start | bytes 245768 | tf_op jit(solution)/shard_map/ppermute | solution.py:333
  74.2 0.5 collective-permute-start.11
  74.6 0.0 copy-start.1
  74.6 8.8 %shard_map.104.refs_6_ = f32[4096,128]{1,0:T(8,128)S(1)} custom-call(s32[8,5]{1,0:T(8,128)S(1)} %copy-done, bf16[1024,128]{1,0:T(8,128)(2,1)} %collective-permute-done.2.first_before, bf16[1024,128]{1,0:T(8,128)(2,1)} %collective-permute-done.3.first_after, bf16[1536,128]{1,0:T(8,128)(2,1)S(1)} %collective-permute-done.7.before, ...), custom_call_target="tpu_custom_call", output_to_operand_aliasing={{}: (7, {})} | custom-call | flops 10000000000 | bytes 1000 | tf_op jit(solution)/shard_map/pallas_call | solution.py:337
  83.4 0.0 collective-permute-done.11.refs_0_
  83.4 0.0 collective-permute-done.10.after
  83.4 0.0 collective-permute-done.9.before
  83.4 0.0 copy-done.1
  83.4 1.4 %shard_map.105._ = f32[4096,128]{1,0:T(8,128)S(1)} custom-call(s32[1,4]{1,0:T(1,128)S(1)} %copy-done.1, s32[1]{0:T(128)S(6)} %copy.17.far_count, bf16[320,128]{1,0:T(8,128)(2,1)S(1)} %get-tuple-element.76.own, bf16[320,128]{1,0:T(8,128)(2,1)S(1)} %collective-permute-done.9.before, ...), custom_call_target="tpu_custom_call", output_to_operand_aliasing={{}: (11, {})} | custom-call | flops 1000 | bytes 1000 | tf_op jit(solution)/shard_map/pallas_call | solution.py:341
  84.9 0.0 collective-permute-done.4.before
  84.9 0.0 collective-permute-done.5.after
  84.9 2.8 %shard_map.106 = (bf16[4096,128]{1,0:T(8,128)(2,1)}, f32[4096,128]{1,0:T(8,128)S(1)}) custom-call(s32[8,5]{1,0:T(8,128)S(1)} %copy-done, bf16[1536,128]{1,0:T(8,128)(2,1)S(1)} %collective-permute-done.4.before, bf16[1536,128]{1,0:T(8,128)(2,1)S(1)} %collective-permute-done.5.after, ...), custom_call_target="tpu_custom_call", output_to_operand_aliasing={{1}: (4, {})} | custom-call | flops 1000 | bytes 1000 | tf_op jit(solution)/shard_map/pallas_call | solution.py:349
  (3 shorter events, 0.0 us)
Async XLA Ops:
  28.9 22.4 %copy-start = (s32[8,5]{1,0:T(8,128)S(1)}, s32[8,5]{1,0:T(8,128)}, u32[]{:S(2)}) copy-start(s32[8,5]{1,0:T(8,128)} %ids_ref.5) | copy-start | bytes 484
  28.9 13.8 %collective-permute-start = (bf16[1536,128]{1,0:T(8,128)(2,1)}, bf16[1536,128]{1,0:T(8,128)(2,1)}, u32[]{:S(2)}, u32[]{:S(2)}) collective-permute-start(bf16[1536,128]{1,0:T(8,128)(2,1)} %get-tuple-element.56), channel_id=1, source_target_pairs={{3,7},{7,11},{11,15},{4,0},{8,4},{12,8},{19,23},{23,27},{27,31},{2... | collective-permute-start | bytes 1179656 | tf_op jit(solution)/shard_map/ppermute | solution.py:262
  30.9 28.6 %collective-permute-start.2 = (bf16[1024,128]{1,0:T(8,128)(2,1)}, bf16[1024,128]{1,0:T(8,128)(2,1)}, u32[]{:S(2)}, u32[]{:S(2)}) collective-permute-start(bf16[1024,128]{1,0:T(8,128)(2,1)} %get-tuple-element.64), channel_id=1, source_target_pairs={{0,1},{1,2},{2,3},{3,4},{4,5},{5,6},{6,7},{7,8},{8,9},{9,10},{10,1... | collective-permute-start | bytes 786440 | tf_op jit(solution)/shard_map/ppermute | solution.py:262
  34.4 25.2 %collective-permute-start.3 = (bf16[1024,128]{1,0:T(8,128)(2,1)}, bf16[1024,128]{1,0:T(8,128)(2,1)}, u32[]{:S(2)}, u32[]{:S(2)}) collective-permute-start(bf16[1024,128]{1,0:T(8,128)(2,1)} %get-tuple-element.65), channel_id=1, source_target_pairs={{1,0},{2,1},{3,2},{4,3},{5,4},{6,5},{7,6},{8,7},{9,8},{10,9},{11,1... | collective-permute-start | bytes 786440 | tf_op jit(solution)/shard_map/ppermute | solution.py:262
  43.8 15.7 %collective-permute-start.1 = (bf16[128,128]{1,0:T(8,128)(2,1)S(1)}, bf16[128,128]{1,0:T(8,128)(2,1)S(1)}, u32[]{:S(2)}, u32[]{:S(2)}) collective-permute-start(bf16[128,128]{1,0:T(8,128)(2,1)S(1)} %get-tuple-element.61), channel_id=1, source_target_pairs={{0,1},{1,0},{2,3},{3,2},{4,5},{5,4},{6,7},{7,6},{8,9},{9,8},{10,11... | collective-permute-start | bytes 98312 | tf_op jit(solution)/shard_map/ppermute | solution.py:265
  43.9 28.4 %collective-permute-start.7 = (bf16[1536,128]{1,0:T(8,128)(2,1)S(1)}, bf16[1536,128]{1,0:T(8,128)(2,1)S(1)}, u32[]{:S(2)}, u32[]{:S(2)}) collective-permute-start(bf16[1536,128]{1,0:T(8,128)(2,1)S(1)} %get-tuple-element.71), channel_id=1, source_target_pairs={{0,1},{1,2},{2,3},{3,4},{4,5},{5,6},{6,7},{7,8},{8,9},{9,10},{10,1... | collective-permute-start | bytes 1179656 | tf_op jit(solution)/shard_map/ppermute | solution.py:262
  47.3 25.1 %collective-permute-start.8 = (bf16[1536,128]{1,0:T(8,128)(2,1)S(1)}, bf16[1536,128]{1,0:T(8,128)(2,1)S(1)}, u32[]{:S(2)}, u32[]{:S(2)}) collective-permute-start(bf16[1536,128]{1,0:T(8,128)(2,1)S(1)} %get-tuple-element.72), channel_id=1, source_target_pairs={{1,0},{2,1},{3,2},{4,3},{5,4},{6,5},{7,6},{8,7},{9,8},{10,9},{11,1... | collective-permute-start | bytes 1179656 | tf_op jit(solution)/shard_map/ppermute | solution.py:262
  59.6 12.7 %collective-permute-start.6 = (bf16[256,128]{1,0:T(8,128)(2,1)S(1)}, bf16[256,128]{1,0:T(8,128)(2,1)S(1)}, u32[]{:S(2)}, u32[]{:S(2)}) collective-permute-start(bf16[256,128]{1,0:T(8,128)(2,1)S(1)} %pad_maximum_fusion.1), channel_id=1, source_target_pairs={{0,2},{1,3},{2,0},{3,1},{4,6},{5,7},{6,4},{7,5},{8,10},{9,11},{10,... | collective-permute-start | bytes 196616 | tf_op jit(solution)/shard_map/ppermute | solution.py:265
  60.6 24.2 %collective-permute-start.4 = (bf16[1536,128]{1,0:T(8,128)(2,1)S(1)}, bf16[1536,128]{1,0:T(8,128)(2,1)S(1)}, u32[]{:S(2)}, u32[]{:S(2)}) collective-permute-start(bf16[1536,128]{1,0:T(8,128)(2,1)S(1)} %get-tuple-element.67), channel_id=1, source_target_pairs={{0,1},{1,2},{2,3},{4,5},{5,6},{6,7},{8,9},{9,10},{10,11},{12,13},{... | collective-permute-start | bytes 1179656 | tf_op jit(solution)/shard_map/ppermute | solution.py:262
  64.1 20.8 %collective-permute-start.5 = (bf16[1536,128]{1,0:T(8,128)(2,1)S(1)}, bf16[1536,128]{1,0:T(8,128)(2,1)S(1)}, u32[]{:S(2)}, u32[]{:S(2)}) collective-permute-start(bf16[1536,128]{1,0:T(8,128)(2,1)S(1)} %get-tuple-element.68), channel_id=1, source_target_pairs={{1,0},{2,1},{3,2},{5,4},{6,5},{7,6},{9,8},{10,9},{11,10},{13,12},{... | collective-permute-start | bytes 1179656 | tf_op jit(solution)/shard_map/ppermute | solution.py:262
  72.4 11.0 %collective-permute-start.10 = (bf16[320,128]{1,0:T(8,128)(2,1)S(1)}, bf16[320,128]{1,0:T(8,128)(2,1)S(1)}, u32[]{:S(2)}, u32[]{:S(2)}) collective-permute-start(bf16[320,128]{1,0:T(8,128)(2,1)S(1)} %get-tuple-element.76.own), channel_id=1, source_target_pairs={{0,12},{4,0},{8,4},{12,8},{1,13},{5,1},{9,5},{13,9},{2,14},{6,2},{... | collective-permute-start | bytes 245768 | tf_op jit(solution)/shard_map/ppermute | solution.py:333
  73.2 10.2 %collective-permute-start.9 = (bf16[320,128]{1,0:T(8,128)(2,1)S(1)}, bf16[320,128]{1,0:T(8,128)(2,1)S(1)}, u32[]{:S(2)}, u32[]{:S(2)}) collective-permute-start(bf16[320,128]{1,0:T(8,128)(2,1)S(1)} %get-tuple-element.76.own), channel_id=1, source_target_pairs={{0,4},{4,8},{8,12},{12,0},{1,5},{5,9},{9,13},{13,1},{2,6},{6,10},{... | collective-permute-start | bytes 245768 | tf_op jit(solution)/shard_map/ppermute | solution.py:333
  74.2 9.2 %collective-permute-start.11 = (bf16[64,128]{1,0:T(8,128)(2,1)S(1)}, bf16[64,128]{1,0:T(8,128)(2,1)S(1)}, u32[]{:S(2)}, u32[]{:S(2)}) collective-permute-start(bf16[64,128]{1,0:T(8,128)(2,1)S(1)} %get-tuple-element.77), channel_id=1, source_target_pairs={{0,8},{4,12},{8,0},{12,4},{1,9},{5,13},{9,1},{13,5},{2,10},{6,14},... | collective-permute-start | bytes 49160 | tf_op jit(solution)/shard_map/ppermute | solution.py:333
  74.6 8.8 %copy-start.1 = (s32[1,4]{1,0:T(1,128)S(1)}, s32[1,4]{1,0:T(1,128)}, u32[]{:S(2)}) copy-start(s32[1,4]{1,0:T(1,128)} %far_ids.1) | copy-start | bytes 52

commit v7 on v6

--- a/solution.py
+++ b/solution.py
@@ -19,6 +19,14 @@
 
 def resident(*shape, dtype=jnp.bfloat16):
     return pltpu.VMEM(shape, dtype)
+
+
+def turn_of(leaf, inner_size):
+    return (3 * leaf + 2) % inner_size
+
+
+def carrier(turn, inner_size):
+    return lax.rem((turn + inner_size - 2 % inner_size) * pow(3, -1, inner_size), inner_size)
 
 
 def dot(a, b):
@@ -82,45 +90,31 @@
         copy.wait()
 
 
-def group_kernel(count, parts_ref, out_ref, top_ref):
-    rank = top_ref.shape[0]
-    top = jnp.zeros(top_ref.shape, jnp.float32)
-    for i in range(count):
-        at = 2 * i * rank
-        out_ref[i * rank : (i + 1) * rank, :] = parts_ref[at : at + rank, :]
-        top += parts_ref[at + rank : at + 2 * rank, :].astype(jnp.float32)
-    top = top.astype(jnp.bfloat16)
-    out_ref[count * rank :, :] = top
-    top_ref[...] = top
-
-
-def down_kernel(leaf_size, inner_size, far_ids, far_count, own, before, after, *refs):
-    tops = dict(zip(range(2, leaf_size - 1), refs))
-    couple, mid_couple, mid_map, leaf_map, basis, _, out_ref, window = refs[len(tops) :]
+def down_kernel(leaf_size, inner_size, far_ids, far_count, plane, planes, couple, mid_couple, mid_map, leaf_map, basis, _, out_ref):
     rank = mid_map.shape[0]
+    size = 2 * rank
     group = lax.axis_index("leaf")
     inner = lax.axis_index("inner")
-    last = inner_size * rank
-    top_down = jnp.zeros((rank, own.shape[1]), jnp.float32)
-    for shift in range(1, leaf_size):
-        source = lax.rem(group - shift + leaf_size, leaf_size)
-        if shift == 1:
-            top = before[last:, :]
-        elif shift == leaf_size - 1:
-            top = after[last:, :]
-        else:
-            top = tops[shift][...]
-        term = dot(couple[source], top)
-        top_down += jnp.where(jnp.abs(source - group) >= 2, term, 0.0)
-    for i, part in enumerate((before, own, after)):
-        window[i * last : (i + 1) * last, :] = part[:last, :]
+
+    def at_of(step, leaf, offset=0):
+        return pl.ds(pl.multiple_of((step * leaf_size + leaf) * size + offset, rank), rank)
+
+    top_down = jnp.zeros((rank, plane.shape[1]), jnp.float32)
+    for distance in range(1, leaf_size):
+        other = group ^ distance
+        top = plane[at_of(0, other, rank), :].astype(jnp.float32)
+        for step in range(inner_size):
+            top += planes[at_of(step, other, rank), :].astype(jnp.float32)
+        term = dot(couple[other], top.astype(jnp.bfloat16))
+        top_down += jnp.where(jnp.abs(other - group) >= 2, term, 0.0)
     total = dot(mid_map[...], top_down.astype(jnp.bfloat16))
     for slot in range(mid_couple.shape[0]):
         live = slot < far_count[0]
         partner = jnp.where(live, far_ids[0, slot], group * inner_size)
-        side = partner // inner_size - group + 1
-        at = pl.multiple_of((side * inner_size + (inner ^ lax.rem(partner, inner_size))) * rank, rank)
-        term = dot(mid_couple[slot], window[pl.ds(at, rank), :])
+        other, turn = partner // inner_size, inner ^ lax.rem(partner, inner_size)
+        step = (group & (inner_size - 1)) ^ carrier(turn, inner_size)
+        near, far = plane[at_of(0, other), :], planes[at_of(step, other), :]
+        term = dot(mid_couple[slot], jnp.where(turn == 0, near, far))
         total += jnp.where(live, term, 0.0)
     leaf_down = dot(leaf_map[...], total.astype(jnp.bfloat16)).astype(jnp.bfloat16)
     leaves, _, rows = basis.shape
@@ -204,22 +198,16 @@
     lax.fori_loop(0, other_count, finish, 0)
 
 
-def wave_kernel(near_by, far_off, stop, ids_ref, first_before, first_after, before, after, x_ref, blocks, _, total, *lists):
+def wave_kernel(near_by, ids_ref, before, after, blocks, _, total, *lists):
     leaves, near = ids_ref.shape
 
     def kind_of(leaf, offset):
-        return (
-            ((offset < 0) & (offset >= -near_by), offset + near_by),
-            ((offset >= leaves) & (offset < leaves + near_by), offset - leaves),
-            ((offset < -near_by) & (offset >= -far_off), offset + far_off),
-            ((offset >= leaves + near_by) & (offset < leaves + far_off), offset - leaves - near_by),
-            ((offset >= 0) & (offset < leaves) & (leaf >= stop), offset),
-        )
-
-    kinds = [lists[i : i + 2] for i in range(0, len(lists), 2)]
+        return ((offset < 0) & (offset >= -near_by), offset + near_by), ((offset >= leaves) & (offset < leaves + near_by), offset - leaves)
+
+    kinds = (lists[:2], lists[2:])
     counts = listed(ids_ref, kinds, kind_of)
-    for kind, count, partner in zip(kinds, counts, (first_before, first_after, before, after, x_ref)):
-        add_products(near, kind, count, blocks, partner, total)
+    for kind, count, x_ref in zip(kinds, counts, (before, after)):
+        add_products(near, kind, count, blocks, x_ref, total)
 
 
 def last_kernel(near_by, ids_ref, before, after, blocks, _, out_ref, total, *refs):
@@ -261,62 +249,54 @@
     def passed(x, pairs):
         return lax.ppermute(x, ("leaf", "inner"), pairs)
 
-    def doubled(x, axis, reach):
-        partner = lax.ppermute(x, axis, [(i, i ^ reach) for i in range(lax.axis_size(axis))])
-        return jnp.concatenate([x, partner])
+    def swapped(x, reach):
+        return lax.ppermute(x, "leaf", [(i, i ^ reach) for i in groups])
 
     chain = [(i, i + 1) for i in range(leaf_size * inner_size - 1)]
     line = [(place(g, i), place(g, i + 1)) for g in groups for i in range(last)]
     hop = [(place(g, last), place(g + 1, last)) for g in groups[:-1]] + [(place(g, first), place(g - 1, first)) for g in groups[1:]]
 
-    one = leaves // 4
-    two = one + leaves * 3 // 8
-    sizes = [one, one, two - one, two - one, leaves - two, leaves - two]
-    cuts = [(leaves - one, leaves), (0, one), (leaves - two, leaves - one), (one, two), (0, leaves - two), (two, leaves)]
+    one = leaves * 5 // 8
+    rest = leaves - one
+    sizes = [one, one, rest, rest]
+    cuts = [(rest, leaves), (0, one), (0, rest), (one, leaves)]
 
     def kernel(body, out_shape, in_specs, out_specs, scratch, aliases=None, flops=1000):
         return call(body, out_shape, in_specs, out_specs, scratch, flops, 1000, 8 * MIB, aliases)
 
     pieces = [resident(size * rows, columns) for size in sizes]
     ahead, back, relay = kernel(
-        functools.partial(cut_kernel, (*cuts[:2], leaves)), [*pieces[:2], pieces[4]], [ANY], [ANY] * 3, [pltpu.SemaphoreType.DMA((3,))]
+        functools.partial(cut_kernel, (*cuts[:2], leaves)), [*pieces[:2], pieces[2]], [ANY], [VMEM] * 3, [pltpu.SemaphoreType.DMA((3,))]
     )(held(anomalies, pltpu.HBM))
     relayed = passed(relay, hop)
     x_up, ahead, back = lax.optimization_barrier((anomalies, ahead, back))
     halo = [(passed(ahead, chain), passed(back, [(j, i) for i, j in chain]))]
 
     operands = (x_up, leaf_basis, transfer_leaf.reshape(leaves * rank, rank), transfer_mid.reshape(rank, rank), mid_couple[0], top_couple[0])
-    part, x_own, basis, leaf_map, mid_map, mid_links, group_links, *later = kernel(
+    plane, x_own, basis, leaf_map, mid_map, mid_links, group_links, *later = kernel(
         functools.partial(up_kernel, cuts[2:]),
         [resident(2 * rank, columns)] + [resident(*x.shape) for x in operands] + pieces[2:],
         [ANY] * 6,
-        [VMEM] * 7 + [ANY] * 4,
-        [pltpu.VMEM((leaves * rank, columns), bf16), pltpu.SemaphoreType.DMA((2 * leaves + 2,)), pltpu.SemaphoreType.DMA((6,))],
+        [VMEM] * 9,
+        [pltpu.VMEM((leaves * rank, columns), bf16), pltpu.SemaphoreType.DMA((2 * leaves + 2,)), pltpu.SemaphoreType.DMA((4,))],
     )(*[held(x, pltpu.HBM) for x in operands])
-    low, high = jnp.where(inner == last, relayed, later[2]), jnp.where(inner == first, relayed, later[3])
-    part, x_own, ahead, back, low, high = lax.optimization_barrier((part, x_own, *later[:2], low, high))
-    parts = doubled(part, "inner", 1)
-    halo.append((passed(ahead, chain), passed(back, [(j, i) for i, j in chain])))
-
     slots = leaves * near
     lists = [pltpu.SMEM((slots + 1,), jnp.int32)] * 2
     wide = resident(leaves * rows, columns, dtype=jnp.float32)
     total, blocks = kernel(
-        functools.partial(own_kernel, leaves // 2),
+        functools.partial(own_kernel, leaves),
         (wide, resident(slots, rows, rows)),
         [SMEM, VMEM, ANY],
         (VMEM, VMEM),
         lists * 2 + [pltpu.SemaphoreType.DMA((slots,))],
-        flops=4 * 10**9,
+        flops=1000,
     )(near_ids, held(x_own, pltpu.VMEM), held(near_blocks.reshape(slots, rows, rows), pltpu.HBM))
     blocks = held(blocks, pltpu.VMEM)
-
-    parts, total, halo[0] = lax.optimization_barrier((parts, total, halo[0]))
-    reach = 2
-    while reach < inner_size:
-        parts = doubled(parts, "inner", reach)
-        reach *= 2
-    low, high, total = lax.optimization_barrier((low, high, total))
+    plane = lax.all_gather(plane, "leaf", axis=0, tiled=True)
+    low, high = jnp.where(inner == last, relayed, later[0]), jnp.where(inner == first, relayed, later[1])
+    plane, low, high, total = lax.optimization_barrier((plane, low, high, total))
+    turns = [(place(g, i), place(g, i ^ turn_of(g, inner_size))) for g in groups for i in range(inner_size)]
+    planes = passed(plane, [(i, j) for i, j in turns if i != j])
     halo.append(
         (
             passed(low, line + [(place(g, last), place(g, first)) for g in groups[1:]]),
@@ -324,36 +304,26 @@
         )
     )
 
-    parts, halo[1] = lax.optimization_barrier((parts, halo[1]))
-    group, top = kernel(
-        functools.partial(group_kernel, inner_size), (resident((inner_size + 1) * rank, columns), resident(rank, columns)), [VMEM], (VMEM, VMEM), []
-    )(parts)
-
-    def shifted(x, shift):
-        return lax.ppermute(x, "leaf", [(i, (i + shift) % leaf_size) for i in groups])
-
-    found = [shifted(group, 1), shifted(group, leaf_size - 1)] + [shifted(top, s) for s in range(2, leaf_size - 1)]
-    group, total = lax.optimization_barrier((group, total))
-    total = kernel(functools.partial(wave_kernel, one, two, leaves // 2), wide, [SMEM] + [VMEM] * 7, VMEM, lists * 5, aliases={7: 0}, flops=10**10)(
-        near_ids, *halo[0], *halo[1], x_own, blocks, held(total, pltpu.VMEM)
+    planes, halo[0] = lax.optimization_barrier((planes, halo[0]))
+
+    others = [swapped(planes, reach) for reach in range(1, inner_size)]
+    total, planes = lax.optimization_barrier((total, planes))
+    total = kernel(functools.partial(wave_kernel, one), wide, [SMEM] + [VMEM] * 4, VMEM, lists * 2, aliases={4: 0}, flops=10**9)(
+        near_ids, *halo[0], blocks, held(total, pltpu.VMEM)
     )
-    found, total = lax.optimization_barrier((found, total))
+    others, total = lax.optimization_barrier((others, total))
+    planes = jnp.concatenate([planes, *others])
     total = kernel(
-        functools.partial(down_kernel, leaf_size, inner_size),
-        wide,
-        [SMEM, SMEM] + [VMEM] * (7 + len(found)),
-        VMEM,
-        [pltpu.VMEM((3 * inner_size * rank, columns), bf16)],
-        aliases={8 + len(found): 0},
-    )(far_ids, far_count, group, *found, group_links, mid_links, mid_map, leaf_map, basis, held(total, pltpu.VMEM))
+        functools.partial(down_kernel, leaf_size, inner_size), wide, [SMEM, SMEM] + [VMEM] * 8, VMEM, [], aliases={9: 0}
+    )(far_ids, far_count, plane, planes, group_links, mid_links, mid_map, leaf_map, basis, held(total, pltpu.VMEM))
     out, _ = kernel(
-        functools.partial(last_kernel, two),
+        functools.partial(last_kernel, one),
         (jax.ShapeDtypeStruct(anomalies.shape, bf16), wide),
         [SMEM] + [VMEM] * 4,
         (ANY, VMEM),
         lists * 2 + [pltpu.VMEM(anomalies.shape, bf16), pltpu.SemaphoreType.DMA((leaves,))],
         aliases={4: 1},
-    )(near_ids, *halo[2], blocks, held(total, pltpu.VMEM))
+    )(near_ids, *halo[1], blocks, held(total, pltpu.VMEM))
     return out
 
 

time: 87.2 us -> 78 us (0.89)
  Pallas kernels: 52.9 us -> 22.7 us
  local copies, waits for them, and re-layouts: 0.01 us -> 18.7 us
  blocking collectives: 0 us -> 5.88 us
  waiting for transfers between devices: 4.63 us -> 0.02 us
    pallas_call x1, Pallas kernels: 28.9 us -> 2.61 us  [local(): kernel(functools.partial(cut_kernel, (*cuts[:2], leaves)), [*pieces[:2],...]
    unnamed x4 -> x34, local copies, waits for them, and re-layouts: 0.01 us -> 18.7 us
    all_gather x0 -> x1, blocking collectives: none -> 5.88 us  [local(): plane = lax.all_gather(plane, 'leaf', axis=0, tiled=True)]
    ppermute x5 -> x3, starting transfers between devices: 2.7 us -> 7.66 us  [swapped(): return lax.ppermute(x, 'leaf', [(i, i ^ reach) for i in groups])]
    ppermute x7 -> x6, starting transfers between devices: 25.5 us -> 20.7 us  [passed(): return lax.ppermute(x, ('leaf', 'inner'), pairs)]
    ppermute x5 -> x3, waiting for transfers between devices: 4.61 us -> 0.01 us  [swapped(): return lax.ppermute(x, 'leaf', [(i, i ^ reach) for i in groups])]
    pallas_call x4 -> x3, Pallas kernels: 19.8 us -> 15.9 us  [the longest x1 8.35 us: local(): kernel(functools.partial(own_kernel, leaves), (wide, resident(slots, rows...]
  transfers between devices with their start and end apart: 12 -> 9, of which waited for: 1 -> 0; matrix products, arithmetic and copies ran while one was open for 1% -> 2% of each run, Pallas kernels for 24% -> 22%
where the time goes in v7:
time: 78 us; the launch traced here: 77.8 us
  starting transfers between devices  28.3 us (36%)
  Pallas kernels  22.7 us (29%)
  local copies, waits for them, and re-layouts  18.7 us (24%)
  blocking collectives  5.88 us (8%)
  other arithmetic  1.22 us (2%)
  between operations  0.93 us (1%)
    ppermute x6, starting transfers between devices, passed(): return lax.ppermute(x, ('leaf', 'inner'), pairs)  20.7 us
    unnamed x34, local copies, waits for them, and re-layouts  18.7 us
    pallas_call x1, Pallas kernels, local(): kernel(functools.partial(own_kernel, leaves), (wide, resident(slots, rows...  8.35 us
    ppermute x3, starting transfers between devices, swapped(): return lax.ppermute(x, 'leaf', [(i, i ^ reach) for i in groups])  7.66 us
    all_gather x1, blocking collectives, local(): plane = lax.all_gather(plane, 'leaf', axis=0, tiled=True)  5.88 us
    pallas_call x1, Pallas kernels, local(): kernel(functools.partial(wave_kernel, one), wide, [SMEM] + [VMEM] * 4, VM...  4.92 us
    pallas_call x1, Pallas kernels, local(): kernel(functools.partial(up_kernel, cuts[2:]), [resident(2 * rank, column...  2.73 us
    pallas_call x1, Pallas kernels, local(): kernel(functools.partial(last_kernel, one), (jax.ShapeDtypeStruct(anomali...  2.67 us
  transfers between devices with their start and end apart: 9, of which 0 were waited for; matrix products, arithmetic and copies ran while one was open for 2% of the time, Pallas kernels for 22%

profile of v7, /device:TPU:1, one launch (start us, length us, event | category | flops | bytes accessed | tf_op | source)
XLA Modules:
  0.0 77.8 jit_solution(6201479103419404417)
XLA Ops:
  0.0 2.6 %shard_map.100 = (bf16[2560,128]{1,0:T(8,128)(2,1)}, bf16[2560,128]{1,0:T(8,128)(2,1)}, bf16[1536,128]{1,0:T(8,128)(2,1)}) custom-call(bf16[4096,128]{1,0:T(8,128)(2,1)} %x_ref.2), custom_call_target="tpu_custom_call" | custom-call | flops 1000 | bytes 1000 | tf_op jit(solution)/shard_map/pallas_call | solution.py:268
  2.6 2.0 %collective-permute-start = (bf16[1536,128]{1,0:T(8,128)(2,1)}, bf16[1536,128]{1,0:T(8,128)(2,1)}, u32[]{:S(2)}, u32[]{:S(2)}) collective-permute-start(bf16[1536,128]{1,0:T(8,128)(2,1)} %get-tuple-element.40), channel_id=1, source_target_pairs={{3,7},{7,11},{11,15},{4,0},{8,4},{12,8},{19,23},{23,27},{27,31},{2... | collective-permute-start | bytes 1179656 | tf_op jit(solution)/shard_map/ppermute | solution.py:250
  4.6 3.5 %collective-permute-start.4 = (bf16[2560,128]{1,0:T(8,128)(2,1)}, bf16[2560,128]{1,0:T(8,128)(2,1)S(1)}, u32[]{:S(2)}, u32[]{:S(2)}) collective-permute-start(bf16[2560,128]{1,0:T(8,128)(2,1)} %get-tuple-element.50), channel_id=1, source_target_pairs={{0,1},{1,2},{2,3},{3,4},{4,5},{5,6},{6,7},{7,8},{8,9},{9,10},{10,1... | collective-permute-start | bytes 1966088 | tf_op jit(solution)/shard_map/ppermute | solution.py:250
  8.1 5.6 %collective-permute-start.5 = (bf16[2560,128]{1,0:T(8,128)(2,1)}, bf16[2560,128]{1,0:T(8,128)(2,1)S(1)}, u32[]{:S(2)}, u32[]{:S(2)}) collective-permute-start(bf16[2560,128]{1,0:T(8,128)(2,1)} %get-tuple-element.51), channel_id=1, source_target_pairs={{1,0},{2,1},{3,2},{4,3},{5,4},{6,5},{7,6},{8,7},{9,8},{10,9},{11,1... | collective-permute-start | bytes 1966088 | tf_op jit(solution)/shard_map/ppermute | solution.py:250
  13.7 2.7 %shard_map.101 = (bf16[128,128]{1,0:T(8,128)(2,1)S(1)}, bf16[4096,128]{1,0:T(8,128)(2,1)S(1)}, bf16[8,64,512]{2,1,0:T(8,128)(2,1)S(1)}, bf16[512,64]{1,0:T(8,128...) custom-call(bf16[4096,128]{1,0:T(8,128)(2,1)} %x_ref.2, ...), custom_call_target="tpu_custom_call" | custom-call | flops 1000 | bytes 1000 | tf_op jit(solution)/shard_map/pallas_call | solution.py:276
  16.4 0.0 copy-start.5
  16.4 0.8 copy-done.5
  17.2 0.7 copy-done.6
  17.9 0.7 copy-done.7
  18.6 0.6 copy-done.9
  19.2 0.6 copy-done.11
  19.8 0.6 copy-done.14
  20.4 5.9 %all_gather.3.plane = bf16[512,128]{1,0:T(8,128)(2,1)S(1)} all-gather(bf16[128,128]{1,0:T(8,128)(2,1)S(1)} %get-tuple-element.39), channel_id=1, replica_groups=mesh['groups'=2,'leaf'=4,'inner'=4] {'leaf'}, dimensions={0}, use_global_device_ids=true | all-gather | bytes 163840 | tf_op jit(solution)/shard_map/all_gather | solution.py:295
  26.3 0.0 copy-done.13
  26.3 8.3 %shard_map.102 = (f32[4096,128]{1,0:T(8,128)S(1)}, bf16[40,512,512]{2,1,0:T(8,128)(2,1)S(1)}) custom-call(s32[8,5]{1,0:T(8,128)S(1)} %copy-done.13, bf16[4096,128]{1,0:T(8,128)(2,1)S(1)} %get-tuple-element.43.x_ref, bf16[40,512,512]{2,1,0:T(8,128)(2,1)} %bitcast.5), custom_call_target="tpu_custom_call" | custom-call | flops 1000 | bytes 1000 | tf_op jit(solution)/shard_map/pallas_call | solution.py:286
  34.7 0.0 copy-done.3
  34.7 0.0 copy-start
  34.7 7.0 %copy-done = bf16[40,512,512]{2,1,0:T(8,128)(2,1)} copy-done((bf16[40,512,512]{2,1,0:T(8,128)(2,1)}, bf16[40,512,512]{2,1,0:T(8,128)(2,1)S(1)}, u32[]{:S(2)}) %copy-start) | copy-done | bytes 20971544
  41.7 0.0 collective-permute-done
  41.7 1.2 %broadcast_select_fusion = (bf16[1536,128]{1,0:T(8,128)(2,1)S(1)}, bf16[1536,128]{1,0:T(8,128)(2,1)S(1)}) fusion(bf16[1536,128]{1,0:T(8,128)(2,1)} %collective-permute-done, bf16[1536,128]{1,0:T(8,128)(2,1)} %copy-done.6, pred[]{:T(512)S(6)} %eq.7, bf16[1536,128]{1,0:T(8,128)(2,1)} %copy-done.5, pred[]{:T(512)S(6)} %eq.6), kind=kLoop, calls=%fused_computation.1 | loop fusion | flops 393216 | bytes 1966082 | tf_op jit(solution)/shard_map/jit(_where)/select_n | solution.py:296
  42.9 2.6 %collective-permute-start.3 = (bf16[512,128]{1,0:T(8,128)(2,1)S(1)}, bf16[512,128]{1,0:T(8,128)(2,1)S(1)}, u32[]{:S(2)}, u32[]{:S(2)}) collective-permute-start(bf16[512,128]{1,0:T(8,128)(2,1)S(1)} %all_gather.3.plane), channel_id=1, source_target_pairs={{0,2},{1,3},{2,0},{3,1},{4,5},{5,4},{6,7},{7,6},{12,15},{13,14},{1... | collective-permute-start | bytes 393224 | tf_op jit(solution)/shard_map/ppermute | solution.py:250
  45.5 2.7 %collective-permute-start.1 = (bf16[1536,128]{1,0:T(8,128)(2,1)S(1)}, bf16[1536,128]{1,0:T(8,128)(2,1)S(1)}, u32[]{:S(2)}, u32[]{:S(2)}) collective-permute-start(bf16[1536,128]{1,0:T(8,128)(2,1)S(1)} %get-tuple-element.45), channel_id=1, source_target_pairs={{0,1},{1,2},{2,3},{4,5},{5,6},{6,7},{8,9},{9,10},{10,11},{12,13},{... | collective-permute-start | bytes 1179656 | tf_op jit(solution)/shard_map/ppermute | solution.py:250
  48.2 4.4 %collective-permute-start.2 = (bf16[1536,128]{1,0:T(8,128)(2,1)S(1)}, bf16[1536,128]{1,0:T(8,128)(2,1)S(1)}, u32[]{:S(2)}, u32[]{:S(2)}) collective-permute-start(bf16[1536,128]{1,0:T(8,128)(2,1)S(1)} %get-tuple-element.46), channel_id=1, source_target_pairs={{1,0},{2,1},{3,2},{5,4},{6,5},{7,6},{9,8},{10,9},{11,10},{13,12},{... | collective-permute-start | bytes 1179656 | tf_op jit(solution)/shard_map/ppermute | solution.py:250
  52.5 0.0 collective-permute-done.3
  52.6 0.0 collective-permute-done.4.before
  52.6 0.0 collective-permute-done.5.after
  52.6 6.0 %collective-permute-start.6 = (bf16[512,128]{1,0:T(8,128)(2,1)S(1)}, bf16[512,128]{1,0:T(8,128)(2,1)S(1)}, u32[]{:S(2)}, u32[]{:S(2)}) collective-permute-start(bf16[512,128]{1,0:T(8,128)(2,1)S(1)} %collective-permute-done.3), channel_id=1, source_target_pairs={{0,4},{4,0},{8,12},{12,8},{1,5},{5,1},{9,13},{13,9},{2,6},{6,2},{1... | collective-permute-start | bytes 393224 | tf_op jit(solution)/shard_map/ppermute | solution.py:253
  58.5 0.0 collective-permute-start.7
  58.5 1.7 %collective-permute-start.8 = (bf16[512,128]{1,0:T(8,128)(2,1)S(1)}, bf16[512,128]{1,0:T(8,128)(2,1)S(1)}, u32[]{:S(2)}, u32[]{:S(2)}) collective-permute-start(bf16[512,128]{1,0:T(8,128)(2,1)S(1)} %collective-permute-done.3), channel_id=1, source_target_pairs={{0,12},{4,8},{8,4},{12,0},{1,13},{5,9},{9,5},{13,1},{2,14},{6,10},... | collective-permute-start | bytes 393224 | tf_op jit(solution)/shard_map/ppermute | solution.py:253
  60.9 0.0 copy-start.1
  60.9 7.0 %copy-done.1 = bf16[40,512,512]{2,1,0:T(8,128)(2,1)S(1)} copy-done((bf16[40,512,512]{2,1,0:T(8,128)(2,1)S(1)}, bf16[40,512,512]{2,1,0:T(8,128)(2,1)}, u32[]{:S(2)}) %copy-start.1) | copy-done | bytes 20971544
  67.9 0.0 copy-start.15
  67.9 0.0 copy-start.16
  67.9 0.0 copy-start.2
  67.9 4.9 %shard_map.103._ = f32[4096,128]{1,0:T(8,128)S(1)} custom-call(s32[8,5]{1,0:T(8,128)S(1)} %copy-done.13, bf16[2560,128]{1,0:T(8,128)(2,1)S(1)} %collective-permute-done.4.before, bf16[2560,128]{1,0:T(8,128)(2,1)S(1)} %collective-permute-done.5.after, bf16[40,512,512]{2,1,0:T(8,128)(2,1)S(1)} %copy-done.1, ...), custom_call_target="tpu_custom_call", output_to_operand_aliasing={{}: (4, {})} | custom-call | flops 1000000000 | bytes 1000 | tf_op jit(solution)/shard_map/pallas_call | solution.py:311
  72.8 0.0 collective-permute-done.6
  72.8 0.0 collective-permute-done.7
  72.8 0.0 collective-permute-done.8
  72.9 0.0 copy-done.4
  72.9 0.0 copy-done.8
  72.9 0.0 copy-done.10
  72.9 0.0 copy-done.12
  72.9 0.0 copy-done.15
  73.0 1.4 %shard_map.104._ = f32[4096,128]{1,0:T(8,128)S(1)} custom-call(s32[1,4]{1,0:T(1,128)S(1)} %copy-done.16, s32[1]{0:T(128)S(6)} %copy.17.far_count, bf16[512,128]{1,0:T(8,128)(2,1)S(1)} %all_gather.3.plane, bf16[2048,128]{1,0:T(8,128)(2,1)S(1)} %pad_maximum_fusion.planes, bf16[4,64,64]{2,1,0:T(8,128)(2,1)S(1)} %copy-done.12, ...), custom_call_target="tpu_custom_call", output_to_operand_aliasing={{}: (9, {})} | custom-call | flops 1000 | bytes 1000 | tf_op jit(solution)/shard_map/pallas_call | solution.py:316
  74.4 0.0 collective-permute-done.1.before
  74.4 0.0 collective-permute-done.2.after
  74.4 0.7 copy-done.2
  75.1 2.7 %shard_map.105 = (bf16[4096,128]{1,0:T(8,128)(2,1)}, f32[4096,128]{1,0:T(8,128)S(1)}) custom-call(s32[8,5]{1,0:T(8,128)S(1)} %copy-done.13, bf16[1536,128]{1,0:T(8,128)(2,1)S(1)} %collective-permute-done.1.before, bf16[1536,128]{1,0:T(8,128)(2,1)S(1)} %collective-permute-done.2.after, ...), custom_call_target="tpu_custom_call", output_to_operand_aliasing={{1}: (4, {})} | custom-call | flops 1000 | bytes 1000 | tf_op jit(solution)/shard_map/pallas_call | solution.py:319
  (13 shorter events, 0.1 us)
Async XLA Ops:
  0.0 26.3 %copy-start.13 = (s32[8,5]{1,0:T(8,128)S(1)}, s32[8,5]{1,0:T(8,128)}, u32[]{:S(2)}) copy-start(s32[8,5]{1,0:T(8,128)} %ids_ref.5) | copy-start | bytes 484
  2.6 39.1 %collective-permute-start = (bf16[1536,128]{1,0:T(8,128)(2,1)}, bf16[1536,128]{1,0:T(8,128)(2,1)}, u32[]{:S(2)}, u32[]{:S(2)}) collective-permute-start(bf16[1536,128]{1,0:T(8,128)(2,1)} %get-tuple-element.40), channel_id=1, source_target_pairs={{3,7},{7,11},{11,15},{4,0},{8,4},{12,8},{19,23},{23,27},{27,31},{2... | collective-permute-start | bytes 1179656 | tf_op jit(solution)/shard_map/ppermute | solution.py:250
  4.6 48.0 %collective-permute-start.4 = (bf16[2560,128]{1,0:T(8,128)(2,1)}, bf16[2560,128]{1,0:T(8,128)(2,1)S(1)}, u32[]{:S(2)}, u32[]{:S(2)}) collective-permute-start(bf16[2560,128]{1,0:T(8,128)(2,1)} %get-tuple-element.50), channel_id=1, source_target_pairs={{0,1},{1,2},{2,3},{3,4},{4,5},{5,6},{6,7},{7,8},{8,9},{9,10},{10,1... | collective-permute-start | bytes 1966088 | tf_op jit(solution)/shard_map/ppermute | solution.py:250
  8.1 44.5 %collective-permute-start.5 = (bf16[2560,128]{1,0:T(8,128)(2,1)}, bf16[2560,128]{1,0:T(8,128)(2,1)S(1)}, u32[]{:S(2)}, u32[]{:S(2)}) collective-permute-start(bf16[2560,128]{1,0:T(8,128)(2,1)} %get-tuple-element.51), channel_id=1, source_target_pairs={{1,0},{2,1},{3,2},{4,3},{5,4},{6,5},{7,6},{8,7},{9,8},{10,9},{11,1... | collective-permute-start | bytes 1966088 | tf_op jit(solution)/shard_map/ppermute | solution.py:250
  16.4 0.8 copy-start.5
  17.2 0.7 copy-start.6
  17.9 0.7 copy-start.7
  18.6 0.6 copy-start.9
  19.2 0.6 copy-start.11
  19.8 0.6 copy-start.14
  20.4 14.2 %copy-start.3 = (bf16[8,64,512]{2,1,0:T(8,128)(2,1)}, bf16[8,64,512]{2,1,0:T(8,128)(2,1)S(1)}, u32[]{:S(2)}) copy-start(bf16[8,64,512]{2,1,0:T(8,128)(2,1)S(1)} %get-tuple-element.64.basis) | copy-start | bytes 1572868
  34.7 7.0 %copy-start = (bf16[40,512,512]{2,1,0:T(8,128)(2,1)}, bf16[40,512,512]{2,1,0:T(8,128)(2,1)S(1)}, u32[]{:S(2)}) copy-start(bf16[40,512,512]{2,1,0:T(8,128)(2,1)S(1)} %get-tuple-element.47.blocks) | copy-start | bytes 62914564
  42.9 9.7 %collective-permute-start.3 = (bf16[512,128]{1,0:T(8,128)(2,1)S(1)}, bf16[512,128]{1,0:T(8,128)(2,1)S(1)}, u32[]{:S(2)}, u32[]{:S(2)}) collective-permute-start(bf16[512,128]{1,0:T(8,128)(2,1)S(1)} %all_gather.3.plane), channel_id=1, source_target_pairs={{0,2},{1,3},{2,0},{3,1},{4,5},{5,4},{6,7},{7,6},{12,15},{13,14},{1... | collective-permute-start | bytes 393224 | tf_op jit(solution)/shard_map/ppermute | solution.py:250
  45.5 28.9 %collective-permute-start.1 = (bf16[1536,128]{1,0:T(8,128)(2,1)S(1)}, bf16[1536,128]{1,0:T(8,128)(2,1)S(1)}, u32[]{:S(2)}, u32[]{:S(2)}) collective-permute-start(bf16[1536,128]{1,0:T(8,128)(2,1)S(1)} %get-tuple-element.45), channel_id=1, source_target_pairs={{0,1},{1,2},{2,3},{4,5},{5,6},{6,7},{8,9},{9,10},{10,11},{12,13},{... | collective-permute-start | bytes 1179656 | tf_op jit(solution)/shard_map/ppermute | solution.py:250
  48.2 26.2 %collective-permute-start.2 = (bf16[1536,128]{1,0:T(8,128)(2,1)S(1)}, bf16[1536,128]{1,0:T(8,128)(2,1)S(1)}, u32[]{:S(2)}, u32[]{:S(2)}) collective-permute-start(bf16[1536,128]{1,0:T(8,128)(2,1)S(1)} %get-tuple-element.46), channel_id=1, source_target_pairs={{1,0},{2,1},{3,2},{5,4},{6,5},{7,6},{9,8},{10,9},{11,10},{13,12},{... | collective-permute-start | bytes 1179656 | tf_op jit(solution)/shard_map/ppermute | solution.py:250
  52.6 20.2 %collective-permute-start.6 = (bf16[512,128]{1,0:T(8,128)(2,1)S(1)}, bf16[512,128]{1,0:T(8,128)(2,1)S(1)}, u32[]{:S(2)}, u32[]{:S(2)}) collective-permute-start(bf16[512,128]{1,0:T(8,128)(2,1)S(1)} %collective-permute-done.3), channel_id=1, source_target_pairs={{0,4},{4,0},{8,12},{12,8},{1,5},{5,1},{9,13},{13,9},{2,6},{6,2},{1... | collective-permute-start | bytes 393224 | tf_op jit(solution)/shard_map/ppermute | solution.py:253
  58.5 14.3 %collective-permute-start.7 = (bf16[512,128]{1,0:T(8,128)(2,1)S(1)}, bf16[512,128]{1,0:T(8,128)(2,1)S(1)}, u32[]{:S(2)}, u32[]{:S(2)}) collective-permute-start(bf16[512,128]{1,0:T(8,128)(2,1)S(1)} %collective-permute-done.3), channel_id=1, source_target_pairs={{0,8},{4,12},{8,0},{12,4},{1,9},{5,13},{9,1},{13,5},{2,10},{6,14},... | collective-permute-start | bytes 393224 | tf_op jit(solution)/shard_map/ppermute | solution.py:253
  58.5 14.3 %collective-permute-start.8 = (bf16[512,128]{1,0:T(8,128)(2,1)S(1)}, bf16[512,128]{1,0:T(8,128)(2,1)S(1)}, u32[]{:S(2)}, u32[]{:S(2)}) collective-permute-start(bf16[512,128]{1,0:T(8,128)(2,1)S(1)} %collective-permute-done.3), channel_id=1, source_target_pairs={{0,12},{4,8},{8,4},{12,0},{1,13},{5,9},{9,5},{13,1},{2,14},{6,10},... | collective-permute-start | bytes 393224 | tf_op jit(solution)/shard_map/ppermute | solution.py:253
  60.9 7.0 %copy-start.1 = (bf16[40,512,512]{2,1,0:T(8,128)(2,1)S(1)}, bf16[40,512,512]{2,1,0:T(8,128)(2,1)}, u32[]{:S(2)}) copy-start(bf16[40,512,512]{2,1,0:T(8,128)(2,1)} %copy-done) | copy-start | bytes 62914564
  67.9 5.0 %copy-start.4 = (bf16[8,64,512]{2,1,0:T(8,128)(2,1)S(1)}, bf16[8,64,512]{2,1,0:T(8,128)(2,1)}, u32[]{:S(2)}) copy-start(bf16[8,64,512]{2,1,0:T(8,128)(2,1)} %copy-done.3) | copy-start | bytes 1572868
  67.9 5.1 %copy-start.8 = (bf16[512,64]{1,0:T(8,128)(2,1)S(1)}, bf16[512,64]{1,0:T(8,128)(2,1)}, u32[]{:S(2)}) copy-start(bf16[512,64]{1,0:T(8,128)(2,1)} %copy-done.7) | copy-start | bytes 196612
  67.9 5.1 %copy-start.10 = (bf16[4,64,64]{2,1,0:T(8,128)(2,1)S(1)}, bf16[4,64,64]{2,1,0:T(8,128)(2,1)}, u32[]{:S(2)}) copy-start(bf16[4,64,64]{2,1,0:T(8,128)(2,1)} %copy-done.9) | copy-start | bytes 98308
  67.9 5.1 %copy-start.12 = (bf16[4,64,64]{2,1,0:T(8,128)(2,1)S(1)}, bf16[4,64,64]{2,1,0:T(8,128)(2,1)}, u32[]{:S(2)}) copy-start(bf16[4,64,64]{2,1,0:T(8,128)(2,1)} %copy-done.11) | copy-start | bytes 98308
  67.9 5.1 %copy-start.15 = (bf16[64,64]{1,0:T(8,128)(2,1)S(1)}, bf16[64,64]{1,0:T(8,128)(2,1)}, u32[]{:S(2)}) copy-start(bf16[64,64]{1,0:T(8,128)(2,1)} %copy-done.14) | copy-start | bytes 24580
  67.9 5.1 %copy-start.16 = (s32[1,4]{1,0:T(1,128)S(1)}, s32[1,4]{1,0:T(1,128)}, u32[]{:S(2)}) copy-start(s32[1,4]{1,0:T(1,128)} %far_ids.1) | copy-start | bytes 52
  67.9 7.2 %copy-start.2 = (bf16[40,512,512]{2,1,0:T(8,128)(2,1)S(1)}, bf16[40,512,512]{2,1,0:T(8,128)(2,1)}, u32[]{:S(2)}) copy-start(bf16[40,512,512]{2,1,0:T(8,128)(2,1)} %copy-done) | copy-start | bytes 62914564

commit v8 on v7

--- a/solution.py
+++ b/solution.py
@@ -50,22 +50,7 @@
     )
 
 
-def cut_kernel(cuts, x_ref, *refs):
-    pieces, relay, sems = refs[:-2], refs[-2], refs[-1]
-    rows = x_ref.shape[0] // cuts[-1]
-    edge = jnp.where(lax.axis_index("inner") == 0, (cuts[-1] - relay.shape[0] // rows) * rows, 0)
-    sources = [x_ref.at[a * rows : b * rows] for a, b in cuts[:-1]] + [x_ref.at[pl.ds(pl.multiple_of(edge, rows), relay.shape[0])]]
-    copies = [pltpu.make_async_copy(source, piece, sems.at[i]) for i, (source, piece) in enumerate(zip(sources, (*pieces, relay)))]
-    for copy in copies:
-        copy.start()
-    for copy in copies:
-        copy.wait()
-
-
-def up_kernel(
-    cuts, x_ref, basis_ref, leaf_map_ref, mid_map_ref, mid_couple_ref, couple_ref, out_ref, x, basis, leaf_map, mid_map, mid_couple, couple, *refs
-):
-    pieces, (skeleton, sems, piece_sems) = refs[:-3], refs[-3:]
+def up_kernel(x_ref, basis_ref, leaf_map_ref, mid_map_ref, out_ref, x, basis, leaf_map, mid_map, skeleton, sems):
     leaves, rank, rows = basis.shape
     parts = []
     for leaf in range(leaves):
@@ -73,9 +58,7 @@
         parts.append(pltpu.make_async_copy(x_ref.at[here], x.at[here], sems.at[leaf]))
         parts.append(pltpu.make_async_copy(basis_ref.at[leaf], basis.at[leaf], sems.at[leaves + leaf]))
     maps = [pltpu.make_async_copy(leaf_map_ref, leaf_map, sems.at[2 * leaves]), pltpu.make_async_copy(mid_map_ref, mid_map, sems.at[2 * leaves + 1])]
-    moves = [(x_ref.at[a * rows : b * rows], piece) for (a, b), piece in zip(cuts, pieces)] + [(mid_couple_ref, mid_couple), (couple_ref, couple)]
-    copies = [pltpu.make_async_copy(source, target, piece_sems.at[i]) for i, (source, target) in enumerate(moves)]
-    for copy in parts + maps + copies:
+    for copy in parts + maps:
         copy.start()
     for leaf in range(leaves):
         parts[2 * leaf].wait()
@@ -86,13 +69,32 @@
     mid = dot_t(leaf_map[...], skeleton[...]).astype(jnp.bfloat16)
     out_ref[:rank, :] = mid
     out_ref[rank:, :] = dot_t(mid_map[...], mid).astype(jnp.bfloat16)
-    for copy in copies:
-        copy.wait()
-
-
-def down_kernel(leaf_size, inner_size, far_ids, far_count, plane, planes, couple, mid_couple, mid_map, leaf_map, basis, _, out_ref):
+
+
+def pieces_kernel(x_ref, relayed, low, high, sems):
+    inner = lax.axis_index("inner")
+    size = low.shape[0]
+    ends = (inner == lax.axis_size("inner") - 1, inner == 0)
+    for i, (piece, at_end, first) in enumerate(zip((low, high), ends, (0, x_ref.shape[0] - size))):
+
+        @pl.when(at_end)
+        def _():
+            pltpu.make_async_copy(relayed, piece, sems.at[i]).start()
+
+        @pl.when(jnp.logical_not(at_end))
+        def _():
+            pltpu.make_async_copy(x_ref.at[first : first + size], piece, sems.at[i]).start()
+
+    for i, piece in enumerate((low, high)):
+        pltpu.make_async_copy(relayed, piece, sems.at[i]).wait()
+
+
+def down_kernel(leaf_size, inner_size, far_ids, far_count, plane, *refs):
+    found, (couple, mid_couple, mid_map, leaf_map, basis, _, out_ref, planes) = refs[:inner_size], refs[inner_size:]
     rank = mid_map.shape[0]
     size = 2 * rank
+    for step, part in enumerate(found):
+        planes[step * leaf_size * size : (step + 1) * leaf_size * size, :] = part[...]
     group = lax.axis_index("leaf")
     inner = lax.axis_index("inner")
 
@@ -166,11 +168,17 @@
         total[here, :] += term
 
 
-def own_kernel(stop, ids_ref, x_ref, blocks_ref, total, blocks, own_slots, own_places, other_slots, other_places, sems):
+def own_kernel(ids_ref, x_hbm, blocks_ref, *refs):
+    count = (len(refs) - 8) // 2
+    sources, total, blocks, targets = refs[:count], refs[count], refs[count + 1], refs[count + 2 : 2 * count + 2]
+    own_slots, own_places, other_slots, other_places, x_ref, sems = refs[2 * count + 2 :]
     leaves, near = ids_ref.shape
+    slots = leaves * near
+    load = pltpu.make_async_copy(x_hbm, x_ref, sems.at[slots])
+    load.start()
 
     def kind_of(leaf, offset):
-        own = (offset >= 0) & (offset < leaves) & (leaf < stop)
+        own = (offset >= 0) & (offset < leaves)
         return (own, offset), (jnp.logical_not(own), 0)
 
     kinds = ((own_slots, own_places), (other_slots, other_places))
@@ -188,7 +196,11 @@
 
     lax.fori_loop(0, own_count, begin(own_slots), 0)
     lax.fori_loop(0, other_count, begin(other_slots), 0)
+    others = [pltpu.make_async_copy(source, target, sems.at[slots + 1 + i]) for i, (source, target) in enumerate(zip(sources, targets))]
+    for other in others:
+        other.start()
     total[...] = jnp.zeros_like(total)
+    load.wait()
     add_products(near, kinds[0], own_count, blocks, x_ref, total, lambda slot: copy(slot).wait())
 
     def finish(i, carry):
@@ -196,6 +208,8 @@
         return carry
 
     lax.fori_loop(0, other_count, finish, 0)
+    for other in others:
+        other.wait()
 
 
 def wave_kernel(near_by, ids_ref, before, after, blocks, _, total, *lists):
@@ -258,43 +272,29 @@
 
     one = leaves * 5 // 8
     rest = leaves - one
-    sizes = [one, one, rest, rest]
-    cuts = [(rest, leaves), (0, one), (0, rest), (one, leaves)]
-
     def kernel(body, out_shape, in_specs, out_specs, scratch, aliases=None, flops=1000):
         return call(body, out_shape, in_specs, out_specs, scratch, flops, 1000, 8 * MIB, aliases)
 
-    pieces = [resident(size * rows, columns) for size in sizes]
-    ahead, back, relay = kernel(
-        functools.partial(cut_kernel, (*cuts[:2], leaves)), [*pieces[:2], pieces[2]], [ANY], [VMEM] * 3, [pltpu.SemaphoreType.DMA((3,))]
-    )(held(anomalies, pltpu.HBM))
-    relayed = passed(relay, hop)
+    ahead, back = lax.slice_in_dim(anomalies, rest * rows, leaves * rows), lax.slice_in_dim(anomalies, 0, one * rows)
+    edge = jnp.where(inner == first, one * rows, 0)
+    relayed = passed(lax.dynamic_slice_in_dim(anomalies, edge, rest * rows), hop)
     x_up, ahead, back = lax.optimization_barrier((anomalies, ahead, back))
     halo = [(passed(ahead, chain), passed(back, [(j, i) for i, j in chain]))]
 
-    operands = (x_up, leaf_basis, transfer_leaf.reshape(leaves * rank, rank), transfer_mid.reshape(rank, rank), mid_couple[0], top_couple[0])
-    plane, x_own, basis, leaf_map, mid_map, mid_links, group_links, *later = kernel(
-        functools.partial(up_kernel, cuts[2:]),
-        [resident(2 * rank, columns)] + [resident(*x.shape) for x in operands] + pieces[2:],
-        [ANY] * 6,
-        [VMEM] * 9,
-        [pltpu.VMEM((leaves * rank, columns), bf16), pltpu.SemaphoreType.DMA((2 * leaves + 2,)), pltpu.SemaphoreType.DMA((4,))],
+    maps = (transfer_leaf.reshape(leaves * rank, rank), transfer_mid.reshape(rank, rank))
+    operands = (x_up, leaf_basis, *maps)
+    part = kernel(
+        up_kernel,
+        jax.ShapeDtypeStruct((2 * rank, columns), bf16),
+        [ANY] * 4,
+        VMEM,
+        [pltpu.VMEM(x.shape, bf16) for x in operands] + [pltpu.VMEM((leaves * rank, columns), bf16), pltpu.SemaphoreType.DMA((2 * leaves + 2,))],
     )(*[held(x, pltpu.HBM) for x in operands])
-    slots = leaves * near
-    lists = [pltpu.SMEM((slots + 1,), jnp.int32)] * 2
-    wide = resident(leaves * rows, columns, dtype=jnp.float32)
-    total, blocks = kernel(
-        functools.partial(own_kernel, leaves),
-        (wide, resident(slots, rows, rows)),
-        [SMEM, VMEM, ANY],
-        (VMEM, VMEM),
-        lists * 2 + [pltpu.SemaphoreType.DMA((slots,))],
-        flops=1000,
-    )(near_ids, held(x_own, pltpu.VMEM), held(near_blocks.reshape(slots, rows, rows), pltpu.HBM))
-    blocks = held(blocks, pltpu.VMEM)
-    plane = lax.all_gather(plane, "leaf", axis=0, tiled=True)
-    low, high = jnp.where(inner == last, relayed, later[0]), jnp.where(inner == first, relayed, later[1])
-    plane, low, high, total = lax.optimization_barrier((plane, low, high, total))
+    plane = lax.all_gather(part, "leaf", axis=0, tiled=True)
+    plane, x_late, relayed = lax.optimization_barrier((plane, x_up, relayed))
+    piece = jax.ShapeDtypeStruct((rest * rows, columns), bf16)
+    low, high = kernel(pieces_kernel, (piece, piece), [ANY] * 2, (VMEM, VMEM), [pltpu.SemaphoreType.DMA((2,))])(held(x_late, pltpu.HBM), relayed)
+    plane, x_late, low, high = lax.optimization_barrier((plane, x_late, low, high))
     turns = [(place(g, i), place(g, i ^ turn_of(g, inner_size))) for g in groups for i in range(inner_size)]
     planes = passed(plane, [(i, j) for i, j in turns if i != j])
     halo.append(
@@ -304,18 +304,33 @@
         )
     )
 
-    planes, halo[0] = lax.optimization_barrier((planes, halo[0]))
-
+    slots = leaves * near
+    lists = [pltpu.SMEM((slots + 1,), jnp.int32)] * 2
+    wide = resident(leaves * rows, columns, dtype=jnp.float32)
+    later = (top_couple[0], mid_couple[0], maps[1], maps[0], leaf_basis)
+    total, blocks, *later = kernel(
+        own_kernel,
+        [wide, resident(slots, rows, rows)] + [resident(*x.shape) for x in later],
+        [SMEM] + [ANY] * (2 + len(later)),
+        [VMEM] * (2 + len(later)),
+        lists * 2 + [pltpu.VMEM(anomalies.shape, bf16), pltpu.SemaphoreType.DMA((slots + 1 + len(later),))],
+    )(near_ids, *[held(x, pltpu.HBM) for x in (x_late, near_blocks.reshape(slots, rows, rows), *later)])
+    blocks = held(blocks, pltpu.VMEM)
+    planes, halo[0], total = lax.optimization_barrier((planes, halo[0], total))
     others = [swapped(planes, reach) for reach in range(1, inner_size)]
     total, planes = lax.optimization_barrier((total, planes))
-    total = kernel(functools.partial(wave_kernel, one), wide, [SMEM] + [VMEM] * 4, VMEM, lists * 2, aliases={4: 0}, flops=10**9)(
+    total = kernel(functools.partial(wave_kernel, one), wide, [SMEM] + [VMEM] * 4, VMEM, lists * 2, aliases={4: 0}, flops=10**10)(
         near_ids, *halo[0], blocks, held(total, pltpu.VMEM)
     )
     others, total = lax.optimization_barrier((others, total))
-    planes = jnp.concatenate([planes, *others])
     total = kernel(
-        functools.partial(down_kernel, leaf_size, inner_size), wide, [SMEM, SMEM] + [VMEM] * 8, VMEM, [], aliases={9: 0}
-    )(far_ids, far_count, plane, planes, group_links, mid_links, mid_map, leaf_map, basis, held(total, pltpu.VMEM))
+        functools.partial(down_kernel, leaf_size, inner_size),
+        wide,
+        [SMEM, SMEM] + [VMEM] * (7 + inner_size),
+        VMEM,
+        [pltpu.VMEM((inner_size * leaf_size * 2 * rank, columns), bf16)],
+        aliases={8 + inner_size: 0},
+    )(far_ids, far_count, plane, planes, *others, *later, held(total, pltpu.VMEM))
     out, _ = kernel(
         functools.partial(last_kernel, one),
         (jax.ShapeDtypeStruct(anomalies.shape, bf16), wide),

time: 78 us -> 57 us (0.73)
  local copies, waits for them, and re-layouts: 18.7 us -> 2.41 us
  starting transfers between devices: 28.3 us -> 21.7 us
  waiting for transfers between devices: 0.02 us -> 3.15 us
  blocking collectives: 5.88 us -> 7.14 us
  other arithmetic: 1.22 us -> 0 us
  Pallas kernels: 22.7 us -> 21.6 us
    unnamed x34 -> x4, local copies, waits for them, and re-layouts: 18.7 us -> 0.01 us
    ppermute x3, starting transfers between devices: 7.66 us -> 2.21 us  [swapped(): return lax.ppermute(x, 'leaf', [(i, i ^ reach) for i in groups])]
    ppermute x3, waiting for transfers between devices: 0.01 us -> 3.14 us  [swapped(): return lax.ppermute(x, 'leaf', [(i, i ^ reach) for i in groups])]
    pallas_call x1, Pallas kernels: 4.92 us -> 3.15 us  [local(): kernel(functools.partial(wave_kernel, one), wide, [SMEM] + [VMEM] * 4, VM...]
    slice x0 -> x1, local copies, waits for them, and re-layouts: none -> 1.37 us  [local(): lax.slice_in_dim(anomalies, 0, one * rows)]
    all_gather x1, blocking collectives: 5.88 us -> 7.14 us  [local(): plane = lax.all_gather(part, 'leaf', axis=0, tiled=True)]
    ppermute x6, starting transfers between devices: 20.7 us -> 19.5 us  [passed(): return lax.ppermute(x, ('leaf', 'inner'), pairs)]
    select_n x1 -> x0, other arithmetic: 1.18 us -> none  [local(): jnp.where(inner == first, relayed, later[1])]
  transfers between devices with their start and end apart: 9 -> 9, of which waited for: 0 -> 1; matrix products, arithmetic and copies ran while one was open for 2% -> 2% of each run, Pallas kernels for 22% -> 32%
where the time goes in v8:
time: 57 us; the launch traced here: 56.8 us
  starting transfers between devices  21.7 us (38%)
  Pallas kernels  21.6 us (38%)
  blocking collectives  7.14 us (13%)
  waiting for transfers between devices  3.15 us (6%)
  local copies, waits for them, and re-layouts  2.41 us (4%)
  between operations  0.82 us (1%)
    ppermute x6, starting transfers between devices, passed(): return lax.ppermute(x, ('leaf', 'inner'), pairs)  19.5 us
    pallas_call x1, Pallas kernels, local(): kernel(own_kernel, [wide, resident(slots, rows, rows)] + [resident(*x.sha...  9.76 us
    all_gather x1, blocking collectives, local(): plane = lax.all_gather(part, 'leaf', axis=0, tiled=True)  7.14 us
    pallas_call x1, Pallas kernels, local(): kernel(functools.partial(last_kernel, one), (jax.ShapeDtypeStruct(anomali...  3.56 us
    pallas_call x1, Pallas kernels, local(): kernel(functools.partial(wave_kernel, one), wide, [SMEM] + [VMEM] * 4, VM...  3.15 us
    ppermute x3, waiting for transfers between devices, swapped(): return lax.ppermute(x, 'leaf', [(i, i ^ reach) for i in groups])  3.14 us
    pallas_call x1, Pallas kernels, local(): kernel(up_kernel, jax.ShapeDtypeStruct((2 * rank, columns), bf16), [ANY]...  2.69 us
    ppermute x3, starting transfers between devices, swapped(): return lax.ppermute(x, 'leaf', [(i, i ^ reach) for i in groups])  2.21 us
  transfers between devices with their start and end apart: 9, of which 1 were waited for; matrix products, arithmetic and copies ran while one was open for 2% of the time, Pallas kernels for 32%

profile of v8, /device:TPU:1, one launch (start us, length us, event | category | flops | bytes accessed | tf_op | source)
XLA Modules:
  0.0 56.8 jit_solution(14019145860597335809)
XLA Ops:
  0.0 1.4 %fusion = (bf16[2560,128]{1,0:T(8,128)(2,1)S(1)}, bf16[2560,128]{1,0:T(8,128)(2,1)S(1)}) fusion(bf16[4096,128]{1,0:T(8,128)(2,1)} %x_hbm), kind=kLoop, calls=%fused_computation.1 | loop fusion | bytes 2621440 | tf_op jit(solution)/shard_map/slice | solution.py:278
  1.4 0.0 copy-start
  1.4 4.0 %collective-permute-start.4 = (bf16[2560,128]{1,0:T(8,128)(2,1)S(1)}, bf16[2560,128]{1,0:T(8,128)(2,1)S(1)}, u32[]{:S(2)}, u32[]{:S(2)}) collective-permute-start(bf16[2560,128]{1,0:T(8,128)(2,1)S(1)} %get-tuple-element.46), channel_id=1, source_target_pairs={{0,1},{1,2},{2,3},{3,4},{4,5},{5,6},{6,7},{7,8},{8,9},{9,10},{10,1... | collective-permute-start | bytes 1966088 | tf_op jit(solution)/shard_map/ppermute | solution.py:264
  5.4 4.5 %collective-permute-start.5 = (bf16[2560,128]{1,0:T(8,128)(2,1)S(1)}, bf16[2560,128]{1,0:T(8,128)(2,1)S(1)}, u32[]{:S(2)}, u32[]{:S(2)}) collective-permute-start(bf16[2560,128]{1,0:T(8,128)(2,1)S(1)} %get-tuple-element.47), channel_id=1, source_target_pairs={{1,0},{2,1},{3,2},{4,3},{5,4},{6,5},{7,6},{8,7},{9,8},{10,9},{11,1... | collective-permute-start | bytes 1966088 | tf_op jit(solution)/shard_map/ppermute | solution.py:264
  9.9 1.0 %constant_dynamic-slice_fusion = bf16[1536,128]{1,0:T(8,128)(2,1)S(1)} fusion(bf16[4096,128]{1,0:T(8,128)(2,1)} %x_hbm, s32[]{:T(128)S(6)} %select_n.5), kind=kLoop, calls=%fused_computation | loop fusion | bytes 786436 | tf_op jit(solution)/shard_map/dynamic_slice | solution.py:280
  11.0 1.9 %collective-permute-start = (bf16[1536,128]{1,0:T(8,128)(2,1)S(1)}, bf16[1536,128]{1,0:T(8,128)(2,1)S(1)}, u32[]{:S(2)}, u32[]{:S(2)}) collective-permute-start(bf16[1536,128]{1,0:T(8,128)(2,1)S(1)} %constant_dynamic-slice_fusion), channel_id=1, source_target_pairs={{3,7},{7,11},{11,15},{4,0},{8,4},{12,8},{19,23},{23,27},{27,31},{2... | collective-permute-start | bytes 1179656 | tf_op jit(solution)/shard_map/ppermute | solution.py:264
  12.9 2.7 %shard_map.100 = bf16[128,128]{1,0:T(8,128)(2,1)S(1)} custom-call(bf16[4096,128]{1,0:T(8,128)(2,1)} %x_hbm, bf16[8,64,512]{2,1,0:T(8,128)(2,1)} %refs_4_.1, bf16[512,64]{1,0:T(8,128)(2,1)} %bitcast.6, bf16[64,64]{1,0:T(8,128)(2,1)} %bitcast.10), custom_call_target="tpu_custom_call" | custom-call | flops 1000 | bytes 1000 | tf_op jit(solution)/shard_map/pallas_call | solution.py:286
  15.6 7.1 %all_gather.3.plane = bf16[512,128]{1,0:T(8,128)(2,1)S(1)} all-gather(bf16[128,128]{1,0:T(8,128)(2,1)S(1)} %shard_map.100), channel_id=1, replica_groups=mesh['groups'=2,'leaf'=4,'inner'=4] {'leaf'}, dimensions={0}, use_global_device_ids=true | all-gather | bytes 163840 | tf_op jit(solution)/shard_map/all_gather | solution.py:293
  22.7 0.0 collective-permute-done.relayed
  22.7 1.0 %shard_map.101 = (bf16[1536,128]{1,0:T(8,128)(2,1)S(1)}, bf16[1536,128]{1,0:T(8,128)(2,1)S(1)}) custom-call(bf16[4096,128]{1,0:T(8,128)(2,1)} %x_hbm, bf16[1536,128]{1,0:T(8,128)(2,1)S(1)} %collective-permute-done.relayed), custom_call_target="tpu_custom_call" | custom-call | flops 1000 | bytes 1000 | tf_op jit(solution)/shard_map/pallas_call | solution.py:296
  23.8 1.9 %collective-permute-start.3 = (bf16[512,128]{1,0:T(8,128)(2,1)S(1)}, bf16[512,128]{1,0:T(8,128)(2,1)S(1)}, u32[]{:S(2)}, u32[]{:S(2)}) collective-permute-start(bf16[512,128]{1,0:T(8,128)(2,1)S(1)} %all_gather.3.plane), channel_id=1, source_target_pairs={{0,2},{1,3},{2,0},{3,1},{4,5},{5,4},{6,7},{7,6},{12,15},{13,14},{1... | collective-permute-start | bytes 393224 | tf_op jit(solution)/shard_map/ppermute | solution.py:264
  26.3 3.4 %collective-permute-start.1 = (bf16[1536,128]{1,0:T(8,128)(2,1)S(1)}, bf16[1536,128]{1,0:T(8,128)(2,1)S(1)}, u32[]{:S(2)}, u32[]{:S(2)}) collective-permute-start(bf16[1536,128]{1,0:T(8,128)(2,1)S(1)} %get-tuple-element.41), channel_id=1, source_target_pairs={{0,1},{1,2},{2,3},{4,5},{5,6},{6,7},{8,9},{9,10},{10,11},{12,13},{... | collective-permute-start | bytes 1179656 | tf_op jit(solution)/shard_map/ppermute | solution.py:264
  29.7 3.7 %collective-permute-start.2 = (bf16[1536,128]{1,0:T(8,128)(2,1)S(1)}, bf16[1536,128]{1,0:T(8,128)(2,1)S(1)}, u32[]{:S(2)}, u32[]{:S(2)}) collective-permute-start(bf16[1536,128]{1,0:T(8,128)(2,1)S(1)} %get-tuple-element.42), channel_id=1, source_target_pairs={{1,0},{2,1},{3,2},{5,4},{6,5},{7,6},{9,8},{10,9},{11,10},{13,12},{... | collective-permute-start | bytes 1179656 | tf_op jit(solution)/shard_map/ppermute | solution.py:264
  33.4 0.0 copy-done
  33.5 9.8 %shard_map.102 = (f32[4096,128]{1,0:T(8,128)S(1)}, bf16[40,512,512]{2,1,0:T(8,128)(2,1)S(1)}, bf16[4,64,64]{2,1,0:T(8,128)(2,1)S(1)}, bf16[4,64,64]{2,1,0:T(8,12...) custom-call(s32[8,5]{1,0:T(8,128)S(1)} %copy-done, ...), custom_call_target="tpu_custom_call" | custom-call | flops 1000 | bytes 1000 | tf_op jit(solution)/shard_map/pallas_call | solution.py:311
  43.2 0.0 collective-permute-done.3.refs_0_
  43.2 0.0 collective-permute-done.4.before
  43.2 0.0 collective-permute-done.5.after
  43.3 0.4 collective-permute-start.6
  43.6 0.0 collective-permute-start.7
  43.6 1.8 %collective-permute-start.8 = (bf16[512,128]{1,0:T(8,128)(2,1)S(1)}, bf16[512,128]{1,0:T(8,128)(2,1)S(1)}, u32[]{:S(2)}, u32[]{:S(2)}) collective-permute-start(bf16[512,128]{1,0:T(8,128)(2,1)S(1)} %collective-permute-done.3.refs_0_), channel_id=1, source_target_pairs={{0,12},{4,8},{8,4},{12,0},{1,13},{5,9},{9,5},{13,1},{2,14},{6,10},... | collective-permute-start | bytes 393224 | tf_op jit(solution)/shard_map/ppermute | solution.py:267
  45.5 0.0 copy-start.1
  45.5 3.1 %shard_map.103.refs_9_ = f32[4096,128]{1,0:T(8,128)S(1)} custom-call(s32[8,5]{1,0:T(8,128)S(1)} %copy-done, bf16[2560,128]{1,0:T(8,128)(2,1)S(1)} %collective-permute-done.4.before, bf16[2560,128]{1,0:T(8,128)(2,1)S(1)} %collective-permute-done.5.after, bf16[40,512,512]{2,1,0:T(8,128)(2,1)S(1)} %get-tuple-element.44.blocks, ...), custom_call_target="tpu_custom_call", output_to_operand_aliasing={{}: (4, {})} | custom-call | flops 10000000000 | bytes 1000 | tf_op jit(solution)/shard_map/pallas_call | solution.py:322
  48.6 0.0 collective-permute-done.6.refs_1_
  48.6 0.0 collective-permute-done.7.refs_2_
  48.6 3.1 %collective-permute-done.8.refs_3_ = bf16[512,128]{1,0:T(8,128)(2,1)S(1)} collective-permute-done((bf16[512,128]{1,0:T(8,128)(2,1)S(1)}, bf16[512,128]{1,0:T(8,128)(2,1)S(1)}, u32[]{:S(2)}, u32[]{:S(2)}) %collective-permute-start.8) | collective-permute-done | bytes 131104 | tf_op jit(solution)/shard_map/ppermute | solution.py:267
  51.8 0.0 copy-done.1
  51.8 1.4 %shard_map.104._ = f32[4096,128]{1,0:T(8,128)S(1)} custom-call(s32[1,4]{1,0:T(1,128)S(1)} %copy-done.1, s32[1]{0:T(128)S(6)} %copy.17.far_count, bf16[512,128]{1,0:T(8,128)(2,1)S(1)} %all_gather.3.plane, bf16[512,128]{1,0:T(8,128)(2,1)S(1)} %collective-permute-done.3.refs_0_, ...), custom_call_target="tpu_custom_call", output_to_operand_aliasing={{}: (12, {})} | custom-call | flops 1000 | bytes 1000 | tf_op jit(solution)/shard_map/pallas_call | solution.py:326
  53.2 0.0 collective-permute-done.1.before
  53.2 0.0 collective-permute-done.2.after
  53.2 3.6 %shard_map.105 = (bf16[4096,128]{1,0:T(8,128)(2,1)}, f32[4096,128]{1,0:T(8,128)S(1)}) custom-call(s32[8,5]{1,0:T(8,128)S(1)} %copy-done, bf16[1536,128]{1,0:T(8,128)(2,1)S(1)} %collective-permute-done.1.before, bf16[1536,128]{1,0:T(8,128)(2,1)S(1)} %collective-permute-done.2.after, ...), custom_call_target="tpu_custom_call", output_to_operand_aliasing={{1}: (4, {})} | custom-call | flops 1000 | bytes 1000 | tf_op jit(solution)/shard_map/pallas_call | solution.py:334
Async XLA Ops:
  1.4 32.1 %copy-start = (s32[8,5]{1,0:T(8,128)S(1)}, s32[8,5]{1,0:T(8,128)}, u32[]{:S(2)}) copy-start(s32[8,5]{1,0:T(8,128)} %ids_ref.5) | copy-start | bytes 484
  1.4 41.8 %collective-permute-start.4 = (bf16[2560,128]{1,0:T(8,128)(2,1)S(1)}, bf16[2560,128]{1,0:T(8,128)(2,1)S(1)}, u32[]{:S(2)}, u32[]{:S(2)}) collective-permute-start(bf16[2560,128]{1,0:T(8,128)(2,1)S(1)} %get-tuple-element.46), channel_id=1, source_target_pairs={{0,1},{1,2},{2,3},{3,4},{4,5},{5,6},{6,7},{7,8},{8,9},{9,10},{10,1... | collective-permute-start | bytes 1966088 | tf_op jit(solution)/shard_map/ppermute | solution.py:264
  5.4 37.8 %collective-permute-start.5 = (bf16[2560,128]{1,0:T(8,128)(2,1)S(1)}, bf16[2560,128]{1,0:T(8,128)(2,1)S(1)}, u32[]{:S(2)}, u32[]{:S(2)}) collective-permute-start(bf16[2560,128]{1,0:T(8,128)(2,1)S(1)} %get-tuple-element.47), channel_id=1, source_target_pairs={{1,0},{2,1},{3,2},{4,3},{5,4},{6,5},{7,6},{8,7},{9,8},{10,9},{11,1... | collective-permute-start | bytes 1966088 | tf_op jit(solution)/shard_map/ppermute | solution.py:264
  11.0 11.8 %collective-permute-start = (bf16[1536,128]{1,0:T(8,128)(2,1)S(1)}, bf16[1536,128]{1,0:T(8,128)(2,1)S(1)}, u32[]{:S(2)}, u32[]{:S(2)}) collective-permute-start(bf16[1536,128]{1,0:T(8,128)(2,1)S(1)} %constant_dynamic-slice_fusion), channel_id=1, source_target_pairs={{3,7},{7,11},{11,15},{4,0},{8,4},{12,8},{19,23},{23,27},{27,31},{2... | collective-permute-start | bytes 1179656 | tf_op jit(solution)/shard_map/ppermute | solution.py:264
  23.8 19.4 %collective-permute-start.3 = (bf16[512,128]{1,0:T(8,128)(2,1)S(1)}, bf16[512,128]{1,0:T(8,128)(2,1)S(1)}, u32[]{:S(2)}, u32[]{:S(2)}) collective-permute-start(bf16[512,128]{1,0:T(8,128)(2,1)S(1)} %all_gather.3.plane), channel_id=1, source_target_pairs={{0,2},{1,3},{2,0},{3,1},{4,5},{5,4},{6,7},{7,6},{12,15},{13,14},{1... | collective-permute-start | bytes 393224 | tf_op jit(solution)/shard_map/ppermute | solution.py:264
  26.3 26.9 %collective-permute-start.1 = (bf16[1536,128]{1,0:T(8,128)(2,1)S(1)}, bf16[1536,128]{1,0:T(8,128)(2,1)S(1)}, u32[]{:S(2)}, u32[]{:S(2)}) collective-permute-start(bf16[1536,128]{1,0:T(8,128)(2,1)S(1)} %get-tuple-element.41), channel_id=1, source_target_pairs={{0,1},{1,2},{2,3},{4,5},{5,6},{6,7},{8,9},{9,10},{10,11},{12,13},{... | collective-permute-start | bytes 1179656 | tf_op jit(solution)/shard_map/ppermute | solution.py:264
  29.7 23.5 %collective-permute-start.2 = (bf16[1536,128]{1,0:T(8,128)(2,1)S(1)}, bf16[1536,128]{1,0:T(8,128)(2,1)S(1)}, u32[]{:S(2)}, u32[]{:S(2)}) collective-permute-start(bf16[1536,128]{1,0:T(8,128)(2,1)S(1)} %get-tuple-element.42), channel_id=1, source_target_pairs={{1,0},{2,1},{3,2},{5,4},{6,5},{7,6},{9,8},{10,9},{11,10},{13,12},{... | collective-permute-start | bytes 1179656 | tf_op jit(solution)/shard_map/ppermute | solution.py:264
  43.3 5.4 %collective-permute-start.6 = (bf16[512,128]{1,0:T(8,128)(2,1)S(1)}, bf16[512,128]{1,0:T(8,128)(2,1)S(1)}, u32[]{:S(2)}, u32[]{:S(2)}) collective-permute-start(bf16[512,128]{1,0:T(8,128)(2,1)S(1)} %collective-permute-done.3.refs_0_), channel_id=1, source_target_pairs={{0,4},{4,0},{8,12},{12,8},{1,5},{5,1},{9,13},{13,9},{2,6},{6,2},{1... | collective-permute-start | bytes 393224 | tf_op jit(solution)/shard_map/ppermute | solution.py:267
  43.6 5.0 %collective-permute-start.7 = (bf16[512,128]{1,0:T(8,128)(2,1)S(1)}, bf16[512,128]{1,0:T(8,128)(2,1)S(1)}, u32[]{:S(2)}, u32[]{:S(2)}) collective-permute-start(bf16[512,128]{1,0:T(8,128)(2,1)S(1)} %collective-permute-done.3.refs_0_), channel_id=1, source_target_pairs={{0,8},{4,12},{8,0},{12,4},{1,9},{5,13},{9,1},{13,5},{2,10},{6,14},... | collective-permute-start | bytes 393224 | tf_op jit(solution)/shard_map/ppermute | solution.py:267
  43.6 8.1 %collective-permute-start.8 = (bf16[512,128]{1,0:T(8,128)(2,1)S(1)}, bf16[512,128]{1,0:T(8,128)(2,1)S(1)}, u32[]{:S(2)}, u32[]{:S(2)}) collective-permute-start(bf16[512,128]{1,0:T(8,128)(2,1)S(1)} %collective-permute-done.3.refs_0_), channel_id=1, source_target_pairs={{0,12},{4,8},{8,4},{12,0},{1,13},{5,9},{9,5},{13,1},{2,14},{6,10},... | collective-permute-start | bytes 393224 | tf_op jit(solution)/shard_map/ppermute | solution.py:267
  45.5 6.3 %copy-start.1 = (s32[1,4]{1,0:T(1,128)S(1)}, s32[1,4]{1,0:T(1,128)}, u32[]{:S(2)}) copy-start(s32[1,4]{1,0:T(1,128)} %far_ids.1) | copy-start | bytes 52

commit v9 on v8

--- a/solution.py
+++ b/solution.py
@@ -50,7 +50,7 @@
     )
 
 
-def up_kernel(x_ref, basis_ref, leaf_map_ref, mid_map_ref, out_ref, x, basis, leaf_map, mid_map, skeleton, sems):
+def up_kernel(x_ref, basis_ref, leaf_map_ref, mid_map_ref, out_ref, relay, x, basis, leaf_map, mid_map, skeleton, sems):
     leaves, rank, rows = basis.shape
     parts = []
     for leaf in range(leaves):
@@ -58,7 +58,9 @@
         parts.append(pltpu.make_async_copy(x_ref.at[here], x.at[here], sems.at[leaf]))
         parts.append(pltpu.make_async_copy(basis_ref.at[leaf], basis.at[leaf], sems.at[leaves + leaf]))
     maps = [pltpu.make_async_copy(leaf_map_ref, leaf_map, sems.at[2 * leaves]), pltpu.make_async_copy(mid_map_ref, mid_map, sems.at[2 * leaves + 1])]
-    for copy in parts + maps:
+    edge = jnp.where(lax.axis_index("inner") == 0, x.shape[0] - relay.shape[0], 0)
+    handed = pltpu.make_async_copy(x_ref.at[pl.ds(pl.multiple_of(edge, rows), relay.shape[0])], relay, sems.at[2 * leaves + 2])
+    for copy in [*parts, *maps, handed]:
         copy.start()
     for leaf in range(leaves):
         parts[2 * leaf].wait()
@@ -69,9 +71,11 @@
     mid = dot_t(leaf_map[...], skeleton[...]).astype(jnp.bfloat16)
     out_ref[:rank, :] = mid
     out_ref[rank:, :] = dot_t(mid_map[...], mid).astype(jnp.bfloat16)
-
-
-def pieces_kernel(x_ref, relayed, low, high, sems):
+    handed.wait()
+
+
+def pieces_kernel(x_ref, relayed, *refs):
+    parts, (low, high, plane, sems) = refs[:-4], refs[-4:]
     inner = lax.axis_index("inner")
     size = low.shape[0]
     ends = (inner == lax.axis_size("inner") - 1, inner == 0)
@@ -85,6 +89,9 @@
         def _():
             pltpu.make_async_copy(x_ref.at[first : first + size], piece, sems.at[i]).start()
 
+    height = parts[0].shape[0]
+    for i, part in enumerate(parts):
+        plane[i * height : (i + 1) * height, :] = part[...]
     for i, piece in enumerate((low, high)):
         pltpu.make_async_copy(relayed, piece, sems.at[i]).wait()
 
@@ -98,15 +105,15 @@
     group = lax.axis_index("leaf")
     inner = lax.axis_index("inner")
 
-    def at_of(step, leaf, offset=0):
-        return pl.ds(pl.multiple_of((step * leaf_size + leaf) * size + offset, rank), rank)
+    def at_of(step, distance, offset=0):
+        return pl.ds(pl.multiple_of((step * leaf_size + distance) * size + offset, rank), rank)
 
     top_down = jnp.zeros((rank, plane.shape[1]), jnp.float32)
     for distance in range(1, leaf_size):
         other = group ^ distance
-        top = plane[at_of(0, other, rank), :].astype(jnp.float32)
+        top = plane[at_of(0, distance, rank), :].astype(jnp.float32)
         for step in range(inner_size):
-            top += planes[at_of(step, other, rank), :].astype(jnp.float32)
+            top += planes[at_of(step, step ^ distance, rank), :].astype(jnp.float32)
         term = dot(couple[other], top.astype(jnp.bfloat16))
         top_down += jnp.where(jnp.abs(other - group) >= 2, term, 0.0)
     total = dot(mid_map[...], top_down.astype(jnp.bfloat16))
@@ -115,7 +122,7 @@
         partner = jnp.where(live, far_ids[0, slot], group * inner_size)
         other, turn = partner // inner_size, inner ^ lax.rem(partner, inner_size)
         step = (group & (inner_size - 1)) ^ carrier(turn, inner_size)
-        near, far = plane[at_of(0, other), :], planes[at_of(step, other), :]
+        near, far = plane[at_of(0, group ^ other), :], planes[at_of(step, group ^ step ^ other), :]
         term = dot(mid_couple[slot], jnp.where(turn == 0, near, far))
         total += jnp.where(live, term, 0.0)
     leaf_down = dot(leaf_map[...], total.astype(jnp.bfloat16)).astype(jnp.bfloat16)
@@ -270,39 +277,28 @@
     line = [(place(g, i), place(g, i + 1)) for g in groups for i in range(last)]
     hop = [(place(g, last), place(g + 1, last)) for g in groups[:-1]] + [(place(g, first), place(g - 1, first)) for g in groups[1:]]
 
-    one = leaves * 5 // 8
+    one = leaves * 3 // 4
     rest = leaves - one
     def kernel(body, out_shape, in_specs, out_specs, scratch, aliases=None, flops=1000):
         return call(body, out_shape, in_specs, out_specs, scratch, flops, 1000, 8 * MIB, aliases)
 
     ahead, back = lax.slice_in_dim(anomalies, rest * rows, leaves * rows), lax.slice_in_dim(anomalies, 0, one * rows)
-    edge = jnp.where(inner == first, one * rows, 0)
-    relayed = passed(lax.dynamic_slice_in_dim(anomalies, edge, rest * rows), hop)
     x_up, ahead, back = lax.optimization_barrier((anomalies, ahead, back))
     halo = [(passed(ahead, chain), passed(back, [(j, i) for i, j in chain]))]
 
     maps = (transfer_leaf.reshape(leaves * rank, rank), transfer_mid.reshape(rank, rank))
     operands = (x_up, leaf_basis, *maps)
-    part = kernel(
+    piece = jax.ShapeDtypeStruct((rest * rows, columns), bf16)
+    part, relay = kernel(
         up_kernel,
-        jax.ShapeDtypeStruct((2 * rank, columns), bf16),
+        (jax.ShapeDtypeStruct((2 * rank, columns), bf16), piece),
         [ANY] * 4,
-        VMEM,
-        [pltpu.VMEM(x.shape, bf16) for x in operands] + [pltpu.VMEM((leaves * rank, columns), bf16), pltpu.SemaphoreType.DMA((2 * leaves + 2,))],
+        (VMEM, VMEM),
+        [pltpu.VMEM(x.shape, bf16) for x in operands] + [pltpu.VMEM((leaves * rank, columns), bf16), pltpu.SemaphoreType.DMA((2 * leaves + 3,))],
     )(*[held(x, pltpu.HBM) for x in operands])
-    plane = lax.all_gather(part, "leaf", axis=0, tiled=True)
-    plane, x_late, relayed = lax.optimization_barrier((plane, x_up, relayed))
-    piece = jax.ShapeDtypeStruct((rest * rows, columns), bf16)
-    low, high = kernel(pieces_kernel, (piece, piece), [ANY] * 2, (VMEM, VMEM), [pltpu.SemaphoreType.DMA((2,))])(held(x_late, pltpu.HBM), relayed)
-    plane, x_late, low, high = lax.optimization_barrier((plane, x_late, low, high))
-    turns = [(place(g, i), place(g, i ^ turn_of(g, inner_size))) for g in groups for i in range(inner_size)]
-    planes = passed(plane, [(i, j) for i, j in turns if i != j])
-    halo.append(
-        (
-            passed(low, line + [(place(g, last), place(g, first)) for g in groups[1:]]),
-            passed(high, [(j, i) for i, j in line] + [(place(g, first), place(g, last)) for g in groups[:-1]]),
-        )
-    )
+    relayed = passed(relay, hop)
+    parts = [part] + [swapped(part, reach) for reach in groups[1:]]
+    x_late, part = lax.optimization_barrier((x_up, part))
 
     slots = leaves * near
     lists = [pltpu.SMEM((slots + 1,), jnp.int32)] * 2
@@ -314,8 +310,25 @@
         [SMEM] + [ANY] * (2 + len(later)),
         [VMEM] * (2 + len(later)),
         lists * 2 + [pltpu.VMEM(anomalies.shape, bf16), pltpu.SemaphoreType.DMA((slots + 1 + len(later),))],
+        flops=1000,
     )(near_ids, *[held(x, pltpu.HBM) for x in (x_late, near_blocks.reshape(slots, rows, rows), *later)])
     blocks = held(blocks, pltpu.VMEM)
+    parts, x_late, relayed, total = lax.optimization_barrier((parts, x_late, relayed, total))
+    low, high, plane = kernel(
+        pieces_kernel,
+        (piece, piece, jax.ShapeDtypeStruct((leaf_size * 2 * rank, columns), bf16)),
+        [ANY] * 2 + [VMEM] * leaf_size,
+        [VMEM] * 3,
+        [pltpu.SemaphoreType.DMA((2,))],
+    )(held(x_late, pltpu.HBM), relayed, *parts)
+    turns = [(place(g, i), place(g, i ^ turn_of(g, inner_size))) for g in groups for i in range(inner_size)]
+    planes = passed(plane, [(i, j) for i, j in turns if i != j])
+    halo.append(
+        (
+            passed(low, line + [(place(g, last), place(g, first)) for g in groups[1:]]),
+            passed(high, [(j, i) for i, j in line] + [(place(g, first), place(g, last)) for g in groups[:-1]]),
+        )
+    )
     planes, halo[0], total = lax.optimization_barrier((planes, halo[0], total))
     others = [swapped(planes, reach) for reach in range(1, inner_size)]
     total, planes = lax.optimization_barrier((total, planes))

time: 57 us -> 60.4 us (1.060)
  blocking collectives: 7.14 us -> 0 us
  waiting for transfers between devices: 3.15 us -> 9.84 us
  starting transfers between devices: 21.7 us -> 26.2 us
  local copies, waits for them, and re-layouts: 2.41 us -> 1.49 us
    ppermute x6, waiting for transfers between devices: 0.02 us -> 9.68 us  [passed(): return lax.ppermute(x, ('leaf', 'inner'), pairs)]
    all_gather x1 -> x0, blocking collectives: 7.14 us -> none  [local(): plane = lax.all_gather(part, 'leaf', axis=0, tiled=True)]
    ppermute x3 -> x6, starting transfers between devices: 2.21 us -> 6.69 us  [swapped(): return lax.ppermute(x, 'leaf', [(i, i ^ reach) for i in groups])]
    ppermute x3 -> x6, waiting for transfers between devices: 3.14 us -> 0.16 us  [swapped(): return lax.ppermute(x, 'leaf', [(i, i ^ reach) for i in groups])]
    pallas_call x1, Pallas kernels: 3.15 us -> 5.06 us  [local(): kernel(functools.partial(wave_kernel, one), wide, [SMEM] + [VMEM] * 4, VM...]
    pallas_call x1, Pallas kernels: 3.56 us -> 2.53 us  [local(): kernel(functools.partial(last_kernel, one), (jax.ShapeDtypeStruct(anomali...]
    dynamic_slice x1 -> x0, local copies, waits for them, and re-layouts: 1.03 us -> none  [local(): lax.dynamic_slice_in_dim(anomalies, edge, rest * rows)]
    pallas_call x1, Pallas kernels: 9.76 us -> 8.85 us  [local(): kernel(own_kernel, [wide, resident(slots, rows, rows)] + [resident(*x.sha...]
  transfers between devices with their start and end apart: 9 -> 12, of which waited for: 1 -> 2; matrix products, arithmetic and copies ran while one was open for 2% -> 0% of each run, Pallas kernels for 32% -> 32%
where the time goes in v9:
time: 60.4 us; the launch traced here: 59.8 us
  starting transfers between devices  26.2 us (43%)
  Pallas kernels  21.5 us (36%)
  waiting for transfers between devices  9.84 us (16%)
  local copies, waits for them, and re-layouts  1.49 us (2%)
  between operations  0.8 us (1%)
    ppermute x6, starting transfers between devices, passed(): return lax.ppermute(x, ('leaf', 'inner'), pairs)  19.5 us
    ppermute x6, waiting for transfers between devices, passed(): return lax.ppermute(x, ('leaf', 'inner'), pairs)  9.68 us
    pallas_call x1, Pallas kernels, local(): kernel(own_kernel, [wide, resident(slots, rows, rows)] + [resident(*x.sha...  8.85 us
    ppermute x6, starting transfers between devices, swapped(): return lax.ppermute(x, 'leaf', [(i, i ^ reach) for i in groups])  6.69 us
    pallas_call x1, Pallas kernels, local(): kernel(functools.partial(wave_kernel, one), wide, [SMEM] + [VMEM] * 4, VM...  5.06 us
    pallas_call x1, Pallas kernels, local(): kernel(up_kernel, (jax.ShapeDtypeStruct((2 * rank, columns), bf16), piece...  2.7 us
    pallas_call x1, Pallas kernels, local(): kernel(functools.partial(last_kernel, one), (jax.ShapeDtypeStruct(anomali...  2.53 us
    slice x1, local copies, waits for them, and re-layouts, local(): lax.slice_in_dim(anomalies, 0, one * rows)  1.49 us
  transfers between devices with their start and end apart: 12, of which 2 were waited for; matrix products, arithmetic and copies ran while one was open for 0% of the time, Pallas kernels for 32%

profile of v9, /device:TPU:1, one launch (start us, length us, event | category | flops | bytes accessed | tf_op | source)
XLA Modules:
  0.0 59.8 jit_solution(12540958282315842108)
XLA Ops:
  0.0 0.0 copy-start
  0.0 1.5 %fusion = (bf16[3072,128]{1,0:T(8,128)(2,1)S(1)}, bf16[3072,128]{1,0:T(8,128)(2,1)S(1)}) fusion(bf16[4096,128]{1,0:T(8,128)(2,1)} %x_ref.1), kind=kLoop, calls=%fused_computation | loop fusion | bytes 3145728 | tf_op jit(solution)/shard_map/slice | solution.py:285
  1.5 4.0 %collective-permute-start.7 = (bf16[3072,128]{1,0:T(8,128)(2,1)S(1)}, bf16[3072,128]{1,0:T(8,128)(2,1)S(1)}, u32[]{:S(2)}, u32[]{:S(2)}) collective-permute-start(bf16[3072,128]{1,0:T(8,128)(2,1)S(1)} %get-tuple-element.54), channel_id=1, source_target_pairs={{0,1},{1,2},{2,3},{3,4},{4,5},{5,6},{6,7},{7,8},{8,9},{9,10},{10,1... | collective-permute-start | bytes 2359304 | tf_op jit(solution)/shard_map/ppermute | solution.py:271
  5.5 4.5 %collective-permute-start.8 = (bf16[3072,128]{1,0:T(8,128)(2,1)S(1)}, bf16[3072,128]{1,0:T(8,128)(2,1)S(1)}, u32[]{:S(2)}, u32[]{:S(2)}) collective-permute-start(bf16[3072,128]{1,0:T(8,128)(2,1)S(1)} %get-tuple-element.55), channel_id=1, source_target_pairs={{1,0},{2,1},{3,2},{4,3},{5,4},{6,5},{7,6},{8,7},{9,8},{10,9},{11,1... | collective-permute-start | bytes 2359304 | tf_op jit(solution)/shard_map/ppermute | solution.py:271
  10.0 2.7 %shard_map.100 = (bf16[128,128]{1,0:T(8,128)(2,1)S(1)}, bf16[1024,128]{1,0:T(8,128)(2,1)S(1)}) custom-call(bf16[4096,128]{1,0:T(8,128)(2,1)} %x_ref.1, bf16[8,64,512]{2,1,0:T(8,128)(2,1)} %refs_4_.1, bf16[512,64]{1,0:T(8,128)(2,1)} %bitcast.6, bf16[64,64]{1,0:T(8,128)(2,1)} %bitcast.10), custom_call_target="tpu_custom_call" | custom-call | flops 1000 | bytes 1000 | tf_op jit(solution)/shard_map/pallas_call | solution.py:292
  12.8 1.9 %collective-permute-start.3 = (bf16[1024,128]{1,0:T(8,128)(2,1)S(1)}, bf16[1024,128]{1,0:T(8,128)(2,1)S(1)}, u32[]{:S(2)}, u32[]{:S(2)}) collective-permute-start(bf16[1024,128]{1,0:T(8,128)(2,1)S(1)} %get-tuple-element.42), channel_id=1, source_target_pairs={{3,7},{7,11},{11,15},{4,0},{8,4},{12,8},{19,23},{23,27},{27,31},{2... | collective-permute-start | bytes 786440 | tf_op jit(solution)/shard_map/ppermute | solution.py:271
  14.7 0.1 collective-permute-start
  14.8 2.5 %collective-permute-start.1 = (bf16[128,128]{1,0:T(8,128)(2,1)S(1)}, bf16[128,128]{1,0:T(8,128)(2,1)S(1)}, u32[]{:S(2)}, u32[]{:S(2)}) collective-permute-start(bf16[128,128]{1,0:T(8,128)(2,1)S(1)} %get-tuple-element.46.refs_0_), channel_id=1, source_target_pairs={{0,8},{4,12},{8,0},{12,4},{1,9},{5,13},{9,1},{13,5},{2,10},{6,14},... | collective-permute-start | bytes 98312 | tf_op jit(solution)/shard_map/ppermute | solution.py:274
  17.3 0.0 collective-permute-done.refs_1_
  17.3 1.3 %collective-permute-start.2 = (bf16[128,128]{1,0:T(8,128)(2,1)S(1)}, bf16[128,128]{1,0:T(8,128)(2,1)S(1)}, u32[]{:S(2)}, u32[]{:S(2)}) collective-permute-start(bf16[128,128]{1,0:T(8,128)(2,1)S(1)} %get-tuple-element.46.refs_0_), channel_id=1, source_target_pairs={{0,12},{4,8},{8,4},{12,0},{1,13},{5,9},{9,5},{13,1},{2,14},{6,10},... | collective-permute-start | bytes 98312 | tf_op jit(solution)/shard_map/ppermute | solution.py:274
  18.6 0.0 copy-done
  18.6 8.9 %shard_map.101 = (f32[4096,128]{1,0:T(8,128)S(1)}, bf16[40,512,512]{2,1,0:T(8,128)(2,1)S(1)}, bf16[4,64,64]{2,1,0:T(8,128)(2,1)S(1)}, bf16[4,64,64]{2,1,0:T(8,12...) custom-call(s32[8,5]{1,0:T(8,128)S(1)} %copy-done, ...), custom_call_target="tpu_custom_call" | custom-call | flops 1000 | bytes 1000 | tf_op jit(solution)/shard_map/pallas_call | solution.py:307
  27.4 0.0 collective-permute-done.1.refs_2_
  27.5 0.0 collective-permute-done.2.refs_3_
  27.5 0.0 collective-permute-done.3.relayed
  27.5 1.0 %shard_map.102 = (bf16[1024,128]{1,0:T(8,128)(2,1)S(1)}, bf16[1024,128]{1,0:T(8,128)(2,1)S(1)}, bf16[512,128]{1,0:T(8,128)(2,1)S(1)}) custom-call(bf16[4096,128]{1,0:T(8,128)(2,1)} %x_ref.1, bf16[1024,128]{1,0:T(8,128)(2,1)S(1)} %collective-permute-done.3.relayed, bf16[128,128]{1,0:T(8,128)(2,1)S(1)} %get-tuple-element.46.refs_0_, ...), custom_call_target="tpu_custom_call" | custom-call | flops 1000 | bytes 1000 | tf_op jit(solution)/shard_map/pallas_call | solution.py:317
  28.5 1.9 %collective-permute-start.6 = (bf16[512,128]{1,0:T(8,128)(2,1)S(1)}, bf16[512,128]{1,0:T(8,128)(2,1)S(1)}, u32[]{:S(2)}, u32[]{:S(2)}) collective-permute-start(bf16[512,128]{1,0:T(8,128)(2,1)S(1)} %get-tuple-element.53.plane), channel_id=1, source_target_pairs={{0,2},{1,3},{2,0},{3,1},{4,5},{5,4},{6,7},{7,6},{12,15},{13,14},{1... | collective-permute-start | bytes 393224 | tf_op jit(solution)/shard_map/ppermute | solution.py:271
  31.0 3.4 %collective-permute-start.4 = (bf16[1024,128]{1,0:T(8,128)(2,1)S(1)}, bf16[1024,128]{1,0:T(8,128)(2,1)S(1)}, u32[]{:S(2)}, u32[]{:S(2)}) collective-permute-start(bf16[1024,128]{1,0:T(8,128)(2,1)S(1)} %get-tuple-element.50), channel_id=1, source_target_pairs={{0,1},{1,2},{2,3},{4,5},{5,6},{6,7},{8,9},{9,10},{10,11},{12,13},{... | collective-permute-start | bytes 786440 | tf_op jit(solution)/shard_map/ppermute | solution.py:271
  34.4 3.7 %collective-permute-start.5 = (bf16[1024,128]{1,0:T(8,128)(2,1)S(1)}, bf16[1024,128]{1,0:T(8,128)(2,1)S(1)}, u32[]{:S(2)}, u32[]{:S(2)}) collective-permute-start(bf16[1024,128]{1,0:T(8,128)(2,1)S(1)} %get-tuple-element.51), channel_id=1, source_target_pairs={{1,0},{2,1},{3,2},{5,4},{6,5},{7,6},{9,8},{10,9},{11,10},{13,12},{... | collective-permute-start | bytes 786440 | tf_op jit(solution)/shard_map/ppermute | solution.py:271
  38.1 9.7 %collective-permute-done.6.refs_0_ = bf16[512,128]{1,0:T(8,128)(2,1)S(1)} collective-permute-done((bf16[512,128]{1,0:T(8,128)(2,1)S(1)}, bf16[512,128]{1,0:T(8,128)(2,1)S(1)}, u32[]{:S(2)}, u32[]{:S(2)}) %collective-permute-start.6) | collective-permute-done | bytes 131104 | tf_op jit(solution)/shard_map/ppermute | solution.py:271
  47.8 0.0 collective-permute-done.7.before
  47.8 0.0 collective-permute-done.8.after
  47.8 0.0 collective-permute-start.10
  47.8 2.8 %collective-permute-start.11 = (bf16[512,128]{1,0:T(8,128)(2,1)S(1)}, bf16[512,128]{1,0:T(8,128)(2,1)S(1)}, u32[]{:S(2)}, u32[]{:S(2)}) collective-permute-start(bf16[512,128]{1,0:T(8,128)(2,1)S(1)} %collective-permute-done.6.refs_0_), channel_id=1, source_target_pairs={{0,12},{4,8},{8,4},{12,0},{1,13},{5,9},{9,5},{13,1},{2,14},{6,10},... | collective-permute-start | bytes 393224 | tf_op jit(solution)/shard_map/ppermute | solution.py:274
  50.6 0.0 collective-permute-start.9
  50.6 0.0 copy-start.1
  50.6 5.1 %shard_map.103.refs_9_ = f32[4096,128]{1,0:T(8,128)S(1)} custom-call(s32[8,5]{1,0:T(8,128)S(1)} %copy-done, bf16[3072,128]{1,0:T(8,128)(2,1)S(1)} %collective-permute-done.7.before, bf16[3072,128]{1,0:T(8,128)(2,1)S(1)} %collective-permute-done.8.after, bf16[40,512,512]{2,1,0:T(8,128)(2,1)S(1)} %get-tuple-element.52.blocks, ...), custom_call_target="tpu_custom_call", output_to_operand_aliasing={{}: (4, {})} | custom-call | flops 10000000000 | bytes 1000 | tf_op jit(solution)/shard_map/pallas_call | solution.py:335
  55.7 0.0 collective-permute-done.10.refs_2_
  55.7 0.1 collective-permute-done.11.refs_3_
  55.8 0.0 collective-permute-done.9.refs_1_
  55.8 0.0 copy-done.1
  55.8 1.4 %shard_map.104._ = f32[4096,128]{1,0:T(8,128)S(1)} custom-call(s32[1,4]{1,0:T(1,128)S(1)} %copy-done.1, s32[1]{0:T(128)S(6)} %copy.17.far_count, bf16[512,128]{1,0:T(8,128)(2,1)S(1)} %get-tuple-element.53.plane, bf16[512,128]{1,0:T(8,128)(2,1)S(1)} %collective-permute-done.6.refs_0_, ...), custom_call_target="tpu_custom_call", output_to_operand_aliasing={{}: (12, {})} | custom-call | flops 1000 | bytes 1000 | tf_op jit(solution)/shard_map/pallas_call | solution.py:339
  57.3 0.0 collective-permute-done.4.before
  57.3 0.0 collective-permute-done.5.after
  57.3 2.5 %shard_map.105 = (bf16[4096,128]{1,0:T(8,128)(2,1)}, f32[4096,128]{1,0:T(8,128)S(1)}) custom-call(s32[8,5]{1,0:T(8,128)S(1)} %copy-done, bf16[1024,128]{1,0:T(8,128)(2,1)S(1)} %collective-permute-done.4.before, bf16[1024,128]{1,0:T(8,128)(2,1)S(1)} %collective-permute-done.5.after, ...), custom_call_target="tpu_custom_call", output_to_operand_aliasing={{1}: (4, {})} | custom-call | flops 1000 | bytes 1000 | tf_op jit(solution)/shard_map/pallas_call | solution.py:347
Async XLA Ops:
  0.0 18.6 %copy-start = (s32[8,5]{1,0:T(8,128)S(1)}, s32[8,5]{1,0:T(8,128)}, u32[]{:S(2)}) copy-start(s32[8,5]{1,0:T(8,128)} %ids_ref.5) | copy-start | bytes 484
  1.5 46.3 %collective-permute-start.7 = (bf16[3072,128]{1,0:T(8,128)(2,1)S(1)}, bf16[3072,128]{1,0:T(8,128)(2,1)S(1)}, u32[]{:S(2)}, u32[]{:S(2)}) collective-permute-start(bf16[3072,128]{1,0:T(8,128)(2,1)S(1)} %get-tuple-element.54), channel_id=1, source_target_pairs={{0,1},{1,2},{2,3},{3,4},{4,5},{5,6},{6,7},{7,8},{8,9},{9,10},{10,1... | collective-permute-start | bytes 2359304 | tf_op jit(solution)/shard_map/ppermute | solution.py:271
  5.5 42.3 %collective-permute-start.8 = (bf16[3072,128]{1,0:T(8,128)(2,1)S(1)}, bf16[3072,128]{1,0:T(8,128)(2,1)S(1)}, u32[]{:S(2)}, u32[]{:S(2)}) collective-permute-start(bf16[3072,128]{1,0:T(8,128)(2,1)S(1)} %get-tuple-element.55), channel_id=1, source_target_pairs={{1,0},{2,1},{3,2},{4,3},{5,4},{6,5},{7,6},{8,7},{9,8},{10,9},{11,1... | collective-permute-start | bytes 2359304 | tf_op jit(solution)/shard_map/ppermute | solution.py:271
  12.8 14.7 %collective-permute-start.3 = (bf16[1024,128]{1,0:T(8,128)(2,1)S(1)}, bf16[1024,128]{1,0:T(8,128)(2,1)S(1)}, u32[]{:S(2)}, u32[]{:S(2)}) collective-permute-start(bf16[1024,128]{1,0:T(8,128)(2,1)S(1)} %get-tuple-element.42), channel_id=1, source_target_pairs={{3,7},{7,11},{11,15},{4,0},{8,4},{12,8},{19,23},{23,27},{27,31},{2... | collective-permute-start | bytes 786440 | tf_op jit(solution)/shard_map/ppermute | solution.py:271
  14.7 2.6 %collective-permute-start = (bf16[128,128]{1,0:T(8,128)(2,1)S(1)}, bf16[128,128]{1,0:T(8,128)(2,1)S(1)}, u32[]{:S(2)}, u32[]{:S(2)}) collective-permute-start(bf16[128,128]{1,0:T(8,128)(2,1)S(1)} %get-tuple-element.46.refs_0_), channel_id=1, source_target_pairs={{0,4},{4,0},{8,12},{12,8},{1,5},{5,1},{9,13},{13,9},{2,6},{6,2},{1... | collective-permute-start | bytes 98312 | tf_op jit(solution)/shard_map/ppermute | solution.py:274
  14.8 12.7 %collective-permute-start.1 = (bf16[128,128]{1,0:T(8,128)(2,1)S(1)}, bf16[128,128]{1,0:T(8,128)(2,1)S(1)}, u32[]{:S(2)}, u32[]{:S(2)}) collective-permute-start(bf16[128,128]{1,0:T(8,128)(2,1)S(1)} %get-tuple-element.46.refs_0_), channel_id=1, source_target_pairs={{0,8},{4,12},{8,0},{12,4},{1,9},{5,13},{9,1},{13,5},{2,10},{6,14},... | collective-permute-start | bytes 98312 | tf_op jit(solution)/shard_map/ppermute | solution.py:274
  17.3 10.2 %collective-permute-start.2 = (bf16[128,128]{1,0:T(8,128)(2,1)S(1)}, bf16[128,128]{1,0:T(8,128)(2,1)S(1)}, u32[]{:S(2)}, u32[]{:S(2)}) collective-permute-start(bf16[128,128]{1,0:T(8,128)(2,1)S(1)} %get-tuple-element.46.refs_0_), channel_id=1, source_target_pairs={{0,12},{4,8},{8,4},{12,0},{1,13},{5,9},{9,5},{13,1},{2,14},{6,10},... | collective-permute-start | bytes 98312 | tf_op jit(solution)/shard_map/ppermute | solution.py:274
  28.5 19.3 %collective-permute-start.6 = (bf16[512,128]{1,0:T(8,128)(2,1)S(1)}, bf16[512,128]{1,0:T(8,128)(2,1)S(1)}, u32[]{:S(2)}, u32[]{:S(2)}) collective-permute-start(bf16[512,128]{1,0:T(8,128)(2,1)S(1)} %get-tuple-element.53.plane), channel_id=1, source_target_pairs={{0,2},{1,3},{2,0},{3,1},{4,5},{5,4},{6,7},{7,6},{12,15},{13,14},{1... | collective-permute-start | bytes 393224 | tf_op jit(solution)/shard_map/ppermute | solution.py:271
  31.0 26.2 %collective-permute-start.4 = (bf16[1024,128]{1,0:T(8,128)(2,1)S(1)}, bf16[1024,128]{1,0:T(8,128)(2,1)S(1)}, u32[]{:S(2)}, u32[]{:S(2)}) collective-permute-start(bf16[1024,128]{1,0:T(8,128)(2,1)S(1)} %get-tuple-element.50), channel_id=1, source_target_pairs={{0,1},{1,2},{2,3},{4,5},{5,6},{6,7},{8,9},{9,10},{10,11},{12,13},{... | collective-permute-start | bytes 786440 | tf_op jit(solution)/shard_map/ppermute | solution.py:271
  34.4 22.9 %collective-permute-start.5 = (bf16[1024,128]{1,0:T(8,128)(2,1)S(1)}, bf16[1024,128]{1,0:T(8,128)(2,1)S(1)}, u32[]{:S(2)}, u32[]{:S(2)}) collective-permute-start(bf16[1024,128]{1,0:T(8,128)(2,1)S(1)} %get-tuple-element.51), channel_id=1, source_target_pairs={{1,0},{2,1},{3,2},{5,4},{6,5},{7,6},{9,8},{10,9},{11,10},{13,12},{... | collective-permute-start | bytes 786440 | tf_op jit(solution)/shard_map/ppermute | solution.py:271
  47.8 7.9 %collective-permute-start.10 = (bf16[512,128]{1,0:T(8,128)(2,1)S(1)}, bf16[512,128]{1,0:T(8,128)(2,1)S(1)}, u32[]{:S(2)}, u32[]{:S(2)}) collective-permute-start(bf16[512,128]{1,0:T(8,128)(2,1)S(1)} %collective-permute-done.6.refs_0_), channel_id=1, source_target_pairs={{0,8},{4,12},{8,0},{12,4},{1,9},{5,13},{9,1},{13,5},{2,10},{6,14},... | collective-permute-start | bytes 393224 | tf_op jit(solution)/shard_map/ppermute | solution.py:274
  47.8 8.0 %collective-permute-start.11 = (bf16[512,128]{1,0:T(8,128)(2,1)S(1)}, bf16[512,128]{1,0:T(8,128)(2,1)S(1)}, u32[]{:S(2)}, u32[]{:S(2)}) collective-permute-start(bf16[512,128]{1,0:T(8,128)(2,1)S(1)} %collective-permute-done.6.refs_0_), channel_id=1, source_target_pairs={{0,12},{4,8},{8,4},{12,0},{1,13},{5,9},{9,5},{13,1},{2,14},{6,10},... | collective-permute-start | bytes 393224 | tf_op jit(solution)/shard_map/ppermute | solution.py:274
  50.6 5.2 %collective-permute-start.9 = (bf16[512,128]{1,0:T(8,128)(2,1)S(1)}, bf16[512,128]{1,0:T(8,128)(2,1)S(1)}, u32[]{:S(2)}, u32[]{:S(2)}) collective-permute-start(bf16[512,128]{1,0:T(8,128)(2,1)S(1)} %collective-permute-done.6.refs_0_), channel_id=1, source_target_pairs={{0,4},{4,0},{8,12},{12,8},{1,5},{5,1},{9,13},{13,9},{2,6},{6,2},{1... | collective-permute-start | bytes 393224 | tf_op jit(solution)/shard_map/ppermute | solution.py:274
  50.6 5.2 %copy-start.1 = (s32[1,4]{1,0:T(1,128)S(1)}, s32[1,4]{1,0:T(1,128)}, u32[]{:S(2)}) copy-start(s32[1,4]{1,0:T(1,128)} %far_ids.1) | copy-start | bytes 52

commit v10 on v9

--- a/solution.py
+++ b/solution.py
@@ -277,7 +277,7 @@
     line = [(place(g, i), place(g, i + 1)) for g in groups for i in range(last)]
     hop = [(place(g, last), place(g + 1, last)) for g in groups[:-1]] + [(place(g, first), place(g - 1, first)) for g in groups[1:]]
 
-    one = leaves * 3 // 4
+    one = leaves * 5 // 8
     rest = leaves - one
     def kernel(body, out_shape, in_specs, out_specs, scratch, aliases=None, flops=1000):
         return call(body, out_shape, in_specs, out_specs, scratch, flops, 1000, 8 * MIB, aliases)
@@ -298,9 +298,24 @@
     )(*[held(x, pltpu.HBM) for x in operands])
     relayed = passed(relay, hop)
     parts = [part] + [swapped(part, reach) for reach in groups[1:]]
-    x_late, part = lax.optimization_barrier((x_up, part))
-
     slots = leaves * near
+    parts, x_late, relayed = lax.optimization_barrier((parts, x_up, relayed))
+    low, high, plane = kernel(
+        pieces_kernel,
+        (piece, piece, jax.ShapeDtypeStruct((leaf_size * 2 * rank, columns), bf16)),
+        [ANY] * 2 + [VMEM] * leaf_size,
+        [VMEM] * 3,
+        [pltpu.SemaphoreType.DMA((2,))],
+    )(held(x_late, pltpu.HBM), relayed, *parts)
+    low, high, plane, x_late = lax.optimization_barrier((low, high, plane, x_late))
+    turns = [(place(g, i), place(g, i ^ turn_of(g, inner_size))) for g in groups for i in range(inner_size)]
+    planes = passed(plane, [(i, j) for i, j in turns if i != j])
+    halo.append(
+        (
+            passed(low, line + [(place(g, last), place(g, first)) for g in groups[1:]]),
+            passed(high, [(j, i) for i, j in line] + [(place(g, first), place(g, last)) for g in groups[:-1]]),
+        )
+    )
     lists = [pltpu.SMEM((slots + 1,), jnp.int32)] * 2
     wide = resident(leaves * rows, columns, dtype=jnp.float32)
     later = (top_couple[0], mid_couple[0], maps[1], maps[0], leaf_basis)
@@ -313,22 +328,6 @@
         flops=1000,
     )(near_ids, *[held(x, pltpu.HBM) for x in (x_late, near_blocks.reshape(slots, rows, rows), *later)])
     blocks = held(blocks, pltpu.VMEM)
-    parts, x_late, relayed, total = lax.optimization_barrier((parts, x_late, relayed, total))
-    low, high, plane = kernel(
-        pieces_kernel,
-        (piece, piece, jax.ShapeDtypeStruct((leaf_size * 2 * rank, columns), bf16)),
-        [ANY] * 2 + [VMEM] * leaf_size,
-        [VMEM] * 3,
-        [pltpu.SemaphoreType.DMA((2,))],
-    )(held(x_late, pltpu.HBM), relayed, *parts)
-    turns = [(place(g, i), place(g, i ^ turn_of(g, inner_size))) for g in groups for i in range(inner_size)]
-    planes = passed(plane, [(i, j) for i, j in turns if i != j])
-    halo.append(
-        (
-            passed(low, line + [(place(g, last), place(g, first)) for g in groups[1:]]),
-            passed(high, [(j, i) for i, j in line] + [(place(g, first), place(g, last)) for g in groups[:-1]]),
-        )
-    )
     planes, halo[0], total = lax.optimization_barrier((planes, halo[0], total))
     others = [swapped(planes, reach) for reach in range(1, inner_size)]
     total, planes = lax.optimization_barrier((total, planes))

time: 60.4 us -> 57 us (0.944)
  the two profiles are of different devices: /device:TPU:1 before, /device:TPU:0 now
where the time goes in v10:
time: 57 us; the launch traced here: 56.5 us
  starting transfers between devices  23.5 us (41%)
  Pallas kernels  21.9 us (38%)
  waiting for transfers between devices  8.95 us (16%)
  local copies, waits for them, and re-layouts  1.38 us (2%)
  between operations  0.79 us (1%)
    ppermute x6, starting transfers between devices, passed(): return lax.ppermute(x, ('leaf', 'inner'), pairs)  12.9 us
    pallas_call x1, Pallas kernels, local(): kernel(own_kernel, [wide, resident(slots, rows, rows)] + [resident(*x.sha...  10.7 us
    ppermute x6, starting transfers between devices, swapped(): return lax.ppermute(x, 'leaf', [(i, i ^ reach) for i in groups])  10.6 us
    ppermute x6, waiting for transfers between devices, swapped(): return lax.ppermute(x, 'leaf', [(i, i ^ reach) for i in groups])  7.5 us
    pallas_call x1, Pallas kernels, local(): kernel(functools.partial(wave_kernel, one), wide, [SMEM] + [VMEM] * 4, VM...  3.44 us
    pallas_call x1, Pallas kernels, local(): kernel(up_kernel, (jax.ShapeDtypeStruct((2 * rank, columns), bf16), piece...  2.7 us
    pallas_call x1, Pallas kernels, local(): kernel(functools.partial(last_kernel, one), (jax.ShapeDtypeStruct(anomali...  2.69 us
    ppermute x6, waiting for transfers between devices, passed(): return lax.ppermute(x, ('leaf', 'inner'), pairs)  1.44 us
  transfers between devices with their start and end apart: 12, of which 3 were waited for; matrix products, arithmetic and copies ran while one was open for 0% of the time, Pallas kernels for 34%

profile of v10, /device:TPU:0, one launch (start us, length us, event | category | flops | bytes accessed | tf_op | source)
XLA Modules:
  0.0 56.5 jit_solution(14486992216905223327)
XLA Ops:
  0.0 1.4 %fusion = (bf16[2560,128]{1,0:T(8,128)(2,1)S(1)}, bf16[2560,128]{1,0:T(8,128)(2,1)S(1)}) fusion(bf16[4096,128]{1,0:T(8,128)(2,1)} %x_hbm), kind=kLoop, calls=%fused_computation | loop fusion | bytes 2621440 | tf_op jit(solution)/shard_map/slice | solution.py:285
  1.4 0.0 copy-start
  1.4 5.0 %collective-permute-start.7 = (bf16[2560,128]{1,0:T(8,128)(2,1)S(1)}, bf16[2560,128]{1,0:T(8,128)(2,1)S(1)}, u32[]{:S(2)}, u32[]{:S(2)}) collective-permute-start(bf16[2560,128]{1,0:T(8,128)(2,1)S(1)} %get-tuple-element.58), channel_id=1, source_target_pairs={{0,1},{1,2},{2,3},{3,4},{4,5},{5,6},{6,7},{7,8},{8,9},{9,10},{10,1... | collective-permute-start | bytes 1966088 | tf_op jit(solution)/shard_map/ppermute | solution.py:271
  6.4 1.3 %collective-permute-start.8 = (bf16[2560,128]{1,0:T(8,128)(2,1)S(1)}, bf16[2560,128]{1,0:T(8,128)(2,1)S(1)}, u32[]{:S(2)}, u32[]{:S(2)}) collective-permute-start(bf16[2560,128]{1,0:T(8,128)(2,1)S(1)} %get-tuple-element.59), channel_id=1, source_target_pairs={{1,0},{2,1},{3,2},{4,3},{5,4},{6,5},{7,6},{8,7},{9,8},{10,9},{11,1... | collective-permute-start | bytes 1966088 | tf_op jit(solution)/shard_map/ppermute | solution.py:271
  7.7 2.7 %shard_map.100 = (bf16[128,128]{1,0:T(8,128)(2,1)S(1)}, bf16[1536,128]{1,0:T(8,128)(2,1)S(1)}) custom-call(bf16[4096,128]{1,0:T(8,128)(2,1)} %x_hbm, bf16[8,64,512]{2,1,0:T(8,128)(2,1)} %refs_4_.1, bf16[512,64]{1,0:T(8,128)(2,1)} %bitcast.6, bf16[64,64]{1,0:T(8,128)(2,1)} %bitcast.10), custom_call_target="tpu_custom_call" | custom-call | flops 1000 | bytes 1000 | tf_op jit(solution)/shard_map/pallas_call | solution.py:292
  10.4 1.3 %collective-permute-start.3 = (bf16[1536,128]{1,0:T(8,128)(2,1)S(1)}, bf16[1536,128]{1,0:T(8,128)(2,1)S(1)}, u32[]{:S(2)}, u32[]{:S(2)}) collective-permute-start(bf16[1536,128]{1,0:T(8,128)(2,1)S(1)} %get-tuple-element.43), channel_id=1, source_target_pairs={{3,7},{7,11},{11,15},{4,0},{8,4},{12,8},{19,23},{23,27},{27,31},{2... | collective-permute-start | bytes 1179656 | tf_op jit(solution)/shard_map/ppermute | solution.py:271
  11.7 3.4 %collective-permute-start = (bf16[128,128]{1,0:T(8,128)(2,1)S(1)}, bf16[128,128]{1,0:T(8,128)(2,1)S(1)}, u32[]{:S(2)}, u32[]{:S(2)}) collective-permute-start(bf16[128,128]{1,0:T(8,128)(2,1)S(1)} %get-tuple-element.46.refs_0_), channel_id=1, source_target_pairs={{0,4},{4,0},{8,12},{12,8},{1,5},{5,1},{9,13},{13,9},{2,6},{6,2},{1... | collective-permute-start | bytes 98312 | tf_op jit(solution)/shard_map/ppermute | solution.py:274
  15.1 2.7 %collective-permute-start.1 = (bf16[128,128]{1,0:T(8,128)(2,1)S(1)}, bf16[128,128]{1,0:T(8,128)(2,1)S(1)}, u32[]{:S(2)}, u32[]{:S(2)}) collective-permute-start(bf16[128,128]{1,0:T(8,128)(2,1)S(1)} %get-tuple-element.46.refs_0_), channel_id=1, source_target_pairs={{0,8},{4,12},{8,0},{12,4},{1,9},{5,13},{9,1},{13,5},{2,10},{6,14},... | collective-permute-start | bytes 98312 | tf_op jit(solution)/shard_map/ppermute | solution.py:274
  17.8 0.0 collective-permute-done.refs_1_
  17.8 0.9 %collective-permute-start.2 = (bf16[128,128]{1,0:T(8,128)(2,1)S(1)}, bf16[128,128]{1,0:T(8,128)(2,1)S(1)}, u32[]{:S(2)}, u32[]{:S(2)}) collective-permute-start(bf16[128,128]{1,0:T(8,128)(2,1)S(1)} %get-tuple-element.46.refs_0_), channel_id=1, source_target_pairs={{0,12},{4,8},{8,4},{12,0},{1,13},{5,9},{9,5},{13,1},{2,14},{6,10},... | collective-permute-start | bytes 98312 | tf_op jit(solution)/shard_map/ppermute | solution.py:274
  18.7 5.3 %collective-permute-done.1.refs_2_ = bf16[128,128]{1,0:T(8,128)(2,1)S(1)} collective-permute-done((bf16[128,128]{1,0:T(8,128)(2,1)S(1)}, bf16[128,128]{1,0:T(8,128)(2,1)S(1)}, u32[]{:S(2)}, u32[]{:S(2)}) %collective-permute-start.1) | collective-permute-done | bytes 32800 | tf_op jit(solution)/shard_map/ppermute | solution.py:274
  24.0 0.0 collective-permute-done.2.refs_3_
  24.0 0.0 collective-permute-done.3.relayed
  24.0 1.0 %shard_map.101 = (bf16[1536,128]{1,0:T(8,128)(2,1)S(1)}, bf16[1536,128]{1,0:T(8,128)(2,1)S(1)}, bf16[512,128]{1,0:T(8,128)(2,1)S(1)}) custom-call(bf16[4096,128]{1,0:T(8,128)(2,1)} %x_hbm, bf16[1536,128]{1,0:T(8,128)(2,1)S(1)} %collective-permute-done.3.relayed, bf16[128,128]{1,0:T(8,128)(2,1)S(1)} %get-tuple-element.46.refs_0_, ...), custom_call_target="tpu_custom_call" | custom-call | flops 1000 | bytes 1000 | tf_op jit(solution)/shard_map/pallas_call | solution.py:303
  25.1 1.9 %collective-permute-start.6 = (bf16[512,128]{1,0:T(8,128)(2,1)S(1)}, bf16[512,128]{1,0:T(8,128)(2,1)S(1)}, u32[]{:S(2)}, u32[]{:S(2)}) collective-permute-start(bf16[512,128]{1,0:T(8,128)(2,1)S(1)} %get-tuple-element.57.plane), channel_id=1, source_target_pairs={{0,2},{1,3},{2,0},{3,1},{4,5},{5,4},{6,7},{7,6},{12,15},{13,14},{1... | collective-permute-start | bytes 393224 | tf_op jit(solution)/shard_map/ppermute | solution.py:271
  27.6 1.5 %collective-permute-start.4 = (bf16[1536,128]{1,0:T(8,128)(2,1)S(1)}, bf16[1536,128]{1,0:T(8,128)(2,1)S(1)}, u32[]{:S(2)}, u32[]{:S(2)}) collective-permute-start(bf16[1536,128]{1,0:T(8,128)(2,1)S(1)} %get-tuple-element.53), channel_id=1, source_target_pairs={{0,1},{1,2},{2,3},{4,5},{5,6},{6,7},{8,9},{9,10},{10,11},{12,13},{... | collective-permute-start | bytes 1179656 | tf_op jit(solution)/shard_map/ppermute | solution.py:271
  29.2 1.9 %collective-permute-start.5 = (bf16[1536,128]{1,0:T(8,128)(2,1)S(1)}, bf16[1536,128]{1,0:T(8,128)(2,1)S(1)}, u32[]{:S(2)}, u32[]{:S(2)}) collective-permute-start(bf16[1536,128]{1,0:T(8,128)(2,1)S(1)} %get-tuple-element.54), channel_id=1, source_target_pairs={{1,0},{2,1},{3,2},{5,4},{6,5},{7,6},{9,8},{10,9},{11,10},{13,12},{... | collective-permute-start | bytes 1179656 | tf_op jit(solution)/shard_map/ppermute | solution.py:271
  31.1 0.0 copy-done
  31.1 10.7 %shard_map.102 = (f32[4096,128]{1,0:T(8,128)S(1)}, bf16[40,512,512]{2,1,0:T(8,128)(2,1)S(1)}, bf16[4,64,64]{2,1,0:T(8,128)(2,1)S(1)}, bf16[4,64,64]{2,1,0:T(8,12...) custom-call(s32[8,5]{1,0:T(8,128)S(1)} %copy-done, ...), custom_call_target="tpu_custom_call" | custom-call | flops 1000 | bytes 1000 | tf_op jit(solution)/shard_map/pallas_call | solution.py:322
  41.8 1.4 %collective-permute-done.6.refs_0_ = bf16[512,128]{1,0:T(8,128)(2,1)S(1)} collective-permute-done((bf16[512,128]{1,0:T(8,128)(2,1)S(1)}, bf16[512,128]{1,0:T(8,128)(2,1)S(1)}, u32[]{:S(2)}, u32[]{:S(2)}) %collective-permute-start.6) | collective-permute-done | bytes 131104 | tf_op jit(solution)/shard_map/ppermute | solution.py:271
  43.2 0.0 collective-permute-done.7.before
  43.2 0.0 collective-permute-done.8.after
  43.2 0.0 collective-permute-start.10
  43.2 3.5 %collective-permute-start.11 = (bf16[512,128]{1,0:T(8,128)(2,1)S(1)}, bf16[512,128]{1,0:T(8,128)(2,1)S(1)}, u32[]{:S(2)}, u32[]{:S(2)}) collective-permute-start(bf16[512,128]{1,0:T(8,128)(2,1)S(1)} %collective-permute-done.6.refs_0_), channel_id=1, source_target_pairs={{0,12},{4,8},{8,4},{12,0},{1,13},{5,9},{9,5},{13,1},{2,14},{6,10},... | collective-permute-start | bytes 393224 | tf_op jit(solution)/shard_map/ppermute | solution.py:274
  46.7 0.0 collective-permute-start.9
  46.7 0.0 copy-start.1
  46.7 3.4 %shard_map.103.refs_9_ = f32[4096,128]{1,0:T(8,128)S(1)} custom-call(s32[8,5]{1,0:T(8,128)S(1)} %copy-done, bf16[2560,128]{1,0:T(8,128)(2,1)S(1)} %collective-permute-done.7.before, bf16[2560,128]{1,0:T(8,128)(2,1)S(1)} %collective-permute-done.8.after, bf16[40,512,512]{2,1,0:T(8,128)(2,1)S(1)} %get-tuple-element.56.blocks, ...), custom_call_target="tpu_custom_call", output_to_operand_aliasing={{}: (4, {})} | custom-call | flops 10000000000 | bytes 1000 | tf_op jit(solution)/shard_map/pallas_call | solution.py:334
  50.2 0.0 collective-permute-done.10.refs_2_
  50.2 2.2 %collective-permute-done.11.refs_3_ = bf16[512,128]{1,0:T(8,128)(2,1)S(1)} collective-permute-done((bf16[512,128]{1,0:T(8,128)(2,1)S(1)}, bf16[512,128]{1,0:T(8,128)(2,1)S(1)}, u32[]{:S(2)}, u32[]{:S(2)}) %collective-permute-start.11) | collective-permute-done | bytes 131104 | tf_op jit(solution)/shard_map/ppermute | solution.py:274
  52.4 0.0 collective-permute-done.9.refs_1_
  52.4 0.0 copy-done.1
  52.4 1.4 %shard_map.104._ = f32[4096,128]{1,0:T(8,128)S(1)} custom-call(s32[1,4]{1,0:T(1,128)S(1)} %copy-done.1, s32[1]{0:T(128)S(6)} %copy.17.far_count, bf16[512,128]{1,0:T(8,128)(2,1)S(1)} %get-tuple-element.57.plane, bf16[512,128]{1,0:T(8,128)(2,1)S(1)} %collective-permute-done.6.refs_0_, ...), custom_call_target="tpu_custom_call", output_to_operand_aliasing={{}: (12, {})} | custom-call | flops 1000 | bytes 1000 | tf_op jit(solution)/shard_map/pallas_call | solution.py:338
  53.8 0.0 collective-permute-done.4.before
  53.8 0.0 collective-permute-done.5.after
  53.8 2.7 %shard_map.105 = (bf16[4096,128]{1,0:T(8,128)(2,1)}, f32[4096,128]{1,0:T(8,128)S(1)}) custom-call(s32[8,5]{1,0:T(8,128)S(1)} %copy-done, bf16[1536,128]{1,0:T(8,128)(2,1)S(1)} %collective-permute-done.4.before, bf16[1536,128]{1,0:T(8,128)(2,1)S(1)} %collective-permute-done.5.after, ...), custom_call_target="tpu_custom_call", output_to_operand_aliasing={{1}: (4, {})} | custom-call | flops 1000 | bytes 1000 | tf_op jit(solution)/shard_map/pallas_call | solution.py:346
Async XLA Ops:
  1.4 29.7 %copy-start = (s32[8,5]{1,0:T(8,128)S(1)}, s32[8,5]{1,0:T(8,128)}, u32[]{:S(2)}) copy-start(s32[8,5]{1,0:T(8,128)} %ids_ref.5) | copy-start | bytes 484
  1.4 41.8 %collective-permute-start.7 = (bf16[2560,128]{1,0:T(8,128)(2,1)S(1)}, bf16[2560,128]{1,0:T(8,128)(2,1)S(1)}, u32[]{:S(2)}, u32[]{:S(2)}) collective-permute-start(bf16[2560,128]{1,0:T(8,128)(2,1)S(1)} %get-tuple-element.58), channel_id=1, source_target_pairs={{0,1},{1,2},{2,3},{3,4},{4,5},{5,6},{6,7},{7,8},{8,9},{9,10},{10,1... | collective-permute-start | bytes 1966088 | tf_op jit(solution)/shard_map/ppermute | solution.py:271
  6.4 36.8 %collective-permute-start.8 = (bf16[2560,128]{1,0:T(8,128)(2,1)S(1)}, bf16[2560,128]{1,0:T(8,128)(2,1)S(1)}, u32[]{:S(2)}, u32[]{:S(2)}) collective-permute-start(bf16[2560,128]{1,0:T(8,128)(2,1)S(1)} %get-tuple-element.59), channel_id=1, source_target_pairs={{1,0},{2,1},{3,2},{4,3},{5,4},{6,5},{7,6},{8,7},{9,8},{10,9},{11,1... | collective-permute-start | bytes 1966088 | tf_op jit(solution)/shard_map/ppermute | solution.py:271
  10.4 13.7 %collective-permute-start.3 = (bf16[1536,128]{1,0:T(8,128)(2,1)S(1)}, bf16[1536,128]{1,0:T(8,128)(2,1)S(1)}, u32[]{:S(2)}, u32[]{:S(2)}) collective-permute-start(bf16[1536,128]{1,0:T(8,128)(2,1)S(1)} %get-tuple-element.43), channel_id=1, source_target_pairs={{3,7},{7,11},{11,15},{4,0},{8,4},{12,8},{19,23},{23,27},{27,31},{2... | collective-permute-start | bytes 1179656 | tf_op jit(solution)/shard_map/ppermute | solution.py:271
  11.7 6.2 %collective-permute-start = (bf16[128,128]{1,0:T(8,128)(2,1)S(1)}, bf16[128,128]{1,0:T(8,128)(2,1)S(1)}, u32[]{:S(2)}, u32[]{:S(2)}) collective-permute-start(bf16[128,128]{1,0:T(8,128)(2,1)S(1)} %get-tuple-element.46.refs_0_), channel_id=1, source_target_pairs={{0,4},{4,0},{8,12},{12,8},{1,5},{5,1},{9,13},{13,9},{2,6},{6,2},{1... | collective-permute-start | bytes 98312 | tf_op jit(solution)/shard_map/ppermute | solution.py:274
  15.1 8.9 %collective-permute-start.1 = (bf16[128,128]{1,0:T(8,128)(2,1)S(1)}, bf16[128,128]{1,0:T(8,128)(2,1)S(1)}, u32[]{:S(2)}, u32[]{:S(2)}) collective-permute-start(bf16[128,128]{1,0:T(8,128)(2,1)S(1)} %get-tuple-element.46.refs_0_), channel_id=1, source_target_pairs={{0,8},{4,12},{8,0},{12,4},{1,9},{5,13},{9,1},{13,5},{2,10},{6,14},... | collective-permute-start | bytes 98312 | tf_op jit(solution)/shard_map/ppermute | solution.py:274
  17.8 6.2 %collective-permute-start.2 = (bf16[128,128]{1,0:T(8,128)(2,1)S(1)}, bf16[128,128]{1,0:T(8,128)(2,1)S(1)}, u32[]{:S(2)}, u32[]{:S(2)}) collective-permute-start(bf16[128,128]{1,0:T(8,128)(2,1)S(1)} %get-tuple-element.46.refs_0_), channel_id=1, source_target_pairs={{0,12},{4,8},{8,4},{12,0},{1,13},{5,9},{9,5},{13,1},{2,14},{6,10},... | collective-permute-start | bytes 98312 | tf_op jit(solution)/shard_map/ppermute | solution.py:274
  25.1 18.1 %collective-permute-start.6 = (bf16[512,128]{1,0:T(8,128)(2,1)S(1)}, bf16[512,128]{1,0:T(8,128)(2,1)S(1)}, u32[]{:S(2)}, u32[]{:S(2)}) collective-permute-start(bf16[512,128]{1,0:T(8,128)(2,1)S(1)} %get-tuple-element.57.plane), channel_id=1, source_target_pairs={{0,2},{1,3},{2,0},{3,1},{4,5},{5,4},{6,7},{7,6},{12,15},{13,14},{1... | collective-permute-start | bytes 393224 | tf_op jit(solution)/shard_map/ppermute | solution.py:271
  27.6 26.2 %collective-permute-start.4 = (bf16[1536,128]{1,0:T(8,128)(2,1)S(1)}, bf16[1536,128]{1,0:T(8,128)(2,1)S(1)}, u32[]{:S(2)}, u32[]{:S(2)}) collective-permute-start(bf16[1536,128]{1,0:T(8,128)(2,1)S(1)} %get-tuple-element.53), channel_id=1, source_target_pairs={{0,1},{1,2},{2,3},{4,5},{5,6},{6,7},{8,9},{9,10},{10,11},{12,13},{... | collective-permute-start | bytes 1179656 | tf_op jit(solution)/shard_map/ppermute | solution.py:271
  29.2 24.7 %collective-permute-start.5 = (bf16[1536,128]{1,0:T(8,128)(2,1)S(1)}, bf16[1536,128]{1,0:T(8,128)(2,1)S(1)}, u32[]{:S(2)}, u32[]{:S(2)}) collective-permute-start(bf16[1536,128]{1,0:T(8,128)(2,1)S(1)} %get-tuple-element.54), channel_id=1, source_target_pairs={{1,0},{2,1},{3,2},{5,4},{6,5},{7,6},{9,8},{10,9},{11,10},{13,12},{... | collective-permute-start | bytes 1179656 | tf_op jit(solution)/shard_map/ppermute | solution.py:271
  43.2 7.0 %collective-permute-start.10 = (bf16[512,128]{1,0:T(8,128)(2,1)S(1)}, bf16[512,128]{1,0:T(8,128)(2,1)S(1)}, u32[]{:S(2)}, u32[]{:S(2)}) collective-permute-start(bf16[512,128]{1,0:T(8,128)(2,1)S(1)} %collective-permute-done.6.refs_0_), channel_id=1, source_target_pairs={{0,8},{4,12},{8,0},{12,4},{1,9},{5,13},{9,1},{13,5},{2,10},{6,14},... | collective-permute-start | bytes 393224 | tf_op jit(solution)/shard_map/ppermute | solution.py:274
  43.2 9.2 %collective-permute-start.11 = (bf16[512,128]{1,0:T(8,128)(2,1)S(1)}, bf16[512,128]{1,0:T(8,128)(2,1)S(1)}, u32[]{:S(2)}, u32[]{:S(2)}) collective-permute-start(bf16[512,128]{1,0:T(8,128)(2,1)S(1)} %collective-permute-done.6.refs_0_), channel_id=1, source_target_pairs={{0,12},{4,8},{8,4},{12,0},{1,13},{5,9},{9,5},{13,1},{2,14},{6,10},... | collective-permute-start | bytes 393224 | tf_op jit(solution)/shard_map/ppermute | solution.py:274
  46.7 5.7 %collective-permute-start.9 = (bf16[512,128]{1,0:T(8,128)(2,1)S(1)}, bf16[512,128]{1,0:T(8,128)(2,1)S(1)}, u32[]{:S(2)}, u32[]{:S(2)}) collective-permute-start(bf16[512,128]{1,0:T(8,128)(2,1)S(1)} %collective-permute-done.6.refs_0_), channel_id=1, source_target_pairs={{0,4},{4,0},{8,12},{12,8},{1,5},{5,1},{9,13},{13,9},{2,6},{6,2},{1... | collective-permute-start | bytes 393224 | tf_op jit(solution)/shard_map/ppermute | solution.py:274
  46.7 5.7 %copy-start.1 = (s32[1,4]{1,0:T(1,128)S(1)}, s32[1,4]{1,0:T(1,128)}, u32[]{:S(2)}) copy-start(s32[1,4]{1,0:T(1,128)} %far_ids.1) | copy-start | bytes 52

commit v11 on v10

--- a/solution.py
+++ b/solution.py
@@ -74,8 +74,14 @@
     handed.wait()
 
 
-def pieces_kernel(x_ref, relayed, *refs):
-    parts, (low, high, plane, sems) = refs[:-4], refs[-4:]
+def join_kernel(*refs):
+    parts, plane = refs[:-1], refs[-1]
+    height = parts[0].shape[0]
+    for i, part in enumerate(parts):
+        plane[i * height : (i + 1) * height, :] = part[...]
+
+
+def pieces_kernel(x_ref, relayed, low, high, sems):
     inner = lax.axis_index("inner")
     size = low.shape[0]
     ends = (inner == lax.axis_size("inner") - 1, inner == 0)
@@ -89,9 +95,6 @@
         def _():
             pltpu.make_async_copy(x_ref.at[first : first + size], piece, sems.at[i]).start()
 
-    height = parts[0].shape[0]
-    for i, part in enumerate(parts):
-        plane[i * height : (i + 1) * height, :] = part[...]
     for i, piece in enumerate((low, high)):
         pltpu.make_async_copy(relayed, piece, sems.at[i]).wait()
 
@@ -152,27 +155,32 @@
 def add_products(near, kind, count, blocks, x_ref, total, arrived=lambda slot: None):
     slots, places = kind
     rows = blocks.shape[1]
+    half = rows // 2
 
     def product(i):
         slot = slots[i]
         arrived(slot)
         at = pl.ds(pl.multiple_of(places[i] * rows, rows), rows)
-        here = pl.ds(pl.multiple_of(slot // near * rows, rows), rows)
-        return here, dot(blocks[slot], x_ref[at, :])
+        here = slot // near * rows
+        partner = x_ref[at, :]
+        return here, [dot(blocks[slot, :half, :], partner), dot(blocks[slot, half:, :], partner)]
+
+    def add(start, terms):
+        for i, term in enumerate(terms):
+            total[pl.ds(pl.multiple_of(start + i * half, half), half), :] += term
 
     def pair(j, carry):
         one, first = product(2 * j)
         two, second = product(2 * j + 1)
-        total[one, :] += first
-        total[two, :] += second
+        add(one, first)
+        add(two, second)
         return carry
 
     lax.fori_loop(0, count // 2, pair, 0)
 
     @pl.when(lax.rem(count, 2) == 1)
     def _():
-        here, term = product(count - 1)
-        total[here, :] += term
+        add(*product(count - 1))
 
 
 def own_kernel(ids_ref, x_hbm, blocks_ref, *refs):
@@ -296,20 +304,16 @@
         (VMEM, VMEM),
         [pltpu.VMEM(x.shape, bf16) for x in operands] + [pltpu.VMEM((leaves * rank, columns), bf16), pltpu.SemaphoreType.DMA((2 * leaves + 3,))],
     )(*[held(x, pltpu.HBM) for x in operands])
+    parts = [part] + [swapped(part, reach) for reach in groups[1:]]
+    relay, parts = lax.optimization_barrier((relay, parts))
     relayed = passed(relay, hop)
-    parts = [part] + [swapped(part, reach) for reach in groups[1:]]
     slots = leaves * near
-    parts, x_late, relayed = lax.optimization_barrier((parts, x_up, relayed))
-    low, high, plane = kernel(
-        pieces_kernel,
-        (piece, piece, jax.ShapeDtypeStruct((leaf_size * 2 * rank, columns), bf16)),
-        [ANY] * 2 + [VMEM] * leaf_size,
-        [VMEM] * 3,
-        [pltpu.SemaphoreType.DMA((2,))],
-    )(held(x_late, pltpu.HBM), relayed, *parts)
-    low, high, plane, x_late = lax.optimization_barrier((low, high, plane, x_late))
+    plane = kernel(join_kernel, jax.ShapeDtypeStruct((leaf_size * 2 * rank, columns), bf16), [VMEM] * leaf_size, VMEM, [])(*parts)
+    plane, x_late = lax.optimization_barrier((plane, x_up))
     turns = [(place(g, i), place(g, i ^ turn_of(g, inner_size))) for g in groups for i in range(inner_size)]
     planes = passed(plane, [(i, j) for i, j in turns if i != j])
+    low, high = kernel(pieces_kernel, (piece, piece), [ANY] * 2, (VMEM, VMEM), [pltpu.SemaphoreType.DMA((2,))])(held(x_late, pltpu.HBM), relayed)
+    low, high, x_late = lax.optimization_barrier((low, high, x_late))
     halo.append(
         (
             passed(low, line + [(place(g, last), place(g, first)) for g in groups[1:]]),

time: 57 us -> 58 us (1.018)
  starting transfers between devices: 23.5 us -> 26.8 us
  waiting for transfers between devices: 8.95 us -> 7.7 us
  Pallas kernels: 21.9 us -> 21.2 us
    ppermute x6, starting transfers between devices: 12.9 us -> 16.3 us  [passed(): return lax.ppermute(x, ('leaf', 'inner'), pairs)]
    ppermute x6, waiting for transfers between devices: 7.5 us -> 4.55 us  [swapped(): return lax.ppermute(x, 'leaf', [(i, i ^ reach) for i in groups])]
    ppermute x6, waiting for transfers between devices: 1.44 us -> 3.15 us  [passed(): return lax.ppermute(x, ('leaf', 'inner'), pairs)]
    pallas_call x1, Pallas kernels: 10.7 us -> 9.46 us  [local(): kernel(own_kernel, [wide, resident(slots, rows, rows)] + [resident(*x.sha...]
    pallas_call x1, Pallas kernels: 3.44 us -> 4.21 us  [local(): kernel(functools.partial(wave_kernel, one), wide, [SMEM] + [VMEM] * 4, VM...]
  transfers between devices with their start and end apart: 12 -> 12, of which waited for: 3 -> 4; matrix products, arithmetic and copies ran while one was open for 0% -> 0% of each run, Pallas kernels for 34% -> 33%
where the time goes in v11:
time: 58 us; the launch traced here: 57.9 us
  starting transfers between devices  26.8 us (46%)
  Pallas kernels  21.2 us (37%)
  waiting for transfers between devices  7.7 us (13%)
  local copies, waits for them, and re-layouts  1.38 us (2%)
  between operations  0.8 us (1%)
    ppermute x6, starting transfers between devices, passed(): return lax.ppermute(x, ('leaf', 'inner'), pairs)  16.3 us
    ppermute x6, starting transfers between devices, swapped(): return lax.ppermute(x, 'leaf', [(i, i ^ reach) for i in groups])  10.6 us
    pallas_call x1, Pallas kernels, local(): kernel(own_kernel, [wide, resident(slots, rows, rows)] + [resident(*x.sha...  9.46 us
    ppermute x6, waiting for transfers between devices, swapped(): return lax.ppermute(x, 'leaf', [(i, i ^ reach) for i in groups])  4.55 us
    pallas_call x1, Pallas kernels, local(): kernel(functools.partial(wave_kernel, one), wide, [SMEM] + [VMEM] * 4, VM...  4.21 us
    ppermute x6, waiting for transfers between devices, passed(): return lax.ppermute(x, ('leaf', 'inner'), pairs)  3.15 us
    pallas_call x1, Pallas kernels, local(): kernel(up_kernel, (jax.ShapeDtypeStruct((2 * rank, columns), bf16), piece...  2.7 us
    pallas_call x1, Pallas kernels, local(): kernel(functools.partial(last_kernel, one), (jax.ShapeDtypeStruct(anomali...  2.37 us
  transfers between devices with their start and end apart: 12, of which 4 were waited for; matrix products, arithmetic and copies ran while one was open for 0% of the time, Pallas kernels for 33%

profile of v11, /device:TPU:0, one launch (start us, length us, event | category | flops | bytes accessed | tf_op | source)
XLA Modules:
  0.0 57.9 jit_solution(2066333112655025523)
XLA Ops:
  0.0 1.4 %fusion = (bf16[2560,128]{1,0:T(8,128)(2,1)S(1)}, bf16[2560,128]{1,0:T(8,128)(2,1)S(1)}) fusion(bf16[4096,128]{1,0:T(8,128)(2,1)} %x_hbm), kind=kLoop, calls=%fused_computation | loop fusion | bytes 2621440 | tf_op jit(solution)/shard_map/slice | solution.py:293
  1.4 0.0 copy-start
  1.4 5.0 %collective-permute-start.7 = (bf16[2560,128]{1,0:T(8,128)(2,1)S(1)}, bf16[2560,128]{1,0:T(8,128)(2,1)S(1)}, u32[]{:S(2)}, u32[]{:S(2)}) collective-permute-start(bf16[2560,128]{1,0:T(8,128)(2,1)S(1)} %get-tuple-element.56), channel_id=1, source_target_pairs={{0,1},{1,2},{2,3},{3,4},{4,5},{5,6},{6,7},{7,8},{8,9},{9,10},{10,1... | collective-permute-start | bytes 1966088 | tf_op jit(solution)/shard_map/ppermute | solution.py:279
  6.4 1.3 %collective-permute-start.8 = (bf16[2560,128]{1,0:T(8,128)(2,1)S(1)}, bf16[2560,128]{1,0:T(8,128)(2,1)S(1)}, u32[]{:S(2)}, u32[]{:S(2)}) collective-permute-start(bf16[2560,128]{1,0:T(8,128)(2,1)S(1)} %get-tuple-element.57), channel_id=1, source_target_pairs={{1,0},{2,1},{3,2},{4,3},{5,4},{6,5},{7,6},{8,7},{9,8},{10,9},{11,1... | collective-permute-start | bytes 1966088 | tf_op jit(solution)/shard_map/ppermute | solution.py:279
  7.7 2.7 %shard_map.100 = (bf16[128,128]{1,0:T(8,128)(2,1)S(1)}, bf16[1536,128]{1,0:T(8,128)(2,1)S(1)}) custom-call(bf16[4096,128]{1,0:T(8,128)(2,1)} %x_hbm, bf16[8,64,512]{2,1,0:T(8,128)(2,1)} %refs_4_.1, bf16[512,64]{1,0:T(8,128)(2,1)} %bitcast.6, bf16[64,64]{1,0:T(8,128)(2,1)} %bitcast.10), custom_call_target="tpu_custom_call" | custom-call | flops 1000 | bytes 1000 | tf_op jit(solution)/shard_map/pallas_call | solution.py:300
  10.4 2.8 %collective-permute-start = (bf16[128,128]{1,0:T(8,128)(2,1)S(1)}, bf16[128,128]{1,0:T(8,128)(2,1)S(1)}, u32[]{:S(2)}, u32[]{:S(2)}) collective-permute-start(bf16[128,128]{1,0:T(8,128)(2,1)S(1)} %get-tuple-element.43.refs_0_), channel_id=1, source_target_pairs={{0,4},{4,0},{8,12},{12,8},{1,5},{5,1},{9,13},{13,9},{2,6},{6,2},{1... | collective-permute-start | bytes 98312 | tf_op jit(solution)/shard_map/ppermute | solution.py:282
  13.2 2.3 %collective-permute-start.1 = (bf16[128,128]{1,0:T(8,128)(2,1)S(1)}, bf16[128,128]{1,0:T(8,128)(2,1)S(1)}, u32[]{:S(2)}, u32[]{:S(2)}) collective-permute-start(bf16[128,128]{1,0:T(8,128)(2,1)S(1)} %get-tuple-element.43.refs_0_), channel_id=1, source_target_pairs={{0,8},{4,12},{8,0},{12,4},{1,9},{5,13},{9,1},{13,5},{2,10},{6,14},... | collective-permute-start | bytes 98312 | tf_op jit(solution)/shard_map/ppermute | solution.py:282
  15.5 0.1 collective-permute-start.2
  15.5 0.0 collective-permute-done.refs_1_
  15.5 1.9 %collective-permute-done.1.refs_2_ = bf16[128,128]{1,0:T(8,128)(2,1)S(1)} collective-permute-done((bf16[128,128]{1,0:T(8,128)(2,1)S(1)}, bf16[128,128]{1,0:T(8,128)(2,1)S(1)}, u32[]{:S(2)}, u32[]{:S(2)}) %collective-permute-start.1) | collective-permute-done | bytes 32800 | tf_op jit(solution)/shard_map/ppermute | solution.py:282
  17.5 1.4 %collective-permute-done.2.refs_3_ = bf16[128,128]{1,0:T(8,128)(2,1)S(1)} collective-permute-done((bf16[128,128]{1,0:T(8,128)(2,1)S(1)}, bf16[128,128]{1,0:T(8,128)(2,1)S(1)}, u32[]{:S(2)}, u32[]{:S(2)}) %collective-permute-start.2) | collective-permute-done | bytes 32800 | tf_op jit(solution)/shard_map/ppermute | solution.py:282
  18.8 1.3 %collective-permute-start.3 = (bf16[1536,128]{1,0:T(8,128)(2,1)S(1)}, bf16[1536,128]{1,0:T(8,128)(2,1)S(1)}, u32[]{:S(2)}, u32[]{:S(2)}) collective-permute-start(bf16[1536,128]{1,0:T(8,128)(2,1)S(1)} %get-tuple-element.48), channel_id=1, source_target_pairs={{3,7},{7,11},{11,15},{4,0},{8,4},{12,8},{19,23},{23,27},{27,31},{2... | collective-permute-start | bytes 1179656 | tf_op jit(solution)/shard_map/ppermute | solution.py:279
  20.1 1.9 %collective-permute-start.6 = (bf16[512,128]{1,0:T(8,128)(2,1)S(1)}, bf16[512,128]{1,0:T(8,128)(2,1)S(1)}, u32[]{:S(2)}, u32[]{:S(2)}) collective-permute-start(bf16[512,128]{1,0:T(8,128)(2,1)S(1)} %shard_map.101.plane), channel_id=1, source_target_pairs={{0,2},{1,3},{2,0},{3,1},{4,5},{5,4},{6,7},{7,6},{12,15},{13,14},{1... | collective-permute-start | bytes 393224 | tf_op jit(solution)/shard_map/ppermute | solution.py:279
  22.7 0.0 collective-permute-done.3.relayed
  22.7 1.0 %shard_map.102 = (bf16[1536,128]{1,0:T(8,128)(2,1)S(1)}, bf16[1536,128]{1,0:T(8,128)(2,1)S(1)}) custom-call(bf16[4096,128]{1,0:T(8,128)(2,1)} %x_hbm, bf16[1536,128]{1,0:T(8,128)(2,1)S(1)} %collective-permute-done.3.relayed), custom_call_target="tpu_custom_call" | custom-call | flops 1000 | bytes 1000 | tf_op jit(solution)/shard_map/pallas_call | solution.py:315
  23.8 4.9 %collective-permute-start.4 = (bf16[1536,128]{1,0:T(8,128)(2,1)S(1)}, bf16[1536,128]{1,0:T(8,128)(2,1)S(1)}, u32[]{:S(2)}, u32[]{:S(2)}) collective-permute-start(bf16[1536,128]{1,0:T(8,128)(2,1)S(1)} %get-tuple-element.51), channel_id=1, source_target_pairs={{0,1},{1,2},{2,3},{4,5},{5,6},{6,7},{8,9},{9,10},{10,11},{12,13},{... | collective-permute-start | bytes 1179656 | tf_op jit(solution)/shard_map/ppermute | solution.py:279
  28.6 1.9 %collective-permute-start.5 = (bf16[1536,128]{1,0:T(8,128)(2,1)S(1)}, bf16[1536,128]{1,0:T(8,128)(2,1)S(1)}, u32[]{:S(2)}, u32[]{:S(2)}) collective-permute-start(bf16[1536,128]{1,0:T(8,128)(2,1)S(1)} %get-tuple-element.52), channel_id=1, source_target_pairs={{1,0},{2,1},{3,2},{5,4},{6,5},{7,6},{9,8},{10,9},{11,10},{13,12},{... | collective-permute-start | bytes 1179656 | tf_op jit(solution)/shard_map/ppermute | solution.py:279
  30.6 0.0 copy-done
  30.6 9.5 %shard_map.103 = (f32[4096,128]{1,0:T(8,128)S(1)}, bf16[40,512,512]{2,1,0:T(8,128)(2,1)S(1)}, bf16[4,64,64]{2,1,0:T(8,128)(2,1)S(1)}, bf16[4,64,64]{2,1,0:T(8,12...) custom-call(s32[8,5]{1,0:T(8,128)S(1)} %copy-done, ...), custom_call_target="tpu_custom_call" | custom-call | flops 1000 | bytes 1000 | tf_op jit(solution)/shard_map/pallas_call | solution.py:326
  40.1 3.1 %collective-permute-done.6.refs_0_ = bf16[512,128]{1,0:T(8,128)(2,1)S(1)} collective-permute-done((bf16[512,128]{1,0:T(8,128)(2,1)S(1)}, bf16[512,128]{1,0:T(8,128)(2,1)S(1)}, u32[]{:S(2)}, u32[]{:S(2)}) %collective-permute-start.6) | collective-permute-done | bytes 131104 | tf_op jit(solution)/shard_map/ppermute | solution.py:279
  43.2 0.0 collective-permute-done.7.before
  43.2 0.0 collective-permute-done.8.after
  43.2 3.7 %collective-permute-start.10 = (bf16[512,128]{1,0:T(8,128)(2,1)S(1)}, bf16[512,128]{1,0:T(8,128)(2,1)S(1)}, u32[]{:S(2)}, u32[]{:S(2)}) collective-permute-start(bf16[512,128]{1,0:T(8,128)(2,1)S(1)} %collective-permute-done.6.refs_0_), channel_id=1, source_target_pairs={{0,8},{4,12},{8,0},{12,4},{1,9},{5,13},{9,1},{13,5},{2,10},{6,14},... | collective-permute-start | bytes 393224 | tf_op jit(solution)/shard_map/ppermute | solution.py:282
  46.9 1.7 %collective-permute-start.11 = (bf16[512,128]{1,0:T(8,128)(2,1)S(1)}, bf16[512,128]{1,0:T(8,128)(2,1)S(1)}, u32[]{:S(2)}, u32[]{:S(2)}) collective-permute-start(bf16[512,128]{1,0:T(8,128)(2,1)S(1)} %collective-permute-done.6.refs_0_), channel_id=1, source_target_pairs={{0,12},{4,8},{8,4},{12,0},{1,13},{5,9},{9,5},{13,1},{2,14},{6,10},... | collective-permute-start | bytes 393224 | tf_op jit(solution)/shard_map/ppermute | solution.py:282
  48.6 0.0 collective-permute-start.9
  48.6 0.0 copy-start.1
  48.6 4.2 %shard_map.104.refs_9_ = f32[4096,128]{1,0:T(8,128)S(1)} custom-call(s32[8,5]{1,0:T(8,128)S(1)} %copy-done, bf16[2560,128]{1,0:T(8,128)(2,1)S(1)} %collective-permute-done.7.before, bf16[2560,128]{1,0:T(8,128)(2,1)S(1)} %collective-permute-done.8.after, bf16[40,512,512]{2,1,0:T(8,128)(2,1)S(1)} %get-tuple-element.54.blocks, ...), custom_call_target="tpu_custom_call", output_to_operand_aliasing={{}: (4, {})} | custom-call | flops 10000000000 | bytes 1000 | tf_op jit(solution)/shard_map/pallas_call | solution.py:338
  52.8 0.0 collective-permute-done.10.refs_2_
  52.8 1.3 %collective-permute-done.11.refs_3_ = bf16[512,128]{1,0:T(8,128)(2,1)S(1)} collective-permute-done((bf16[512,128]{1,0:T(8,128)(2,1)S(1)}, bf16[512,128]{1,0:T(8,128)(2,1)S(1)}, u32[]{:S(2)}, u32[]{:S(2)}) %collective-permute-start.11) | collective-permute-done | bytes 131104 | tf_op jit(solution)/shard_map/ppermute | solution.py:282
  54.1 0.0 collective-permute-done.9.refs_1_
  54.1 0.0 copy-done.1
  54.1 1.4 %shard_map.105._ = f32[4096,128]{1,0:T(8,128)S(1)} custom-call(s32[1,4]{1,0:T(1,128)S(1)} %copy-done.1, s32[1]{0:T(128)S(6)} %copy.17.far_count, bf16[512,128]{1,0:T(8,128)(2,1)S(1)} %shard_map.101.plane, bf16[512,128]{1,0:T(8,128)(2,1)S(1)} %collective-permute-done.6.refs_0_, ...), custom_call_target="tpu_custom_call", output_to_operand_aliasing={{}: (12, {})} | custom-call | flops 1000 | bytes 1000 | tf_op jit(solution)/shard_map/pallas_call | solution.py:342
  55.5 0.0 collective-permute-done.4.before
  55.5 0.0 collective-permute-done.5.after
  55.5 2.4 %shard_map.106 = (bf16[4096,128]{1,0:T(8,128)(2,1)}, f32[4096,128]{1,0:T(8,128)S(1)}) custom-call(s32[8,5]{1,0:T(8,128)S(1)} %copy-done, bf16[1536,128]{1,0:T(8,128)(2,1)S(1)} %collective-permute-done.4.before, bf16[1536,128]{1,0:T(8,128)(2,1)S(1)} %collective-permute-done.5.after, ...), custom_call_target="tpu_custom_call", output_to_operand_aliasing={{1}: (4, {})} | custom-call | flops 1000 | bytes 1000 | tf_op jit(solution)/shard_map/pallas_call | solution.py:350
  (1 shorter events, 0.0 us)
Async XLA Ops:
  1.4 29.2 %copy-start = (s32[8,5]{1,0:T(8,128)S(1)}, s32[8,5]{1,0:T(8,128)}, u32[]{:S(2)}) copy-start(s32[8,5]{1,0:T(8,128)} %ids_ref.5) | copy-start | bytes 484
  1.4 41.8 %collective-permute-start.7 = (bf16[2560,128]{1,0:T(8,128)(2,1)S(1)}, bf16[2560,128]{1,0:T(8,128)(2,1)S(1)}, u32[]{:S(2)}, u32[]{:S(2)}) collective-permute-start(bf16[2560,128]{1,0:T(8,128)(2,1)S(1)} %get-tuple-element.56), channel_id=1, source_target_pairs={{0,1},{1,2},{2,3},{3,4},{4,5},{5,6},{6,7},{7,8},{8,9},{9,10},{10,1... | collective-permute-start | bytes 1966088 | tf_op jit(solution)/shard_map/ppermute | solution.py:279
  6.4 36.8 %collective-permute-start.8 = (bf16[2560,128]{1,0:T(8,128)(2,1)S(1)}, bf16[2560,128]{1,0:T(8,128)(2,1)S(1)}, u32[]{:S(2)}, u32[]{:S(2)}) collective-permute-start(bf16[2560,128]{1,0:T(8,128)(2,1)S(1)} %get-tuple-element.57), channel_id=1, source_target_pairs={{1,0},{2,1},{3,2},{4,3},{5,4},{6,5},{7,6},{8,7},{9,8},{10,9},{11,1... | collective-permute-start | bytes 1966088 | tf_op jit(solution)/shard_map/ppermute | solution.py:279
  10.4 5.2 %collective-permute-start = (bf16[128,128]{1,0:T(8,128)(2,1)S(1)}, bf16[128,128]{1,0:T(8,128)(2,1)S(1)}, u32[]{:S(2)}, u32[]{:S(2)}) collective-permute-start(bf16[128,128]{1,0:T(8,128)(2,1)S(1)} %get-tuple-element.43.refs_0_), channel_id=1, source_target_pairs={{0,4},{4,0},{8,12},{12,8},{1,5},{5,1},{9,13},{13,9},{2,6},{6,2},{1... | collective-permute-start | bytes 98312 | tf_op jit(solution)/shard_map/ppermute | solution.py:282
  13.2 4.3 %collective-permute-start.1 = (bf16[128,128]{1,0:T(8,128)(2,1)S(1)}, bf16[128,128]{1,0:T(8,128)(2,1)S(1)}, u32[]{:S(2)}, u32[]{:S(2)}) collective-permute-start(bf16[128,128]{1,0:T(8,128)(2,1)S(1)} %get-tuple-element.43.refs_0_), channel_id=1, source_target_pairs={{0,8},{4,12},{8,0},{12,4},{1,9},{5,13},{9,1},{13,5},{2,10},{6,14},... | collective-permute-start | bytes 98312 | tf_op jit(solution)/shard_map/ppermute | solution.py:282
  15.5 3.3 %collective-permute-start.2 = (bf16[128,128]{1,0:T(8,128)(2,1)S(1)}, bf16[128,128]{1,0:T(8,128)(2,1)S(1)}, u32[]{:S(2)}, u32[]{:S(2)}) collective-permute-start(bf16[128,128]{1,0:T(8,128)(2,1)S(1)} %get-tuple-element.43.refs_0_), channel_id=1, source_target_pairs={{0,12},{4,8},{8,4},{12,0},{1,13},{5,9},{9,5},{13,1},{2,14},{6,10},... | collective-permute-start | bytes 98312 | tf_op jit(solution)/shard_map/ppermute | solution.py:282
  18.8 3.9 %collective-permute-start.3 = (bf16[1536,128]{1,0:T(8,128)(2,1)S(1)}, bf16[1536,128]{1,0:T(8,128)(2,1)S(1)}, u32[]{:S(2)}, u32[]{:S(2)}) collective-permute-start(bf16[1536,128]{1,0:T(8,128)(2,1)S(1)} %get-tuple-element.48), channel_id=1, source_target_pairs={{3,7},{7,11},{11,15},{4,0},{8,4},{12,8},{19,23},{23,27},{27,31},{2... | collective-permute-start | bytes 1179656 | tf_op jit(solution)/shard_map/ppermute | solution.py:279
  20.1 23.1 %collective-permute-start.6 = (bf16[512,128]{1,0:T(8,128)(2,1)S(1)}, bf16[512,128]{1,0:T(8,128)(2,1)S(1)}, u32[]{:S(2)}, u32[]{:S(2)}) collective-permute-start(bf16[512,128]{1,0:T(8,128)(2,1)S(1)} %shard_map.101.plane), channel_id=1, source_target_pairs={{0,2},{1,3},{2,0},{3,1},{4,5},{5,4},{6,7},{7,6},{12,15},{13,14},{1... | collective-permute-start | bytes 393224 | tf_op jit(solution)/shard_map/ppermute | solution.py:279
  23.8 31.8 %collective-permute-start.4 = (bf16[1536,128]{1,0:T(8,128)(2,1)S(1)}, bf16[1536,128]{1,0:T(8,128)(2,1)S(1)}, u32[]{:S(2)}, u32[]{:S(2)}) collective-permute-start(bf16[1536,128]{1,0:T(8,128)(2,1)S(1)} %get-tuple-element.51), channel_id=1, source_target_pairs={{0,1},{1,2},{2,3},{4,5},{5,6},{6,7},{8,9},{9,10},{10,11},{12,13},{... | collective-permute-start | bytes 1179656 | tf_op jit(solution)/shard_map/ppermute | solution.py:279
  28.6 26.9 %collective-permute-start.5 = (bf16[1536,128]{1,0:T(8,128)(2,1)S(1)}, bf16[1536,128]{1,0:T(8,128)(2,1)S(1)}, u32[]{:S(2)}, u32[]{:S(2)}) collective-permute-start(bf16[1536,128]{1,0:T(8,128)(2,1)S(1)} %get-tuple-element.52), channel_id=1, source_target_pairs={{1,0},{2,1},{3,2},{5,4},{6,5},{7,6},{9,8},{10,9},{11,10},{13,12},{... | collective-permute-start | bytes 1179656 | tf_op jit(solution)/shard_map/ppermute | solution.py:279
  43.2 9.6 %collective-permute-start.10 = (bf16[512,128]{1,0:T(8,128)(2,1)S(1)}, bf16[512,128]{1,0:T(8,128)(2,1)S(1)}, u32[]{:S(2)}, u32[]{:S(2)}) collective-permute-start(bf16[512,128]{1,0:T(8,128)(2,1)S(1)} %collective-permute-done.6.refs_0_), channel_id=1, source_target_pairs={{0,8},{4,12},{8,0},{12,4},{1,9},{5,13},{9,1},{13,5},{2,10},{6,14},... | collective-permute-start | bytes 393224 | tf_op jit(solution)/shard_map/ppermute | solution.py:282
  46.9 7.2 %collective-permute-start.11 = (bf16[512,128]{1,0:T(8,128)(2,1)S(1)}, bf16[512,128]{1,0:T(8,128)(2,1)S(1)}, u32[]{:S(2)}, u32[]{:S(2)}) collective-permute-start(bf16[512,128]{1,0:T(8,128)(2,1)S(1)} %collective-permute-done.6.refs_0_), channel_id=1, source_target_pairs={{0,12},{4,8},{8,4},{12,0},{1,13},{5,9},{9,5},{13,1},{2,14},{6,10},... | collective-permute-start | bytes 393224 | tf_op jit(solution)/shard_map/ppermute | solution.py:282
  48.6 5.5 %collective-permute-start.9 = (bf16[512,128]{1,0:T(8,128)(2,1)S(1)}, bf16[512,128]{1,0:T(8,128)(2,1)S(1)}, u32[]{:S(2)}, u32[]{:S(2)}) collective-permute-start(bf16[512,128]{1,0:T(8,128)(2,1)S(1)} %collective-permute-done.6.refs_0_), channel_id=1, source_target_pairs={{0,4},{4,0},{8,12},{12,8},{1,5},{5,1},{9,13},{13,9},{2,6},{6,2},{1... | collective-permute-start | bytes 393224 | tf_op jit(solution)/shard_map/ppermute | solution.py:282
  48.6 5.5 %copy-start.1 = (s32[1,4]{1,0:T(1,128)S(1)}, s32[1,4]{1,0:T(1,128)}, u32[]{:S(2)}) copy-start(s32[1,4]{1,0:T(1,128)} %far_ids.1) | copy-start | bytes 52

commit v12 on v11

--- a/solution.py
+++ b/solution.py
@@ -99,8 +99,18 @@
         pltpu.make_async_copy(relayed, piece, sems.at[i]).wait()
 
 
-def down_kernel(leaf_size, inner_size, far_ids, far_count, plane, *refs):
-    found, (couple, mid_couple, mid_map, leaf_map, basis, _, out_ref, planes) = refs[:inner_size], refs[inner_size:]
+def close_kernel(near_by, leaf_size, inner_size, ids_ref, far_ids, far_count, before, after, blocks, plane, *refs):
+    found, refs = refs[:inner_size], refs[inner_size:]
+    couple, mid_couple, mid_map, leaf_map, basis, _, out_ref, total_ref, planes, *lists, result, sems = refs
+    leaves, near = ids_ref.shape
+
+    def kind_of(leaf, offset):
+        return (offset < -near_by, offset + leaves), (offset >= leaves + near_by, offset - leaves - near_by)
+
+    kinds = (lists[:2], lists[2:])
+    counts = listed(ids_ref, kinds, kind_of)
+    for kind, count, x_ref in zip(kinds, counts, (before, after)):
+        add_products(near, kind, count, blocks, x_ref, total_ref)
     rank = mid_map.shape[0]
     size = 2 * rank
     for step, part in enumerate(found):
@@ -125,13 +135,20 @@
         partner = jnp.where(live, far_ids[0, slot], group * inner_size)
         other, turn = partner // inner_size, inner ^ lax.rem(partner, inner_size)
         step = (group & (inner_size - 1)) ^ carrier(turn, inner_size)
-        near, far = plane[at_of(0, group ^ other), :], planes[at_of(step, group ^ step ^ other), :]
-        term = dot(mid_couple[slot], jnp.where(turn == 0, near, far))
+        here, there = plane[at_of(0, group ^ other), :], planes[at_of(step, group ^ step ^ other), :]
+        term = dot(mid_couple[slot], jnp.where(turn == 0, here, there))
         total += jnp.where(live, term, 0.0)
     leaf_down = dot(leaf_map[...], total.astype(jnp.bfloat16)).astype(jnp.bfloat16)
-    leaves, _, rows = basis.shape
+    rows = basis.shape[2]
+    stores = []
     for leaf in range(leaves):
-        out_ref[leaf * rows : (leaf + 1) * rows, :] += dot_t(basis[leaf], leaf_down[leaf * rank : (leaf + 1) * rank, :])
+        here = slice(leaf * rows, (leaf + 1) * rows)
+        far = dot_t(basis[leaf], leaf_down[leaf * rank : (leaf + 1) * rank, :])
+        result[here, :] = (total_ref[here, :] + far).astype(result.dtype)
+        stores.append(pltpu.make_async_copy(result.at[here], out_ref.at[here], sems.at[leaf]))
+        stores[-1].start()
+    for store in stores:
+        store.wait()
 
 
 def listed(ids_ref, lists, kind_of):
@@ -237,28 +254,6 @@
     counts = listed(ids_ref, kinds, kind_of)
     for kind, count, x_ref in zip(kinds, counts, (before, after)):
         add_products(near, kind, count, blocks, x_ref, total)
-
-
-def last_kernel(near_by, ids_ref, before, after, blocks, _, out_ref, total, *refs):
-    lists, (result, sems) = refs[:4], refs[4:]
-    leaves, near = ids_ref.shape
-    rows = blocks.shape[1]
-
-    def kind_of(leaf, offset):
-        return (offset < -near_by, offset + leaves), (offset >= leaves + near_by, offset - leaves - near_by)
-
-    kinds = (lists[:2], lists[2:])
-    counts = listed(ids_ref, kinds, kind_of)
-    for kind, count, x_ref in zip(kinds, counts, (before, after)):
-        add_products(near, kind, count, blocks, x_ref, total)
-    stores = []
-    for leaf in range(leaves):
-        here = slice(leaf * rows, (leaf + 1) * rows)
-        result[here, :] = total[here, :].astype(result.dtype)
-        stores.append(pltpu.make_async_copy(result.at[here], out_ref.at[here], sems.at[leaf]))
-        stores[-1].start()
-    for store in stores:
-        store.wait()
 
 
 def local(anomalies, leaf_basis, near_blocks, near_ids, transfer_leaf, transfer_mid, far_ids, far_count, mid_couple, top_couple):
@@ -332,29 +327,25 @@
         flops=1000,
     )(near_ids, *[held(x, pltpu.HBM) for x in (x_late, near_blocks.reshape(slots, rows, rows), *later)])
     blocks = held(blocks, pltpu.VMEM)
-    planes, halo[0], total = lax.optimization_barrier((planes, halo[0], total))
-    others = [swapped(planes, reach) for reach in range(1, inner_size)]
-    total, planes = lax.optimization_barrier((total, planes))
+    halo[0], total = lax.optimization_barrier((halo[0], total))
     total = kernel(functools.partial(wave_kernel, one), wide, [SMEM] + [VMEM] * 4, VMEM, lists * 2, aliases={4: 0}, flops=10**10)(
         near_ids, *halo[0], blocks, held(total, pltpu.VMEM)
     )
-    others, total = lax.optimization_barrier((others, total))
-    total = kernel(
-        functools.partial(down_kernel, leaf_size, inner_size),
-        wide,
-        [SMEM, SMEM] + [VMEM] * (7 + inner_size),
-        VMEM,
-        [pltpu.VMEM((inner_size * leaf_size * 2 * rank, columns), bf16)],
-        aliases={8 + inner_size: 0},
-    )(far_ids, far_count, plane, planes, *others, *later, held(total, pltpu.VMEM))
+    planes, total = lax.optimization_barrier((planes, total))
+    found = [planes] + [swapped(planes, reach) for reach in range(1, inner_size)]
     out, _ = kernel(
-        functools.partial(last_kernel, one),
+        functools.partial(close_kernel, one, leaf_size, inner_size),
         (jax.ShapeDtypeStruct(anomalies.shape, bf16), wide),
-        [SMEM] + [VMEM] * 4,
+        [SMEM] * 3 + [VMEM] * (10 + inner_size),
         (ANY, VMEM),
-        lists * 2 + [pltpu.VMEM(anomalies.shape, bf16), pltpu.SemaphoreType.DMA((leaves,))],
-        aliases={4: 1},
-    )(near_ids, *halo[1], blocks, held(total, pltpu.VMEM))
+        [
+            pltpu.VMEM((inner_size * leaf_size * 2 * rank, columns), bf16),
+            *lists * 2,
+            pltpu.VMEM(anomalies.shape, bf16),
+            pltpu.SemaphoreType.DMA((leaves,)),
+        ],
+        aliases={12 + inner_size: 1},
+    )(near_ids, far_ids, far_count, *halo[1], blocks, plane, *found, *later, held(total, pltpu.VMEM))
     return out
 
 

time: 58 us -> 60.6 us (1.045)
  starting transfers between devices: 26.8 us -> 29.3 us
    ppermute x6, starting transfers between devices: 10.6 us -> 13.4 us  [swapped(): return lax.ppermute(x, 'leaf', [(i, i ^ reach) for i in groups])]
    ppermute x6, waiting for transfers between devices: 4.55 us -> 7.38 us  [swapped(): return lax.ppermute(x, 'leaf', [(i, i ^ reach) for i in groups])]
    ppermute x6, waiting for transfers between devices: 3.15 us -> 0.62 us  [passed(): return lax.ppermute(x, ('leaf', 'inner'), pairs)]
    pallas_call x1, Pallas kernels: 4.21 us -> 3.51 us  [local(): kernel(functools.partial(wave_kernel, one), wide, [SMEM] + [VMEM] * 4, VM...]
    pallas_call x2 -> x1, Pallas kernels: 3.79 us -> 3.33 us  [local(): kernel(functools.partial(close_kernel, one, leaf_size, inner_size), (jax....]
  transfers between devices with their start and end apart: 12 -> 12, of which waited for: 4 -> 5; matrix products, arithmetic and copies ran while one was open for 0% -> 0% of each run, Pallas kernels for 33% -> 29%
where the time goes in v12:
time: 60.6 us; the launch traced here: 60.1 us
  starting transfers between devices  29.3 us (48%)
  Pallas kernels  20.6 us (34%)
  waiting for transfers between devices  8.01 us (13%)
  local copies, waits for them, and re-layouts  1.38 us (2%)
  between operations  0.81 us (1%)
    ppermute x6, starting transfers between devices, passed(): return lax.ppermute(x, ('leaf', 'inner'), pairs)  15.8 us
    ppermute x6, starting transfers between devices, swapped(): return lax.ppermute(x, 'leaf', [(i, i ^ reach) for i in groups])  13.4 us
    pallas_call x1, Pallas kernels, local(): kernel(own_kernel, [wide, resident(slots, rows, rows)] + [resident(*x.sha...  10.1 us
    ppermute x6, waiting for transfers between devices, swapped(): return lax.ppermute(x, 'leaf', [(i, i ^ reach) for i in groups])  7.38 us
    pallas_call x1, Pallas kernels, local(): kernel(functools.partial(wave_kernel, one), wide, [SMEM] + [VMEM] * 4, VM...  3.51 us
    pallas_call x1, Pallas kernels, local(): kernel(functools.partial(close_kernel, one, leaf_size, inner_size), (jax....  3.33 us
    pallas_call x1, Pallas kernels, local(): kernel(up_kernel, (jax.ShapeDtypeStruct((2 * rank, columns), bf16), piece...  2.7 us
    slice x1, local copies, waits for them, and re-layouts, local(): lax.slice_in_dim(anomalies, 0, one * rows)  1.37 us
  transfers between devices with their start and end apart: 12, of which 5 were waited for; matrix products, arithmetic and copies ran while one was open for 0% of the time, Pallas kernels for 29%

profile of v12, /device:TPU:0, one launch (start us, length us, event | category | flops | bytes accessed | tf_op | source)
XLA Modules:
  0.0 60.1 jit_solution(13470628136927624440)
XLA Ops:
  0.0 1.4 %fusion = (bf16[2560,128]{1,0:T(8,128)(2,1)S(1)}, bf16[2560,128]{1,0:T(8,128)(2,1)S(1)}) fusion(bf16[4096,128]{1,0:T(8,128)(2,1)} %x_hbm), kind=kLoop, calls=%fused_computation | loop fusion | bytes 2621440 | tf_op jit(solution)/shard_map/slice | solution.py:288
  1.4 0.0 copy-start
  1.4 5.0 %collective-permute-start.7 = (bf16[2560,128]{1,0:T(8,128)(2,1)S(1)}, bf16[2560,128]{1,0:T(8,128)(2,1)S(1)}, u32[]{:S(2)}, u32[]{:S(2)}) collective-permute-start(bf16[2560,128]{1,0:T(8,128)(2,1)S(1)} %get-tuple-element.51), channel_id=1, source_target_pairs={{0,1},{1,2},{2,3},{3,4},{4,5},{5,6},{6,7},{7,8},{8,9},{9,10},{10,1... | collective-permute-start | bytes 1966088 | tf_op jit(solution)/shard_map/ppermute | solution.py:274
  6.4 1.3 %collective-permute-start.8 = (bf16[2560,128]{1,0:T(8,128)(2,1)S(1)}, bf16[2560,128]{1,0:T(8,128)(2,1)S(1)}, u32[]{:S(2)}, u32[]{:S(2)}) collective-permute-start(bf16[2560,128]{1,0:T(8,128)(2,1)S(1)} %get-tuple-element.52), channel_id=1, source_target_pairs={{1,0},{2,1},{3,2},{4,3},{5,4},{6,5},{7,6},{8,7},{9,8},{10,9},{11,1... | collective-permute-start | bytes 1966088 | tf_op jit(solution)/shard_map/ppermute | solution.py:274
  7.7 2.7 %shard_map.100 = (bf16[128,128]{1,0:T(8,128)(2,1)S(1)}, bf16[1536,128]{1,0:T(8,128)(2,1)S(1)}) custom-call(bf16[4096,128]{1,0:T(8,128)(2,1)} %x_hbm, bf16[8,64,512]{2,1,0:T(8,128)(2,1)} %refs_4_.1, bf16[512,64]{1,0:T(8,128)(2,1)} %bitcast.6, bf16[64,64]{1,0:T(8,128)(2,1)} %bitcast.10), custom_call_target="tpu_custom_call" | custom-call | flops 1000 | bytes 1000 | tf_op jit(solution)/shard_map/pallas_call | solution.py:295
  10.4 3.9 %collective-permute-start.2 = (bf16[128,128]{1,0:T(8,128)(2,1)S(1)}, bf16[128,128]{1,0:T(8,128)(2,1)S(1)}, u32[]{:S(2)}, u32[]{:S(2)}) collective-permute-start(bf16[128,128]{1,0:T(8,128)(2,1)S(1)} %get-tuple-element.38.refs_0_), channel_id=1, source_target_pairs={{0,12},{4,8},{8,4},{12,0},{1,13},{5,9},{9,5},{13,1},{2,14},{6,10},... | collective-permute-start | bytes 98312 | tf_op jit(solution)/shard_map/ppermute | solution.py:277
  14.3 1.2 %collective-permute-start.1 = (bf16[128,128]{1,0:T(8,128)(2,1)S(1)}, bf16[128,128]{1,0:T(8,128)(2,1)S(1)}, u32[]{:S(2)}, u32[]{:S(2)}) collective-permute-start(bf16[128,128]{1,0:T(8,128)(2,1)S(1)} %get-tuple-element.38.refs_0_), channel_id=1, source_target_pairs={{0,8},{4,12},{8,0},{12,4},{1,9},{5,13},{9,1},{13,5},{2,10},{6,14},... | collective-permute-start | bytes 98312 | tf_op jit(solution)/shard_map/ppermute | solution.py:277
  15.5 0.0 collective-permute-start
  15.5 0.4 collective-permute-done.2.refs_3_
  15.9 2.4 %collective-permute-done.1.refs_2_ = bf16[128,128]{1,0:T(8,128)(2,1)S(1)} collective-permute-done((bf16[128,128]{1,0:T(8,128)(2,1)S(1)}, bf16[128,128]{1,0:T(8,128)(2,1)S(1)}, u32[]{:S(2)}, u32[]{:S(2)}) %collective-permute-start.1) | collective-permute-done | bytes 32800 | tf_op jit(solution)/shard_map/ppermute | solution.py:277
  18.3 0.0 collective-permute-done.refs_1_
  18.3 1.3 %collective-permute-start.3 = (bf16[1536,128]{1,0:T(8,128)(2,1)S(1)}, bf16[1536,128]{1,0:T(8,128)(2,1)S(1)}, u32[]{:S(2)}, u32[]{:S(2)}) collective-permute-start(bf16[1536,128]{1,0:T(8,128)(2,1)S(1)} %get-tuple-element.43), channel_id=1, source_target_pairs={{3,7},{7,11},{11,15},{4,0},{8,4},{12,8},{19,23},{23,27},{27,31},{2... | collective-permute-start | bytes 1179656 | tf_op jit(solution)/shard_map/ppermute | solution.py:274
  19.6 1.9 %collective-permute-start.6 = (bf16[512,128]{1,0:T(8,128)(2,1)S(1)}, bf16[512,128]{1,0:T(8,128)(2,1)S(1)}, u32[]{:S(2)}, u32[]{:S(2)}) collective-permute-start(bf16[512,128]{1,0:T(8,128)(2,1)S(1)} %shard_map.101.plane), channel_id=1, source_target_pairs={{0,2},{1,3},{2,0},{3,1},{4,5},{5,4},{6,7},{7,6},{12,15},{13,14},{1... | collective-permute-start | bytes 393224 | tf_op jit(solution)/shard_map/ppermute | solution.py:274
  21.5 0.4 collective-permute-done.3.relayed
  21.9 1.0 %shard_map.102 = (bf16[1536,128]{1,0:T(8,128)(2,1)S(1)}, bf16[1536,128]{1,0:T(8,128)(2,1)S(1)}) custom-call(bf16[4096,128]{1,0:T(8,128)(2,1)} %x_hbm, bf16[1536,128]{1,0:T(8,128)(2,1)S(1)} %collective-permute-done.3.relayed), custom_call_target="tpu_custom_call" | custom-call | flops 1000 | bytes 1000 | tf_op jit(solution)/shard_map/pallas_call | solution.py:310
  22.9 4.5 %collective-permute-start.4 = (bf16[1536,128]{1,0:T(8,128)(2,1)S(1)}, bf16[1536,128]{1,0:T(8,128)(2,1)S(1)}, u32[]{:S(2)}, u32[]{:S(2)}) collective-permute-start(bf16[1536,128]{1,0:T(8,128)(2,1)S(1)} %get-tuple-element.46), channel_id=1, source_target_pairs={{0,1},{1,2},{2,3},{4,5},{5,6},{6,7},{8,9},{9,10},{10,11},{12,13},{... | collective-permute-start | bytes 1179656 | tf_op jit(solution)/shard_map/ppermute | solution.py:274
  27.4 1.9 %collective-permute-start.5 = (bf16[1536,128]{1,0:T(8,128)(2,1)S(1)}, bf16[1536,128]{1,0:T(8,128)(2,1)S(1)}, u32[]{:S(2)}, u32[]{:S(2)}) collective-permute-start(bf16[1536,128]{1,0:T(8,128)(2,1)S(1)} %get-tuple-element.47), channel_id=1, source_target_pairs={{1,0},{2,1},{3,2},{5,4},{6,5},{7,6},{9,8},{10,9},{11,10},{13,12},{... | collective-permute-start | bytes 1179656 | tf_op jit(solution)/shard_map/ppermute | solution.py:274
  29.3 0.0 copy-done
  29.3 10.1 %shard_map.103 = (f32[4096,128]{1,0:T(8,128)S(1)}, bf16[40,512,512]{2,1,0:T(8,128)(2,1)S(1)}, bf16[4,64,64]{2,1,0:T(8,128)(2,1)S(1)}, bf16[4,64,64]{2,1,0:T(8,12...) custom-call(s32[8,5]{1,0:T(8,128)S(1)} %copy-done, ...), custom_call_target="tpu_custom_call" | custom-call | flops 1000 | bytes 1000 | tf_op jit(solution)/shard_map/pallas_call | solution.py:321
  39.4 0.0 collective-permute-done.7.before
  39.4 0.0 collective-permute-done.8.after
  39.4 0.0 copy-start.1
  39.4 3.5 %shard_map.104.refs_9_ = f32[4096,128]{1,0:T(8,128)S(1)} custom-call(s32[8,5]{1,0:T(8,128)S(1)} %copy-done, bf16[2560,128]{1,0:T(8,128)(2,1)S(1)} %collective-permute-done.7.before, bf16[2560,128]{1,0:T(8,128)(2,1)S(1)} %collective-permute-done.8.after, bf16[40,512,512]{2,1,0:T(8,128)(2,1)S(1)} %get-tuple-element.49.blocks, ...), custom_call_target="tpu_custom_call", output_to_operand_aliasing={{}: (4, {})} | custom-call | flops 10000000000 | bytes 1000 | tf_op jit(solution)/shard_map/pallas_call | solution.py:331
  43.0 0.2 collective-permute-done.6.refs_0_
  43.2 0.0 collective-permute-start.11
  43.2 8.3 %collective-permute-start.10 = (bf16[512,128]{1,0:T(8,128)(2,1)S(1)}, bf16[512,128]{1,0:T(8,128)(2,1)S(1)}, u32[]{:S(2)}, u32[]{:S(2)}) collective-permute-start(bf16[512,128]{1,0:T(8,128)(2,1)S(1)} %collective-permute-done.6.refs_0_), channel_id=1, source_target_pairs={{0,8},{4,12},{8,0},{12,4},{1,9},{5,13},{9,1},{13,5},{2,10},{6,14},... | collective-permute-start | bytes 393224 | tf_op jit(solution)/shard_map/ppermute | solution.py:277
  51.5 0.0 collective-permute-start.9
  52.1 0.0 collective-permute-done.11.refs_3_
  52.1 4.6 %collective-permute-done.10.refs_2_ = bf16[512,128]{1,0:T(8,128)(2,1)S(1)} collective-permute-done((bf16[512,128]{1,0:T(8,128)(2,1)S(1)}, bf16[512,128]{1,0:T(8,128)(2,1)S(1)}, u32[]{:S(2)}, u32[]{:S(2)}) %collective-permute-start.10) | collective-permute-done | bytes 131104 | tf_op jit(solution)/shard_map/ppermute | solution.py:277
  56.7 0.0 collective-permute-done.9.refs_1_
  56.7 0.0 collective-permute-done.4.before
  56.7 0.0 collective-permute-done.5.after
  56.8 0.0 copy-done.1
  56.8 3.3 %shard_map.105 = (bf16[4096,128]{1,0:T(8,128)(2,1)}, f32[4096,128]{1,0:T(8,128)S(1)}) custom-call(s32[8,5]{1,0:T(8,128)S(1)} %copy-done, s32[1,4]{1,0:T(1,128)S(1)} %copy-done.1, s32[1]{0:T(128)S(6)} %copy.15.far_count, bf16[1536,128]{1,0:T(8,128)(2,1)S(1)} %collective-permute-done.4.before, ...), custom_call_target="tpu_custom_call", output_to_operand_aliasing={{1}: (16, {})} | custom-call | flops 1000 | bytes 1000 | tf_op jit(solution)/shard_map/pallas_call | solution.py:336
  (1 shorter events, 0.0 us)
Async XLA Ops:
  1.4 28.0 %copy-start = (s32[8,5]{1,0:T(8,128)S(1)}, s32[8,5]{1,0:T(8,128)}, u32[]{:S(2)}) copy-start(s32[8,5]{1,0:T(8,128)} %ids_ref.5) | copy-start | bytes 484
  1.4 38.0 %collective-permute-start.7 = (bf16[2560,128]{1,0:T(8,128)(2,1)S(1)}, bf16[2560,128]{1,0:T(8,128)(2,1)S(1)}, u32[]{:S(2)}, u32[]{:S(2)}) collective-permute-start(bf16[2560,128]{1,0:T(8,128)(2,1)S(1)} %get-tuple-element.51), channel_id=1, source_target_pairs={{0,1},{1,2},{2,3},{3,4},{4,5},{5,6},{6,7},{7,8},{8,9},{9,10},{10,1... | collective-permute-start | bytes 1966088 | tf_op jit(solution)/shard_map/ppermute | solution.py:274
  6.4 33.1 %collective-permute-start.8 = (bf16[2560,128]{1,0:T(8,128)(2,1)S(1)}, bf16[2560,128]{1,0:T(8,128)(2,1)S(1)}, u32[]{:S(2)}, u32[]{:S(2)}) collective-permute-start(bf16[2560,128]{1,0:T(8,128)(2,1)S(1)} %get-tuple-element.52), channel_id=1, source_target_pairs={{1,0},{2,1},{3,2},{4,3},{5,4},{6,5},{7,6},{8,7},{9,8},{10,9},{11,1... | collective-permute-start | bytes 1966088 | tf_op jit(solution)/shard_map/ppermute | solution.py:274
  10.4 5.6 %collective-permute-start.2 = (bf16[128,128]{1,0:T(8,128)(2,1)S(1)}, bf16[128,128]{1,0:T(8,128)(2,1)S(1)}, u32[]{:S(2)}, u32[]{:S(2)}) collective-permute-start(bf16[128,128]{1,0:T(8,128)(2,1)S(1)} %get-tuple-element.38.refs_0_), channel_id=1, source_target_pairs={{0,12},{4,8},{8,4},{12,0},{1,13},{5,9},{9,5},{13,1},{2,14},{6,10},... | collective-permute-start | bytes 98312 | tf_op jit(solution)/shard_map/ppermute | solution.py:277
  14.3 4.0 %collective-permute-start.1 = (bf16[128,128]{1,0:T(8,128)(2,1)S(1)}, bf16[128,128]{1,0:T(8,128)(2,1)S(1)}, u32[]{:S(2)}, u32[]{:S(2)}) collective-permute-start(bf16[128,128]{1,0:T(8,128)(2,1)S(1)} %get-tuple-element.38.refs_0_), channel_id=1, source_target_pairs={{0,8},{4,12},{8,0},{12,4},{1,9},{5,13},{9,1},{13,5},{2,10},{6,14},... | collective-permute-start | bytes 98312 | tf_op jit(solution)/shard_map/ppermute | solution.py:277
  15.5 2.8 %collective-permute-start = (bf16[128,128]{1,0:T(8,128)(2,1)S(1)}, bf16[128,128]{1,0:T(8,128)(2,1)S(1)}, u32[]{:S(2)}, u32[]{:S(2)}) collective-permute-start(bf16[128,128]{1,0:T(8,128)(2,1)S(1)} %get-tuple-element.38.refs_0_), channel_id=1, source_target_pairs={{0,4},{4,0},{8,12},{12,8},{1,5},{5,1},{9,13},{13,9},{2,6},{6,2},{1... | collective-permute-start | bytes 98312 | tf_op jit(solution)/shard_map/ppermute | solution.py:277
  18.3 3.6 %collective-permute-start.3 = (bf16[1536,128]{1,0:T(8,128)(2,1)S(1)}, bf16[1536,128]{1,0:T(8,128)(2,1)S(1)}, u32[]{:S(2)}, u32[]{:S(2)}) collective-permute-start(bf16[1536,128]{1,0:T(8,128)(2,1)S(1)} %get-tuple-element.43), channel_id=1, source_target_pairs={{3,7},{7,11},{11,15},{4,0},{8,4},{12,8},{19,23},{23,27},{27,31},{2... | collective-permute-start | bytes 1179656 | tf_op jit(solution)/shard_map/ppermute | solution.py:274
  19.6 23.6 %collective-permute-start.6 = (bf16[512,128]{1,0:T(8,128)(2,1)S(1)}, bf16[512,128]{1,0:T(8,128)(2,1)S(1)}, u32[]{:S(2)}, u32[]{:S(2)}) collective-permute-start(bf16[512,128]{1,0:T(8,128)(2,1)S(1)} %shard_map.101.plane), channel_id=1, source_target_pairs={{0,2},{1,3},{2,0},{3,1},{4,5},{5,4},{6,7},{7,6},{12,15},{13,14},{1... | collective-permute-start | bytes 393224 | tf_op jit(solution)/shard_map/ppermute | solution.py:274
  22.9 33.8 %collective-permute-start.4 = (bf16[1536,128]{1,0:T(8,128)(2,1)S(1)}, bf16[1536,128]{1,0:T(8,128)(2,1)S(1)}, u32[]{:S(2)}, u32[]{:S(2)}) collective-permute-start(bf16[1536,128]{1,0:T(8,128)(2,1)S(1)} %get-tuple-element.46), channel_id=1, source_target_pairs={{0,1},{1,2},{2,3},{4,5},{5,6},{6,7},{8,9},{9,10},{10,11},{12,13},{... | collective-permute-start | bytes 1179656 | tf_op jit(solution)/shard_map/ppermute | solution.py:274
  27.4 29.3 %collective-permute-start.5 = (bf16[1536,128]{1,0:T(8,128)(2,1)S(1)}, bf16[1536,128]{1,0:T(8,128)(2,1)S(1)}, u32[]{:S(2)}, u32[]{:S(2)}) collective-permute-start(bf16[1536,128]{1,0:T(8,128)(2,1)S(1)} %get-tuple-element.47), channel_id=1, source_target_pairs={{1,0},{2,1},{3,2},{5,4},{6,5},{7,6},{9,8},{10,9},{11,10},{13,12},{... | collective-permute-start | bytes 1179656 | tf_op jit(solution)/shard_map/ppermute | solution.py:274
  39.4 17.3 %copy-start.1 = (s32[1,4]{1,0:T(1,128)S(1)}, s32[1,4]{1,0:T(1,128)}, u32[]{:S(2)}) copy-start(s32[1,4]{1,0:T(1,128)} %far_ids.1) | copy-start | bytes 52
  43.2 8.9 %collective-permute-start.11 = (bf16[512,128]{1,0:T(8,128)(2,1)S(1)}, bf16[512,128]{1,0:T(8,128)(2,1)S(1)}, u32[]{:S(2)}, u32[]{:S(2)}) collective-permute-start(bf16[512,128]{1,0:T(8,128)(2,1)S(1)} %collective-permute-done.6.refs_0_), channel_id=1, source_target_pairs={{0,12},{4,8},{8,4},{12,0},{1,13},{5,9},{9,5},{13,1},{2,14},{6,10},... | collective-permute-start | bytes 393224 | tf_op jit(solution)/shard_map/ppermute | solution.py:277
  43.2 13.5 %collective-permute-start.10 = (bf16[512,128]{1,0:T(8,128)(2,1)S(1)}, bf16[512,128]{1,0:T(8,128)(2,1)S(1)}, u32[]{:S(2)}, u32[]{:S(2)}) collective-permute-start(bf16[512,128]{1,0:T(8,128)(2,1)S(1)} %collective-permute-done.6.refs_0_), channel_id=1, source_target_pairs={{0,8},{4,12},{8,0},{12,4},{1,9},{5,13},{9,1},{13,5},{2,10},{6,14},... | collective-permute-start | bytes 393224 | tf_op jit(solution)/shard_map/ppermute | solution.py:277
  51.5 5.3 %collective-permute-start.9 = (bf16[512,128]{1,0:T(8,128)(2,1)S(1)}, bf16[512,128]{1,0:T(8,128)(2,1)S(1)}, u32[]{:S(2)}, u32[]{:S(2)}) collective-permute-start(bf16[512,128]{1,0:T(8,128)(2,1)S(1)} %collective-permute-done.6.refs_0_), channel_id=1, source_target_pairs={{0,4},{4,0},{8,12},{12,8},{1,5},{5,1},{9,13},{13,9},{2,6},{6,2},{1... | collective-permute-start | bytes 393224 | tf_op jit(solution)/shard_map/ppermute | solution.py:277

commit v13 on v12

--- a/solution.py
+++ b/solution.py
@@ -50,7 +50,7 @@
     )
 
 
-def up_kernel(x_ref, basis_ref, leaf_map_ref, mid_map_ref, out_ref, relay, x, basis, leaf_map, mid_map, skeleton, sems):
+def up_kernel(x_ref, basis_ref, leaf_map_ref, mid_map_ref, out_ref, x, basis, leaf_map, mid_map, skeleton, sems):
     leaves, rank, rows = basis.shape
     parts = []
     for leaf in range(leaves):
@@ -58,9 +58,7 @@
         parts.append(pltpu.make_async_copy(x_ref.at[here], x.at[here], sems.at[leaf]))
         parts.append(pltpu.make_async_copy(basis_ref.at[leaf], basis.at[leaf], sems.at[leaves + leaf]))
     maps = [pltpu.make_async_copy(leaf_map_ref, leaf_map, sems.at[2 * leaves]), pltpu.make_async_copy(mid_map_ref, mid_map, sems.at[2 * leaves + 1])]
-    edge = jnp.where(lax.axis_index("inner") == 0, x.shape[0] - relay.shape[0], 0)
-    handed = pltpu.make_async_copy(x_ref.at[pl.ds(pl.multiple_of(edge, rows), relay.shape[0])], relay, sems.at[2 * leaves + 2])
-    for copy in [*parts, *maps, handed]:
+    for copy in parts + maps:
         copy.start()
     for leaf in range(leaves):
         parts[2 * leaf].wait()
@@ -71,17 +69,10 @@
     mid = dot_t(leaf_map[...], skeleton[...]).astype(jnp.bfloat16)
     out_ref[:rank, :] = mid
     out_ref[rank:, :] = dot_t(mid_map[...], mid).astype(jnp.bfloat16)
-    handed.wait()
-
-
-def join_kernel(*refs):
-    parts, plane = refs[:-1], refs[-1]
-    height = parts[0].shape[0]
-    for i, part in enumerate(parts):
-        plane[i * height : (i + 1) * height, :] = part[...]
-
-
-def pieces_kernel(x_ref, relayed, low, high, sems):
+
+
+def pieces_kernel(x_ref, relayed, *refs):
+    parts, (low, high, plane, sems) = refs[:-4], refs[-4:]
     inner = lax.axis_index("inner")
     size = low.shape[0]
     ends = (inner == lax.axis_size("inner") - 1, inner == 0)
@@ -95,6 +86,9 @@
         def _():
             pltpu.make_async_copy(x_ref.at[first : first + size], piece, sems.at[i]).start()
 
+    height = parts[0].shape[0]
+    for i, part in enumerate(parts):
+        plane[i * height : (i + 1) * height, :] = part[...]
     for i, piece in enumerate((low, high)):
         pltpu.make_async_copy(relayed, piece, sems.at[i]).wait()
 
@@ -280,35 +274,40 @@
     line = [(place(g, i), place(g, i + 1)) for g in groups for i in range(last)]
     hop = [(place(g, last), place(g + 1, last)) for g in groups[:-1]] + [(place(g, first), place(g - 1, first)) for g in groups[1:]]
 
-    one = leaves * 5 // 8
+    one = leaves // 2
     rest = leaves - one
     def kernel(body, out_shape, in_specs, out_specs, scratch, aliases=None, flops=1000):
         return call(body, out_shape, in_specs, out_specs, scratch, flops, 1000, 8 * MIB, aliases)
 
     ahead, back = lax.slice_in_dim(anomalies, rest * rows, leaves * rows), lax.slice_in_dim(anomalies, 0, one * rows)
-    x_up, ahead, back = lax.optimization_barrier((anomalies, ahead, back))
+    relay = jnp.where(inner == first, lax.slice_in_dim(anomalies, one * rows, leaves * rows), lax.slice_in_dim(anomalies, 0, rest * rows))
+    x_up, ahead, back, relay = lax.optimization_barrier((anomalies, ahead, back, relay))
+    relayed = passed(relay, hop)
     halo = [(passed(ahead, chain), passed(back, [(j, i) for i, j in chain]))]
 
     maps = (transfer_leaf.reshape(leaves * rank, rank), transfer_mid.reshape(rank, rank))
     operands = (x_up, leaf_basis, *maps)
     piece = jax.ShapeDtypeStruct((rest * rows, columns), bf16)
-    part, relay = kernel(
+    part = kernel(
         up_kernel,
-        (jax.ShapeDtypeStruct((2 * rank, columns), bf16), piece),
+        jax.ShapeDtypeStruct((2 * rank, columns), bf16),
         [ANY] * 4,
-        (VMEM, VMEM),
-        [pltpu.VMEM(x.shape, bf16) for x in operands] + [pltpu.VMEM((leaves * rank, columns), bf16), pltpu.SemaphoreType.DMA((2 * leaves + 3,))],
+        VMEM,
+        [pltpu.VMEM(x.shape, bf16) for x in operands] + [pltpu.VMEM((leaves * rank, columns), bf16), pltpu.SemaphoreType.DMA((2 * leaves + 2,))],
     )(*[held(x, pltpu.HBM) for x in operands])
     parts = [part] + [swapped(part, reach) for reach in groups[1:]]
-    relay, parts = lax.optimization_barrier((relay, parts))
-    relayed = passed(relay, hop)
     slots = leaves * near
-    plane = kernel(join_kernel, jax.ShapeDtypeStruct((leaf_size * 2 * rank, columns), bf16), [VMEM] * leaf_size, VMEM, [])(*parts)
-    plane, x_late = lax.optimization_barrier((plane, x_up))
+    parts, x_late, relayed = lax.optimization_barrier((parts, x_up, relayed))
+    low, high, plane = kernel(
+        pieces_kernel,
+        (piece, piece, jax.ShapeDtypeStruct((leaf_size * 2 * rank, columns), bf16)),
+        [ANY] * 2 + [VMEM] * leaf_size,
+        [VMEM] * 3,
+        [pltpu.SemaphoreType.DMA((2,))],
+    )(held(x_late, pltpu.HBM), relayed, *parts)
+    low, high, plane, x_late = lax.optimization_barrier((low, high, plane, x_late))
     turns = [(place(g, i), place(g, i ^ turn_of(g, inner_size))) for g in groups for i in range(inner_size)]
     planes = passed(plane, [(i, j) for i, j in turns if i != j])
-    low, high = kernel(pieces_kernel, (piece, piece), [ANY] * 2, (VMEM, VMEM), [pltpu.SemaphoreType.DMA((2,))])(held(x_late, pltpu.HBM), relayed)
-    low, high, x_late = lax.optimization_barrier((low, high, x_late))
     halo.append(
         (
             passed(low, line + [(place(g, last), place(g, first)) for g in groups[1:]]),
@@ -327,12 +326,13 @@
         flops=1000,
     )(near_ids, *[held(x, pltpu.HBM) for x in (x_late, near_blocks.reshape(slots, rows, rows), *later)])
     blocks = held(blocks, pltpu.VMEM)
-    halo[0], total = lax.optimization_barrier((halo[0], total))
+    planes, halo[0], total = lax.optimization_barrier((planes, halo[0], total))
+    others = [swapped(planes, reach) for reach in range(1, inner_size)]
+    total, planes = lax.optimization_barrier((total, planes))
     total = kernel(functools.partial(wave_kernel, one), wide, [SMEM] + [VMEM] * 4, VMEM, lists * 2, aliases={4: 0}, flops=10**10)(
         near_ids, *halo[0], blocks, held(total, pltpu.VMEM)
     )
-    planes, total = lax.optimization_barrier((planes, total))
-    found = [planes] + [swapped(planes, reach) for reach in range(1, inner_size)]
+    others, total = lax.optimization_barrier((others, total))
     out, _ = kernel(
         functools.partial(close_kernel, one, leaf_size, inner_size),
         (jax.ShapeDtypeStruct(anomalies.shape, bf16), wide),
@@ -345,7 +345,7 @@
             pltpu.SemaphoreType.DMA((leaves,)),
         ],
         aliases={12 + inner_size: 1},
-    )(near_ids, far_ids, far_count, *halo[1], blocks, plane, *found, *later, held(total, pltpu.VMEM))
+    )(near_ids, far_ids, far_count, *halo[1], blocks, plane, planes, *others, *later, held(total, pltpu.VMEM))
     return out
 
 

time: 60.6 us -> 57.2 us (0.944)
  the two profiles are of different devices: /device:TPU:0 before, /device:TPU:1 now
where the time goes in v13:
time: 57.2 us; the launch traced here: 56.1 us
  starting transfers between devices  24.6 us (43%)
  Pallas kernels  20.8 us (36%)
  waiting for transfers between devices  8.61 us (15%)
  other arithmetic  1.3 us (2%)
  between operations  0.78 us (1%)
    ppermute x6, starting transfers between devices, passed(): return lax.ppermute(x, ('leaf', 'inner'), pairs)  19.3 us
    pallas_call x1, Pallas kernels, local(): kernel(own_kernel, [wide, resident(slots, rows, rows)] + [resident(*x.sha...  9.77 us
    ppermute x6, waiting for transfers between devices, swapped(): return lax.ppermute(x, 'leaf', [(i, i ^ reach) for i in groups])  6.04 us
    ppermute x6, starting transfers between devices, swapped(): return lax.ppermute(x, 'leaf', [(i, i ^ reach) for i in groups])  5.33 us
    pallas_call x1, Pallas kernels, local(): kernel(functools.partial(wave_kernel, one), wide, [SMEM] + [VMEM] * 4, VM...  3.64 us
    pallas_call x1, Pallas kernels, local(): kernel(functools.partial(close_kernel, one, leaf_size, inner_size), (jax....  3.6 us
    pallas_call x1, Pallas kernels, local(): kernel(up_kernel, jax.ShapeDtypeStruct((2 * rank, columns), bf16), [ANY]...  2.69 us
    ppermute x6, waiting for transfers between devices, passed(): return lax.ppermute(x, ('leaf', 'inner'), pairs)  2.57 us
  transfers between devices with their start and end apart: 12, of which 4 were waited for; matrix products, arithmetic and copies ran while one was open for 0% of the time, Pallas kernels for 31%

profile of v13, /device:TPU:1, one launch (start us, length us, event | category | flops | bytes accessed | tf_op | source)
XLA Modules:
  0.0 56.1 jit_solution(537886109607540137)
XLA Ops:
  0.0 1.3 %broadcast_select_fusion = (bf16[2048,128]{1,0:T(8,128)(2,1)S(1)}, bf16[2048,128]{1,0:T(8,128)(2,1)S(1)}, bf16[2048,128]{1,0:T(8,128)(2,1)S(1)}) fusion(pred[]{:T(512)S(6)} %eq.3, bf16[4096,128]{1,0:T(8,128)(2,1)} %x_hbm), kind=kLoop, calls=%fused_computation | loop fusion | flops 262144 | bytes 2621441 | tf_op jit(solution)/shard_map/jit(_where)/select_n | solution.py:283
  1.3 0.0 copy-start
  1.3 2.0 %collective-permute-start.3 = (bf16[2048,128]{1,0:T(8,128)(2,1)S(1)}, bf16[2048,128]{1,0:T(8,128)(2,1)S(1)}, u32[]{:S(2)}, u32[]{:S(2)}) collective-permute-start(bf16[2048,128]{1,0:T(8,128)(2,1)S(1)} %get-tuple-element.41), channel_id=1, source_target_pairs={{3,7},{7,11},{11,15},{4,0},{8,4},{12,8},{19,23},{23,27},{27,31},{2... | collective-permute-start | bytes 1572872 | tf_op jit(solution)/shard_map/ppermute | solution.py:268
  3.3 2.8 %collective-permute-start.7 = (bf16[2048,128]{1,0:T(8,128)(2,1)S(1)}, bf16[2048,128]{1,0:T(8,128)(2,1)S(1)}, u32[]{:S(2)}, u32[]{:S(2)}) collective-permute-start(bf16[2048,128]{1,0:T(8,128)(2,1)S(1)} %get-tuple-element.56), channel_id=1, source_target_pairs={{0,1},{1,2},{2,3},{3,4},{4,5},{5,6},{6,7},{7,8},{8,9},{9,10},{10,1... | collective-permute-start | bytes 1572872 | tf_op jit(solution)/shard_map/ppermute | solution.py:268
  6.1 5.6 %collective-permute-start.8 = (bf16[2048,128]{1,0:T(8,128)(2,1)S(1)}, bf16[2048,128]{1,0:T(8,128)(2,1)S(1)}, u32[]{:S(2)}, u32[]{:S(2)}) collective-permute-start(bf16[2048,128]{1,0:T(8,128)(2,1)S(1)} %get-tuple-element.57), channel_id=1, source_target_pairs={{1,0},{2,1},{3,2},{4,3},{5,4},{6,5},{7,6},{8,7},{9,8},{10,9},{11,1... | collective-permute-start | bytes 1572872 | tf_op jit(solution)/shard_map/ppermute | solution.py:268
  11.7 2.7 %shard_map.100.refs_0_ = bf16[128,128]{1,0:T(8,128)(2,1)S(1)} custom-call(bf16[4096,128]{1,0:T(8,128)(2,1)} %x_hbm, bf16[8,64,512]{2,1,0:T(8,128)(2,1)} %refs_4_.1, bf16[512,64]{1,0:T(8,128)(2,1)} %bitcast.6, bf16[64,64]{1,0:T(8,128)(2,1)} %bitcast.10), custom_call_target="tpu_custom_call" | custom-call | flops 1000 | bytes 1000 | tf_op jit(solution)/shard_map/pallas_call | solution.py:291
  14.3 2.9 %collective-permute-start.2 = (bf16[128,128]{1,0:T(8,128)(2,1)S(1)}, bf16[128,128]{1,0:T(8,128)(2,1)S(1)}, u32[]{:S(2)}, u32[]{:S(2)}) collective-permute-start(bf16[128,128]{1,0:T(8,128)(2,1)S(1)} %shard_map.100.refs_0_), channel_id=1, source_target_pairs={{0,12},{4,8},{8,4},{12,0},{1,13},{5,9},{9,5},{13,1},{2,14},{6,10},... | collective-permute-start | bytes 98312 | tf_op jit(solution)/shard_map/ppermute | solution.py:271
  17.3 0.0 collective-permute-start.1
  17.3 1.9 %collective-permute-done.2.refs_3_ = bf16[128,128]{1,0:T(8,128)(2,1)S(1)} collective-permute-done((bf16[128,128]{1,0:T(8,128)(2,1)S(1)}, bf16[128,128]{1,0:T(8,128)(2,1)S(1)}, u32[]{:S(2)}, u32[]{:S(2)}) %collective-permute-start.2) | collective-permute-done | bytes 32800 | tf_op jit(solution)/shard_map/ppermute | solution.py:271
  19.2 0.0 collective-permute-start
  19.2 1.3 %collective-permute-done.1.refs_2_ = bf16[128,128]{1,0:T(8,128)(2,1)S(1)} collective-permute-done((bf16[128,128]{1,0:T(8,128)(2,1)S(1)}, bf16[128,128]{1,0:T(8,128)(2,1)S(1)}, u32[]{:S(2)}, u32[]{:S(2)}) %collective-permute-start.1) | collective-permute-done | bytes 32800 | tf_op jit(solution)/shard_map/ppermute | solution.py:271
  20.4 0.0 collective-permute-done.refs_1_
  20.4 0.0 collective-permute-done.3.relayed
  20.4 1.1 %shard_map.101 = (bf16[2048,128]{1,0:T(8,128)(2,1)S(1)}, bf16[2048,128]{1,0:T(8,128)(2,1)S(1)}, bf16[512,128]{1,0:T(8,128)(2,1)S(1)}) custom-call(bf16[4096,128]{1,0:T(8,128)(2,1)} %x_hbm, bf16[2048,128]{1,0:T(8,128)(2,1)S(1)} %collective-permute-done.3.relayed, bf16[128,128]{1,0:T(8,128)(2,1)S(1)} %shard_map.100.refs_0_, ...), custom_call_target="tpu_custom_call" | custom-call | flops 1000 | bytes 1000 | tf_op jit(solution)/shard_map/pallas_call | solution.py:301
  21.5 1.9 %collective-permute-start.6 = (bf16[512,128]{1,0:T(8,128)(2,1)S(1)}, bf16[512,128]{1,0:T(8,128)(2,1)S(1)}, u32[]{:S(2)}, u32[]{:S(2)}) collective-permute-start(bf16[512,128]{1,0:T(8,128)(2,1)S(1)} %get-tuple-element.55.plane), channel_id=1, source_target_pairs={{0,2},{1,3},{2,0},{3,1},{4,5},{5,4},{6,7},{7,6},{12,15},{13,14},{1... | collective-permute-start | bytes 393224 | tf_op jit(solution)/shard_map/ppermute | solution.py:268
  24.1 3.4 %collective-permute-start.4 = (bf16[2048,128]{1,0:T(8,128)(2,1)S(1)}, bf16[2048,128]{1,0:T(8,128)(2,1)S(1)}, u32[]{:S(2)}, u32[]{:S(2)}) collective-permute-start(bf16[2048,128]{1,0:T(8,128)(2,1)S(1)} %get-tuple-element.51), channel_id=1, source_target_pairs={{0,1},{1,2},{2,3},{4,5},{5,6},{6,7},{8,9},{9,10},{10,11},{12,13},{... | collective-permute-start | bytes 1572872 | tf_op jit(solution)/shard_map/ppermute | solution.py:268
  27.4 3.7 %collective-permute-start.5 = (bf16[2048,128]{1,0:T(8,128)(2,1)S(1)}, bf16[2048,128]{1,0:T(8,128)(2,1)S(1)}, u32[]{:S(2)}, u32[]{:S(2)}) collective-permute-start(bf16[2048,128]{1,0:T(8,128)(2,1)S(1)} %get-tuple-element.52), channel_id=1, source_target_pairs={{1,0},{2,1},{3,2},{5,4},{6,5},{7,6},{9,8},{10,9},{11,10},{13,12},{... | collective-permute-start | bytes 1572872 | tf_op jit(solution)/shard_map/ppermute | solution.py:268
  31.2 0.0 copy-done
  31.2 9.8 %shard_map.102 = (f32[4096,128]{1,0:T(8,128)S(1)}, bf16[40,512,512]{2,1,0:T(8,128)(2,1)S(1)}, bf16[4,64,64]{2,1,0:T(8,128)(2,1)S(1)}, bf16[4,64,64]{2,1,0:T(8,12...) custom-call(s32[8,5]{1,0:T(8,128)S(1)} %copy-done, ...), custom_call_target="tpu_custom_call" | custom-call | flops 1000 | bytes 1000 | tf_op jit(solution)/shard_map/pallas_call | solution.py:320
  40.9 0.0 collective-permute-done.7.before
  41.0 0.0 collective-permute-done.8.after
  41.0 0.0 collective-permute-done.6.refs_0_
  41.0 0.9 %collective-permute-start.11 = (bf16[512,128]{1,0:T(8,128)(2,1)S(1)}, bf16[512,128]{1,0:T(8,128)(2,1)S(1)}, u32[]{:S(2)}, u32[]{:S(2)}) collective-permute-start(bf16[512,128]{1,0:T(8,128)(2,1)S(1)} %collective-permute-done.6.refs_0_), channel_id=1, source_target_pairs={{0,12},{4,8},{8,4},{12,0},{1,13},{5,9},{9,5},{13,1},{2,14},{6,10},... | collective-permute-start | bytes 393224 | tf_op jit(solution)/shard_map/ppermute | solution.py:271
  41.9 1.5 %collective-permute-start.10 = (bf16[512,128]{1,0:T(8,128)(2,1)S(1)}, bf16[512,128]{1,0:T(8,128)(2,1)S(1)}, u32[]{:S(2)}, u32[]{:S(2)}) collective-permute-start(bf16[512,128]{1,0:T(8,128)(2,1)S(1)} %collective-permute-done.6.refs_0_), channel_id=1, source_target_pairs={{0,8},{4,12},{8,0},{12,4},{1,9},{5,13},{9,1},{13,5},{2,10},{6,14},... | collective-permute-start | bytes 393224 | tf_op jit(solution)/shard_map/ppermute | solution.py:271
  43.4 0.0 collective-permute-start.9
  43.4 0.0 copy-start.1
  43.4 3.6 %shard_map.103.refs_9_ = f32[4096,128]{1,0:T(8,128)S(1)} custom-call(s32[8,5]{1,0:T(8,128)S(1)} %copy-done, bf16[2048,128]{1,0:T(8,128)(2,1)S(1)} %collective-permute-done.7.before, bf16[2048,128]{1,0:T(8,128)(2,1)S(1)} %collective-permute-done.8.after, bf16[40,512,512]{2,1,0:T(8,128)(2,1)S(1)} %get-tuple-element.54.blocks, ...), custom_call_target="tpu_custom_call", output_to_operand_aliasing={{}: (4, {})} | custom-call | flops 10000000000 | bytes 1000 | tf_op jit(solution)/shard_map/pallas_call | solution.py:332
  47.0 0.0 collective-permute-done.11.refs_3_
  47.1 2.9 %collective-permute-done.10.refs_2_ = bf16[512,128]{1,0:T(8,128)(2,1)S(1)} collective-permute-done((bf16[512,128]{1,0:T(8,128)(2,1)S(1)}, bf16[512,128]{1,0:T(8,128)(2,1)S(1)}, u32[]{:S(2)}, u32[]{:S(2)}) %collective-permute-start.10) | collective-permute-done | bytes 131104 | tf_op jit(solution)/shard_map/ppermute | solution.py:271
  49.9 0.0 collective-permute-done.9.refs_1_
  49.9 0.0 collective-permute-done.4.before
  49.9 2.6 %collective-permute-done.5.after = bf16[2048,128]{1,0:T(8,128)(2,1)S(1)} collective-permute-done((bf16[2048,128]{1,0:T(8,128)(2,1)S(1)}, bf16[2048,128]{1,0:T(8,128)(2,1)S(1)}, u32[]{:S(2)}, u32[]{:S(2)}) %collective-permute-start.5) | collective-permute-done | bytes 524320 | tf_op jit(solution)/shard_map/ppermute | solution.py:268
  52.5 0.0 copy-done.1
  52.5 3.6 %shard_map.104 = (bf16[4096,128]{1,0:T(8,128)(2,1)}, f32[4096,128]{1,0:T(8,128)S(1)}) custom-call(s32[8,5]{1,0:T(8,128)S(1)} %copy-done, s32[1,4]{1,0:T(1,128)S(1)} %copy-done.1, s32[1]{0:T(128)S(6)} %copy.15.far_count, bf16[2048,128]{1,0:T(8,128)(2,1)S(1)} %collective-permute-done.4.before, ...), custom_call_target="tpu_custom_call", output_to_operand_aliasing={{1}: (16, {})} | custom-call | flops 1000 | bytes 1000 | tf_op jit(solution)/shard_map/pallas_call | solution.py:336
Async XLA Ops:
  1.3 29.9 %copy-start = (s32[8,5]{1,0:T(8,128)S(1)}, s32[8,5]{1,0:T(8,128)}, u32[]{:S(2)}) copy-start(s32[8,5]{1,0:T(8,128)} %ids_ref.5) | copy-start | bytes 484
  1.3 19.1 %collective-permute-start.3 = (bf16[2048,128]{1,0:T(8,128)(2,1)S(1)}, bf16[2048,128]{1,0:T(8,128)(2,1)S(1)}, u32[]{:S(2)}, u32[]{:S(2)}) collective-permute-start(bf16[2048,128]{1,0:T(8,128)(2,1)S(1)} %get-tuple-element.41), channel_id=1, source_target_pairs={{3,7},{7,11},{11,15},{4,0},{8,4},{12,8},{19,23},{23,27},{27,31},{2... | collective-permute-start | bytes 1572872 | tf_op jit(solution)/shard_map/ppermute | solution.py:268
  3.3 37.7 %collective-permute-start.7 = (bf16[2048,128]{1,0:T(8,128)(2,1)S(1)}, bf16[2048,128]{1,0:T(8,128)(2,1)S(1)}, u32[]{:S(2)}, u32[]{:S(2)}) collective-permute-start(bf16[2048,128]{1,0:T(8,128)(2,1)S(1)} %get-tuple-element.56), channel_id=1, source_target_pairs={{0,1},{1,2},{2,3},{3,4},{4,5},{5,6},{6,7},{7,8},{8,9},{9,10},{10,1... | collective-permute-start | bytes 1572872 | tf_op jit(solution)/shard_map/ppermute | solution.py:268
  6.1 34.9 %collective-permute-start.8 = (bf16[2048,128]{1,0:T(8,128)(2,1)S(1)}, bf16[2048,128]{1,0:T(8,128)(2,1)S(1)}, u32[]{:S(2)}, u32[]{:S(2)}) collective-permute-start(bf16[2048,128]{1,0:T(8,128)(2,1)S(1)} %get-tuple-element.57), channel_id=1, source_target_pairs={{1,0},{2,1},{3,2},{4,3},{5,4},{6,5},{7,6},{8,7},{9,8},{10,9},{11,1... | collective-permute-start | bytes 1572872 | tf_op jit(solution)/shard_map/ppermute | solution.py:268
  14.3 4.8 %collective-permute-start.2 = (bf16[128,128]{1,0:T(8,128)(2,1)S(1)}, bf16[128,128]{1,0:T(8,128)(2,1)S(1)}, u32[]{:S(2)}, u32[]{:S(2)}) collective-permute-start(bf16[128,128]{1,0:T(8,128)(2,1)S(1)} %shard_map.100.refs_0_), channel_id=1, source_target_pairs={{0,12},{4,8},{8,4},{12,0},{1,13},{5,9},{9,5},{13,1},{2,14},{6,10},... | collective-permute-start | bytes 98312 | tf_op jit(solution)/shard_map/ppermute | solution.py:271
  17.3 3.2 %collective-permute-start.1 = (bf16[128,128]{1,0:T(8,128)(2,1)S(1)}, bf16[128,128]{1,0:T(8,128)(2,1)S(1)}, u32[]{:S(2)}, u32[]{:S(2)}) collective-permute-start(bf16[128,128]{1,0:T(8,128)(2,1)S(1)} %shard_map.100.refs_0_), channel_id=1, source_target_pairs={{0,8},{4,12},{8,0},{12,4},{1,9},{5,13},{9,1},{13,5},{2,10},{6,14},... | collective-permute-start | bytes 98312 | tf_op jit(solution)/shard_map/ppermute | solution.py:271
  19.2 1.3 %collective-permute-start = (bf16[128,128]{1,0:T(8,128)(2,1)S(1)}, bf16[128,128]{1,0:T(8,128)(2,1)S(1)}, u32[]{:S(2)}, u32[]{:S(2)}) collective-permute-start(bf16[128,128]{1,0:T(8,128)(2,1)S(1)} %shard_map.100.refs_0_), channel_id=1, source_target_pairs={{0,4},{4,0},{8,12},{12,8},{1,5},{5,1},{9,13},{13,9},{2,6},{6,2},{1... | collective-permute-start | bytes 98312 | tf_op jit(solution)/shard_map/ppermute | solution.py:271
  21.5 19.5 %collective-permute-start.6 = (bf16[512,128]{1,0:T(8,128)(2,1)S(1)}, bf16[512,128]{1,0:T(8,128)(2,1)S(1)}, u32[]{:S(2)}, u32[]{:S(2)}) collective-permute-start(bf16[512,128]{1,0:T(8,128)(2,1)S(1)} %get-tuple-element.55.plane), channel_id=1, source_target_pairs={{0,2},{1,3},{2,0},{3,1},{4,5},{5,4},{6,7},{7,6},{12,15},{13,14},{1... | collective-permute-start | bytes 393224 | tf_op jit(solution)/shard_map/ppermute | solution.py:268
  24.1 25.9 %collective-permute-start.4 = (bf16[2048,128]{1,0:T(8,128)(2,1)S(1)}, bf16[2048,128]{1,0:T(8,128)(2,1)S(1)}, u32[]{:S(2)}, u32[]{:S(2)}) collective-permute-start(bf16[2048,128]{1,0:T(8,128)(2,1)S(1)} %get-tuple-element.51), channel_id=1, source_target_pairs={{0,1},{1,2},{2,3},{4,5},{5,6},{6,7},{8,9},{9,10},{10,11},{12,13},{... | collective-permute-start | bytes 1572872 | tf_op jit(solution)/shard_map/ppermute | solution.py:268
  27.4 25.1 %collective-permute-start.5 = (bf16[2048,128]{1,0:T(8,128)(2,1)S(1)}, bf16[2048,128]{1,0:T(8,128)(2,1)S(1)}, u32[]{:S(2)}, u32[]{:S(2)}) collective-permute-start(bf16[2048,128]{1,0:T(8,128)(2,1)S(1)} %get-tuple-element.52), channel_id=1, source_target_pairs={{1,0},{2,1},{3,2},{5,4},{6,5},{7,6},{9,8},{10,9},{11,10},{13,12},{... | collective-permute-start | bytes 1572872 | tf_op jit(solution)/shard_map/ppermute | solution.py:268
  41.0 6.1 %collective-permute-start.11 = (bf16[512,128]{1,0:T(8,128)(2,1)S(1)}, bf16[512,128]{1,0:T(8,128)(2,1)S(1)}, u32[]{:S(2)}, u32[]{:S(2)}) collective-permute-start(bf16[512,128]{1,0:T(8,128)(2,1)S(1)} %collective-permute-done.6.refs_0_), channel_id=1, source_target_pairs={{0,12},{4,8},{8,4},{12,0},{1,13},{5,9},{9,5},{13,1},{2,14},{6,10},... | collective-permute-start | bytes 393224 | tf_op jit(solution)/shard_map/ppermute | solution.py:271
  41.9 8.1 %collective-permute-start.10 = (bf16[512,128]{1,0:T(8,128)(2,1)S(1)}, bf16[512,128]{1,0:T(8,128)(2,1)S(1)}, u32[]{:S(2)}, u32[]{:S(2)}) collective-permute-start(bf16[512,128]{1,0:T(8,128)(2,1)S(1)} %collective-permute-done.6.refs_0_), channel_id=1, source_target_pairs={{0,8},{4,12},{8,0},{12,4},{1,9},{5,13},{9,1},{13,5},{2,10},{6,14},... | collective-permute-start | bytes 393224 | tf_op jit(solution)/shard_map/ppermute | solution.py:271
  43.4 6.6 %collective-permute-start.9 = (bf16[512,128]{1,0:T(8,128)(2,1)S(1)}, bf16[512,128]{1,0:T(8,128)(2,1)S(1)}, u32[]{:S(2)}, u32[]{:S(2)}) collective-permute-start(bf16[512,128]{1,0:T(8,128)(2,1)S(1)} %collective-permute-done.6.refs_0_), channel_id=1, source_target_pairs={{0,4},{4,0},{8,12},{12,8},{1,5},{5,1},{9,13},{13,9},{2,6},{6,2},{1... | collective-permute-start | bytes 393224 | tf_op jit(solution)/shard_map/ppermute | solution.py:271
  43.4 9.1 %copy-start.1 = (s32[1,4]{1,0:T(1,128)S(1)}, s32[1,4]{1,0:T(1,128)}, u32[]{:S(2)}) copy-start(s32[1,4]{1,0:T(1,128)} %far_ids.1) | copy-start | bytes 52

commit v14 on v13

--- a/solution.py
+++ b/solution.py
@@ -274,14 +274,14 @@
     line = [(place(g, i), place(g, i + 1)) for g in groups for i in range(last)]
     hop = [(place(g, last), place(g + 1, last)) for g in groups[:-1]] + [(place(g, first), place(g - 1, first)) for g in groups[1:]]
 
-    one = leaves // 2
+    one = leaves * 5 // 8
     rest = leaves - one
     def kernel(body, out_shape, in_specs, out_specs, scratch, aliases=None, flops=1000):
         return call(body, out_shape, in_specs, out_specs, scratch, flops, 1000, 8 * MIB, aliases)
 
     ahead, back = lax.slice_in_dim(anomalies, rest * rows, leaves * rows), lax.slice_in_dim(anomalies, 0, one * rows)
     relay = jnp.where(inner == first, lax.slice_in_dim(anomalies, one * rows, leaves * rows), lax.slice_in_dim(anomalies, 0, rest * rows))
-    x_up, ahead, back, relay = lax.optimization_barrier((anomalies, ahead, back, relay))
+    x_up, ahead, back = lax.optimization_barrier((anomalies, ahead, back))
     relayed = passed(relay, hop)
     halo = [(passed(ahead, chain), passed(back, [(j, i) for i, j in chain]))]
 

time: 57.2 us -> 57.8 us (1.010)
  local copies, waits for them, and re-layouts: 0.01 us -> 2.31 us
  starting transfers between devices: 24.6 us -> 26 us
  other arithmetic: 1.3 us -> 0.04 us
  waiting for transfers between devices: 8.61 us -> 7.47 us
    slice x0 -> x1, local copies, waits for them, and re-layouts: none -> 2.29 us  [local(): lax.slice_in_dim(anomalies, 0, one * rows)]
    select_n x1, other arithmetic: 1.3 us -> 0.04 us  [local(): jnp.where(inner == first, lax.slice_in_dim(anomalies, one * rows, leaves...]
    ppermute x6, starting transfers between devices: 5.33 us -> 6.58 us  [swapped(): return lax.ppermute(x, 'leaf', [(i, i ^ reach) for i in groups])]
    ppermute x6, waiting for transfers between devices: 6.04 us -> 4.87 us  [swapped(): return lax.ppermute(x, 'leaf', [(i, i ^ reach) for i in groups])]
  transfers between devices with their start and end apart: 12 -> 12, of which waited for: 4 -> 5; matrix products, arithmetic and copies ran while one was open for 0% -> 0% of each run, Pallas kernels for 31% -> 30%
where the time goes in v14:
time: 57.8 us; the launch traced here: 57.2 us
  starting transfers between devices  26 us (45%)
  Pallas kernels  20.6 us (36%)
  waiting for transfers between devices  7.47 us (13%)
  local copies, waits for them, and re-layouts  2.31 us (4%)
  between operations  0.79 us (1%)
    ppermute x6, starting transfers between devices, passed(): return lax.ppermute(x, ('leaf', 'inner'), pairs)  19.4 us
    pallas_call x1, Pallas kernels, local(): kernel(own_kernel, [wide, resident(slots, rows, rows)] + [resident(*x.sha...  9.77 us
    ppermute x6, starting transfers between devices, swapped(): return lax.ppermute(x, 'leaf', [(i, i ^ reach) for i in groups])  6.58 us
    ppermute x6, waiting for transfers between devices, swapped(): return lax.ppermute(x, 'leaf', [(i, i ^ reach) for i in groups])  4.87 us
    pallas_call x1, Pallas kernels, local(): kernel(functools.partial(wave_kernel, one), wide, [SMEM] + [VMEM] * 4, VM...  3.78 us
    pallas_call x1, Pallas kernels, local(): kernel(functools.partial(close_kernel, one, leaf_size, inner_size), (jax....  3.31 us
    pallas_call x1, Pallas kernels, local(): kernel(up_kernel, jax.ShapeDtypeStruct((2 * rank, columns), bf16), [ANY]...  2.69 us
    ppermute x6, waiting for transfers between devices, passed(): return lax.ppermute(x, ('leaf', 'inner'), pairs)  2.6 us
  transfers between devices with their start and end apart: 12, of which 5 were waited for; matrix products, arithmetic and copies ran while one was open for 0% of the time, Pallas kernels for 30%

profile of v14, /device:TPU:1, one launch (start us, length us, event | category | flops | bytes accessed | tf_op | source)
XLA Modules:
  0.0 57.2 jit_solution(4386667081437770314)
XLA Ops:
  0.0 0.0 copy-start.2
  0.0 2.3 %fusion = (bf16[2560,128]{1,0:T(8,128)(2,1)S(1)}, bf16[2560,128]{1,0:T(8,128)(2,1)}) fusion(bf16[4096,128]{1,0:T(8,128)(2,1)} %x_hbm), kind=kLoop, calls=%fused_computation.1 | loop fusion | bytes 2621440 | tf_op jit(solution)/shard_map/slice | solution.py:282
  2.3 4.0 %collective-permute-start.7 = (bf16[2560,128]{1,0:T(8,128)(2,1)}, bf16[2560,128]{1,0:T(8,128)(2,1)S(1)}, u32[]{:S(2)}, u32[]{:S(2)}) collective-permute-start(bf16[2560,128]{1,0:T(8,128)(2,1)} %get-tuple-element.54), channel_id=1, source_target_pairs={{0,1},{1,2},{2,3},{3,4},{4,5},{5,6},{6,7},{7,8},{8,9},{9,10},{10,1... | collective-permute-start | bytes 1966088 | tf_op jit(solution)/shard_map/ppermute | solution.py:268
  6.3 4.5 %collective-permute-start.8 = (bf16[2560,128]{1,0:T(8,128)(2,1)S(1)}, bf16[2560,128]{1,0:T(8,128)(2,1)S(1)}, u32[]{:S(2)}, u32[]{:S(2)}) collective-permute-start(bf16[2560,128]{1,0:T(8,128)(2,1)S(1)} %get-tuple-element.55), channel_id=1, source_target_pairs={{1,0},{2,1},{3,2},{4,3},{5,4},{6,5},{7,6},{8,7},{9,8},{10,9},{11,1... | collective-permute-start | bytes 1966088 | tf_op jit(solution)/shard_map/ppermute | solution.py:268
  10.8 0.0 copy-done.2
  10.9 0.0 copy-start
  10.9 1.9 %collective-permute-start.3 = (bf16[1536,128]{1,0:T(8,128)(2,1)S(1)}, bf16[1536,128]{1,0:T(8,128)(2,1)S(1)}, u32[]{:S(2)}, u32[]{:S(2)}) collective-permute-start(bf16[1536,128]{1,0:T(8,128)(2,1)S(1)} %slice_select_fusion), channel_id=1, source_target_pairs={{3,7},{7,11},{11,15},{4,0},{8,4},{12,8},{19,23},{23,27},{27,31},{2... | collective-permute-start | bytes 1179656 | tf_op jit(solution)/shard_map/ppermute | solution.py:268
  12.8 2.7 %shard_map.100.refs_0_ = bf16[128,128]{1,0:T(8,128)(2,1)S(1)} custom-call(bf16[4096,128]{1,0:T(8,128)(2,1)} %x_hbm, bf16[8,64,512]{2,1,0:T(8,128)(2,1)} %refs_4_.1, bf16[512,64]{1,0:T(8,128)(2,1)} %bitcast.6, bf16[64,64]{1,0:T(8,128)(2,1)} %bitcast.10), custom_call_target="tpu_custom_call" | custom-call | flops 1000 | bytes 1000 | tf_op jit(solution)/shard_map/pallas_call | solution.py:291
  15.5 0.1 collective-permute-start
  15.6 2.5 %collective-permute-start.1 = (bf16[128,128]{1,0:T(8,128)(2,1)S(1)}, bf16[128,128]{1,0:T(8,128)(2,1)S(1)}, u32[]{:S(2)}, u32[]{:S(2)}) collective-permute-start(bf16[128,128]{1,0:T(8,128)(2,1)S(1)} %shard_map.100.refs_0_), channel_id=1, source_target_pairs={{0,8},{4,12},{8,0},{12,4},{1,9},{5,13},{9,1},{13,5},{2,10},{6,14},... | collective-permute-start | bytes 98312 | tf_op jit(solution)/shard_map/ppermute | solution.py:271
  18.2 0.0 collective-permute-done.refs_1_
  18.2 1.2 %collective-permute-start.2 = (bf16[128,128]{1,0:T(8,128)(2,1)S(1)}, bf16[128,128]{1,0:T(8,128)(2,1)S(1)}, u32[]{:S(2)}, u32[]{:S(2)}) collective-permute-start(bf16[128,128]{1,0:T(8,128)(2,1)S(1)} %shard_map.100.refs_0_), channel_id=1, source_target_pairs={{0,12},{4,8},{8,4},{12,0},{1,13},{5,9},{9,5},{13,1},{2,14},{6,10},... | collective-permute-start | bytes 98312 | tf_op jit(solution)/shard_map/ppermute | solution.py:271
  19.3 0.8 %collective-permute-done.1.refs_2_ = bf16[128,128]{1,0:T(8,128)(2,1)S(1)} collective-permute-done((bf16[128,128]{1,0:T(8,128)(2,1)S(1)}, bf16[128,128]{1,0:T(8,128)(2,1)S(1)}, u32[]{:S(2)}, u32[]{:S(2)}) %collective-permute-start.1) | collective-permute-done | bytes 32800 | tf_op jit(solution)/shard_map/ppermute | solution.py:271
  20.2 2.2 %collective-permute-done.2.refs_3_ = bf16[128,128]{1,0:T(8,128)(2,1)S(1)} collective-permute-done((bf16[128,128]{1,0:T(8,128)(2,1)S(1)}, bf16[128,128]{1,0:T(8,128)(2,1)S(1)}, u32[]{:S(2)}, u32[]{:S(2)}) %collective-permute-start.2) | collective-permute-done | bytes 32800 | tf_op jit(solution)/shard_map/ppermute | solution.py:271
  22.3 0.0 collective-permute-done.3.relayed
  22.3 1.0 %shard_map.101 = (bf16[1536,128]{1,0:T(8,128)(2,1)S(1)}, bf16[1536,128]{1,0:T(8,128)(2,1)S(1)}, bf16[512,128]{1,0:T(8,128)(2,1)S(1)}) custom-call(bf16[4096,128]{1,0:T(8,128)(2,1)} %x_hbm, bf16[1536,128]{1,0:T(8,128)(2,1)S(1)} %collective-permute-done.3.relayed, bf16[128,128]{1,0:T(8,128)(2,1)S(1)} %shard_map.100.refs_0_, ...), custom_call_target="tpu_custom_call" | custom-call | flops 1000 | bytes 1000 | tf_op jit(solution)/shard_map/pallas_call | solution.py:301
  23.4 1.9 %collective-permute-start.6 = (bf16[512,128]{1,0:T(8,128)(2,1)S(1)}, bf16[512,128]{1,0:T(8,128)(2,1)S(1)}, u32[]{:S(2)}, u32[]{:S(2)}) collective-permute-start(bf16[512,128]{1,0:T(8,128)(2,1)S(1)} %get-tuple-element.53.plane), channel_id=1, source_target_pairs={{0,2},{1,3},{2,0},{3,1},{4,5},{5,4},{6,7},{7,6},{12,15},{13,14},{1... | collective-permute-start | bytes 393224 | tf_op jit(solution)/shard_map/ppermute | solution.py:268
  25.9 3.4 %collective-permute-start.4 = (bf16[1536,128]{1,0:T(8,128)(2,1)S(1)}, bf16[1536,128]{1,0:T(8,128)(2,1)S(1)}, u32[]{:S(2)}, u32[]{:S(2)}) collective-permute-start(bf16[1536,128]{1,0:T(8,128)(2,1)S(1)} %get-tuple-element.49), channel_id=1, source_target_pairs={{0,1},{1,2},{2,3},{4,5},{5,6},{6,7},{8,9},{9,10},{10,11},{12,13},{... | collective-permute-start | bytes 1179656 | tf_op jit(solution)/shard_map/ppermute | solution.py:268
  29.3 3.7 %collective-permute-start.5 = (bf16[1536,128]{1,0:T(8,128)(2,1)S(1)}, bf16[1536,128]{1,0:T(8,128)(2,1)S(1)}, u32[]{:S(2)}, u32[]{:S(2)}) collective-permute-start(bf16[1536,128]{1,0:T(8,128)(2,1)S(1)} %get-tuple-element.50), channel_id=1, source_target_pairs={{1,0},{2,1},{3,2},{5,4},{6,5},{7,6},{9,8},{10,9},{11,10},{13,12},{... | collective-permute-start | bytes 1179656 | tf_op jit(solution)/shard_map/ppermute | solution.py:268
  33.0 0.0 copy-done
  33.0 9.8 %shard_map.102 = (f32[4096,128]{1,0:T(8,128)S(1)}, bf16[40,512,512]{2,1,0:T(8,128)(2,1)S(1)}, bf16[4,64,64]{2,1,0:T(8,128)(2,1)S(1)}, bf16[4,64,64]{2,1,0:T(8,12...) custom-call(s32[8,5]{1,0:T(8,128)S(1)} %copy-done, ...), custom_call_target="tpu_custom_call" | custom-call | flops 1000 | bytes 1000 | tf_op jit(solution)/shard_map/pallas_call | solution.py:320
  42.8 0.4 collective-permute-done.6.refs_0_
  43.2 0.0 collective-permute-done.7.before
  43.2 0.0 collective-permute-done.8.after
  43.2 0.0 collective-permute-start.10
  43.2 2.8 %collective-permute-start.11 = (bf16[512,128]{1,0:T(8,128)(2,1)S(1)}, bf16[512,128]{1,0:T(8,128)(2,1)S(1)}, u32[]{:S(2)}, u32[]{:S(2)}) collective-permute-start(bf16[512,128]{1,0:T(8,128)(2,1)S(1)} %collective-permute-done.6.refs_0_), channel_id=1, source_target_pairs={{0,12},{4,8},{8,4},{12,0},{1,13},{5,9},{9,5},{13,1},{2,14},{6,10},... | collective-permute-start | bytes 393224 | tf_op jit(solution)/shard_map/ppermute | solution.py:271
  46.0 0.0 collective-permute-start.9
  46.0 0.0 copy-start.1
  46.0 3.8 %shard_map.103.refs_9_ = f32[4096,128]{1,0:T(8,128)S(1)} custom-call(s32[8,5]{1,0:T(8,128)S(1)} %copy-done, bf16[2560,128]{1,0:T(8,128)(2,1)S(1)} %collective-permute-done.7.before, bf16[2560,128]{1,0:T(8,128)(2,1)S(1)} %collective-permute-done.8.after, bf16[40,512,512]{2,1,0:T(8,128)(2,1)S(1)} %get-tuple-element.52.blocks, ...), custom_call_target="tpu_custom_call", output_to_operand_aliasing={{}: (4, {})} | custom-call | flops 10000000000 | bytes 1000 | tf_op jit(solution)/shard_map/pallas_call | solution.py:332
  49.8 0.0 collective-permute-done.10.refs_2_
  49.8 1.9 %collective-permute-done.11.refs_3_ = bf16[512,128]{1,0:T(8,128)(2,1)S(1)} collective-permute-done((bf16[512,128]{1,0:T(8,128)(2,1)S(1)}, bf16[512,128]{1,0:T(8,128)(2,1)S(1)}, u32[]{:S(2)}, u32[]{:S(2)}) %collective-permute-start.11) | collective-permute-done | bytes 131104 | tf_op jit(solution)/shard_map/ppermute | solution.py:271
  51.7 0.0 collective-permute-done.9.refs_1_
  51.7 0.0 collective-permute-done.4.before
  51.7 2.2 %collective-permute-done.5.after = bf16[1536,128]{1,0:T(8,128)(2,1)S(1)} collective-permute-done((bf16[1536,128]{1,0:T(8,128)(2,1)S(1)}, bf16[1536,128]{1,0:T(8,128)(2,1)S(1)}, u32[]{:S(2)}, u32[]{:S(2)}) %collective-permute-start.5) | collective-permute-done | bytes 393248 | tf_op jit(solution)/shard_map/ppermute | solution.py:268
  53.9 0.0 copy-done.1
  53.9 3.3 %shard_map.104 = (bf16[4096,128]{1,0:T(8,128)(2,1)}, f32[4096,128]{1,0:T(8,128)S(1)}) custom-call(s32[8,5]{1,0:T(8,128)S(1)} %copy-done, s32[1,4]{1,0:T(1,128)S(1)} %copy-done.1, s32[1]{0:T(128)S(6)} %copy.15.far_count, bf16[1536,128]{1,0:T(8,128)(2,1)S(1)} %collective-permute-done.4.before, ...), custom_call_target="tpu_custom_call", output_to_operand_aliasing={{1}: (16, {})} | custom-call | flops 1000 | bytes 1000 | tf_op jit(solution)/shard_map/pallas_call | solution.py:336
  (1 shorter events, 0.0 us)
Async XLA Ops:
  0.0 10.8 %copy-start.2 = (bf16[4096,128]{1,0:T(8,128)(2,1)S(1)}, bf16[4096,128]{1,0:T(8,128)(2,1)}, u32[]{:S(2)}) copy-start(bf16[4096,128]{1,0:T(8,128)(2,1)} %x_hbm) | copy-start | bytes 3145732
  2.3 40.9 %collective-permute-start.7 = (bf16[2560,128]{1,0:T(8,128)(2,1)}, bf16[2560,128]{1,0:T(8,128)(2,1)S(1)}, u32[]{:S(2)}, u32[]{:S(2)}) collective-permute-start(bf16[2560,128]{1,0:T(8,128)(2,1)} %get-tuple-element.54), channel_id=1, source_target_pairs={{0,1},{1,2},{2,3},{3,4},{4,5},{5,6},{6,7},{7,8},{8,9},{9,10},{10,1... | collective-permute-start | bytes 1966088 | tf_op jit(solution)/shard_map/ppermute | solution.py:268
  6.3 36.9 %collective-permute-start.8 = (bf16[2560,128]{1,0:T(8,128)(2,1)S(1)}, bf16[2560,128]{1,0:T(8,128)(2,1)S(1)}, u32[]{:S(2)}, u32[]{:S(2)}) collective-permute-start(bf16[2560,128]{1,0:T(8,128)(2,1)S(1)} %get-tuple-element.55), channel_id=1, source_target_pairs={{1,0},{2,1},{3,2},{4,3},{5,4},{6,5},{7,6},{8,7},{9,8},{10,9},{11,1... | collective-permute-start | bytes 1966088 | tf_op jit(solution)/shard_map/ppermute | solution.py:268
  10.9 22.2 %copy-start = (s32[8,5]{1,0:T(8,128)S(1)}, s32[8,5]{1,0:T(8,128)}, u32[]{:S(2)}) copy-start(s32[8,5]{1,0:T(8,128)} %ids_ref.5) | copy-start | bytes 484
  10.9 11.4 %collective-permute-start.3 = (bf16[1536,128]{1,0:T(8,128)(2,1)S(1)}, bf16[1536,128]{1,0:T(8,128)(2,1)S(1)}, u32[]{:S(2)}, u32[]{:S(2)}) collective-permute-start(bf16[1536,128]{1,0:T(8,128)(2,1)S(1)} %slice_select_fusion), channel_id=1, source_target_pairs={{3,7},{7,11},{11,15},{4,0},{8,4},{12,8},{19,23},{23,27},{27,31},{2... | collective-permute-start | bytes 1179656 | tf_op jit(solution)/shard_map/ppermute | solution.py:268
  15.5 2.6 %collective-permute-start = (bf16[128,128]{1,0:T(8,128)(2,1)S(1)}, bf16[128,128]{1,0:T(8,128)(2,1)S(1)}, u32[]{:S(2)}, u32[]{:S(2)}) collective-permute-start(bf16[128,128]{1,0:T(8,128)(2,1)S(1)} %shard_map.100.refs_0_), channel_id=1, source_target_pairs={{0,4},{4,0},{8,12},{12,8},{1,5},{5,1},{9,13},{13,9},{2,6},{6,2},{1... | collective-permute-start | bytes 98312 | tf_op jit(solution)/shard_map/ppermute | solution.py:271
  15.6 4.5 %collective-permute-start.1 = (bf16[128,128]{1,0:T(8,128)(2,1)S(1)}, bf16[128,128]{1,0:T(8,128)(2,1)S(1)}, u32[]{:S(2)}, u32[]{:S(2)}) collective-permute-start(bf16[128,128]{1,0:T(8,128)(2,1)S(1)} %shard_map.100.refs_0_), channel_id=1, source_target_pairs={{0,8},{4,12},{8,0},{12,4},{1,9},{5,13},{9,1},{13,5},{2,10},{6,14},... | collective-permute-start | bytes 98312 | tf_op jit(solution)/shard_map/ppermute | solution.py:271
  18.2 4.2 %collective-permute-start.2 = (bf16[128,128]{1,0:T(8,128)(2,1)S(1)}, bf16[128,128]{1,0:T(8,128)(2,1)S(1)}, u32[]{:S(2)}, u32[]{:S(2)}) collective-permute-start(bf16[128,128]{1,0:T(8,128)(2,1)S(1)} %shard_map.100.refs_0_), channel_id=1, source_target_pairs={{0,12},{4,8},{8,4},{12,0},{1,13},{5,9},{9,5},{13,1},{2,14},{6,10},... | collective-permute-start | bytes 98312 | tf_op jit(solution)/shard_map/ppermute | solution.py:271
  23.4 19.8 %collective-permute-start.6 = (bf16[512,128]{1,0:T(8,128)(2,1)S(1)}, bf16[512,128]{1,0:T(8,128)(2,1)S(1)}, u32[]{:S(2)}, u32[]{:S(2)}) collective-permute-start(bf16[512,128]{1,0:T(8,128)(2,1)S(1)} %get-tuple-element.53.plane), channel_id=1, source_target_pairs={{0,2},{1,3},{2,0},{3,1},{4,5},{5,4},{6,7},{7,6},{12,15},{13,14},{1... | collective-permute-start | bytes 393224 | tf_op jit(solution)/shard_map/ppermute | solution.py:268
  25.9 25.7 %collective-permute-start.4 = (bf16[1536,128]{1,0:T(8,128)(2,1)S(1)}, bf16[1536,128]{1,0:T(8,128)(2,1)S(1)}, u32[]{:S(2)}, u32[]{:S(2)}) collective-permute-start(bf16[1536,128]{1,0:T(8,128)(2,1)S(1)} %get-tuple-element.49), channel_id=1, source_target_pairs={{0,1},{1,2},{2,3},{4,5},{5,6},{6,7},{8,9},{9,10},{10,11},{12,13},{... | collective-permute-start | bytes 1179656 | tf_op jit(solution)/shard_map/ppermute | solution.py:268
  29.3 24.6 %collective-permute-start.5 = (bf16[1536,128]{1,0:T(8,128)(2,1)S(1)}, bf16[1536,128]{1,0:T(8,128)(2,1)S(1)}, u32[]{:S(2)}, u32[]{:S(2)}) collective-permute-start(bf16[1536,128]{1,0:T(8,128)(2,1)S(1)} %get-tuple-element.50), channel_id=1, source_target_pairs={{1,0},{2,1},{3,2},{5,4},{6,5},{7,6},{9,8},{10,9},{11,10},{13,12},{... | collective-permute-start | bytes 1179656 | tf_op jit(solution)/shard_map/ppermute | solution.py:268
  43.2 6.6 %collective-permute-start.10 = (bf16[512,128]{1,0:T(8,128)(2,1)S(1)}, bf16[512,128]{1,0:T(8,128)(2,1)S(1)}, u32[]{:S(2)}, u32[]{:S(2)}) collective-permute-start(bf16[512,128]{1,0:T(8,128)(2,1)S(1)} %collective-permute-done.6.refs_0_), channel_id=1, source_target_pairs={{0,8},{4,12},{8,0},{12,4},{1,9},{5,13},{9,1},{13,5},{2,10},{6,14},... | collective-permute-start | bytes 393224 | tf_op jit(solution)/shard_map/ppermute | solution.py:271
  43.2 8.5 %collective-permute-start.11 = (bf16[512,128]{1,0:T(8,128)(2,1)S(1)}, bf16[512,128]{1,0:T(8,128)(2,1)S(1)}, u32[]{:S(2)}, u32[]{:S(2)}) collective-permute-start(bf16[512,128]{1,0:T(8,128)(2,1)S(1)} %collective-permute-done.6.refs_0_), channel_id=1, source_target_pairs={{0,12},{4,8},{8,4},{12,0},{1,13},{5,9},{9,5},{13,1},{2,14},{6,10},... | collective-permute-start | bytes 393224 | tf_op jit(solution)/shard_map/ppermute | solution.py:271
  46.0 5.7 %collective-permute-start.9 = (bf16[512,128]{1,0:T(8,128)(2,1)S(1)}, bf16[512,128]{1,0:T(8,128)(2,1)S(1)}, u32[]{:S(2)}, u32[]{:S(2)}) collective-permute-start(bf16[512,128]{1,0:T(8,128)(2,1)S(1)} %collective-permute-done.6.refs_0_), channel_id=1, source_target_pairs={{0,4},{4,0},{8,12},{12,8},{1,5},{5,1},{9,13},{13,9},{2,6},{6,2},{1... | collective-permute-start | bytes 393224 | tf_op jit(solution)/shard_map/ppermute | solution.py:271
  46.0 7.9 %copy-start.1 = (s32[1,4]{1,0:T(1,128)S(1)}, s32[1,4]{1,0:T(1,128)}, u32[]{:S(2)}) copy-start(s32[1,4]{1,0:T(1,128)} %far_ids.1) | copy-start | bytes 52

commit v15 on v10

--- a/solution.py
+++ b/solution.py
@@ -22,11 +22,11 @@
 
 
 def turn_of(leaf, inner_size):
-    return (3 * leaf + 2) % inner_size
+    return (leaf + inner_size - 1) % inner_size
 
 
 def carrier(turn, inner_size):
-    return lax.rem((turn + inner_size - 2 % inner_size) * pow(3, -1, inner_size), inner_size)
+    return lax.rem(turn + 1, inner_size)
 
 
 def dot(a, b):
@@ -50,7 +50,7 @@
     )
 
 
-def up_kernel(x_ref, basis_ref, leaf_map_ref, mid_map_ref, out_ref, relay, x, basis, leaf_map, mid_map, skeleton, sems):
+def up_kernel(x_ref, basis_ref, leaf_map_ref, mid_map_ref, out_ref, x, basis, leaf_map, mid_map, skeleton, sems):
     leaves, rank, rows = basis.shape
     parts = []
     for leaf in range(leaves):
@@ -58,9 +58,7 @@
         parts.append(pltpu.make_async_copy(x_ref.at[here], x.at[here], sems.at[leaf]))
         parts.append(pltpu.make_async_copy(basis_ref.at[leaf], basis.at[leaf], sems.at[leaves + leaf]))
     maps = [pltpu.make_async_copy(leaf_map_ref, leaf_map, sems.at[2 * leaves]), pltpu.make_async_copy(mid_map_ref, mid_map, sems.at[2 * leaves + 1])]
-    edge = jnp.where(lax.axis_index("inner") == 0, x.shape[0] - relay.shape[0], 0)
-    handed = pltpu.make_async_copy(x_ref.at[pl.ds(pl.multiple_of(edge, rows), relay.shape[0])], relay, sems.at[2 * leaves + 2])
-    for copy in [*parts, *maps, handed]:
+    for copy in parts + maps:
         copy.start()
     for leaf in range(leaves):
         parts[2 * leaf].wait()
@@ -71,7 +69,6 @@
     mid = dot_t(leaf_map[...], skeleton[...]).astype(jnp.bfloat16)
     out_ref[:rank, :] = mid
     out_ref[rank:, :] = dot_t(mid_map[...], mid).astype(jnp.bfloat16)
-    handed.wait()
 
 
 def pieces_kernel(x_ref, relayed, *refs):
@@ -97,7 +94,8 @@
 
 
 def down_kernel(leaf_size, inner_size, far_ids, far_count, plane, *refs):
-    found, (couple, mid_couple, mid_map, leaf_map, basis, _, out_ref, planes) = refs[:inner_size], refs[inner_size:]
+    found, refs = refs[:inner_size], refs[inner_size:]
+    couple, mid_couple, mid_map, leaf_map, basis, _, total_ref, planes = refs
     rank = mid_map.shape[0]
     size = 2 * rank
     for step, part in enumerate(found):
@@ -122,13 +120,13 @@
         partner = jnp.where(live, far_ids[0, slot], group * inner_size)
         other, turn = partner // inner_size, inner ^ lax.rem(partner, inner_size)
         step = (group & (inner_size - 1)) ^ carrier(turn, inner_size)
-        near, far = plane[at_of(0, group ^ other), :], planes[at_of(step, group ^ step ^ other), :]
-        term = dot(mid_couple[slot], jnp.where(turn == 0, near, far))
+        here, there = plane[at_of(0, group ^ other), :], planes[at_of(step, group ^ step ^ other), :]
+        term = dot(mid_couple[slot], jnp.where(turn == 0, here, there))
         total += jnp.where(live, term, 0.0)
     leaf_down = dot(leaf_map[...], total.astype(jnp.bfloat16)).astype(jnp.bfloat16)
     leaves, _, rows = basis.shape
     for leaf in range(leaves):
-        out_ref[leaf * rows : (leaf + 1) * rows, :] += dot_t(basis[leaf], leaf_down[leaf * rank : (leaf + 1) * rank, :])
+        total_ref[leaf * rows : (leaf + 1) * rows, :] += dot_t(basis[leaf], leaf_down[leaf * rank : (leaf + 1) * rank, :])
 
 
 def listed(ids_ref, lists, kind_of):
@@ -152,27 +150,32 @@
 def add_products(near, kind, count, blocks, x_ref, total, arrived=lambda slot: None):
     slots, places = kind
     rows = blocks.shape[1]
+    half = rows // 2
 
     def product(i):
         slot = slots[i]
         arrived(slot)
         at = pl.ds(pl.multiple_of(places[i] * rows, rows), rows)
-        here = pl.ds(pl.multiple_of(slot // near * rows, rows), rows)
-        return here, dot(blocks[slot], x_ref[at, :])
+        here = slot // near * rows
+        partner = x_ref[at, :]
+        return here, [dot(blocks[slot, :half, :], partner), dot(blocks[slot, half:, :], partner)]
+
+    def add(start, terms):
+        for i, term in enumerate(terms):
+            total[pl.ds(pl.multiple_of(start + i * half, half), half), :] += term
 
     def pair(j, carry):
         one, first = product(2 * j)
         two, second = product(2 * j + 1)
-        total[one, :] += first
-        total[two, :] += second
+        add(one, first)
+        add(two, second)
         return carry
 
     lax.fori_loop(0, count // 2, pair, 0)
 
     @pl.when(lax.rem(count, 2) == 1)
     def _():
-        here, term = product(count - 1)
-        total[here, :] += term
+        add(*product(count - 1))
 
 
 def own_kernel(ids_ref, x_hbm, blocks_ref, *refs):
@@ -284,19 +287,20 @@
 
     ahead, back = lax.slice_in_dim(anomalies, rest * rows, leaves * rows), lax.slice_in_dim(anomalies, 0, one * rows)
     x_up, ahead, back = lax.optimization_barrier((anomalies, ahead, back))
+    relay = jnp.where(inner == first, lax.slice_in_dim(x_up, one * rows, leaves * rows), lax.slice_in_dim(x_up, 0, rest * rows))
+    relayed = passed(relay, hop)
     halo = [(passed(ahead, chain), passed(back, [(j, i) for i, j in chain]))]
 
     maps = (transfer_leaf.reshape(leaves * rank, rank), transfer_mid.reshape(rank, rank))
     operands = (x_up, leaf_basis, *maps)
     piece = jax.ShapeDtypeStruct((rest * rows, columns), bf16)
-    part, relay = kernel(
+    part = kernel(
         up_kernel,
-        (jax.ShapeDtypeStruct((2 * rank, columns), bf16), piece),
+        jax.ShapeDtypeStruct((2 * rank, columns), bf16),
         [ANY] * 4,
-        (VMEM, VMEM),
-        [pltpu.VMEM(x.shape, bf16) for x in operands] + [pltpu.VMEM((leaves * rank, columns), bf16), pltpu.SemaphoreType.DMA((2 * leaves + 3,))],
+        VMEM,
+        [pltpu.VMEM(x.shape, bf16) for x in operands] + [pltpu.VMEM((leaves * rank, columns), bf16), pltpu.SemaphoreType.DMA((2 * leaves + 2,))],
     )(*[held(x, pltpu.HBM) for x in operands])
-    relayed = passed(relay, hop)
     parts = [part] + [swapped(part, reach) for reach in groups[1:]]
     slots = leaves * near
     parts, x_late, relayed = lax.optimization_barrier((parts, x_up, relayed))
@@ -338,7 +342,7 @@
     total = kernel(
         functools.partial(down_kernel, leaf_size, inner_size),
         wide,
-        [SMEM, SMEM] + [VMEM] * (7 + inner_size),
+        [SMEM] * 2 + [VMEM] * (7 + inner_size),
         VMEM,
         [pltpu.VMEM((inner_size * leaf_size * 2 * rank, columns), bf16)],
         aliases={8 + inner_size: 0},

time: 57 us -> 56.9 us (level)
  the two profiles are of different devices: /device:TPU:0 before, /device:TPU:9 now
where the time goes in v15:
time: 56.9 us; the launch traced here: 56.3 us
  starting transfers between devices  28.1 us (49%)
  Pallas kernels  21.3 us (37%)
  waiting for transfers between devices  3.68 us (6%)
  local copies, waits for them, and re-layouts  2.31 us (4%)
  between operations  0.82 us (1%)
    ppermute x6, starting transfers between devices, passed(): return lax.ppermute(x, ('leaf', 'inner'), pairs)  14.8 us
    ppermute x6, starting transfers between devices, swapped(): return lax.ppermute(x, 'leaf', [(i, i ^ reach) for i in groups])  13.4 us
    pallas_call x1, Pallas kernels, local(): kernel(own_kernel, [wide, resident(slots, rows, rows)] + [resident(*x.sha...  9.19 us
    pallas_call x1, Pallas kernels, local(): kernel(functools.partial(wave_kernel, one), wide, [SMEM] + [VMEM] * 4, VM...  4.21 us
    ppermute x6, waiting for transfers between devices, swapped(): return lax.ppermute(x, 'leaf', [(i, i ^ reach) for i in groups])  3.58 us
    pallas_call x1, Pallas kernels, local(): kernel(up_kernel, jax.ShapeDtypeStruct((2 * rank, columns), bf16), [ANY]...  2.69 us
    pallas_call x1, Pallas kernels, local(): kernel(functools.partial(last_kernel, one), (jax.ShapeDtypeStruct(anomali...  2.65 us
    slice x1, local copies, waits for them, and re-layouts, local(): lax.slice_in_dim(anomalies, 0, one * rows)  2.29 us
  transfers between devices with their start and end apart: 12, of which 4 were waited for; matrix products, arithmetic and copies ran while one was open for 0% of the time, Pallas kernels for 33%

profile of v15, /device:TPU:9, one launch (start us, length us, event | category | flops | bytes accessed | tf_op | source)
XLA Modules:
  0.0 56.3 jit_solution(8966106393100105785)
XLA Ops:
  0.0 0.0 copy-start.2
  0.0 2.3 %fusion = (bf16[2560,128]{1,0:T(8,128)(2,1)S(1)}, bf16[2560,128]{1,0:T(8,128)(2,1)}) fusion(bf16[4096,128]{1,0:T(8,128)(2,1)} %x_hbm), kind=kLoop, calls=%fused_computation.1 | loop fusion | bytes 2621440 | tf_op jit(solution)/shard_map/slice | solution.py:288
  2.3 3.2 %collective-permute-start.7 = (bf16[2560,128]{1,0:T(8,128)(2,1)}, bf16[2560,128]{1,0:T(8,128)(2,1)S(1)}, u32[]{:S(2)}, u32[]{:S(2)}) collective-permute-start(bf16[2560,128]{1,0:T(8,128)(2,1)} %get-tuple-element.54), channel_id=1, source_target_pairs={{0,1},{1,2},{2,3},{3,4},{4,5},{5,6},{6,7},{7,8},{8,9},{9,10},{10,1... | collective-permute-start | bytes 1966088 | tf_op jit(solution)/shard_map/ppermute | solution.py:274
  5.5 2.1 %collective-permute-start.8 = (bf16[2560,128]{1,0:T(8,128)(2,1)S(1)}, bf16[2560,128]{1,0:T(8,128)(2,1)S(1)}, u32[]{:S(2)}, u32[]{:S(2)}) collective-permute-start(bf16[2560,128]{1,0:T(8,128)(2,1)S(1)} %get-tuple-element.55), channel_id=1, source_target_pairs={{1,0},{2,1},{3,2},{4,3},{5,4},{6,5},{7,6},{8,7},{9,8},{10,9},{11,1... | collective-permute-start | bytes 1966088 | tf_op jit(solution)/shard_map/ppermute | solution.py:274
  7.6 0.0 copy-done.2
  7.6 0.0 copy-start
  7.7 0.7 %collective-permute-start.3 = (bf16[1536,128]{1,0:T(8,128)(2,1)S(1)}, bf16[1536,128]{1,0:T(8,128)(2,1)S(1)}, u32[]{:S(2)}, u32[]{:S(2)}) collective-permute-start(bf16[1536,128]{1,0:T(8,128)(2,1)S(1)} %slice_select_fusion), channel_id=1, source_target_pairs={{3,7},{7,11},{11,15},{4,0},{8,4},{12,8},{19,23},{23,27},{27,31},{2... | collective-permute-start | bytes 1179656 | tf_op jit(solution)/shard_map/ppermute | solution.py:274
  8.4 2.7 %shard_map.100.refs_0_ = bf16[128,128]{1,0:T(8,128)(2,1)S(1)} custom-call(bf16[4096,128]{1,0:T(8,128)(2,1)} %x_hbm, bf16[8,64,512]{2,1,0:T(8,128)(2,1)} %refs_4_.1, bf16[512,64]{1,0:T(8,128)(2,1)} %bitcast.6, bf16[64,64]{1,0:T(8,128)(2,1)} %bitcast.10), custom_call_target="tpu_custom_call" | custom-call | flops 1000 | bytes 1000 | tf_op jit(solution)/shard_map/pallas_call | solution.py:297
  11.1 1.3 %collective-permute-start = (bf16[128,128]{1,0:T(8,128)(2,1)S(1)}, bf16[128,128]{1,0:T(8,128)(2,1)S(1)}, u32[]{:S(2)}, u32[]{:S(2)}) collective-permute-start(bf16[128,128]{1,0:T(8,128)(2,1)S(1)} %shard_map.100.refs_0_), channel_id=1, source_target_pairs={{0,4},{4,0},{8,12},{12,8},{1,5},{5,1},{9,13},{13,9},{2,6},{6,2},{1... | collective-permute-start | bytes 98312 | tf_op jit(solution)/shard_map/ppermute | solution.py:277
  12.4 1.2 %collective-permute-start.1 = (bf16[128,128]{1,0:T(8,128)(2,1)S(1)}, bf16[128,128]{1,0:T(8,128)(2,1)S(1)}, u32[]{:S(2)}, u32[]{:S(2)}) collective-permute-start(bf16[128,128]{1,0:T(8,128)(2,1)S(1)} %shard_map.100.refs_0_), channel_id=1, source_target_pairs={{0,8},{4,12},{8,0},{12,4},{1,9},{5,13},{9,1},{13,5},{2,10},{6,14},... | collective-permute-start | bytes 98312 | tf_op jit(solution)/shard_map/ppermute | solution.py:277
  13.6 0.0 collective-permute-done.refs_1_
  13.6 1.1 %collective-permute-start.2 = (bf16[128,128]{1,0:T(8,128)(2,1)S(1)}, bf16[128,128]{1,0:T(8,128)(2,1)S(1)}, u32[]{:S(2)}, u32[]{:S(2)}) collective-permute-start(bf16[128,128]{1,0:T(8,128)(2,1)S(1)} %shard_map.100.refs_0_), channel_id=1, source_target_pairs={{0,12},{4,8},{8,4},{12,0},{1,13},{5,9},{9,5},{13,1},{2,14},{6,10},... | collective-permute-start | bytes 98312 | tf_op jit(solution)/shard_map/ppermute | solution.py:277
  14.7 0.8 %collective-permute-done.1.refs_2_ = bf16[128,128]{1,0:T(8,128)(2,1)S(1)} collective-permute-done((bf16[128,128]{1,0:T(8,128)(2,1)S(1)}, bf16[128,128]{1,0:T(8,128)(2,1)S(1)}, u32[]{:S(2)}, u32[]{:S(2)}) %collective-permute-start.1) | collective-permute-done | bytes 32800 | tf_op jit(solution)/shard_map/ppermute | solution.py:277
  15.5 1.8 %collective-permute-done.2.refs_3_ = bf16[128,128]{1,0:T(8,128)(2,1)S(1)} collective-permute-done((bf16[128,128]{1,0:T(8,128)(2,1)S(1)}, bf16[128,128]{1,0:T(8,128)(2,1)S(1)}, u32[]{:S(2)}, u32[]{:S(2)}) %collective-permute-start.2) | collective-permute-done | bytes 32800 | tf_op jit(solution)/shard_map/ppermute | solution.py:277
  17.2 0.0 collective-permute-done.3.relayed
  17.2 1.1 %shard_map.101 = (bf16[1536,128]{1,0:T(8,128)(2,1)S(1)}, bf16[1536,128]{1,0:T(8,128)(2,1)S(1)}, bf16[512,128]{1,0:T(8,128)(2,1)S(1)}) custom-call(bf16[4096,128]{1,0:T(8,128)(2,1)} %x_hbm, bf16[1536,128]{1,0:T(8,128)(2,1)S(1)} %collective-permute-done.3.relayed, bf16[128,128]{1,0:T(8,128)(2,1)S(1)} %shard_map.100.refs_0_, ...), custom_call_target="tpu_custom_call" | custom-call | flops 1000 | bytes 1000 | tf_op jit(solution)/shard_map/pallas_call | solution.py:307
  18.4 0.7 %collective-permute-start.6 = (bf16[512,128]{1,0:T(8,128)(2,1)S(1)}, bf16[512,128]{1,0:T(8,128)(2,1)S(1)}, u32[]{:S(2)}, u32[]{:S(2)}) collective-permute-start(bf16[512,128]{1,0:T(8,128)(2,1)S(1)} %get-tuple-element.53.plane), channel_id=1, source_target_pairs={{0,3},{1,2},{2,1},{3,0},{8,9},{9,8},{10,11},{11,10},{12,14},{13,15... | collective-permute-start | bytes 393224 | tf_op jit(solution)/shard_map/ppermute | solution.py:274
  19.7 3.2 %collective-permute-start.4 = (bf16[1536,128]{1,0:T(8,128)(2,1)S(1)}, bf16[1536,128]{1,0:T(8,128)(2,1)S(1)}, u32[]{:S(2)}, u32[]{:S(2)}) collective-permute-start(bf16[1536,128]{1,0:T(8,128)(2,1)S(1)} %get-tuple-element.49), channel_id=1, source_target_pairs={{0,1},{1,2},{2,3},{4,5},{5,6},{6,7},{8,9},{9,10},{10,11},{12,13},{... | collective-permute-start | bytes 1179656 | tf_op jit(solution)/shard_map/ppermute | solution.py:274
  22.9 4.9 %collective-permute-start.5 = (bf16[1536,128]{1,0:T(8,128)(2,1)S(1)}, bf16[1536,128]{1,0:T(8,128)(2,1)S(1)}, u32[]{:S(2)}, u32[]{:S(2)}) collective-permute-start(bf16[1536,128]{1,0:T(8,128)(2,1)S(1)} %get-tuple-element.50), channel_id=1, source_target_pairs={{1,0},{2,1},{3,2},{5,4},{6,5},{7,6},{9,8},{10,9},{11,10},{13,12},{... | collective-permute-start | bytes 1179656 | tf_op jit(solution)/shard_map/ppermute | solution.py:274
  27.9 0.0 copy-done
  27.9 9.2 %shard_map.102 = (f32[4096,128]{1,0:T(8,128)S(1)}, bf16[40,512,512]{2,1,0:T(8,128)(2,1)S(1)}, bf16[4,64,64]{2,1,0:T(8,128)(2,1)S(1)}, bf16[4,64,64]{2,1,0:T(8,12...) custom-call(s32[8,5]{1,0:T(8,128)S(1)} %copy-done, ...), custom_call_target="tpu_custom_call" | custom-call | flops 1000 | bytes 1000 | tf_op jit(solution)/shard_map/pallas_call | solution.py:326
  37.1 0.0 collective-permute-done.6.refs_0_
  37.1 0.0 collective-permute-done.7.before
  37.1 0.1 collective-permute-done.8.after
  37.2 6.0 %collective-permute-start.10 = (bf16[512,128]{1,0:T(8,128)(2,1)S(1)}, bf16[512,128]{1,0:T(8,128)(2,1)S(1)}, u32[]{:S(2)}, u32[]{:S(2)}) collective-permute-start(bf16[512,128]{1,0:T(8,128)(2,1)S(1)} %collective-permute-done.6.refs_0_), channel_id=1, source_target_pairs={{0,8},{4,12},{8,0},{12,4},{1,9},{5,13},{9,1},{13,5},{2,10},{6,14},... | collective-permute-start | bytes 393224 | tf_op jit(solution)/shard_map/ppermute | solution.py:277
  43.1 3.8 %collective-permute-start.11 = (bf16[512,128]{1,0:T(8,128)(2,1)S(1)}, bf16[512,128]{1,0:T(8,128)(2,1)S(1)}, u32[]{:S(2)}, u32[]{:S(2)}) collective-permute-start(bf16[512,128]{1,0:T(8,128)(2,1)S(1)} %collective-permute-done.6.refs_0_), channel_id=1, source_target_pairs={{0,12},{4,8},{8,4},{12,0},{1,13},{5,9},{9,5},{13,1},{2,14},{6,10},... | collective-permute-start | bytes 393224 | tf_op jit(solution)/shard_map/ppermute | solution.py:277
  46.9 0.0 collective-permute-start.9
  46.9 0.0 copy-start.1
  46.9 4.2 %shard_map.103.refs_9_ = f32[4096,128]{1,0:T(8,128)S(1)} custom-call(s32[8,5]{1,0:T(8,128)S(1)} %copy-done, bf16[2560,128]{1,0:T(8,128)(2,1)S(1)} %collective-permute-done.7.before, bf16[2560,128]{1,0:T(8,128)(2,1)S(1)} %collective-permute-done.8.after, bf16[40,512,512]{2,1,0:T(8,128)(2,1)S(1)} %get-tuple-element.52.blocks, ...), custom_call_target="tpu_custom_call", output_to_operand_aliasing={{}: (4, {})} | custom-call | flops 10000000000 | bytes 1000 | tf_op jit(solution)/shard_map/pallas_call | solution.py:338
  51.2 0.0 collective-permute-done.10.refs_2_
  51.2 1.0 %collective-permute-done.11.refs_3_ = bf16[512,128]{1,0:T(8,128)(2,1)S(1)} collective-permute-done((bf16[512,128]{1,0:T(8,128)(2,1)S(1)}, bf16[512,128]{1,0:T(8,128)(2,1)S(1)}, u32[]{:S(2)}, u32[]{:S(2)}) %collective-permute-start.11) | collective-permute-done | bytes 131104 | tf_op jit(solution)/shard_map/ppermute | solution.py:277
  52.2 0.0 collective-permute-done.9.refs_1_
  52.2 0.0 copy-done.1
  52.2 1.4 %shard_map.104._ = f32[4096,128]{1,0:T(8,128)S(1)} custom-call(s32[1,4]{1,0:T(1,128)S(1)} %copy-done.1, s32[1]{0:T(128)S(6)} %copy.17.far_count, bf16[512,128]{1,0:T(8,128)(2,1)S(1)} %get-tuple-element.53.plane, bf16[512,128]{1,0:T(8,128)(2,1)S(1)} %collective-permute-done.6.refs_0_, ...), custom_call_target="tpu_custom_call", output_to_operand_aliasing={{}: (12, {})} | custom-call | flops 1000 | bytes 1000 | tf_op jit(solution)/shard_map/pallas_call | solution.py:342
  53.6 0.0 collective-permute-done.4.before
  53.6 0.0 collective-permute-done.5.after
  53.6 2.7 %shard_map.105 = (bf16[4096,128]{1,0:T(8,128)(2,1)}, f32[4096,128]{1,0:T(8,128)S(1)}) custom-call(s32[8,5]{1,0:T(8,128)S(1)} %copy-done, bf16[1536,128]{1,0:T(8,128)(2,1)S(1)} %collective-permute-done.4.before, bf16[1536,128]{1,0:T(8,128)(2,1)S(1)} %collective-permute-done.5.after, ...), custom_call_target="tpu_custom_call", output_to_operand_aliasing={{1}: (4, {})} | custom-call | flops 1000 | bytes 1000 | tf_op jit(solution)/shard_map/pallas_call | solution.py:350
  (1 shorter events, 0.0 us)
Async XLA Ops:
  0.0 7.6 %copy-start.2 = (bf16[4096,128]{1,0:T(8,128)(2,1)S(1)}, bf16[4096,128]{1,0:T(8,128)(2,1)}, u32[]{:S(2)}) copy-start(bf16[4096,128]{1,0:T(8,128)(2,1)} %x_hbm) | copy-start | bytes 3145732
  2.3 34.8 %collective-permute-start.7 = (bf16[2560,128]{1,0:T(8,128)(2,1)}, bf16[2560,128]{1,0:T(8,128)(2,1)S(1)}, u32[]{:S(2)}, u32[]{:S(2)}) collective-permute-start(bf16[2560,128]{1,0:T(8,128)(2,1)} %get-tuple-element.54), channel_id=1, source_target_pairs={{0,1},{1,2},{2,3},{3,4},{4,5},{5,6},{6,7},{7,8},{8,9},{9,10},{10,1... | collective-permute-start | bytes 1966088 | tf_op jit(solution)/shard_map/ppermute | solution.py:274
  5.5 31.7 %collective-permute-start.8 = (bf16[2560,128]{1,0:T(8,128)(2,1)S(1)}, bf16[2560,128]{1,0:T(8,128)(2,1)S(1)}, u32[]{:S(2)}, u32[]{:S(2)}) collective-permute-start(bf16[2560,128]{1,0:T(8,128)(2,1)S(1)} %get-tuple-element.55), channel_id=1, source_target_pairs={{1,0},{2,1},{3,2},{4,3},{5,4},{6,5},{7,6},{8,7},{9,8},{10,9},{11,1... | collective-permute-start | bytes 1966088 | tf_op jit(solution)/shard_map/ppermute | solution.py:274
  7.6 20.3 %copy-start = (s32[8,5]{1,0:T(8,128)S(1)}, s32[8,5]{1,0:T(8,128)}, u32[]{:S(2)}) copy-start(s32[8,5]{1,0:T(8,128)} %ids_ref.5) | copy-start | bytes 484
  7.7 9.6 %collective-permute-start.3 = (bf16[1536,128]{1,0:T(8,128)(2,1)S(1)}, bf16[1536,128]{1,0:T(8,128)(2,1)S(1)}, u32[]{:S(2)}, u32[]{:S(2)}) collective-permute-start(bf16[1536,128]{1,0:T(8,128)(2,1)S(1)} %slice_select_fusion), channel_id=1, source_target_pairs={{3,7},{7,11},{11,15},{4,0},{8,4},{12,8},{19,23},{23,27},{27,31},{2... | collective-permute-start | bytes 1179656 | tf_op jit(solution)/shard_map/ppermute | solution.py:274
  11.1 2.6 %collective-permute-start = (bf16[128,128]{1,0:T(8,128)(2,1)S(1)}, bf16[128,128]{1,0:T(8,128)(2,1)S(1)}, u32[]{:S(2)}, u32[]{:S(2)}) collective-permute-start(bf16[128,128]{1,0:T(8,128)(2,1)S(1)} %shard_map.100.refs_0_), channel_id=1, source_target_pairs={{0,4},{4,0},{8,12},{12,8},{1,5},{5,1},{9,13},{13,9},{2,6},{6,2},{1... | collective-permute-start | bytes 98312 | tf_op jit(solution)/shard_map/ppermute | solution.py:277
  12.4 3.1 %collective-permute-start.1 = (bf16[128,128]{1,0:T(8,128)(2,1)S(1)}, bf16[128,128]{1,0:T(8,128)(2,1)S(1)}, u32[]{:S(2)}, u32[]{:S(2)}) collective-permute-start(bf16[128,128]{1,0:T(8,128)(2,1)S(1)} %shard_map.100.refs_0_), channel_id=1, source_target_pairs={{0,8},{4,12},{8,0},{12,4},{1,9},{5,13},{9,1},{13,5},{2,10},{6,14},... | collective-permute-start | bytes 98312 | tf_op jit(solution)/shard_map/ppermute | solution.py:277
  13.6 3.6 %collective-permute-start.2 = (bf16[128,128]{1,0:T(8,128)(2,1)S(1)}, bf16[128,128]{1,0:T(8,128)(2,1)S(1)}, u32[]{:S(2)}, u32[]{:S(2)}) collective-permute-start(bf16[128,128]{1,0:T(8,128)(2,1)S(1)} %shard_map.100.refs_0_), channel_id=1, source_target_pairs={{0,12},{4,8},{8,4},{12,0},{1,13},{5,9},{9,5},{13,1},{2,14},{6,10},... | collective-permute-start | bytes 98312 | tf_op jit(solution)/shard_map/ppermute | solution.py:277
  18.4 18.7 %collective-permute-start.6 = (bf16[512,128]{1,0:T(8,128)(2,1)S(1)}, bf16[512,128]{1,0:T(8,128)(2,1)S(1)}, u32[]{:S(2)}, u32[]{:S(2)}) collective-permute-start(bf16[512,128]{1,0:T(8,128)(2,1)S(1)} %get-tuple-element.53.plane), channel_id=1, source_target_pairs={{0,3},{1,2},{2,1},{3,0},{8,9},{9,8},{10,11},{11,10},{12,14},{13,15... | collective-permute-start | bytes 393224 | tf_op jit(solution)/shard_map/ppermute | solution.py:274
  19.7 33.9 %collective-permute-start.4 = (bf16[1536,128]{1,0:T(8,128)(2,1)S(1)}, bf16[1536,128]{1,0:T(8,128)(2,1)S(1)}, u32[]{:S(2)}, u32[]{:S(2)}) collective-permute-start(bf16[1536,128]{1,0:T(8,128)(2,1)S(1)} %get-tuple-element.49), channel_id=1, source_target_pairs={{0,1},{1,2},{2,3},{4,5},{5,6},{6,7},{8,9},{9,10},{10,11},{12,13},{... | collective-permute-start | bytes 1179656 | tf_op jit(solution)/shard_map/ppermute | solution.py:274
  22.9 30.7 %collective-permute-start.5 = (bf16[1536,128]{1,0:T(8,128)(2,1)S(1)}, bf16[1536,128]{1,0:T(8,128)(2,1)S(1)}, u32[]{:S(2)}, u32[]{:S(2)}) collective-permute-start(bf16[1536,128]{1,0:T(8,128)(2,1)S(1)} %get-tuple-element.50), channel_id=1, source_target_pairs={{1,0},{2,1},{3,2},{5,4},{6,5},{7,6},{9,8},{10,9},{11,10},{13,12},{... | collective-permute-start | bytes 1179656 | tf_op jit(solution)/shard_map/ppermute | solution.py:274
  37.2 14.0 %collective-permute-start.10 = (bf16[512,128]{1,0:T(8,128)(2,1)S(1)}, bf16[512,128]{1,0:T(8,128)(2,1)S(1)}, u32[]{:S(2)}, u32[]{:S(2)}) collective-permute-start(bf16[512,128]{1,0:T(8,128)(2,1)S(1)} %collective-permute-done.6.refs_0_), channel_id=1, source_target_pairs={{0,8},{4,12},{8,0},{12,4},{1,9},{5,13},{9,1},{13,5},{2,10},{6,14},... | collective-permute-start | bytes 393224 | tf_op jit(solution)/shard_map/ppermute | solution.py:277
  43.1 9.0 %collective-permute-start.11 = (bf16[512,128]{1,0:T(8,128)(2,1)S(1)}, bf16[512,128]{1,0:T(8,128)(2,1)S(1)}, u32[]{:S(2)}, u32[]{:S(2)}) collective-permute-start(bf16[512,128]{1,0:T(8,128)(2,1)S(1)} %collective-permute-done.6.refs_0_), channel_id=1, source_target_pairs={{0,12},{4,8},{8,4},{12,0},{1,13},{5,9},{9,5},{13,1},{2,14},{6,10},... | collective-permute-start | bytes 393224 | tf_op jit(solution)/shard_map/ppermute | solution.py:277
  46.9 5.3 %collective-permute-start.9 = (bf16[512,128]{1,0:T(8,128)(2,1)S(1)}, bf16[512,128]{1,0:T(8,128)(2,1)S(1)}, u32[]{:S(2)}, u32[]{:S(2)}) collective-permute-start(bf16[512,128]{1,0:T(8,128)(2,1)S(1)} %collective-permute-done.6.refs_0_), channel_id=1, source_target_pairs={{0,4},{4,0},{8,12},{12,8},{1,5},{5,1},{9,13},{13,9},{2,6},{6,2},{1... | collective-permute-start | bytes 393224 | tf_op jit(solution)/shard_map/ppermute | solution.py:277
  46.9 5.3 %copy-start.1 = (s32[1,4]{1,0:T(1,128)S(1)}, s32[1,4]{1,0:T(1,128)}, u32[]{:S(2)}) copy-start(s32[1,4]{1,0:T(1,128)} %far_ids.1) | copy-start | bytes 52
